TPU v7x, 32 devices: a whole 2x2x4 slice. The times are simulated.
32 devices in a mesh: seq: 4 (over y, x), ctx: 4 (over z), fsdp: 2 (over core).
Axes of the slice: x: 2, y: 2, z: 4, core: 2. Of those that a mesh axis runs over, the one named last changes fastest.
Arguments:
- block_input: bfloat16 [8, 2048, 896], P(('seq', 'fsdp'), 'ctx'), may hold values from -6 to 6
- segment_ids: int32 [8, 2048], P(('seq', 'fsdp')), may hold values from 0 to 3, as said below
- out_cotangent: bfloat16 [8, 2048, 896], P(('seq', 'fsdp'), 'ctx'), may hold values from -6 to 6
- input_gain: bfloat16 [896], P('fsdp'), may hold values from 0.5 to 1.5
- query_weight: bfloat16 [896, 896], P('fsdp'), may hold values from -0.1875 to 0.1875
- query_bias: bfloat16 [896], P('fsdp'), may hold values from -3 to 3
- key_weight: bfloat16 [896, 128], P('fsdp'), may hold values from -0.1875 to 0.1875
- key_bias: bfloat16 [128], P('fsdp'), may hold values from -3 to 3
- value_weight: bfloat16 [896, 128], P('fsdp'), may hold values from -0.1875 to 0.1875
- value_bias: bfloat16 [128], P('fsdp'), may hold values from -3 to 3
- output_weight: bfloat16 [896, 896], P('fsdp'), may hold values from -0.75 to 0.75
- middle_gain: bfloat16 [896], P('fsdp'), may hold values from 0.5 to 1.5
- gate_weight: bfloat16 [896, 4864], P('fsdp'), may hold values from -0.1875 to 0.1875
- up_weight: bfloat16 [896, 4864], P('fsdp'), may hold values from -0.1875 to 0.1875
- down_weight: bfloat16 [4864, 896], P('fsdp'), may hold values from -0.078125 to 0.078125
Outputs:
- block_output: bfloat16 [8, 2048, 896], P(('seq', 'fsdp'), 'ctx')
- input_grad: bfloat16 [8, 2048, 896], P(('seq', 'fsdp'), 'ctx')
- input_gain_grad: float32 [896], P('fsdp')
- query_weight_grad: float32 [896, 896], P('fsdp')
- query_bias_grad: float32 [896], P('fsdp')
- key_weight_grad: float32 [896, 128], P('fsdp')
- key_bias_grad: float32 [128], P('fsdp')
- value_weight_grad: float32 [896, 128], P('fsdp')
- value_bias_grad: float32 [128], P('fsdp')
- output_weight_grad: float32 [896, 896], P('fsdp')
- middle_gain_grad: float32 [896], P('fsdp')
- gate_weight_grad: float32 [896, 4864], P('fsdp')
- up_weight_grad: float32 [896, 4864], P('fsdp')
- down_weight_grad: float32 [4864, 896], P('fsdp')
Inputs may be any that keep to these rules, and one draw needn't show every extreme that they name: `segment_ids`: along each sequence the document numbers never fall; every sequence holds four documents 0, 1, 2, 3, and document 2 begins within the first 512 positions and ends within the last 512.
All inputs are finite; a program needn't handle non-finite values.
Results may differ from a plain program's by a relative error of at most 0.023.
Values may be sent and summed in bfloat16 or wider, within the bound.
No kernel may reach another device: no remote copies, remote signals or barrier semaphores. Data moves between devices by JAX's collectives and lax.ppermute only.
A program may use at most 320 MiB of HBM per device.

v0:
```python
import jax
import jax.numpy as jnp
from jax import lax
from jax.sharding import PartitionSpec as P

HQ = 14
KVH = 2
HD = 64
WINDOW = 1024


theta_base = 1000000.0
eps_norm = 1e-06


def rotate_half(values):
    half = values.shape[-1] // 2
    return jnp.concatenate([-values[..., half:], values[..., :half]], -1)


def rotate(values, cosine, sine):
    return values * cosine[:, None, :] + rotate_half(values) * sine[:, None, :]


def unrotate(grads, cosine, sine):
    return grads * cosine[:, None, :] - rotate_half(grads * sine[:, None, :])


def rms_scale(values):
    return lax.rsqrt(jnp.mean(values * values, -1, keepdims=True) + eps_norm)


def norm_back(grad_norm, normal, scale):
    return scale * (grad_norm - normal * jnp.mean(grad_norm * normal, -1, keepdims=True))


def on_device(
    block_input,
    segment_ids,
    out_cotangent,
    input_gain,
    query_weight,
    query_bias,
    key_weight,
    key_bias,
    value_weight,
    value_bias,
    output_weight,
    middle_gain,
    gate_weight,
    up_weight,
    down_weight,
):
    whole_params = (
        lax.all_gather(input_gain, "fsdp", axis=0, tiled=True),
        lax.all_gather(query_weight, "fsdp", axis=0, tiled=True),
        lax.all_gather(query_bias, "fsdp", axis=0, tiled=True),
        lax.all_gather(key_weight, "fsdp", axis=0, tiled=True),
        lax.all_gather(key_bias, "fsdp", axis=0, tiled=True),
        lax.all_gather(value_weight, "fsdp", axis=0, tiled=True),
        lax.all_gather(value_bias, "fsdp", axis=0, tiled=True),
        lax.all_gather(output_weight, "fsdp", axis=0, tiled=True),
        lax.all_gather(middle_gain, "fsdp", axis=0, tiled=True),
        lax.all_gather(gate_weight, "fsdp", axis=0, tiled=True),
        lax.all_gather(up_weight, "fsdp", axis=0, tiled=True),
        lax.all_gather(down_weight, "fsdp", axis=0, tiled=True),
    )
    (
        gain_one,
        w_query,
        b_query,
        w_key,
        b_key,
        w_value,
        b_value,
        w_output,
        gain_two,
        w_gate,
        w_up,
        w_down,
    ) = whole_params
    tokens = block_input[0].astype(jnp.float32)
    count = tokens.shape[0]
    length = segment_ids.shape[1]
    group = HQ // KVH
    kv_width = KVH * HD
    scale = HD ** (-0.5)
    cycle = lax.axis_index("ctx")
    first = cycle * count
    reach = min(WINDOW // count, lax.axis_size("ctx") - 1)
    span = (reach + 1) * count
    positions = (first + jnp.arange(count, dtype=jnp.int32)).astype(jnp.float32)
    inverse = theta_base ** (-jnp.arange(0, HD, 2, dtype=jnp.float32) / HD)
    angle = positions[:, None] * inverse[None, :]
    cosine = jnp.concatenate([jnp.cos(angle), jnp.cos(angle)], -1)
    sine = jnp.concatenate([jnp.sin(angle), jnp.sin(angle)], -1)
    scale_one = rms_scale(tokens)
    normal_one = tokens * scale_one
    gain_first = gain_one.astype(jnp.float32)
    normed_one = (normal_one * gain_first).astype(jnp.bfloat16)
    query_pre = jnp.dot(normed_one, w_query, preferred_element_type=jnp.float32) + b_query.astype(
        jnp.float32
    )
    key_pre = jnp.dot(normed_one, w_key, preferred_element_type=jnp.float32) + b_key.astype(
        jnp.float32
    )
    value_pre = jnp.dot(normed_one, w_value, preferred_element_type=jnp.float32) + b_value.astype(
        jnp.float32
    )
    query_rot = rotate(query_pre.reshape(count, HQ, HD), cosine, sine).astype(jnp.bfloat16)
    key_rot = rotate(key_pre.reshape(count, KVH, HD), cosine, sine).astype(jnp.bfloat16)
    value_low = value_pre.astype(jnp.bfloat16)
    own_pairs = jnp.concatenate([key_rot.reshape(count, kv_width), value_low], -1)
    whole_pairs = lax.all_gather(own_pairs, "ctx", axis=0, tiled=True)
    padded = jnp.concatenate(
        [jnp.zeros((reach * count, 2 * kv_width), jnp.bfloat16), whole_pairs], 0
    )
    pairs = lax.dynamic_slice_in_dim(padded, first, span, 0)
    seg_row = segment_ids[0]
    query_seg = lax.dynamic_slice_in_dim(seg_row, first, count, 0)
    seg_pad = jnp.concatenate([jnp.full((reach * count,), -1, jnp.int32), seg_row], 0)
    key_seg = lax.dynamic_slice_in_dim(seg_pad, first, span, 0)
    query_index = first + jnp.arange(count, dtype=jnp.int32)
    key_index = first - reach * count + jnp.arange(span, dtype=jnp.int32)
    distance = query_index[:, None] - key_index[None, :]
    visible = (
        (key_seg[None, :] == query_seg[:, None])
        & (key_index[None, :] >= 0)
        & (distance >= 0)
        & (distance < WINDOW)
    )
    key_window = pairs[:, :kv_width].reshape(span, KVH, HD).transpose(1, 0, 2)
    value_window = pairs[:, kv_width:].reshape(span, KVH, HD).transpose(1, 0, 2)
    query_groups = query_rot.reshape(count, KVH, group, HD).transpose(1, 0, 2, 3)

    def scores_of(query_g, key_g):
        raw = jnp.einsum("tgd,sd->gts", query_g, key_g, preferred_element_type=jnp.float32) * scale
        return jnp.where(visible[None], raw, -1e30)

    def attend_group(operands):
        query_g, key_g, value_g = operands
        scores = scores_of(query_g, key_g)
        top = jnp.max(scores, -1, keepdims=True)
        expo = jnp.exp(scores - top)
        total = jnp.sum(expo, -1, keepdims=True)
        weights_low = (expo / total).astype(jnp.bfloat16)
        mixed = jnp.einsum("gts,sd->tgd", weights_low, value_g, preferred_element_type=jnp.float32)
        return (mixed.astype(jnp.bfloat16), (top + jnp.log(total))[..., 0])

    mixed_all, log_totals = lax.map(attend_group, (query_groups, key_window, value_window))
    attn_low = mixed_all.transpose(1, 0, 2, 3).reshape(count, HQ * HD)
    branch = jnp.dot(attn_low, w_output, preferred_element_type=jnp.float32)
    hidden_one = tokens + branch
    scale_two = rms_scale(hidden_one)
    normal_two = hidden_one * scale_two
    gain_second = gain_two.astype(jnp.float32)
    normed_two = (normal_two * gain_second).astype(jnp.bfloat16)
    gate_pre = jnp.dot(normed_two, w_gate, preferred_element_type=jnp.float32)
    up_pre = jnp.dot(normed_two, w_up, preferred_element_type=jnp.float32)
    sigmoid_gate = jax.nn.sigmoid(gate_pre)
    activated = gate_pre * sigmoid_gate
    inner = (activated * up_pre).astype(jnp.bfloat16)
    result = hidden_one + jnp.dot(inner, w_down, preferred_element_type=jnp.float32)
    block_output = result.astype(jnp.bfloat16)[None]
    back_params = (
        lax.all_gather(input_gain, "fsdp", axis=0, tiled=True),
        lax.all_gather(query_weight, "fsdp", axis=0, tiled=True),
        lax.all_gather(query_bias, "fsdp", axis=0, tiled=True),
        lax.all_gather(key_weight, "fsdp", axis=0, tiled=True),
        lax.all_gather(key_bias, "fsdp", axis=0, tiled=True),
        lax.all_gather(value_weight, "fsdp", axis=0, tiled=True),
        lax.all_gather(value_bias, "fsdp", axis=0, tiled=True),
        lax.all_gather(output_weight, "fsdp", axis=0, tiled=True),
        lax.all_gather(middle_gain, "fsdp", axis=0, tiled=True),
        lax.all_gather(gate_weight, "fsdp", axis=0, tiled=True),
        lax.all_gather(up_weight, "fsdp", axis=0, tiled=True),
        lax.all_gather(down_weight, "fsdp", axis=0, tiled=True),
    )
    back_query, back_key, back_value, back_output = (
        back_params[1],
        back_params[3],
        back_params[5],
        back_params[7],
    )
    back_gate, back_up, back_down = (back_params[9], back_params[10], back_params[11])
    grad_out = out_cotangent[0].astype(jnp.float32)
    grad_low = out_cotangent[0]
    gw_down = jnp.einsum("tf,td->fd", inner, grad_low, preferred_element_type=jnp.float32)
    grad_inner = jnp.einsum("td,fd->tf", grad_low, back_down, preferred_element_type=jnp.float32)
    grad_gate = (
        grad_inner * up_pre * sigmoid_gate * (1.0 + gate_pre * (1.0 - sigmoid_gate))
    ).astype(jnp.bfloat16)
    grad_up = (grad_inner * activated).astype(jnp.bfloat16)
    gw_gate = jnp.einsum("td,tf->df", normed_two, grad_gate, preferred_element_type=jnp.float32)
    gw_up = jnp.einsum("td,tf->df", normed_two, grad_up, preferred_element_type=jnp.float32)
    grad_normed_two = jnp.einsum(
        "tf,df->td", grad_gate, back_gate, preferred_element_type=jnp.float32
    ) + jnp.einsum("tf,df->td", grad_up, back_up, preferred_element_type=jnp.float32)
    gg_two = jnp.sum(grad_normed_two * normal_two, 0)
    grad_hidden = grad_out + norm_back(grad_normed_two * gain_second, normal_two, scale_two)
    grad_branch = grad_hidden.astype(jnp.bfloat16)
    gw_output = jnp.einsum("tq,td->qd", attn_low, grad_branch, preferred_element_type=jnp.float32)
    grad_attn = jnp.einsum(
        "td,qd->tq", grad_branch, back_output, preferred_element_type=jnp.float32
    ).astype(jnp.bfloat16)
    grad_groups_in = grad_attn.reshape(count, KVH, group, HD).transpose(1, 0, 2, 3)

    def attend_back(operands):
        query_g, key_g, value_g, grad_g, log_g = operands
        scores = scores_of(query_g, key_g)
        weights_full = jnp.exp(scores - log_g[..., None])
        grad_value = jnp.einsum(
            "gts,tgd->sd",
            weights_full.astype(jnp.bfloat16),
            grad_g,
            preferred_element_type=jnp.float32,
        )
        grad_weights = jnp.einsum(
            "tgd,sd->gts", grad_g, value_g, preferred_element_type=jnp.float32
        )
        row_inner = jnp.sum(grad_weights * weights_full, -1, keepdims=True)
        grad_scores = (weights_full * (grad_weights - row_inner)).astype(jnp.bfloat16)
        grad_query = (
            jnp.einsum("gts,sd->tgd", grad_scores, key_g, preferred_element_type=jnp.float32)
            * scale
        )
        grad_key = (
            jnp.einsum("gts,tgd->sd", grad_scores, query_g, preferred_element_type=jnp.float32)
            * scale
        )
        return (grad_query, grad_key, grad_value)

    grad_query_all, grad_key_all, grad_value_all = lax.map(
        attend_back, (query_groups, key_window, value_window, grad_groups_in, log_totals)
    )
    grad_window = jnp.concatenate(
        [
            grad_key_all.transpose(1, 0, 2).reshape(span, kv_width),
            grad_value_all.transpose(1, 0, 2).reshape(span, kv_width),
        ],
        -1,
    )
    full_terms = jnp.zeros((reach * count + length, 2 * kv_width), jnp.float32)
    full_terms = lax.dynamic_update_slice_in_dim(full_terms, grad_window, first, 0)
    own_grads = lax.psum_scatter(
        lax.dynamic_slice_in_dim(full_terms, reach * count, lax.axis_size("ctx") * count, 0),
        "ctx",
        scatter_dimension=0,
        tiled=True,
    )
    grad_query_pre = (
        unrotate(grad_query_all.transpose(1, 0, 2, 3).reshape(count, HQ, HD), cosine, sine)
        .reshape(count, HQ * HD)
        .astype(jnp.bfloat16)
    )
    grad_key_pre = (
        unrotate(own_grads[:, :kv_width].reshape(count, KVH, HD), cosine, sine)
        .reshape(count, kv_width)
        .astype(jnp.bfloat16)
    )
    grad_value_low = own_grads[:, kv_width:].astype(jnp.bfloat16)
    gw_query = jnp.einsum(
        "td,tq->dq", normed_one, grad_query_pre, preferred_element_type=jnp.float32
    )
    gw_key = jnp.einsum("td,tq->dq", normed_one, grad_key_pre, preferred_element_type=jnp.float32)
    gw_value = jnp.einsum(
        "td,tq->dq", normed_one, grad_value_low, preferred_element_type=jnp.float32
    )
    gb_query = jnp.sum(grad_query_pre, 0, dtype=jnp.float32)
    gb_key = jnp.sum(grad_key_pre, 0, dtype=jnp.float32)
    gb_value = jnp.sum(grad_value_low, 0, dtype=jnp.float32)
    grad_normed_one = jnp.einsum(
        "tq,dq->td", grad_query_pre, back_query, preferred_element_type=jnp.float32
    )
    grad_normed_one = grad_normed_one + jnp.einsum(
        "tq,dq->td", grad_key_pre, back_key, preferred_element_type=jnp.float32
    )
    grad_normed_one = grad_normed_one + jnp.einsum(
        "tq,dq->td", grad_value_low, back_value, preferred_element_type=jnp.float32
    )
    gg_one = jnp.sum(grad_normed_one * normal_one, 0)
    grad_tokens = grad_hidden + norm_back(grad_normed_one * gain_first, normal_one, scale_one)
    input_grad = grad_tokens.astype(jnp.bfloat16)[None]
    shares = (
        lax.psum_scatter(gg_one, "fsdp", scatter_dimension=0, tiled=True),
        lax.psum_scatter(gw_query, "fsdp", scatter_dimension=0, tiled=True),
        lax.psum_scatter(gb_query, "fsdp", scatter_dimension=0, tiled=True),
        lax.psum_scatter(gw_key, "fsdp", scatter_dimension=0, tiled=True),
        lax.psum_scatter(gb_key, "fsdp", scatter_dimension=0, tiled=True),
        lax.psum_scatter(gw_value, "fsdp", scatter_dimension=0, tiled=True),
        lax.psum_scatter(gb_value, "fsdp", scatter_dimension=0, tiled=True),
        lax.psum_scatter(gw_output, "fsdp", scatter_dimension=0, tiled=True),
        lax.psum_scatter(gg_two, "fsdp", scatter_dimension=0, tiled=True),
        lax.psum_scatter(gw_gate, "fsdp", scatter_dimension=0, tiled=True),
        lax.psum_scatter(gw_up, "fsdp", scatter_dimension=0, tiled=True),
        lax.psum_scatter(gw_down, "fsdp", scatter_dimension=0, tiled=True),
    )
    totals = lax.psum(
        (
            shares[0],
            shares[1],
            shares[2],
            shares[3],
            shares[4],
            shares[5],
            shares[6],
            shares[7],
            shares[8],
            shares[9],
            shares[10],
            shares[11],
        ),
        ("seq", "ctx"),
    )
    return (
        block_output,
        input_grad,
        totals[0],
        totals[1],
        totals[2],
        totals[3],
        totals[4],
        totals[5],
        totals[6],
        totals[7],
        totals[8],
        totals[9],
        totals[10],
        totals[11],
    )


def solution(mesh):
    return jax.shard_map(
        on_device,
        mesh=mesh,
        in_specs=(
            P(("seq", "fsdp"), "ctx", None),
            P(("seq", "fsdp"), None),
            P(("seq", "fsdp"), "ctx", None),
            P("fsdp"),
            P("fsdp", None),
            P("fsdp"),
            P("fsdp", None),
            P("fsdp"),
            P("fsdp", None),
            P("fsdp"),
            P("fsdp", None),
            P("fsdp"),
            P("fsdp", None),
            P("fsdp", None),
            P("fsdp", None),
        ),
        out_specs=(
            P(("seq", "fsdp"), "ctx", None),
            P(("seq", "fsdp"), "ctx", None),
            P("fsdp"),
            P("fsdp", None),
            P("fsdp"),
            P("fsdp", None),
            P("fsdp"),
            P("fsdp", None),
            P("fsdp"),
            P("fsdp", None),
            P("fsdp"),
            P("fsdp", None),
            P("fsdp", None),
            P("fsdp", None),
        ),
        check_vma=False,
    )
```

profile of v0, /device:TPU:0, one launch (start us, length us, event | category | flops | bytes accessed | tf_op | source)
XLA Modules:
  0.0 1330.4 jit_solution(16679373320466361237)
XLA Ops:
  7.3 2.3 all_gather.49
  16.4 2.5 all-reduce.15
  20.4 2.3 all_gather.47
  23.4 1.7 convolution_add_fusion.3
  31.2 26.4 %all-gather.7.cloned.1.call-done = bf16[2048,256]{0,1:T(8,128)(2,1)} async-done(((bf16[512,256]{0,1:T(8,128)(2,1)}), bf16[2048,256]{0,1:T(8,128)(2,1)}) %all-gather.7.cloned.1.call-update) | async-done | bytes 1048592 | tf_op jit(solution)/shard_map/all_gather | solution.py:114
  57.6 1.8 pad_dynamic-slice_fusion.1
  59.4 9.1 all-gather.9.cloned.1.call-done
  68.6 3.9 convolution_add_fusion
  72.5 1.8 copy.48
  76.0 31.7 %while.28 = (s32[]{:T(128)}, bf16[2,512,7,64]{1,3,2,0:T(8,128)(2,1)}, f32[2,7,512]{2,1,0:T(8,128)}, bf16[2,1536,64]{1,2,0:T(8,128)(2,1)}, bf16[2,1536,64]{1,2,0:...) while((s32[]{:T(128)}, ...), condition=%wide.region_4.5_spmd.clone, body=%wide.region_1.4_spmd.clone.sunk | while | flops 1459057152 | bytes 76424888 | solution.py:150
  76.0 1.7 fusion.175
  77.7 4.5 fusion.176
  82.2 3.2 fusion.177
  85.4 5.4 fusion.178
  91.8 1.7 fusion.175
  93.5 4.5 fusion.176
  98.0 3.2 fusion.177
  101.3 5.4 fusion.178
  107.7 3.1 multiply_reduce_fusion.2
  111.0 13.2 fusion.115
  124.2 4.1 all-gather.15.cloned.1.call-done
  128.4 12.1 fusion.116
  140.5 11.5 all-gather.17.cloned.1.call-done
  152.0 17.6 %multiply_convert_fusion = (bf16[512,4864]{1,0:T(8,128)(2,1)}, bf16[512,4864]{1,0:T(8,128)(2,1)}, bf16[512,4864]{1,0:T(8,128)(2,1)}) fusion(f32[512,4864]{1,0:T(8,128)} %fusion.115, f32[512,4864]{1,0:T(8,128)} %fusion.116, bf16[4864,896]{1,0:T(8,128)(2,1)} %all-gather.17.cloned.1.call-done, bf16[1,512,896]{2,1,0:T(8,128)(2,1)} %param.21), kind=kOutput, calls=%fused_computation.67 | convolution fusion | flops 4500094976 | bytes 44498944 | tf_op jit(solution)/shard_map/td,fd->tf/dot_general | solution.py:189
  169.6 10.8 fusion.117
  180.5 7.8 multiply_reduce_fusion
  188.3 1.8 multiply_add_fusion
  190.1 2.7 convolution_convert_fusion
  194.2 126.8 %while.29 = (s32[]{:T(128)}, f32[2,512,7,64]{1,3,2,0:T(8,128)}, f32[2,1536,64]{1,2,0:T(8,128)}, f32[2,1536,64]{1,2,0:T(8,128)}, bf16[2,1536,64]{1,2,0:T(8,128)(2...) while((s32[]{:T(128)}, f32[2,512,7,64]{1,3,2,0:T(8,128)}, ...), condition=%wide.region_9.10_spmd.clone, body=%wide.region_7.9_spmd.clone.sunk | while | flops 3578589696 | bytes 243301296 | solution.py:233
  194.3 11.6 fusion.187
  206.7 1.7 fusion.188
  208.3 19.0 %fusion.189 = (f32[7,512]{1,0:T(8,128)S(1)}, f32[7,512,1536]{1,2,0:T(8,128)}) fusion(f32[1536,512,7]{1,0,2:T(8,128)} %fusion.187, f32[7,512]{1,0:T(8,128)S(1)} %dynamic-slice_bitcast_fusion.2, bf16[2,512,7,64]{1,3,2,0:T(8,128)(2,1)} %get-tuple-element.516, s32[]{:T(128)S(6)} %copy.78, bf16[2,1536,64]{1,2,0:T(8,128)(2,1)S(1)} %get-tuple-element.515, ...), kind=kOutput, calls=%fused_computation.25.clone.1 | convolution fusion | flops 732164608 | bytes 45513728 | tf_op jit(solution)/shard_map/while/body/eval_jaxpr/tgd,sd->gts/dot_general | solution.py:137
  227.4 15.8 %fusion.190 = bf16[7,512,1536]{1,2,0:T(8,128)(2,1)S(1)} fusion(f32[7,512,1536]{1,2,0:T(8,128)} %get-tuple-element.443, f32[1536,512,7]{1,0,2:T(8,128)} %fusion.187, f32[7,512]{1,0:T(8,128)S(1)} %get-tuple-element.444), kind=kLoop, calls=%fused_computation.27.clone.1 | loop fusion | flops 16515072 | bytes 55064576 | tf_op jit(solution)/shard_map/while/body/eval_jaxpr/convert_element_type | solution.py:222
  243.2 3.0 fusion.191
  246.1 5.3 fusion.192
  252.4 5.3 fusion.193
  257.6 11.6 fusion.187
  271.6 19.0 %fusion.189 = (f32[7,512]{1,0:T(8,128)S(1)}, f32[7,512,1536]{1,2,0:T(8,128)}) fusion(f32[1536,512,7]{1,0,2:T(8,128)} %fusion.187, f32[7,512]{1,0:T(8,128)S(1)} %dynamic-slice_bitcast_fusion.2, bf16[2,512,7,64]{1,3,2,0:T(8,128)(2,1)} %get-tuple-element.516, s32[]{:T(128)S(6)} %copy.78, bf16[2,1536,64]{1,2,0:T(8,128)(2,1)S(1)} %get-tuple-element.515, ...), kind=kOutput, calls=%fused_computation.25.clone.1 | convolution fusion | flops 732164608 | bytes 45513728 | tf_op jit(solution)/shard_map/while/body/eval_jaxpr/tgd,sd->gts/dot_general | solution.py:137
  290.7 15.8 %fusion.190 = bf16[7,512,1536]{1,2,0:T(8,128)(2,1)S(1)} fusion(f32[7,512,1536]{1,2,0:T(8,128)} %get-tuple-element.443, f32[1536,512,7]{1,0,2:T(8,128)} %fusion.187, f32[7,512]{1,0:T(8,128)S(1)} %get-tuple-element.444), kind=kLoop, calls=%fused_computation.27.clone.1 | loop fusion | flops 16515072 | bytes 55064576 | tf_op jit(solution)/shard_map/while/body/eval_jaxpr/convert_element_type | solution.py:222
  306.5 3.0 fusion.191
  309.5 5.3 fusion.192
  315.7 5.3 fusion.193
  324.3 44.9 %reduce-scatter.9.cloned.1.call-done = f32[512,256]{0,1:T(8,128)} async-done(((f32[2048,256]{0,1:T(8,128)}), f32[512,256]{0,1:T(8,128)}) %reduce-scatter.9.cloned.1.call-update) | async-done | bytes 524304 | tf_op jit(solution)/shard_map/reduce_scatter | solution.py:245
  375.5 1.7 slice_negate_fusion
  377.2 1.8 fusion.83
  379.1 3.0 fusion.88
  382.1 4.6 fusion.97
  386.8 13.9 %fusion.120 = f32[896,4864]{1,0:T(8,128)} fusion(bf16[512,896]{1,0:T(8,128)(2,1)} %copy-done.9, bf16[512,4864]{1,0:T(8,128)(2,1)} %get-tuple-element.258), kind=kOutput, calls=%fused_computation.177 | convolution fusion | flops 4462739456 | bytes 23330816 | tf_op jit(solution)/shard_map/td,tf->df/dot_general | solution.py:194
  401.1 14.0 %fusion.121 = f32[896,4864]{1,0:T(8,128)} fusion(bf16[512,896]{1,0:T(8,128)(2,1)} %copy-done.9, bf16[512,4864]{1,0:T(8,128)(2,1)} %get-tuple-element.257), kind=kOutput, calls=%fused_computation.178 | convolution fusion | flops 4462739456 | bytes 23330816 | tf_op jit(solution)/shard_map/td,tf->df/dot_general | solution.py:195
  415.1 11.4 fusion.91
  427.0 23.2 %reduce-scatter.19.cloned.1.call-done = f32[448,4864]{1,0:T(8,128)} async-done(((f32[896,4864]{1,0:T(8,128)}), f32[448,4864]{1,0:T(8,128)}) %reduce-scatter.19.cloned.1.call-update) | async-done | bytes 8716304 | tf_op jit(solution)/shard_map/reduce_scatter | solution.py:294
  450.2 30.3 %reduce-scatter.21.cloned.1.call-done = f32[448,4864]{1,0:T(8,128)} async-done(((f32[896,4864]{1,0:T(8,128)}), f32[448,4864]{1,0:T(8,128)}) %reduce-scatter.21.cloned.1.call-update) | async-done | bytes 8716304 | tf_op jit(solution)/shard_map/reduce_scatter | solution.py:295
  480.5 30.3 %reduce-scatter.23.cloned.1.call-done = f32[2432,896]{1,0:T(8,128)} async-done(((f32[4864,896]{1,0:T(8,128)}), f32[2432,896]{1,0:T(8,128)}) %reduce-scatter.23.cloned.1.call-update) | async-done | bytes 8716304 | tf_op jit(solution)/shard_map/reduce_scatter | solution.py:296
  512.1 3.0 fusion.81
  515.6 3.1 fusion.118
  518.7 10.6 fusion.84
  531.2 3.4 all-reduce.14
  535.0 46.8 %all-reduce.12 = (f32[448]{0:T(512)}, f32[448]{0:T(512)}, f32[64]{0:T(128)}, f32[64]{0:T(128)}, f32[448]{0:T(512)}) all-reduce(f32[448]{0:T(512)S(1)} %dynamic-slice.7, f32[448]{0:T(512)S(1)} %dynamic-slice.9, f32[64]{0:T(128)S(1)} %dynamic-slice.11, ...), channel_id=1, replica_groups=mesh['seq'=4,'ctx'=4,'fsdp'=2] {'seq','ctx'}, use_global_device_ids=true, to_apply=%region_14.15 | all-reduce | flops 1472 | bytes 11776 | tf_op jit(solution)/shard_map/psum | solution.py:298
  581.8 2.9 fusion.90
  584.7 715.1 %all-reduce.18.cloned.1.call-done = (f32[448,896]{1,0:T(8,128)}, f32[448,128]{1,0:T(8,128)}, f32[448,128]{1,0:T(8,128)}, f32[448,896]{1,0:T(8,128)}, f32[448,486...) async-done(((f32[448,896]{1,0:T(8,128)}, f32[448,128]{1,0:T(8,128)}, f32[448,128]{1,0:T(8,128)}, f32[448,896]{1,0:T(8,128)}, f32[448,4864]{1,0:T(8,128)}, ...) | async-done | bytes 29818896 | tf_op jit(solution)/shard_map/psum | solution.py:298
  1299.8 2.8 copy.96
  1305.2 8.6 copy.100
  1313.8 4.4 copy.101
  1319.9 3.5 copy.102
  (234 shorter events, 41.1 us)
Async XLA Ops:
  7.2 50.5 %all-gather.7.cloned.1.call-start = ((), (), s32[]{:S(2)}) async-start(), calls=%async_computation.8 | async-start | bytes 1310720 | tf_op jit(solution)/shard_map/all_gather | solution.py:114
  9.5 16.0 %copy-start.22 = (bf16[896,128]{1,0:T(8,128)(2,1)}, bf16[896,128]{1,0:T(8,128)(2,1)S(1)}, u32[]{:S(2)}) copy-start(bf16[896,128]{1,0:T(8,128)(2,1)S(1)} %all_gather.49) | copy-start | bytes 688132
  19.0 49.6 %copy-start.34 = (f32[896]{0:T(1024)}, f32[896]{0:T(1024)S(1)}, u32[]{:S(2)}) copy-start(f32[896]{0:T(1024)S(1)} %convert_element_type.127) | copy-start | bytes 10756
  20.4 5.2 copy-start.1
  20.4 48.1 %copy-start.37 = (f32[512]{0:T(512)}, f32[512]{0:T(512)S(1)}, u32[]{:S(2)}) copy-start(f32[512]{0:T(512)S(1)} %add_rsqrt_fusion.1) | copy-start | bytes 6148
  25.5 49.0 %copy-start.15 = (f32[512,64]{0,1:T(8,128)}, f32[512,64]{0,1:T(8,128)S(1)}, u32[]{:S(2)}) copy-start(f32[512,64]{0,1:T(8,128)S(1)} %pad_maximum_fusion.4) | copy-start | bytes 393220
  25.6 49.0 %copy-start.12 = (f32[512,64]{0,1:T(8,128)}, f32[512,64]{0,1:T(8,128)S(1)}, u32[]{:S(2)}) copy-start(f32[512,64]{0,1:T(8,128)S(1)} %pad_maximum_fusion.3) | copy-start | bytes 393220
  27.0 41.6 %all-gather.9.cloned.1.call-start = ((), (), s32[]{:S(2)}) async-start(), calls=%async_computation.9 | async-start | bytes 2408448 | tf_op jit(solution)/shard_map/all_gather | solution.py:56
  27.7 79.9 %all-gather.11.cloned.1.call-start = ((), (), s32[]{:S(2)}) async-start(), calls=%async_computation.10 | async-start | bytes 2408448 | tf_op jit(solution)/shard_map/all_gather | solution.py:62
  28.5 82.6 %all-gather.13.cloned.1.call-start = ((), (), s32[]{:S(2)}) async-start(), calls=%async_computation.11 | async-start | bytes 13074432 | tf_op jit(solution)/shard_map/all_gather | solution.py:64
  29.0 99.4 %all-gather.15.cloned.1.call-start = ((), (), s32[]{:S(2)}) async-start(), calls=%async_computation.12 | async-start | bytes 13074432 | tf_op jit(solution)/shard_map/all_gather | solution.py:65
  29.6 122.4 %all-gather.17.cloned.1.call-start = ((), (), s32[]{:S(2)}) async-start(), calls=%async_computation.13 | async-start | bytes 13074432 | tf_op jit(solution)/shard_map/all_gather | solution.py:66
  30.2 339.0 %reduce-scatter.9.cloned.1.call-start = ((), (), s32[]{:S(2)}) async-start(), calls=%async_computation.14 | async-start | bytes 2621440 | tf_op jit(solution)/shard_map/reduce_scatter | solution.py:245
  76.0 31.7 %copy-start.2 = (bf16[1,512,896]{2,1,0:T(8,128)(2,1)S(1)}, bf16[1,512,896]{2,1,0:T(8,128)(2,1)}, u32[]{:S(2)}) copy-start(bf16[1,512,896]{2,1,0:T(8,128)(2,1)} %param.19) | copy-start | bytes 2752516
  82.2 3.2 copy-start.24
  98.0 3.2 copy-start.24
  107.7 3.1 copy-start.36
  110.7 77.6 %copy-start.10 = (f32[512,896]{1,0:T(8,128)}, f32[512,896]{1,0:T(8,128)S(1)}, u32[]{:S(2)}) copy-start(f32[512,896]{1,0:T(8,128)S(1)} %get-tuple-element.278) | copy-start | bytes 5505028
  111.0 17.4 %copy-start.9 = (bf16[512,896]{1,0:T(8,128)(2,1)}, bf16[512,896]{1,0:T(8,128)(2,1)S(1)}, u32[]{:S(2)}) copy-start(bf16[512,896]{1,0:T(8,128)(2,1)S(1)} %multiply_convert_fusion.3) | copy-start | bytes 2752516
  169.6 10.9 copy-start.14
  169.6 10.9 copy-start.41
  180.5 7.8 copy-start.21
  227.3 25.0 %slice-start = ((s8[22020096]{0:T(1024)(128)(4,1)}), s8[4194304]{0:T(1024)(128)(4,1)S(1)}, s32[]{:S(2)}) async-start(s8[22020096]{0:T(1024)(128)(4,1)} %bitcast.293), calls=%async_computation.23 | async-start | bytes 8388608 | tf_op jit(solution)/shard_map/while
  227.3 25.0 %slice-start.1 = ((s8[22020096]{0:T(1024)(128)(4,1)}), s8[4194304]{0:T(1024)(128)(4,1)S(1)}, s32[]{:S(2)}) async-start(s8[22020096]{0:T(1024)(128)(4,1)} %bitcast.293), calls=%async_computation.24 | async-start | bytes 8388608 | tf_op jit(solution)/shard_map/while
  227.3 25.0 %slice-start.2 = ((s8[22020096]{0:T(1024)(128)(4,1)}), s8[4194304]{0:T(1024)(128)(4,1)S(1)}, s32[]{:S(2)}) async-start(s8[22020096]{0:T(1024)(128)(4,1)} %bitcast.293), calls=%async_computation.25 | async-start | bytes 8388608 | tf_op jit(solution)/shard_map/while
  227.3 25.0 %slice-start.3 = ((s8[22020096]{0:T(1024)(128)(4,1)}), s8[4194304]{0:T(1024)(128)(4,1)S(1)}, s32[]{:S(2)}) async-start(s8[22020096]{0:T(1024)(128)(4,1)} %bitcast.293), calls=%async_computation.26 | async-start | bytes 8388608 | tf_op jit(solution)/shard_map/while
  227.4 25.0 %slice-start.4 = ((s8[22020096]{0:T(1024)(128)(4,1)}), s8[4194304]{0:T(1024)(128)(4,1)S(1)}, s32[]{:S(2)}) async-start(s8[22020096]{0:T(1024)(128)(4,1)} %bitcast.293), calls=%async_computation.27 | async-start | bytes 8388608 | tf_op jit(solution)/shard_map/while
  243.2 3.0 copy-start.26
  243.2 9.2 slice-start.5
  290.6 25.0 %slice-start = ((s8[22020096]{0:T(1024)(128)(4,1)}), s8[4194304]{0:T(1024)(128)(4,1)S(1)}, s32[]{:S(2)}) async-start(s8[22020096]{0:T(1024)(128)(4,1)} %bitcast.293), calls=%async_computation.23 | async-start | bytes 8388608 | tf_op jit(solution)/shard_map/while
  290.6 25.0 %slice-start.1 = ((s8[22020096]{0:T(1024)(128)(4,1)}), s8[4194304]{0:T(1024)(128)(4,1)S(1)}, s32[]{:S(2)}) async-start(s8[22020096]{0:T(1024)(128)(4,1)} %bitcast.293), calls=%async_computation.24 | async-start | bytes 8388608 | tf_op jit(solution)/shard_map/while
  290.6 25.0 %slice-start.2 = ((s8[22020096]{0:T(1024)(128)(4,1)}), s8[4194304]{0:T(1024)(128)(4,1)S(1)}, s32[]{:S(2)}) async-start(s8[22020096]{0:T(1024)(128)(4,1)} %bitcast.293), calls=%async_computation.25 | async-start | bytes 8388608 | tf_op jit(solution)/shard_map/while
  290.6 25.0 %slice-start.3 = ((s8[22020096]{0:T(1024)(128)(4,1)}), s8[4194304]{0:T(1024)(128)(4,1)S(1)}, s32[]{:S(2)}) async-start(s8[22020096]{0:T(1024)(128)(4,1)} %bitcast.293), calls=%async_computation.26 | async-start | bytes 8388608 | tf_op jit(solution)/shard_map/while
  290.7 25.0 %slice-start.4 = ((s8[22020096]{0:T(1024)(128)(4,1)}), s8[4194304]{0:T(1024)(128)(4,1)S(1)}, s32[]{:S(2)}) async-start(s8[22020096]{0:T(1024)(128)(4,1)} %bitcast.293), calls=%async_computation.27 | async-start | bytes 8388608 | tf_op jit(solution)/shard_map/while
  306.5 3.0 copy-start.26
  306.5 9.2 slice-start.5
  324.0 46.3 %copy-start.16 = (f32[512,64]{0,1:T(8,128)S(1)}, f32[512,64]{0,1:T(8,128)}, u32[]{:S(2)}) copy-start(f32[512,64]{0,1:T(8,128)} %copy-done.15) | copy-start | bytes 393220
  324.0 46.4 %copy-start.13 = (f32[512,64]{0,1:T(8,128)S(1)}, f32[512,64]{0,1:T(8,128)}, u32[]{:S(2)}) copy-start(f32[512,64]{0,1:T(8,128)} %copy-done.12) | copy-start | bytes 393220
  324.0 47.2 %copy-start.3 = (bf16[1,512,896]{2,1,0:T(8,128)(2,1)S(1)}, bf16[1,512,896]{2,1,0:T(8,128)(2,1)}, u32[]{:S(2)}) copy-start(bf16[1,512,896]{2,1,0:T(8,128)(2,1)} %param.19) | copy-start | bytes 2752516
  324.0 47.2 %copy-start.35 = (f32[896]{0:T(1024)S(1)}, f32[896]{0:T(1024)}, u32[]{:S(2)}) copy-start(f32[896]{0:T(1024)} %copy-done.34) | copy-start | bytes 10756
  324.0 47.1 %copy-start.38 = (f32[512]{0:T(512)S(1)}, f32[512]{0:T(512)}, u32[]{:S(2)}) copy-start(f32[512]{0:T(512)} %copy-done.37) | copy-start | bytes 6148
  324.0 102.8 %reduce-scatter.13.cloned.1.call-start = ((), (), s32[]{:S(2)}) async-start(), calls=%async_computation.16 | async-start | bytes 688128 | tf_op jit(solution)/shard_map/reduce_scatter | solution.py:288
  370.3 2.3 copy-start
  372.5 54.4 %reduce-scatter.15.cloned.1.call-start = ((), (), s32[]{:S(2)}) async-start(), calls=%async_computation.17 | async-start | bytes 688128 | tf_op jit(solution)/shard_map/reduce_scatter | solution.py:290
  375.5 51.5 %reduce-scatter.11.cloned.1.call-start = ((), (), s32[]{:S(2)}) async-start(), calls=%async_computation.15 | async-start | bytes 4816896 | tf_op jit(solution)/shard_map/reduce_scatter | solution.py:286
  377.2 1.8 copy-start.5
  377.2 1.8 copy-start.7
  382.1 44.9 %reduce-scatter.17.cloned.1.call-start = ((), (), s32[]{:S(2)}) async-start(), calls=%async_computation.18 | async-start | bytes 4816896 | tf_op jit(solution)/shard_map/reduce_scatter | solution.py:292
  386.8 63.4 %reduce-scatter.19.cloned.1.call-start = ((), (), s32[]{:S(2)}) async-start(), calls=%async_computation.19 | async-start | bytes 26148864 | tf_op jit(solution)/shard_map/reduce_scatter | solution.py:294
  400.8 79.7 %reduce-scatter.21.cloned.1.call-start = ((), (), s32[]{:S(2)}) async-start(), calls=%async_computation.20 | async-start | bytes 26148864 | tf_op jit(solution)/shard_map/reduce_scatter | solution.py:295
  415.1 95.7 %reduce-scatter.23.cloned.1.call-start = ((), (), s32[]{:S(2)}) async-start(), calls=%async_computation.21 | async-start | bytes 26148864 | tf_op jit(solution)/shard_map/reduce_scatter | solution.py:296
  426.5 873.3 %all-reduce.18.cloned.1.call-start = ((), (), s32[]{:S(2)}) async-start(), calls=%async_computation.22 | async-start | bytes 59637760 | tf_op jit(solution)/shard_map/psum | solution.py:298
  512.1 3.1 copy-start.6
  512.1 3.0 copy-start.8
  515.6 3.1 copy-start.11
  518.7 10.6 copy-start.20
  518.7 10.6 copy-start.31
  1299.8 2.8 copy-start.33
  1299.8 3.5 copy-start.32
  1299.8 4.2 copy-start.18
  1305.2 8.6 copy-start.4
  1305.2 13.0 slice-start.6
  1305.2 14.6 %slice-start.7 = ((s8[8716288]{0:T(1024)(128)(4,1)}), s8[4194304]{0:T(1024)(128)(4,1)S(1)}, s32[]{:S(2)}) async-start(s8[8716288]{0:T(1024)(128)(4,1)} %bitcast.298), calls=%async_computation.30 | async-start | bytes 8388608
  1313.8 6.1 slice-start.8
  (13 other events, 13.9 us)
Sparse Core Ops, SparseCore 0:
  27.1 30.4 all-gather.6
  59.2 9.3 all-gather.8
  70.1 11.0 all-gather.10
  82.6 22.1 all-gather.12
  106.2 22.1 all-gather.14
  129.8 22.1 all-gather.16
  324.1 45.0 reduce-scatter.8
  372.7 7.1 reduce-scatter.12
  382.1 9.0 reduce-scatter.14
  393.4 12.0 reduce-scatter.10
  407.8 12.1 reduce-scatter.16
  422.3 27.8 reduce-scatter.18
  452.5 27.9 reduce-scatter.20
  482.8 27.9 reduce-scatter.22
  517.0 782.7 all-reduce.17
where the time goes:
time: 1330 us
  waiting for transfers between devices  898 us (68%)
  matrix products  246 us (18%)
  other arithmetic  64.9 us (5%)
  blocking collectives  57.3 us (4%)
  local copies, waits for them, and re-layouts  44.2 us (3%)
  between operations  17.6 us (1%)
    psum x1, waiting for transfers between devices, on_device(): lax.psum((shares[0], shares[1], shares[2], shares[3], shares[4], shares[5...  715 us
    dot_general x4, matrix products, scores_of(): jnp.einsum('tgd,sd->gts', query_g, key_g, preferred_element_type=jnp.floa...  47 us
    psum x1, blocking collectives, on_device(): lax.psum((shares[0], shares[1], shares[2], shares[3], shares[4], shares[5...  46.8 us
    reduce_scatter x1, waiting for transfers between devices, on_device(): lax.psum_scatter(lax.dynamic_slice_in_dim(full_terms, reach * count, lax....  44.9 us
    unnamed x107, local copies, waits for them, and re-layouts  32.5 us
    convert_element_type x2, other arithmetic, attend_back(): (weights_full * (grad_weights - row_inner)).astype(jnp.bfloat16)  31.6 us
    reduce_scatter x1, waiting for transfers between devices, on_device(): lax.psum_scatter(gw_up, 'fsdp', scatter_dimension=0, tiled=True)  30.3 us
    reduce_scatter x1, waiting for transfers between devices, on_device(): lax.psum_scatter(gw_down, 'fsdp', scatter_dimension=0, tiled=True)  30.3 us
  transfers between devices with their start and end apart: 15, of which 9 were waited for; matrix products, arithmetic and copies ran while one was open for 11% of the time, Pallas kernels for 0%

commit v1 on v0

v1 whole, which is shorter than its diff:
```python
import functools

import jax
import jax.numpy as jnp
from jax import lax
from jax.experimental import pallas as pl
from jax.experimental.pallas import tpu as pltpu
from jax.sharding import PartitionSpec as P

HQ = 14
KVH = 2
HD = 64
WINDOW = 1024
PAIRS = HQ // 2
LANES = 128
HALF = 256

theta_base = 1000000.0
eps_norm = 1e-06
masked_score = -1e30
f32 = jnp.float32
bf16 = jnp.bfloat16
VMEM_BYTES = 58 * 1024 * 1024


def nn(a, b):
    return lax.dot_general(a, b, (((1,), (0,)), ((), ())), preferred_element_type=f32)


def nt(a, b):
    return lax.dot_general(a, b, (((1,), (1,)), ((), ())), preferred_element_type=f32)


def flip_lanes_half(values):
    width = values.shape[-1]
    lane = lax.broadcasted_iota(jnp.int32, values.shape, len(values.shape) - 1)
    up = pltpu.roll(values, width - 32, len(values.shape) - 1)
    down = pltpu.roll(values, 32, len(values.shape) - 1)
    return jnp.where((lane & 63) < 32, -up, down)


def call(kernel, out_shape, flops, moved, **kwargs):
    return pl.pallas_call(
        kernel,
        out_shape=out_shape,
        compiler_params=pltpu.CompilerParams(vmem_limit_bytes=VMEM_BYTES),
        cost_estimate=pl.CostEstimate(flops=flops, bytes_accessed=moved, transcendentals=0),
        **kwargs,
    )


def project_kernel(x_ref, gain_ref, w_ref, bias_ref, cos_ref, sin_ref, n1_ref, q_ref, kv_ref):
    count = x_ref.shape[0]
    step = 256

    def body(i, carry):
        rows = pl.ds(pl.multiple_of(i * step, step), step)
        x = x_ref[rows, :].astype(f32)
        scale = lax.rsqrt(jnp.mean(x * x, -1, keepdims=True) + eps_norm)
        normed = (x * scale * gain_ref[...]).astype(bf16)
        n1_ref[rows, :] = normed
        cosine = cos_ref[rows, :]
        sine = sin_ref[rows, :]
        out = nn(normed, w_ref[...]) + bias_ref[...]
        for j in range(PAIRS + 1):
            part = out[:, j * LANES : (j + 1) * LANES]
            part = part * cosine + flip_lanes_half(part) * sine
            if j < PAIRS:
                q_ref[rows, j * LANES : (j + 1) * LANES] = (part * HD**-0.5).astype(bf16)
            else:
                kv_ref[rows, :LANES] = part.astype(bf16)
        kv_ref[rows, LANES:] = out[:, (PAIRS + 1) * LANES :].astype(bf16)
        return carry

    lax.fori_loop(0, count // step, body, 0)


def project(x, gain, w, bias, cosine, sine):
    count, width = x.shape
    return call(
        project_kernel,
        (
            jax.ShapeDtypeStruct((count, width), bf16),
            jax.ShapeDtypeStruct((count, HQ * HD), bf16),
            jax.ShapeDtypeStruct((count, 2 * KVH * HD), bf16),
        ),
        2 * count * width * w.shape[1],
        6 * 1024 * 1024,
    )(x, gain, w, bias, cosine, sine)


def lane_low(shape):
    return lax.broadcasted_iota(jnp.int32, shape, len(shape) - 1) < HD


def spread_heads(source, target, row):
    values = source.astype(f32)
    other = pltpu.roll(values, HD, 1)
    low = lane_low(values.shape)
    rows = pl.ds(row, values.shape[0])
    target[0, 0, rows, :] = jnp.where(low, values, 0.0).astype(bf16)
    target[1, 0, rows, :] = jnp.where(low, 0.0, other).astype(bf16)
    target[0, 1, rows, :] = jnp.where(low, other, 0.0).astype(bf16)
    target[1, 1, rows, :] = jnp.where(low, 0.0, values).astype(bf16)


def turn_heads(source, target, column):
    values = source.astype(f32).T.astype(bf16)
    columns = pl.ds(column, values.shape[1])
    target[0, :, columns] = values[:HD]
    target[1, :, columns] = values[HD:]


def fill_bias(qseg_ref, kseg_ref, near_ref, far_ref, count):
    for t in range(count // HALF):
        columns = slice(t * HALF, (t + 1) * HALF)
        query = qseg_ref[:, columns]
        near = kseg_ref[count : 2 * count, :] == query
        near_ref[:, columns] = jnp.where(near, 0.0, masked_score)
        key = lax.broadcasted_iota(jnp.int32, (count, HALF), 0)
        token = lax.broadcasted_iota(jnp.int32, (count, HALF), 1) + t * HALF
        shape = (count, HALF)
        far = jnp.where(
            key <= token,
            jnp.broadcast_to(kseg_ref[:count, :], shape),
            jnp.broadcast_to(kseg_ref[2 * count :, :], shape),
        )
        far_ref[:, columns] = jnp.where(far == query, 0.0, masked_score)


def triangle():
    key = lax.broadcasted_iota(jnp.int32, (HALF, HALF), 0)
    token = lax.broadcasted_iota(jnp.int32, (HALF, HALF), 1)
    return key <= token


def tiles_of(t, count):
    if t == 0:
        plain = 2 * count + HALF
        plain_bias = HALF
    else:
        plain = 0
        plain_bias = 0
    diagonal = t * HALF
    return plain, plain_bias, diagonal, 2 * count + diagonal


def scores_of(keys, query, t, count, near_ref, far_ref, tri):
    plain, plain_bias, own, old = tiles_of(t, count)
    columns = slice(t * HALF, (t + 1) * HALF)
    near = nt(keys(count, count), query) + near_ref[:, columns]
    far = nt(keys(plain, HALF), query) + far_ref[plain_bias : plain_bias + HALF, columns]
    edge = jnp.where(tri, nt(keys(own, HALF), query), nt(keys(old, HALF), query))
    edge = edge + far_ref[own : own + HALF, columns]
    return near, far, edge


def attend_kernel(
    q_ref, kv0_ref, kv1_ref, kv2_ref, qseg_ref, kseg_ref, o_ref, lse_ref, k_s, vt_s, near_s, far_s
):
    count = q_ref.shape[0]
    pair = pl.program_id(0)

    @pl.when(pair == 0)
    def _():
        for i, ref in enumerate((kv0_ref, kv1_ref, kv2_ref)):
            spread_heads(ref[:, :LANES], k_s, i * count)
            turn_heads(ref[:, LANES:], vt_s, i * count)
        fill_bias(qseg_ref, kseg_ref, near_s, far_s, count)

    tri = triangle()
    for t in range(count // HALF):
        plain, _, own, old = tiles_of(t, count)
        rows = slice(t * HALF, (t + 1) * HALF)
        query = q_ref[rows, :]
        turned = []
        for half in range(2):
            group = (2 * pair + half) // (HQ // KVH)
            near, far, edge = scores_of(
                lambda start, size: k_s[half, group, start : start + size, :],
                query,
                t,
                count,
                near_s,
                far_s,
                tri,
            )
            top = jnp.maximum(
                jnp.max(near, 0, keepdims=True),
                jnp.maximum(jnp.max(far, 0, keepdims=True), jnp.max(edge, 0, keepdims=True)),
            )
            near = jnp.exp(near - top)
            far = jnp.exp(far - top)
            edge = jnp.exp(edge - top)
            total = (
                jnp.sum(near, 0, keepdims=True)
                + jnp.sum(far, 0, keepdims=True)
                + jnp.sum(edge, 0, keepdims=True)
            )
            lse_ref[0, half : half + 1, rows] = top + jnp.log(total)
            mixed = nn(vt_s[group, :, count : 2 * count], near.astype(bf16))
            mixed += nn(vt_s[group, :, plain : plain + HALF], far.astype(bf16))
            mixed += nn(vt_s[group, :, own : own + HALF], jnp.where(tri, edge, 0.0).astype(bf16))
            mixed += nn(vt_s[group, :, old : old + HALF], jnp.where(tri, 0.0, edge).astype(bf16))
            turned.append(mixed * (1.0 / total))
        o_ref[rows, :] = jnp.concatenate(turned, 0).T.astype(bf16)


def attend(q, kv0, kv1, kv2, qseg, kseg):
    count = q.shape[0]
    whole = lambda p: (0, 0)
    return call(
        attend_kernel,
        (
            jax.ShapeDtypeStruct((count, HQ * HD), bf16),
            jax.ShapeDtypeStruct((PAIRS, 8, count), f32),
        ),
        4 * HQ * count * 1280 * 256,
        4 * 1024 * 1024,
        grid=(PAIRS,),
        in_specs=[
            pl.BlockSpec((count, LANES), lambda p: (0, p)),
            pl.BlockSpec(kv0.shape, whole),
            pl.BlockSpec(kv1.shape, whole),
            pl.BlockSpec(kv2.shape, whole),
            pl.BlockSpec(qseg.shape, whole),
            pl.BlockSpec(kseg.shape, whole),
        ],
        out_specs=(
            pl.BlockSpec((count, LANES), lambda p: (0, p)),
            pl.BlockSpec((1, 8, count), lambda p: (p, 0, 0)),
        ),
        scratch_shapes=[
            pltpu.VMEM((2, KVH, 3 * count, LANES), bf16),
            pltpu.VMEM((KVH, HD, 3 * count), bf16),
            pltpu.VMEM((count, count), f32),
            pltpu.VMEM((count, count), f32),
        ],
    )(q, kv0, kv1, kv2, qseg, kseg)


def attend_back_kernel(
    q_ref,
    do_ref,
    kv0_ref,
    kv1_ref,
    kv2_ref,
    qseg_ref,
    kseg_ref,
    lse_ref,
    delta_ref,
    cos_ref,
    sin_ref,
    dq_ref,
    own_ref,
    one_ref,
    two_ref,
    k_s,
    v_s,
    kt_s,
    near_s,
    far_s,
    dk_s,
    dv_s,
):
    count = q_ref.shape[0]
    pair = pl.program_id(0)

    @pl.when(pair == 0)
    def _():
        for i, ref in enumerate((kv0_ref, kv1_ref, kv2_ref)):
            spread_heads(ref[:, :LANES], k_s, i * count)
            spread_heads(ref[:, LANES:], v_s, i * count)
            turn_heads(ref[:, :LANES], kt_s, i * count)
        fill_bias(qseg_ref, kseg_ref, near_s, far_s, count)
        dk_s[...] = jnp.zeros_like(dk_s)
        dv_s[...] = jnp.zeros_like(dv_s)

    tri = triangle()
    for t in range(count // HALF):
        plain, _, own, old = tiles_of(t, count)
        rows = slice(t * HALF, (t + 1) * HALF)
        query = q_ref[rows, :]
        grad = do_ref[rows, :]
        low = lane_low(query.shape)
        turned = []
        for half in range(2):
            group = (2 * pair + half) // (HQ // KVH)
            mine = low if half == 0 else jnp.logical_not(low)
            query_half = jnp.where(mine, query.astype(f32), 0.0).astype(bf16)
            grad_half = jnp.where(mine, grad.astype(f32), 0.0).astype(bf16)
            log_total = lse_ref[0, half : half + 1, rows]
            inner = delta_ref[0, half : half + 1, rows]
            scores = scores_of(
                lambda start, size: k_s[half, group, start : start + size, :],
                query,
                t,
                count,
                near_s,
                far_s,
                tri,
            )
            near, far, edge = (jnp.exp(part - log_total) for part in scores)
            values = lambda start, size: v_s[half, group, start : start + size, :]
            near_g = near * (nt(values(count, count), grad) - inner)
            far_g = far * (nt(values(plain, HALF), grad) - inner)
            edge_p = jnp.where(tri, nt(values(own, HALF), grad), nt(values(old, HALF), grad))
            edge_g = edge * (edge_p - inner)
            blocks = (
                (count, count, near, near_g),
                (plain, HALF, far, far_g),
                (own, HALF, jnp.where(tri, edge, 0.0), jnp.where(tri, edge_g, 0.0)),
                (old, HALF, jnp.where(tri, 0.0, edge), jnp.where(tri, 0.0, edge_g)),
            )
            total = None
            for start, size, weight, change in blocks:
                change = change.astype(bf16)
                keys = slice(start, start + size)
                dv_s[group, keys, :] += nn(weight.astype(bf16), grad_half)
                dk_s[group, keys, :] += nn(change, query_half)
                part = nn(kt_s[group, :, keys], change)
                total = part if total is None else total + part
            turned.append(total)
        turned = jnp.concatenate(turned, 0).T * HD**-0.5
        back = turned * cos_ref[rows, :] - flip_lanes_half(turned * sin_ref[rows, :])
        dq_ref[rows, :] = back.astype(bf16)

    @pl.when(pair == PAIRS - 1)
    def _():
        for i, (ref, cast) in enumerate(((own_ref, f32), (one_ref, bf16), (two_ref, bf16))):
            keys = slice(i * count, (i + 1) * count)
            for j, source in enumerate((dk_s, dv_s)):
                first = source[0, keys, :]
                second = source[1, keys, :]
                first = first + pltpu.roll(first, HD, 1)
                second = second + pltpu.roll(second, HD, 1)
                both = jnp.where(lane_low(first.shape), first, second)
                ref[:, j * LANES : (j + 1) * LANES] = both.astype(cast)


def attend_back(q, do, kv0, kv1, kv2, qseg, kseg, lse, delta, cosine, sine):
    count = q.shape[0]
    whole = lambda p: (0, 0)
    lane_block = pl.BlockSpec((count, LANES), lambda p: (0, p))
    row_block = pl.BlockSpec((1, 8, count), lambda p: (p, 0, 0))
    return call(
        attend_back_kernel,
        (
            jax.ShapeDtypeStruct((count, HQ * HD), bf16),
            jax.ShapeDtypeStruct((count, 2 * LANES), f32),
            jax.ShapeDtypeStruct((count, 2 * LANES), bf16),
            jax.ShapeDtypeStruct((count, 2 * LANES), bf16),
        ),
        10 * HQ * count * 1280 * 256,
        6 * 1024 * 1024,
        grid=(PAIRS,),
        in_specs=[
            lane_block,
            lane_block,
            pl.BlockSpec(kv0.shape, whole),
            pl.BlockSpec(kv1.shape, whole),
            pl.BlockSpec(kv2.shape, whole),
            pl.BlockSpec(qseg.shape, whole),
            pl.BlockSpec(kseg.shape, whole),
            row_block,
            row_block,
            pl.BlockSpec(cosine.shape, whole),
            pl.BlockSpec(sine.shape, whole),
        ],
        out_specs=(
            lane_block,
            pl.BlockSpec((count, 2 * LANES), whole),
            pl.BlockSpec((count, 2 * LANES), whole),
            pl.BlockSpec((count, 2 * LANES), whole),
        ),
        scratch_shapes=[
            pltpu.VMEM((2, KVH, 3 * count, LANES), bf16),
            pltpu.VMEM((2, KVH, 3 * count, LANES), bf16),
            pltpu.VMEM((KVH, HD, 3 * count), bf16),
            pltpu.VMEM((count, count), f32),
            pltpu.VMEM((count, count), f32),
            pltpu.VMEM((KVH, 3 * count, LANES), f32),
            pltpu.VMEM((KVH, 3 * count, LANES), f32),
        ],
    )(q, do, kv0, kv1, kv2, qseg, kseg, lse, delta, cosine, sine)


def merge_kernel(x_ref, o_ref, w_ref, gain_ref, h1_ref, n2_ref):
    step = 256

    def body(i, carry):
        rows = pl.ds(pl.multiple_of(i * step, step), step)
        hidden = x_ref[rows, :].astype(f32) + nn(o_ref[rows, :], w_ref[...])
        h1_ref[rows, :] = hidden
        scale = lax.rsqrt(jnp.mean(hidden * hidden, -1, keepdims=True) + eps_norm)
        n2_ref[rows, :] = (hidden * scale * gain_ref[...]).astype(bf16)
        return carry

    lax.fori_loop(0, x_ref.shape[0] // step, body, 0)


def merge(x, o, w, gain):
    return call(
        merge_kernel,
        (jax.ShapeDtypeStruct(x.shape, f32), jax.ShapeDtypeStruct(x.shape, bf16)),
        2 * x.shape[0] * w.shape[0] * w.shape[1],
        6 * 1024 * 1024,
    )(x, o, w, gain)


def feed_kernel(*refs, first, width):
    me_ref, na_ref, nb_ref, ca_ref, cb_ref, wg_ref, wu_ref, wd_ref = refs[:8]
    refs = refs[8:]
    if not first:
        sums = refs[:4]
        refs = refs[4:]
    mine_ref, theirs_ref, down_ref = refs[:3]
    outs = refs[3:7]
    inner_s, gate_s, up_s, inner_t, normed_t = refs[7:]
    count = na_ref.shape[0]
    half_rows = mine_ref.shape[0] // (2 * width // LANES)
    step = 256

    for half, (normed_ref, grad_ref) in enumerate(((na_ref, ca_ref), (nb_ref, cb_ref))):
        result_ref, back_ref = outs[2 * half : 2 * half + 2]

        def body(i, carry, half=half, normed_ref=normed_ref, grad_ref=grad_ref,
                 result_ref=result_ref, back_ref=back_ref):
            rows = pl.ds(pl.multiple_of(i * step, step), step)
            both = pl.ds(pl.multiple_of(half * count + i * step, step), step)
            normed = normed_ref[rows, :]
            gate = nn(normed, wg_ref[...])
            up = nn(normed, wu_ref[...])
            change = nt(grad_ref[rows, :], wd_ref[...])
            sigmoid = 1.0 / (1.0 + jnp.exp(-gate))
            activated = gate * sigmoid
            inner = (activated * up).astype(bf16)
            gate_g = (change * up * sigmoid * (1.0 + gate * (1.0 - sigmoid))).astype(bf16)
            up_g = (change * activated).astype(bf16)
            inner_s[both, :] = inner
            gate_s[both, :] = gate_g
            up_s[both, :] = up_g
            result = nn(inner, wd_ref[...])
            back = nt(gate_g, wg_ref[...]) + nt(up_g, wu_ref[...])
            if not first:
                result = result + sums[2 * half][rows, :]
                back = back + sums[2 * half + 1][rows, :]
            result_ref[rows, :] = result
            back_ref[rows, :] = back
            return carry

        lax.fori_loop(0, count // step, body, 0)
        normed_t[:, half * count : (half + 1) * count] = normed_ref[...].T
        inner_t[:, half * count : (half + 1) * count] = inner_s[half * count : (half + 1) * count, :].T

    me = me_ref[0]
    start = 0
    while start < width:
        size = min(HALF, width - start)
        columns = slice(start, start + size)
        for kind, source in enumerate((gate_s, up_s)):
            grads = nn(normed_t[...], source[:, columns]).astype(bf16)
            for j in range(size // LANES):
                row = (kind * width // LANES + start // LANES + j) * half_rows
                tile = grads[:, j * LANES : (j + 1) * LANES]

                @pl.when(me == 0)
                def _():
                    mine_ref[row : row + half_rows, :] = tile[:half_rows]
                    theirs_ref[row : row + half_rows, :] = tile[half_rows:]

                @pl.when(me == 1)
                def _():
                    mine_ref[row : row + half_rows, :] = tile[half_rows:]
                    theirs_ref[row : row + half_rows, :] = tile[:half_rows]

        down = nn(inner_t[columns, :count], ca_ref[...]) + nn(inner_t[columns, count:], cb_ref[...])
        down = down.astype(bf16)
        for j in range(down.shape[1] // LANES):
            row = j * width + start
            down_ref[row : row + size, :] = down[:, j * LANES : (j + 1) * LANES]
        start += size


def feed(me, na, nb, ca, cb, wg, wu, wd, sums):
    count, features = na.shape
    width = wg.shape[1]
    rows = features * width // LANES
    first = sums is None
    spec = pl.BlockSpec(memory_space=pltpu.VMEM)
    sums = () if first else tuple(sums)
    token_out = jax.ShapeDtypeStruct((count, features), f32)
    return call(
        functools.partial(feed_kernel, first=first, width=width),
        (jax.ShapeDtypeStruct((rows, LANES), bf16),) * 3 + (token_out,) * 4,
        18 * 2 * count * features * width,
        40 * 1024 * 1024,
        in_specs=[pl.BlockSpec(memory_space=pltpu.SMEM)] + [spec] * (7 + len(sums)),
        out_specs=(spec,) * 7,
        scratch_shapes=[
            pltpu.VMEM((2 * count, width), bf16),
            pltpu.VMEM((2 * count, width), bf16),
            pltpu.VMEM((2 * count, width), bf16),
            pltpu.VMEM((width, 2 * count), bf16),
            pltpu.VMEM((features, 2 * count), bf16),
        ],
        input_output_aliases={} if first else {8 + i: 3 + i for i in range(4)},
    )(me, na, nb, ca, cb, wg, wu, wd, *sums)


def middle_kernel(
    me_ref, part_ref, got_ref, h1_ref, dy_ref, gain_ref, w_ref, o_ref, heads_ref,
    dh1_ref, do_ref, delta_ref, gg_ref, mine_ref, theirs_ref, low_s, ot_s,
):
    count, features = part_ref.shape
    step = 256
    gg_ref[...] = jnp.zeros_like(gg_ref)

    def body(i, carry):
        rows = pl.ds(pl.multiple_of(i * step, step), step)
        back = part_ref[rows, :] + got_ref[rows, :].astype(f32)
        hidden = h1_ref[rows, :]
        scale = lax.rsqrt(jnp.mean(hidden * hidden, -1, keepdims=True) + eps_norm)
        normal = hidden * scale
        gg_ref[...] += jnp.sum(back * normal, 0, keepdims=True)
        change = back * gain_ref[...]
        grad = dy_ref[rows, :].astype(f32) + scale * (
            change - normal * jnp.mean(change * normal, -1, keepdims=True)
        )
        dh1_ref[rows, :] = grad
        low = grad.astype(bf16)
        low_s[rows, :] = low
        attn_g = nt(low, w_ref[...]).astype(bf16)
        do_ref[rows, :] = attn_g
        product = attn_g.astype(f32) * o_ref[rows, :].astype(f32)
        sums = lax.dot_general(
            heads_ref[...], product, (((1,), (1,)), ((), ())),
            precision=lax.Precision.HIGHEST, preferred_element_type=f32,
        )
        delta_ref[:, rows] = sums
        return carry

    lax.fori_loop(0, count // step, body, 0)
    ot_s[...] = o_ref[...].T
    store_split(me_ref, nn(ot_s[...], low_s[...]).astype(bf16), mine_ref, theirs_ref, 0)


def store_split(me_ref, grads, mine_ref, theirs_ref, first_tile):
    half_rows = grads.shape[0] // 2
    me = me_ref[0]
    for j in range(grads.shape[1] // LANES):
        row = (first_tile + j) * half_rows
        tile = grads[:, j * LANES : (j + 1) * LANES]

        @pl.when(me == 0)
        def _():
            mine_ref[row : row + half_rows, :] = tile[:half_rows]
            theirs_ref[row : row + half_rows, :] = tile[half_rows:]

        @pl.when(me == 1)
        def _():
            mine_ref[row : row + half_rows, :] = tile[half_rows:]
            theirs_ref[row : row + half_rows, :] = tile[:half_rows]


def middle(me, part, got, h1, dy, gain, w, o, heads):
    count, features = part.shape
    spec = pl.BlockSpec(memory_space=pltpu.VMEM)
    rows = (features // 2) * (features // LANES)
    return call(
        middle_kernel,
        (
            jax.ShapeDtypeStruct((count, features), f32),
            jax.ShapeDtypeStruct((count, HQ * HD), bf16),
            jax.ShapeDtypeStruct((heads.shape[0], count), f32),
            jax.ShapeDtypeStruct((1, features), f32),
            jax.ShapeDtypeStruct((rows, LANES), bf16),
            jax.ShapeDtypeStruct((rows, LANES), bf16),
        ),
        4 * count * features * features,
        12 * 1024 * 1024,
        in_specs=[pl.BlockSpec(memory_space=pltpu.SMEM)] + [spec] * 8,
        out_specs=(spec,) * 6,
        scratch_shapes=[pltpu.VMEM((count, features), bf16), pltpu.VMEM((HQ * HD, count), bf16)],
    )(me, part, got, h1, dy, gain, w, o, heads)


def last_kernel(
    me_ref, dq_ref, own_ref, one_ref, two_ref, n1_ref, x_ref, gain_ref, w_ref, dh1_ref, cos_ref, sin_ref,
    dx_ref, gg_ref, gb_ref, mine_ref, theirs_ref, dp_s, n1t_s,
):
    count, features = n1_ref.shape
    width = HQ * HD
    step = 256
    gg_ref[...] = jnp.zeros_like(gg_ref)
    gb_ref[...] = jnp.zeros_like(gb_ref)

    def body(i, carry):
        rows = pl.ds(pl.multiple_of(i * step, step), step)
        pairs = own_ref[rows, :] + one_ref[rows, :].astype(f32) + two_ref[rows, :].astype(f32)
        key = pairs[:, :LANES]
        key = key * cos_ref[rows, :] - flip_lanes_half(key * sin_ref[rows, :])
        dp_s[rows, :width] = dq_ref[rows, :]
        dp_s[rows, width : width + LANES] = key.astype(bf16)
        dp_s[rows, width + LANES :] = pairs[:, LANES:].astype(bf16)
        grads = dp_s[rows, :]
        gb_ref[...] += jnp.sum(grads.astype(f32), 0, keepdims=True)
        back = nt(grads, w_ref[...])
        x = x_ref[rows, :].astype(f32)
        scale = lax.rsqrt(jnp.mean(x * x, -1, keepdims=True) + eps_norm)
        normal = x * scale
        gg_ref[...] += jnp.sum(back * normal, 0, keepdims=True)
        change = back * gain_ref[...]
        grad = dh1_ref[rows, :] + scale * (
            change - normal * jnp.mean(change * normal, -1, keepdims=True)
        )
        dx_ref[rows, :] = grad.astype(bf16)
        return carry

    lax.fori_loop(0, count // step, body, 0)
    n1t_s[...] = n1_ref[...].T
    store_split(me_ref, nn(n1t_s[...], dp_s[...]).astype(bf16), mine_ref, theirs_ref, 0)


def last(me, dq, own, one, two, n1, x, gain, w, dh1, cosine, sine):
    count, features = n1.shape
    spec = pl.BlockSpec(memory_space=pltpu.VMEM)
    rows = (features // 2) * (w.shape[1] // LANES)
    return call(
        last_kernel,
        (
            jax.ShapeDtypeStruct((count, features), bf16),
            jax.ShapeDtypeStruct((1, features), f32),
            jax.ShapeDtypeStruct((1, w.shape[1]), f32),
            jax.ShapeDtypeStruct((rows, LANES), bf16),
            jax.ShapeDtypeStruct((rows, LANES), bf16),
        ),
        4 * count * features * w.shape[1],
        14 * 1024 * 1024,
        in_specs=[pl.BlockSpec(memory_space=pltpu.SMEM)] + [spec] * 11,
        out_specs=(spec,) * 5,
        scratch_shapes=[
            pltpu.VMEM((count, w.shape[1]), bf16),
            pltpu.VMEM((features, count), bf16),
        ],
    )(me, dq, own, one, two, n1, x, gain, w, dh1, cosine, sine)


def swap(values):
    return lax.ppermute(values, "fsdp", [(0, 1), (1, 0)])


def flip(values, dim):
    axis, bit = dim
    size = lax.axis_size(axis)
    return lax.ppermute(values, axis, [(i, i ^ (1 << bit)) for i in range(size)])


def side(dim):
    axis, bit = dim
    return (lax.axis_index(axis) >> bit) & 1


def add(*terms):
    total = terms[0].astype(f32)
    for term in terms[1:]:
        total = total + term.astype(f32)
    return total.astype(bf16)


def take(array, index):
    return lax.dynamic_index_in_dim(array, index, 0, False)


def join(low, other, index):
    out = jnp.zeros((2,) + low.shape, low.dtype)
    out = lax.dynamic_update_index_in_dim(out, low, index, 0)
    return lax.dynamic_update_index_in_dim(out, other, 1 - index, 0)


def other_dims(dims):
    every = []
    for axis in ("seq", "ctx"):
        for bit in range(lax.axis_size(axis).bit_length() - 1):
            every.append((axis, bit))
    return [dim for dim in every if dim not in dims]


def sum_part(part, dims):
    rows = part.shape[0]
    one, two, three = dims
    a, b, c = (side(dim) for dim in dims)
    whole = part.reshape(2, 2, 2, rows // 8, LANES)
    got_one = flip(take(whole, 1 - a), one)
    kept = take(whole, a)
    got_two = flip(add(take(kept, 1 - b), take(got_one, 1 - b)), two)
    kept, got_one = take(kept, b), take(got_one, b)
    got_three = flip(add(take(kept, 1 - c), take(got_one, 1 - c), take(got_two, 1 - c)), three)
    total = add(take(kept, c), take(got_one, c), take(got_two, c), got_three)
    for dim in other_dims(dims):
        total = add(total, flip(total, dim))
    total = join(total, flip(total, three), c)
    total = join(total, flip(total, two), b)
    total = join(total, flip(total, one), a)
    return total.reshape(rows, LANES)


X, Y, Z = ("seq", 0), ("seq", 1), ("ctx", 0)


def untile(flat, tiles):
    rows = flat.shape[0] // tiles
    return flat.reshape(tiles, rows, LANES).transpose(1, 0, 2).reshape(rows, tiles * LANES)


def on_device(
    block_input,
    segment_ids,
    out_cotangent,
    input_gain,
    query_weight,
    query_bias,
    key_weight,
    key_bias,
    value_weight,
    value_bias,
    output_weight,
    middle_gain,
    gate_weight,
    up_weight,
    down_weight,
):
    me = lax.axis_index("fsdp")
    ctx = lax.axis_index("ctx")
    chunks = lax.axis_size("ctx")
    me_array = me.astype(jnp.int32).reshape(1)
    x = block_input[0]
    dy = out_cotangent[0]
    count, features = x.shape
    hidden = down_weight.shape[0]
    own_rows = query_weight.shape[0]
    kv_width = KVH * HD

    def whole(own, other):
        return join(own, other, me).reshape((2 * own.shape[0],) + own.shape[1:])

    projection = jnp.concatenate([query_weight, key_weight, value_weight], 1)
    w_in = whole(projection, swap(projection))
    vectors = jnp.concatenate([input_gain, query_bias, key_bias, value_bias, middle_gain])
    sizes = [v.shape[0] for v in (input_gain, query_bias, key_bias, value_bias, middle_gain)]
    other_vectors = swap(vectors)
    params = []
    place = 0
    for size in sizes:
        mine, theirs = vectors[place : place + size], other_vectors[place : place + size]
        pair = jnp.where(
            me == 0, jnp.concatenate([mine, theirs]), jnp.concatenate([theirs, mine])
        )
        params.append(pair.astype(f32)[None])
        place += size
    gain_one, b_query, b_key, b_value, gain_two = params
    bias = jnp.concatenate([b_query, b_key, b_value], 1)
    w_out = whole(output_weight, swap(output_weight))
    dy_other = swap(dy)

    first = ctx * count
    positions = (first + jnp.arange(count, dtype=jnp.int32)).astype(f32)
    inverse = theta_base ** (-jnp.arange(0, HD, 2, dtype=f32) / HD)
    angle = positions[:, None] * jnp.tile(inverse, LANES // inverse.shape[0])[None, :]
    cosine, sine = jnp.cos(angle), jnp.sin(angle)

    n1, q, kv = project(x, gain_one, w_in, bias, cosine, sine)

    reach = WINDOW // count
    before = [
        lax.ppermute(kv, "ctx", [(i, i + d) for i in range(chunks - d)])
        for d in range(1, reach + 1)
    ]
    seg_row = segment_ids[0]
    padded = jnp.concatenate([jnp.full((reach * count,), -1, jnp.int32), seg_row])
    query_seg = lax.dynamic_slice_in_dim(seg_row, first, count, 0)[None]
    key_seg = jnp.concatenate(
        [
            lax.dynamic_slice_in_dim(padded, first + (reach - d) * count, count, 0)
            for d in range(reach + 1)
        ]
    )[:, None]
    o, lse = attend(q, kv, *before, query_seg, key_seg)
    h1, n2 = merge(x, o, w_out, gain_two)
    n2_other = swap(n2)

    widths = (768, 768, 896)
    place = 0
    sums = None
    parts = []
    for width in widths:
        gate_up = []
        for weight in (gate_weight, up_weight):
            kept = lax.dynamic_slice_in_dim(weight, me * hidden + place, width, 1)
            sent = lax.dynamic_slice_in_dim(weight, (1 - me) * hidden + place, width, 1)
            gate_up.append(whole(kept, swap(sent)))
        down = down_weight[place : place + width]
        mine, theirs, down_grad, *sums = feed(
            me_array, n2, n2_other, dy, dy_other, *gate_up, down, sums
        )
        parts.append((down_grad, mine, swap(theirs)))
        place += width
    result_own, back_own, result_other, back_other = sums
    result = h1 + result_own + swap(result_other.astype(bf16)).astype(f32)
    block_output = result.astype(bf16)[None]

    row = jnp.arange(PAIRS * 8)[:, None]
    column = jnp.arange(HQ * HD)[None, :]
    heads = ((column // HD) == (row // 8) * 2 + row % 8) & (row % 8 < 2)
    dh1, do, delta, gg_two, out_mine, out_theirs = middle(
        me_array, back_own, swap(back_other.astype(bf16)), h1, dy, gain_two, w_out, o, heads.astype(f32)
    )
    delta = delta.reshape(PAIRS, 8, count)
    dq, own_pairs, *sent_pairs = attend_back(
        q, do, kv, *before, query_seg, key_seg, lse, delta, cosine, sine
    )
    got_pairs = [
        lax.ppermute(pairs, "ctx", [(i + d, i) for i in range(chunks - d)])
        for d, pairs in enumerate(sent_pairs, 1)
    ]
    dx, gg_one, g_bias, in_mine, in_theirs = last(
        me_array, dq, own_pairs, *got_pairs, n1, x, gain_one, w_in, dh1, cosine, sine
    )
    input_grad = dx[None]

    gates = jnp.zeros((own_rows, 2 * hidden), f32)
    ups = jnp.zeros((own_rows, 2 * hidden), f32)
    downs = []
    place = 0
    for width, (down_grad, mine, theirs) in zip(widths, parts):
        down_sum = sum_part(down_grad, (X, Y, Z))
        mine_sum = sum_part(mine, (Y, Z, X))
        theirs_sum = sum_part(theirs, (Z, X, Y))
        tiles = width // LANES
        for total, owner in ((mine_sum, me), (theirs_sum, 1 - me)):
            half = total.shape[0] // 2
            at = owner * hidden + place
            gates = lax.dynamic_update_slice(
                gates, untile(total[:half], tiles).astype(f32), (jnp.int32(0), at)
            )
            ups = lax.dynamic_update_slice(
                ups, untile(total[half:], tiles).astype(f32), (jnp.int32(0), at)
            )
        downs.append(untile(down_sum, features // LANES).astype(f32))
        place += width
    gw_down = jnp.concatenate(downs, 0)

    gw_out = lax.psum(add(out_mine, swap(out_theirs)), ("seq", "ctx"))
    gw_out = untile(gw_out, features // LANES).astype(f32)
    gw_in = lax.psum(add(in_mine, swap(in_theirs)), ("seq", "ctx"))
    gw_in = untile(gw_in, (HQ * HD + 2 * kv_width) // LANES).astype(f32)
    width = HQ * HD
    small = [
        gg_one[0],
        g_bias[0, :width],
        g_bias[0, width : width + kv_width],
        g_bias[0, width + kv_width :],
        gg_two[0],
    ]
    small_sums = lax.psum(jnp.concatenate(small), ("seq", "ctx", "fsdp"))
    shares = []
    place = 0
    for vector in small:
        size = vector.shape[0]
        total = small_sums[place : place + size]
        shares.append(lax.dynamic_slice_in_dim(total, me * (size // 2), size // 2, 0))
        place += size
    gg_one, gb_query, gb_key, gb_value, gg_two = shares
    return (
        block_output,
        input_grad,
        gg_one,
        gw_in[:, :width],
        gb_query,
        gw_in[:, width : width + kv_width],
        gb_key,
        gw_in[:, width + kv_width :],
        gb_value,
        gw_out,
        gg_two,
        gates,
        ups,
        gw_down,
    )


def solution(mesh):
    return jax.shard_map(
        on_device,
        mesh=mesh,
        in_specs=(
            P(("seq", "fsdp"), "ctx", None),
            P(("seq", "fsdp"), None),
            P(("seq", "fsdp"), "ctx", None),
            P("fsdp"),
            P("fsdp", None),
            P("fsdp"),
            P("fsdp", None),
            P("fsdp"),
            P("fsdp", None),
            P("fsdp"),
            P("fsdp", None),
            P("fsdp"),
            P("fsdp", None),
            P("fsdp", None),
            P("fsdp", None),
        ),
        out_specs=(
            P(("seq", "fsdp"), "ctx", None),
            P(("seq", "fsdp"), "ctx", None),
            P("fsdp"),
            P("fsdp", None),
            P("fsdp"),
            P("fsdp", None),
            P("fsdp"),
            P("fsdp", None),
            P("fsdp"),
            P("fsdp", None),
            P("fsdp"),
            P("fsdp", None),
            P("fsdp", None),
            P("fsdp", None),
        ),
        check_vma=False,
    )
```

time: 1330 us -> 829 us (0.62)
  waiting for transfers between devices: 898 us -> 204 us
  matrix products: 246 us -> 0 us
  Pallas kernels: 0 us -> 176 us
  local copies, waits for them, and re-layouts: 44.2 us -> 206 us
  starting transfers between devices: 1.58 us -> 103 us
  blocking collectives: 57.3 us -> 37.1 us
    psum x1, waiting for transfers between devices: 715 us -> 0.01 us  [on_device(): gw_in = lax.psum(add(in_mine, swap(in_theirs)), ('seq', 'ctx'))]
    dot_general x35 -> x0, matrix products: 246 us -> none  [the longest x4 47 us: scores_of(): jnp.einsum('tgd,sd->gts', query_g, key_g, preferred_element_type=jnp.floa...]
    ppermute x0 -> x85, waiting for transfers between devices: none -> 204 us  [the longest x63 189 us: flip(): return lax.ppermute(values, axis, [(i, i ^ 1 << bit) for i in range(size)])]
    pallas_call x0 -> x9, Pallas kernels: none -> 176 us  [the longest x3 93.2 us: feed(): call(functools.partial(feed_kernel, first=first, width=width), (jax.Shape...]
    reduce_scatter x8 -> x0, waiting for transfers between devices: 129 us -> none  [the longest x1 44.9 us: on_device(): lax.psum_scatter(lax.dynamic_slice_in_dim(full_terms, reach * count, lax....]
    ppermute x0 -> x85, starting transfers between devices: none -> 103 us  [the longest x63 88.1 us: flip(): return lax.ppermute(values, axis, [(i, i ^ 1 << bit) for i in range(size)])]
    dynamic_update_slice x0 -> x69, local copies, waits for them, and re-layouts: none -> 63.1 us  [the longest x35 29.9 us: join(): return lax.dynamic_update_index_in_dim(out, other, 1 - index, 0)]
    all_gather x6 -> x0, waiting for transfers between devices: 51.2 us -> none  [the longest x1 26.4 us: on_device(): whole_pairs = lax.all_gather(own_pairs, 'ctx', axis=0, tiled=True)]
  transfers between devices with their start and end apart: 15 -> 86, of which waited for: 9 -> 34; matrix products, arithmetic and copies ran while one was open for 11% -> 32% of each run, Pallas kernels for 0% -> 18%
where the time goes in v1:
time: 829 us; the launch traced here: 820 us
  local copies, waits for them, and re-layouts  206 us (25%)
  waiting for transfers between devices  204 us (25%)
  Pallas kernels  176 us (21%)
  starting transfers between devices  103 us (12%)
  other arithmetic  78.2 us (9%)
  blocking collectives  37.1 us (4%)
  between operations  15.7 us (2%)
    ppermute x63, waiting for transfers between devices, flip(): return lax.ppermute(values, axis, [(i, i ^ 1 << bit) for i in range(size)])  189 us
    pallas_call x3, Pallas kernels, feed(): call(functools.partial(feed_kernel, first=first, width=width), (jax.Shape...  93.2 us
    ppermute x63, starting transfers between devices, flip(): return lax.ppermute(values, axis, [(i, i ^ 1 << bit) for i in range(size)])  88.1 us
    convert_element_type x29, other arithmetic, add(): return total.astype(bf16)  39.9 us
    psum x1, blocking collectives, on_device(): small_sums = lax.psum(jnp.concatenate(small), ('seq', 'ctx', 'fsdp'))  37.1 us
    dynamic_update_slice x35, local copies, waits for them, and re-layouts, join(): return lax.dynamic_update_index_in_dim(out, other, 1 - index, 0)  29.9 us
    pallas_call x1, Pallas kernels, attend_back(): call(attend_back_kernel, (jax.ShapeDtypeStruct((count, HQ * HD), bf16), j...  29.7 us
    unnamed x159, local copies, waits for them, and re-layouts  28.4 us
  transfers between devices with their start and end apart: 86, of which 34 were waited for; matrix products, arithmetic and copies ran while one was open for 32% of the time, Pallas kernels for 18%

profile of v1, /device:TPU:0, one launch (start us, length us, event | category | flops | bytes accessed | tf_op | source)
XLA Modules:
  0.0 820.3 jit_solution(14265766782979175884)
XLA Ops:
  7.3 4.2 concatenate.147
  42.3 3.6 fusion.44
  58.8 2.8 slice.110.refs_7_
  75.7 5.1 shard_map.254
  80.8 5.2 collective-permute-start.2
  86.0 4.7 collective-permute-start.3
  93.0 4.8 collective-permute-done.3.kv2_ref
  98.4 22.7 %shard_map.255 = (bf16[512,896]{1,0:T(8,128)(2,1)}, f32[7,8,512]{2,1,0:T(8,128)}) custom-call(bf16[512,896]{1,0:T(8,128)(2,1)} %get-tuple-element.57.q_ref, bf16[512,256]{1,0:T(8,128)(2,1)} %get-tuple-element.58.kv0_ref, bf16[512,256]{1,0:T(8,128)(2,1)} %copy-done.72, bf16[512,256]{1,0:T(8,128)(2,1)} %copy-done.73, ...), custom_call_target="tpu_custom_call" | custom-call | flops 9395240960 | bytes 4194304 | tf_op jit(solution)/shard_map/pallas_call | solution.py:212
  121.1 5.2 shard_map.256
  135.1 27.3 %shard_map.257 = (bf16[5376,128]{1,0:T(8,128)(2,1)}, bf16[5376,128]{1,0:T(8,128)(2,1)}, bf16[5376,128]{1,0:T(8,128)(2,1)}, f32[512,896]{1,0:T(8,128)}, f32[512,8...) custom-call(s32[1]{0:T(128)} %bitcast.12.refs_0_.me_ref, bf16[512,896]{1,0:T(8,128)(2,1)} %get-tuple-element.61.refs_1_, ...), custom_call_target="tpu_custom_call" | custom-call | flops 12683575296 | bytes 41943040 | tf_op jit(solution)/shard_map/pallas_call | solution.py:493
  165.2 30.1 %shard_map.258 = (bf16[5376,128]{1,0:T(8,128)(2,1)}, bf16[5376,128]{1,0:T(8,128)(2,1)}, bf16[5376,128]{1,0:T(8,128)(2,1)}, f32[512,896]{1,0:T(8,128)}, f32[512,8...) custom-call(s32[1]{0:T(128)} %bitcast.12.refs_0_.me_ref, ...), custom_call_target="tpu_custom_call", output_to_operand_aliasing={{3}: (8, {}), {4}: (9, {}), {5}: (10, {}), {6}: (11, {})} | custom-call | flops 12683575296 | bytes 41943040 | tf_op jit(solution)/shard_map/pallas_call | solution.py:493
  197.0 35.7 %shard_map.259 = (bf16[6272,128]{1,0:T(8,128)(2,1)}, bf16[6272,128]{1,0:T(8,128)(2,1)}, bf16[6272,128]{1,0:T(8,128)(2,1)}, f32[512,896]{1,0:T(8,128)}, f32[512,8...) custom-call(s32[1]{0:T(128)} %bitcast.12.refs_0_.me_ref, ...), custom_call_target="tpu_custom_call", output_to_operand_aliasing={{3}: (8, {}), {4}: (9, {}), {5}: (10, {}), {6}: (11, {})} | custom-call | flops 14797504512 | bytes 41943040 | tf_op jit(solution)/shard_map/pallas_call | solution.py:493
  245.1 9.8 %collective-permute-done.71 = bf16[2,2,672,128]{3,2,1,0:T(8,128)(2,1)S(1)} collective-permute-done((bf16[2,2,672,128]{3,2,1,0:T(8,128)(2,1)S(1)}, bf16[2,2,672,128]{3,2,1,0:T(8,128)(2,1)S(1)}, u32[]{:S(2)}, u32[]{:S(2)}) %collective-permute-start.71) | collective-permute-done | bytes 688160 | tf_op jit(solution)/shard_map/ppermute | solution.py:656
  255.8 13.8 %collective-permute-done.64 = bf16[2,2,672,128]{3,2,1,0:T(8,128)(2,1)S(1)} collective-permute-done((bf16[2,2,672,128]{3,2,1,0:T(8,128)(2,1)S(1)}, bf16[2,2,672,128]{3,2,1,0:T(8,128)(2,1)S(1)}, u32[]{:S(2)}, u32[]{:S(2)}) %collective-permute-start.64) | collective-permute-done | bytes 688160 | tf_op jit(solution)/shard_map/ppermute | solution.py:656
  270.6 7.2 collective-permute-start.20
  278.6 6.9 collective-permute-done.78
  285.6 7.2 collective-permute-start.35
  294.5 11.5 %shard_map.260 = (f32[512,896]{1,0:T(8,128)}, bf16[512,896]{1,0:T(8,128)(2,1)}, f32[56,512]{1,0:T(8,128)}, f32[1,896]{1,0:T(1,128)}, bf16[3136,128]{1,0:T(8,128)(2,1)}, /*index=5*/bf16[3136,128]{1,0:T(8,128)(2,1)}) custom-call(s32[1]{0:T(128)} %bitcast.12.refs_0_.me_ref, f32[512,896]{1,0:T(8,128)} %get-tuple-element.72.part_ref, ...), custom_call_target="tpu_custom_call" | custom-call | flops 1644167168 | bytes 12582912 | tf_op jit(solution)/shard_map/pallas_call | solution.py:570
  306.1 29.7 %shard_map.261 = (bf16[512,896]{1,0:T(8,128)(2,1)}, f32[512,256]{1,0:T(8,128)}, bf16[512,256]{1,0:T(8,128)(2,1)}, bf16[512,256]{1,0:T(8,128)(2,1)}) custom-call(bf16[512,896]{1,0:T(8,128)(2,1)} %get-tuple-element.57.q_ref, bf16[512,896]{1,0:T(8,128)(2,1)} %get-tuple-element.74.do_ref, bf16[512,256]{1,0:T(8,128)(2,1)} %get-tuple-element.58.kv0_ref, ...), custom_call_target="tpu_custom_call" | custom-call | flops 23488102400 | bytes 6291456 | tf_op jit(solution)/shard_map/pallas_call | solution.py:346
  347.7 2.6 collective-permute-start.50
  352.4 8.5 %collective-permute-done.16.two_ref = bf16[512,256]{1,0:T(8,128)(2,1)S(1)} collective-permute-done((bf16[512,256]{1,0:T(8,128)(2,1)}, bf16[512,256]{1,0:T(8,128)(2,1)S(1)}, u32[]{:S(2)}, u32[]{:S(2)}) %collective-permute-start.16) | collective-permute-done | bytes 262176 | tf_op jit(solution)/shard_map/ppermute | solution.py:823
  362.4 8.9 %shard_map.262 = (bf16[512,896]{1,0:T(8,128)(2,1)}, f32[1,896]{1,0:T(1,128)}, f32[1,1152]{1,0:T(1,128)}, bf16[4032,128]{1,0:T(8,128)(2,1)}, bf16[4032,128]{1,0:T(8,128)(2,1)}) custom-call(s32[1]{0:T(128)} %bitcast.12.refs_0_.me_ref, bf16[512,896]{1,0:T(8,128)(2,1)} %get-tuple-element.77.dq_ref, f32[512,256]{1,0:T(8,128)} %get-tuple-element.78.own_ref, ...), custom_call_target="tpu_custom_call" | custom-call | flops 2113929216 | bytes 14680064 | tf_op jit(solution)/shard_map/pallas_call | solution.py:629
  374.0 37.1 %psum.21 = f32[2944]{0:T(1024)S(1)} all-reduce(f32[2944]{0:T(1024)S(1)} %constant_dynamic-update-slice_fusion.13), channel_id=1, replica_groups=mesh['seq'=4,'ctx'=4,'fsdp'=2] {'seq','ctx','fsdp'}, use_global_device_ids=true, to_apply=%region_0.1 | all-reduce | flops 2944 | bytes 23552 | tf_op jit(solution)/shard_map/psum | solution.py:865
  420.2 2.9 collective-permute-start.73
  424.2 2.8 collective-permute-done.73
  438.5 6.8 collective-permute-done.22
  445.4 9.7 %collective-permute-done.37 = bf16[672,128]{1,0:T(8,128)(2,1)S(1)} collective-permute-done((bf16[672,128]{1,0:T(8,128)(2,1)S(1)}, bf16[672,128]{1,0:T(8,128)(2,1)S(1)}, u32[]{:S(2)}, u32[]{:S(2)}) %collective-permute-start.37) | collective-permute-done | bytes 172064 | tf_op jit(solution)/shard_map/ppermute | solution.py:656
  455.3 10.1 %collective-permute-done.74 = bf16[672,128]{1,0:T(8,128)(2,1)S(1)} collective-permute-done((bf16[672,128]{1,0:T(8,128)(2,1)S(1)}, bf16[672,128]{1,0:T(8,128)(2,1)S(1)}, u32[]{:S(2)}, u32[]{:S(2)}) %collective-permute-start.74) | collective-permute-done | bytes 172064 | tf_op jit(solution)/shard_map/ppermute | solution.py:656
  465.5 10.0 %collective-permute-done.67 = bf16[672,128]{1,0:T(8,128)(2,1)S(1)} collective-permute-done((bf16[672,128]{1,0:T(8,128)(2,1)S(1)}, bf16[672,128]{1,0:T(8,128)(2,1)S(1)}, u32[]{:S(2)}, u32[]{:S(2)}) %collective-permute-start.67) | collective-permute-done | bytes 172064 | tf_op jit(solution)/shard_map/ppermute | solution.py:656
  480.4 3.3 collective-permute-done.51
  487.9 3.0 collective-permute-done.23
  490.9 2.6 collective-permute-done.38
  493.6 3.9 collective-permute-done.75
  497.5 3.7 collective-permute-done.68
  505.2 11.4 %collective-permute-done.52 = bf16[784,128]{1,0:T(8,128)(2,1)S(1)} collective-permute-done((bf16[784,128]{1,0:T(8,128)(2,1)S(1)}, bf16[784,128]{1,0:T(8,128)(2,1)S(1)}, u32[]{:S(2)}, u32[]{:S(2)}) %collective-permute-start.52) | collective-permute-done | bytes 200736 | tf_op jit(solution)/shard_map/ppermute | solution.py:656
  516.6 3.4 collective-permute-start.81
  520.1 8.3 %collective-permute-done.81 = bf16[784,128]{1,0:T(8,128)(2,1)S(1)} collective-permute-done((bf16[784,128]{1,0:T(8,128)(2,1)S(1)}, bf16[784,128]{1,0:T(8,128)(2,1)S(1)}, u32[]{:S(2)}, u32[]{:S(2)}) %collective-permute-start.81) | collective-permute-done | bytes 200736 | tf_op jit(solution)/shard_map/ppermute | solution.py:656
  534.8 2.6 collective-permute-done.53
  537.7 18.0 %collective-permute-done.82 = bf16[784,128]{1,0:T(8,128)(2,1)S(1)} collective-permute-done((bf16[784,128]{1,0:T(8,128)(2,1)S(1)}, bf16[784,128]{1,0:T(8,128)(2,1)S(1)}, u32[]{:S(2)}, u32[]{:S(2)}) %collective-permute-start.82) | collective-permute-done | bytes 200736 | tf_op jit(solution)/shard_map/ppermute | solution.py:656
  560.0 3.2 collective-permute-done.39
  582.6 8.9 %collective-permute-done.54 = bf16[2,784,128]{2,1,0:T(8,128)(2,1)S(1)} collective-permute-done((bf16[2,784,128]{2,1,0:T(8,128)(2,1)S(1)}, bf16[2,784,128]{2,1,0:T(8,128)(2,1)S(1)}, u32[]{:S(2)}, u32[]{:S(2)}) %collective-permute-start.54) | collective-permute-done | bytes 401440 | tf_op jit(solution)/shard_map/ppermute | solution.py:656
  598.5 2.6 copy.41
  605.9 7.3 collective-permute-done.43
  623.9 3.0 copy.43
  626.8 3.0 copy.44
  640.2 8.4 %collective-permute-done.70 = bf16[2,2,672,128]{3,2,1,0:T(8,128)(2,1)} collective-permute-done((bf16[2,2,672,128]{3,2,1,0:T(8,128)(2,1)}, bf16[2,2,672,128]{3,2,1,0:T(8,128)(2,1)}, u32[]{:S(2)}, u32[]{:S(2)}) %collective-permute-start.70) | collective-permute-done | bytes 688160 | tf_op jit(solution)/shard_map/ppermute | solution.py:656
  651.0 4.1 broadcast.213.clone
  656.2 3.0 copy.47
  659.2 3.0 copy.48
  662.2 3.0 copy.53
  665.2 2.9 copy.54
  668.1 3.0 copy.57
  671.1 2.9 copy.58
  674.0 2.6 copy.64
  687.5 3.1 collective-permute-done.30
  690.8 3.3 collective-permute-start.31
  708.4 2.9 copy.65
  711.3 5.2 maximum_convert_fusion
  721.3 10.8 %copy.69 = f32[2432,896]{1,0:T(8,128)} copy(f32[2432,896]{0,1:T(8,128)} %maximum_convert_fusion) | data formatting | bytes 17432576
  732.3 2.7 collective-permute-start.61
  741.7 5.8 collective-permute-done.62
  751.1 3.4 collective-permute-done.33
  755.8 13.4 %collective-permute-done.48 = bf16[2,2,672,128]{3,2,1,0:T(8,128)(2,1)S(1)} collective-permute-done((bf16[2,2,672,128]{3,2,1,0:T(8,128)(2,1)S(1)}, bf16[2,2,672,128]{3,2,1,0:T(8,128)(2,1)S(1)}, u32[]{:S(2)}, u32[]{:S(2)}) %collective-permute-start.48) | collective-permute-done | bytes 688160 | tf_op jit(solution)/shard_map/ppermute | solution.py:656
  788.3 2.6 constant_dynamic-update-slice_fusion.5
  (522 shorter events, 293.9 us)
Async XLA Ops:
  7.2 795.1 %all-reduce.4.cloned.1.call-start = ((), (), s32[]{:S(2)}) async-start(), calls=%async_computation | async-start | bytes 3964928 | tf_op jit(solution)/shard_map/psum | solution.py:855
  11.4 52.1 %collective-permute-start = (bf16[1472]{0:T(1024)(128)(2,1)}, bf16[1472]{0:T(1024)(128)(2,1)}, u32[]{:S(2)}, u32[]{:S(2)}) collective-permute-start(bf16[1472]{0:T(1024)(128)(2,1)} %concatenate.147), channel_id=1, source_target_pairs={{0,1},{1,0},{2,3},{3,2},{4,5},{5,4},{6,7},{7,6},{8,9},{9,8},{10,11... | collective-permute-start | bytes 8840 | tf_op jit(solution)/shard_map/ppermute | solution.py:650
  13.2 59.8 %collective-permute-start.1 = (bf16[448,1152]{1,0:T(8,128)(2,1)S(1)}, bf16[448,1152]{1,0:T(8,128)(2,1)}, u32[]{:S(2)}, u32[]{:S(2)}) collective-permute-start(bf16[448,1152]{1,0:T(8,128)(2,1)S(1)} %constant_dynamic-update-slice_fusion.8), channel_id=1, source_target_pairs={{0,1},{1,0},{2,3},{3,2},{4,5},{5,4},{6,7},{7,6},{8,9},{9,8},{10,11... | collective-permute-start | bytes 3096584 | tf_op jit(solution)/shard_map/ppermute | solution.py:650
  13.3 72.7 %collective-permute-start.4 = (bf16[448,896]{1,0:T(8,128)(2,1)}, bf16[448,896]{1,0:T(8,128)(2,1)}, u32[]{:S(2)}, u32[]{:S(2)}) collective-permute-start(bf16[448,896]{1,0:T(8,128)(2,1)} %param.25), channel_id=1, source_target_pairs={{0,1},{1,0},{2,3},{3,2},{4,5},{5,4},{6,7},{7,6},{8,9},{9,8},{10,11... | collective-permute-start | bytes 2408456 | tf_op jit(solution)/shard_map/ppermute | solution.py:650
  13.8 120.4 %collective-permute-start.6 = (bf16[512,896]{1,0:T(8,128)(2,1)S(1)}, bf16[512,896]{1,0:T(8,128)(2,1)}, u32[]{:S(2)}, u32[]{:S(2)}) collective-permute-start(bf16[512,896]{1,0:T(8,128)(2,1)S(1)} %bitcast.573), channel_id=1, source_target_pairs={{0,1},{1,0},{2,3},{3,2},{4,5},{5,4},{6,7},{7,6},{8,9},{9,8},{10,11... | collective-permute-start | bytes 2752520 | tf_op jit(solution)/shard_map/ppermute | solution.py:650
  16.3 53.3 %collective-permute-start.9 = (bf16[448,768]{1,0:T(8,128)(2,1)}, bf16[448,768]{1,0:T(8,128)(2,1)}, u32[]{:S(2)}, u32[]{:S(2)}) collective-permute-start(bf16[448,768]{1,0:T(8,128)(2,1)} %get-tuple-element.139), channel_id=1, source_target_pairs={{0,1},{1,0},{2,3},{3,2},{4,5},{5,4},{6,7},{7,6},{8,9},{9,8},{10,11... | collective-permute-start | bytes 2064392 | tf_op jit(solution)/shard_map/ppermute | solution.py:650
  69.6 60.4 %collective-permute-start.7 = (bf16[448,896]{1,0:T(8,128)(2,1)}, bf16[448,896]{1,0:T(8,128)(2,1)}, u32[]{:S(2)}, u32[]{:S(2)}) collective-permute-start(bf16[448,896]{1,0:T(8,128)(2,1)} %constant_dynamic-slice_fusion.5), channel_id=1, source_target_pairs={{0,1},{1,0},{2,3},{3,2},{4,5},{5,4},{6,7},{7,6},{8,9},{9,8},{10,11... | collective-permute-start | bytes 2408456 | tf_op jit(solution)/shard_map/ppermute | solution.py:650
  72.1 60.0 %collective-permute-start.8 = (bf16[448,896]{1,0:T(8,128)(2,1)}, bf16[448,896]{1,0:T(8,128)(2,1)}, u32[]{:S(2)}, u32[]{:S(2)}) collective-permute-start(bf16[448,896]{1,0:T(8,128)(2,1)} %constant_dynamic-slice_fusion.4), channel_id=1, source_target_pairs={{0,1},{1,0},{2,3},{3,2},{4,5},{5,4},{6,7},{7,6},{8,9},{9,8},{10,11... | collective-permute-start | bytes 2408456 | tf_op jit(solution)/shard_map/ppermute | solution.py:650
  80.8 12.1 %collective-permute-start.2 = (bf16[512,256]{1,0:T(8,128)(2,1)}, bf16[512,256]{1,0:T(8,128)(2,1)S(1)}, u32[]{:S(2)}, u32[]{:S(2)}) collective-permute-start(bf16[512,256]{1,0:T(8,128)(2,1)} %get-tuple-element.58.kv0_ref), channel_id=1, source_target_pairs={{0,2},{2,4},{4,6},{1,3},{3,5},{5,7},{8,10},{10,12},{12,14},{9,11},... | collective-permute-start | bytes 786440 | tf_op jit(solution)/shard_map/ppermute | solution.py:776
  86.0 11.7 %collective-permute-start.3 = (bf16[512,256]{1,0:T(8,128)(2,1)}, bf16[512,256]{1,0:T(8,128)(2,1)S(1)}, u32[]{:S(2)}, u32[]{:S(2)}) collective-permute-start(bf16[512,256]{1,0:T(8,128)(2,1)} %get-tuple-element.58.kv0_ref), channel_id=1, source_target_pairs={{0,4},{2,6},{1,5},{3,7},{8,12},{10,14},{9,13},{11,15},{16,20},{18,... | collective-permute-start | bytes 786440 | tf_op jit(solution)/shard_map/ppermute | solution.py:776
  93.0 33.3 %collective-permute-start.11 = (bf16[448,768]{1,0:T(8,128)(2,1)S(1)}, bf16[448,768]{1,0:T(8,128)(2,1)}, u32[]{:S(2)}, u32[]{:S(2)}) collective-permute-start(bf16[448,768]{1,0:T(8,128)(2,1)S(1)} %copy-done.50), channel_id=1, source_target_pairs={{0,1},{1,0},{2,3},{3,2},{4,5},{5,4},{6,7},{7,6},{8,9},{9,8},{10,11... | collective-permute-start | bytes 2064392 | tf_op jit(solution)/shard_map/ppermute | solution.py:650
  97.7 29.7 %collective-permute-start.12 = (bf16[448,768]{1,0:T(8,128)(2,1)S(1)}, bf16[448,768]{1,0:T(8,128)(2,1)}, u32[]{:S(2)}, u32[]{:S(2)}) collective-permute-start(bf16[448,768]{1,0:T(8,128)(2,1)S(1)} %copy-done.51), channel_id=1, source_target_pairs={{0,1},{1,0},{2,3},{3,2},{4,5},{5,4},{6,7},{7,6},{8,9},{9,8},{10,11... | collective-permute-start | bytes 2064392 | tf_op jit(solution)/shard_map/ppermute | solution.py:650
  163.6 75.1 %collective-permute-start.19 = (bf16[2,2,672,128]{3,2,1,0:T(8,128)(2,1)S(1)}, bf16[2,2,672,128]{3,2,1,0:T(8,128)(2,1)}, u32[]{:S(2)}, u32[]{:S(2)}) collective-permute-start(bf16[2,2,672,128]{3,2,1,0:T(8,128)(2,1)S(1)} %dynamic-slice_bitcast_fusion.8), channel_id=1, source_target_pairs={{0,16},{8,24},{16,0},{24,8},{1,17},{9,25},{17,1},{25,9},{2,18},{10... | collective-permute-start | bytes 2064392 | tf_op jit(solution)/shard_map/ppermute | solution.py:656
  196.4 42.4 %collective-permute-start.34 = (bf16[2,2,672,128]{3,2,1,0:T(8,128)(2,1)S(1)}, bf16[2,2,672,128]{3,2,1,0:T(8,128)(2,1)}, u32[]{:S(2)}, u32[]{:S(2)}) collective-permute-start(bf16[2,2,672,128]{3,2,1,0:T(8,128)(2,1)S(1)} %dynamic-slice_bitcast_fusion.6), channel_id=1, source_target_pairs={{0,16},{8,24},{16,0},{24,8},{1,17},{9,25},{17,1},{25,9},{2,18},{10... | collective-permute-start | bytes 2064392 | tf_op jit(solution)/shard_map/ppermute | solution.py:656
  234.8 35.8 %collective-permute-start.49 = (bf16[2,2,784,128]{3,2,1,0:T(8,128)(2,1)S(1)}, bf16[2,2,784,128]{3,2,1,0:T(8,128)(2,1)S(1)}, u32[]{:S(2)}, u32[]{:S(2)}) collective-permute-start(bf16[2,2,784,128]{3,2,1,0:T(8,128)(2,1)S(1)} %dynamic-slice_bitcast_fusion.2), channel_id=1, source_target_pairs={{0,16},{8,24},{16,0},{24,8},{1,17},{9,25},{17,1},{25,9},{2,18},{10... | collective-permute-start | bytes 2408456 | tf_op jit(solution)/shard_map/ppermute | solution.py:656
  236.5 18.4 %collective-permute-start.71 = (bf16[2,2,672,128]{3,2,1,0:T(8,128)(2,1)S(1)}, bf16[2,2,672,128]{3,2,1,0:T(8,128)(2,1)S(1)}, u32[]{:S(2)}, u32[]{:S(2)}) collective-permute-start(bf16[2,2,672,128]{3,2,1,0:T(8,128)(2,1)S(1)} %dynamic-slice_bitcast_fusion.3), channel_id=1, source_target_pairs={{0,8},{8,0},{16,24},{24,16},{1,9},{9,1},{17,25},{25,17},{2,10},{10... | collective-permute-start | bytes 2064392 | tf_op jit(solution)/shard_map/ppermute | solution.py:656
  238.1 31.5 %collective-permute-start.64 = (bf16[2,2,672,128]{3,2,1,0:T(8,128)(2,1)S(1)}, bf16[2,2,672,128]{3,2,1,0:T(8,128)(2,1)S(1)}, u32[]{:S(2)}, u32[]{:S(2)}) collective-permute-start(bf16[2,2,672,128]{3,2,1,0:T(8,128)(2,1)S(1)} %dynamic-slice_bitcast_fusion.4), channel_id=1, source_target_pairs={{0,8},{8,0},{16,24},{24,16},{1,9},{9,1},{17,25},{25,17},{2,10},{10... | collective-permute-start | bytes 2064392 | tf_op jit(solution)/shard_map/ppermute | solution.py:656
  238.7 54.9 %collective-permute-start.14 = (bf16[512,896]{1,0:T(8,128)(2,1)S(1)}, bf16[512,896]{1,0:T(8,128)(2,1)S(1)}, u32[]{:S(2)}, u32[]{:S(2)}) collective-permute-start(bf16[512,896]{1,0:T(8,128)(2,1)S(1)} %convert_element_type.909), channel_id=1, source_target_pairs={{0,1},{1,0},{2,3},{3,2},{4,5},{5,4},{6,7},{7,6},{8,9},{9,8},{10,11... | collective-permute-start | bytes 2752520 | tf_op jit(solution)/shard_map/ppermute | solution.py:650
  238.8 46.7 %collective-permute-start.78 = (bf16[2,2,784,128]{3,2,1,0:T(8,128)(2,1)S(1)}, bf16[2,2,784,128]{3,2,1,0:T(8,128)(2,1)S(1)}, u32[]{:S(2)}, u32[]{:S(2)}) collective-permute-start(bf16[2,2,784,128]{3,2,1,0:T(8,128)(2,1)S(1)} %dynamic-slice_bitcast_fusion), channel_id=1, source_target_pairs={{0,8},{8,0},{16,24},{24,16},{1,9},{9,1},{17,25},{25,17},{2,10},{10... | collective-permute-start | bytes 2408456 | tf_op jit(solution)/shard_map/ppermute | solution.py:656
  254.9 81.0 %collective-permute-start.13 = (bf16[512,896]{1,0:T(8,128)(2,1)S(1)}, bf16[512,896]{1,0:T(8,128)(2,1)}, u32[]{:S(2)}, u32[]{:S(2)}) collective-permute-start(bf16[512,896]{1,0:T(8,128)(2,1)S(1)} %convert_element_type.906), channel_id=1, source_target_pairs={{0,1},{1,0},{2,3},{3,2},{4,5},{5,4},{6,7},{7,6},{8,9},{9,8},{10,11... | collective-permute-start | bytes 2752520 | tf_op jit(solution)/shard_map/ppermute | solution.py:650
  269.6 206.0 %collective-permute-start.26 = (bf16[5376,128]{1,0:T(8,128)(2,1)}, bf16[5376,128]{1,0:T(8,128)(2,1)}, u32[]{:S(2)}, u32[]{:S(2)}) collective-permute-start(bf16[5376,128]{1,0:T(8,128)(2,1)} %get-tuple-element.92), channel_id=1, source_target_pairs={{0,1},{1,0},{2,3},{3,2},{4,5},{5,4},{6,7},{7,6},{8,9},{9,8},{10,11... | collective-permute-start | bytes 4128776 | tf_op jit(solution)/shard_map/ppermute | solution.py:650
  270.6 68.9 %collective-permute-start.20 = (bf16[2,672,128]{2,1,0:T(8,128)(2,1)}, bf16[2,672,128]{2,1,0:T(8,128)(2,1)}, u32[]{:S(2)}, u32[]{:S(2)}) collective-permute-start(bf16[2,672,128]{2,1,0:T(8,128)(2,1)} %fusion.9), channel_id=1, source_target_pairs={{0,2},{2,0},{4,6},{6,4},{1,3},{3,1},{5,7},{7,5},{8,10},{10,8},{12,... | collective-permute-start | bytes 1032200 | tf_op jit(solution)/shard_map/ppermute | solution.py:656
  285.6 57.2 %collective-permute-start.35 = (bf16[2,672,128]{2,1,0:T(8,128)(2,1)}, bf16[2,672,128]{2,1,0:T(8,128)(2,1)}, u32[]{:S(2)}, u32[]{:S(2)}) collective-permute-start(bf16[2,672,128]{2,1,0:T(8,128)(2,1)} %fusion.7), channel_id=1, source_target_pairs={{0,2},{2,0},{4,6},{6,4},{1,3},{3,1},{5,7},{7,5},{8,10},{10,8},{12,... | collective-permute-start | bytes 1032200 | tf_op jit(solution)/shard_map/ppermute | solution.py:656
  293.6 52.3 %collective-permute-start.72 = (bf16[2,672,128]{2,1,0:T(8,128)(2,1)}, bf16[2,672,128]{2,1,0:T(8,128)(2,1)}, u32[]{:S(2)}, u32[]{:S(2)}) collective-permute-start(bf16[2,672,128]{2,1,0:T(8,128)(2,1)} %fusion.4), channel_id=1, source_target_pairs={{0,16},{8,24},{16,0},{24,8},{1,17},{9,25},{17,1},{25,9},{2,18},{10... | collective-permute-start | bytes 1032200 | tf_op jit(solution)/shard_map/ppermute | solution.py:656
  335.8 11.8 %collective-permute-start.65 = (bf16[2,672,128]{2,1,0:T(8,128)(2,1)}, bf16[2,672,128]{2,1,0:T(8,128)(2,1)}, u32[]{:S(2)}, u32[]{:S(2)}) collective-permute-start(bf16[2,672,128]{2,1,0:T(8,128)(2,1)} %fusion.5), channel_id=1, source_target_pairs={{0,16},{8,24},{16,0},{24,8},{1,17},{9,25},{17,1},{25,9},{2,18},{10... | collective-permute-start | bytes 1032200 | tf_op jit(solution)/shard_map/ppermute | solution.py:656
  339.5 11.9 %collective-permute-start.15 = (bf16[512,256]{1,0:T(8,128)(2,1)}, bf16[512,256]{1,0:T(8,128)(2,1)S(1)}, u32[]{:S(2)}, u32[]{:S(2)}) collective-permute-start(bf16[512,256]{1,0:T(8,128)(2,1)} %get-tuple-element.79), channel_id=1, source_target_pairs={{2,0},{4,2},{6,4},{3,1},{5,3},{7,5},{10,8},{12,10},{14,12},{11,9},... | collective-permute-start | bytes 786440 | tf_op jit(solution)/shard_map/ppermute | solution.py:823
  342.8 18.1 %collective-permute-start.16 = (bf16[512,256]{1,0:T(8,128)(2,1)}, bf16[512,256]{1,0:T(8,128)(2,1)S(1)}, u32[]{:S(2)}, u32[]{:S(2)}) collective-permute-start(bf16[512,256]{1,0:T(8,128)(2,1)} %get-tuple-element.80), channel_id=1, source_target_pairs={{4,0},{6,2},{5,1},{7,3},{12,8},{14,10},{13,9},{15,11},{20,16},{22,... | collective-permute-start | bytes 786440 | tf_op jit(solution)/shard_map/ppermute | solution.py:823
  345.9 133.3 %collective-permute-start.41 = (bf16[5376,128]{1,0:T(8,128)(2,1)}, bf16[5376,128]{1,0:T(8,128)(2,1)}, u32[]{:S(2)}, u32[]{:S(2)}) collective-permute-start(bf16[5376,128]{1,0:T(8,128)(2,1)} %get-tuple-element.94), channel_id=1, source_target_pairs={{0,1},{1,0},{2,3},{3,2},{4,5},{5,4},{6,7},{7,6},{8,9},{9,8},{10,11... | collective-permute-start | bytes 4128776 | tf_op jit(solution)/shard_map/ppermute | solution.py:650
  347.7 86.2 %collective-permute-start.50 = (bf16[2,784,128]{2,1,0:T(8,128)(2,1)}, bf16[2,784,128]{2,1,0:T(8,128)(2,1)}, u32[]{:S(2)}, u32[]{:S(2)}) collective-permute-start(bf16[2,784,128]{2,1,0:T(8,128)(2,1)} %fusion.3), channel_id=1, source_target_pairs={{0,2},{2,0},{4,6},{6,4},{1,3},{3,1},{5,7},{7,5},{8,10},{10,8},{12,... | collective-permute-start | bytes 1204232 | tf_op jit(solution)/shard_map/ppermute | solution.py:656
  351.4 85.7 %collective-permute-start.79 = (bf16[2,784,128]{2,1,0:T(8,128)(2,1)}, bf16[2,784,128]{2,1,0:T(8,128)(2,1)}, u32[]{:S(2)}, u32[]{:S(2)}) collective-permute-start(bf16[2,784,128]{2,1,0:T(8,128)(2,1)} %fusion.1), channel_id=1, source_target_pairs={{0,16},{8,24},{16,0},{24,8},{1,17},{9,25},{17,1},{25,9},{2,18},{10... | collective-permute-start | bytes 1204232 | tf_op jit(solution)/shard_map/ppermute | solution.py:656
  360.9 53.4 %collective-permute-start.21 = (bf16[672,128]{1,0:T(8,128)(2,1)}, bf16[672,128]{1,0:T(8,128)(2,1)}, u32[]{:S(2)}, u32[]{:S(2)}) collective-permute-start(bf16[672,128]{1,0:T(8,128)(2,1)} %fusion.34), channel_id=1, source_target_pairs={{0,8},{8,0},{16,24},{24,16},{1,9},{9,1},{17,25},{25,17},{2,10},{10... | collective-permute-start | bytes 516104 | tf_op jit(solution)/shard_map/ppermute | solution.py:656
  432.7 95.8 %collective-permute-start.56 = (bf16[6272,128]{1,0:T(8,128)(2,1)S(1)}, bf16[6272,128]{1,0:T(8,128)(2,1)S(1)}, u32[]{:S(2)}, u32[]{:S(2)}) collective-permute-start(bf16[6272,128]{1,0:T(8,128)(2,1)S(1)} %copy-done.68), channel_id=1, source_target_pairs={{0,1},{1,0},{2,3},{3,2},{4,5},{5,4},{6,7},{7,6},{8,9},{9,8},{10,11... | collective-permute-start | bytes 4816904 | tf_op jit(solution)/shard_map/ppermute | solution.py:650
  433.9 11.4 %collective-permute-start.22 = (bf16[672,128]{1,0:T(8,128)(2,1)S(1)}, bf16[672,128]{1,0:T(8,128)(2,1)S(1)}, u32[]{:S(2)}, u32[]{:S(2)}) collective-permute-start(bf16[672,128]{1,0:T(8,128)(2,1)S(1)} %fusion.36), channel_id=1, source_target_pairs={{0,4},{2,6},{4,0},{6,2},{1,5},{3,7},{5,1},{7,3},{8,12},{10,14},{12... | collective-permute-start | bytes 516104 | tf_op jit(solution)/shard_map/ppermute | solution.py:656
  437.2 94.5 %collective-permute-start.18 = (bf16[3136,128]{1,0:T(8,128)(2,1)S(1)}, bf16[3136,128]{1,0:T(8,128)(2,1)S(1)}, u32[]{:S(2)}, u32[]{:S(2)}) collective-permute-start(bf16[3136,128]{1,0:T(8,128)(2,1)S(1)} %copy-done.71), channel_id=1, source_target_pairs={{0,1},{1,0},{2,3},{3,2},{4,5},{5,4},{6,7},{7,6},{8,9},{9,8},{10,11... | collective-permute-start | bytes 2408456 | tf_op jit(solution)/shard_map/ppermute | solution.py:650
  455.1 10.2 %collective-permute-start.74 = (bf16[672,128]{1,0:T(8,128)(2,1)S(1)}, bf16[672,128]{1,0:T(8,128)(2,1)S(1)}, u32[]{:S(2)}, u32[]{:S(2)}) collective-permute-start(bf16[672,128]{1,0:T(8,128)(2,1)S(1)} %fusion.21), channel_id=1, source_target_pairs={{0,4},{2,6},{4,0},{6,2},{1,5},{3,7},{5,1},{7,3},{8,12},{10,14},{12... | collective-permute-start | bytes 516104 | tf_op jit(solution)/shard_map/ppermute | solution.py:656
  475.4 120.9 %collective-permute-start.17 = (bf16[4032,128]{1,0:T(8,128)(2,1)S(1)}, bf16[4032,128]{1,0:T(8,128)(2,1)S(1)}, u32[]{:S(2)}, u32[]{:S(2)}) collective-permute-start(bf16[4032,128]{1,0:T(8,128)(2,1)S(1)} %copy-done.69), channel_id=1, source_target_pairs={{0,1},{1,0},{2,3},{3,2},{4,5},{5,4},{6,7},{7,6},{8,9},{9,8},{10,11... | collective-permute-start | bytes 3096584 | tf_op jit(solution)/shard_map/ppermute | solution.py:650
  497.5 79.4 %collective-permute-start.27 = (bf16[2,2,672,128]{3,2,1,0:T(8,128)(2,1)S(1)}, bf16[2,2,672,128]{3,2,1,0:T(8,128)(2,1)S(1)}, u32[]{:S(2)}, u32[]{:S(2)}) collective-permute-start(bf16[2,2,672,128]{3,2,1,0:T(8,128)(2,1)S(1)} %dynamic-slice_bitcast_fusion.7), channel_id=1, source_target_pairs={{0,2},{2,0},{4,6},{6,4},{1,3},{3,1},{5,7},{7,5},{8,10},{10,8},{12,... | collective-permute-start | bytes 2064392 | tf_op jit(solution)/shard_map/ppermute | solution.py:656
  501.2 15.4 %collective-permute-start.52 = (bf16[784,128]{1,0:T(8,128)(2,1)S(1)}, bf16[784,128]{1,0:T(8,128)(2,1)S(1)}, u32[]{:S(2)}, u32[]{:S(2)}) collective-permute-start(bf16[784,128]{1,0:T(8,128)(2,1)S(1)} %fusion.18), channel_id=1, source_target_pairs={{0,4},{2,6},{4,0},{6,2},{1,5},{3,7},{5,1},{7,3},{8,12},{10,14},{12... | collective-permute-start | bytes 602120 | tf_op jit(solution)/shard_map/ppermute | solution.py:656
  516.6 11.8 %collective-permute-start.81 = (bf16[784,128]{1,0:T(8,128)(2,1)S(1)}, bf16[784,128]{1,0:T(8,128)(2,1)S(1)}, u32[]{:S(2)}, u32[]{:S(2)}) collective-permute-start(bf16[784,128]{1,0:T(8,128)(2,1)S(1)} %fusion.12), channel_id=1, source_target_pairs={{0,4},{2,6},{4,0},{6,2},{1,5},{3,7},{5,1},{7,3},{8,12},{10,14},{12... | collective-permute-start | bytes 602120 | tf_op jit(solution)/shard_map/ppermute | solution.py:656
  528.4 51.4 %collective-permute-start.42 = (bf16[2,2,672,128]{3,2,1,0:T(8,128)(2,1)S(1)}, bf16[2,2,672,128]{3,2,1,0:T(8,128)(2,1)S(1)}, u32[]{:S(2)}, u32[]{:S(2)}) collective-permute-start(bf16[2,2,672,128]{3,2,1,0:T(8,128)(2,1)S(1)} %dynamic-slice_bitcast_fusion.5), channel_id=1, source_target_pairs={{0,2},{2,0},{4,6},{6,4},{1,3},{3,1},{5,7},{7,5},{8,10},{10,8},{12,... | collective-permute-start | bytes 2064392 | tf_op jit(solution)/shard_map/ppermute | solution.py:656
  528.6 29.3 %collective-permute-start.24 = (bf16[2,672,128]{2,1,0:T(8,128)(2,1)S(1)}, bf16[2,672,128]{2,1,0:T(8,128)(2,1)S(1)}, u32[]{:S(2)}, u32[]{:S(2)}) collective-permute-start(bf16[2,672,128]{2,1,0:T(8,128)(2,1)S(1)} %bitcast_dynamic-update-slice_fusion.72), channel_id=1, source_target_pairs={{0,2},{2,0},{4,6},{6,4},{1,3},{3,1},{5,7},{7,5},{8,10},{10,8},{12,... | collective-permute-start | bytes 1032200 | tf_op jit(solution)/shard_map/ppermute | solution.py:656
  537.4 18.4 %collective-permute-start.82 = (bf16[784,128]{1,0:T(8,128)(2,1)S(1)}, bf16[784,128]{1,0:T(8,128)(2,1)S(1)}, u32[]{:S(2)}, u32[]{:S(2)}) collective-permute-start(bf16[784,128]{1,0:T(8,128)(2,1)S(1)} %get-tuple-element.121), channel_id=1, source_target_pairs={{0,2},{2,0},{4,6},{6,4},{1,3},{3,1},{5,7},{7,5},{8,10},{10,8},{12,... | collective-permute-start | bytes 602120 | tf_op jit(solution)/shard_map/ppermute | solution.py:656
  557.9 10.4 %collective-permute-start.76 = (bf16[2,672,128]{2,1,0:T(8,128)(2,1)S(1)}, bf16[2,672,128]{2,1,0:T(8,128)(2,1)S(1)}, u32[]{:S(2)}, u32[]{:S(2)}) collective-permute-start(bf16[2,672,128]{2,1,0:T(8,128)(2,1)S(1)} %bitcast_dynamic-update-slice_fusion.62), channel_id=1, source_target_pairs={{0,16},{8,24},{16,0},{24,8},{1,17},{9,25},{17,1},{25,9},{2,18},{10... | collective-permute-start | bytes 1032200 | tf_op jit(solution)/shard_map/ppermute | solution.py:656
  568.3 48.0 %collective-permute-start.57 = (bf16[2,2,784,128]{3,2,1,0:T(8,128)(2,1)}, bf16[2,2,784,128]{3,2,1,0:T(8,128)(2,1)}, u32[]{:S(2)}, u32[]{:S(2)}) collective-permute-start(bf16[2,2,784,128]{3,2,1,0:T(8,128)(2,1)} %dynamic-slice_bitcast_fusion.1), channel_id=1, source_target_pairs={{0,2},{2,0},{4,6},{6,4},{1,3},{3,1},{5,7},{7,5},{8,10},{10,8},{12,... | collective-permute-start | bytes 2408456 | tf_op jit(solution)/shard_map/ppermute | solution.py:656
  572.7 18.8 %collective-permute-start.54 = (bf16[2,784,128]{2,1,0:T(8,128)(2,1)S(1)}, bf16[2,784,128]{2,1,0:T(8,128)(2,1)S(1)}, u32[]{:S(2)}, u32[]{:S(2)}) collective-permute-start(bf16[2,784,128]{2,1,0:T(8,128)(2,1)S(1)} %bitcast_dynamic-update-slice_fusion.60), channel_id=1, source_target_pairs={{0,2},{2,0},{4,6},{6,4},{1,3},{3,1},{5,7},{7,5},{8,10},{10,8},{12,... | collective-permute-start | bytes 1204232 | tf_op jit(solution)/shard_map/ppermute | solution.py:656
  576.9 15.5 %collective-permute-start.83 = (bf16[2,784,128]{2,1,0:T(8,128)(2,1)S(1)}, bf16[2,784,128]{2,1,0:T(8,128)(2,1)S(1)}, u32[]{:S(2)}, u32[]{:S(2)}) collective-permute-start(bf16[2,784,128]{2,1,0:T(8,128)(2,1)S(1)} %bitcast_dynamic-update-slice_fusion.56), channel_id=1, source_target_pairs={{0,16},{8,24},{16,0},{24,8},{1,17},{9,25},{17,1},{25,9},{2,18},{10... | collective-permute-start | bytes 1204232 | tf_op jit(solution)/shard_map/ppermute | solution.py:656
  579.8 39.5 %collective-permute-start.25 = (bf16[2,2,672,128]{3,2,1,0:T(8,128)(2,1)}, bf16[2,2,672,128]{3,2,1,0:T(8,128)(2,1)}, u32[]{:S(2)}, u32[]{:S(2)}) collective-permute-start(bf16[2,2,672,128]{3,2,1,0:T(8,128)(2,1)} %bitcast_dynamic-update-slice_fusion.54), channel_id=1, source_target_pairs={{0,16},{8,24},{16,0},{24,8},{1,17},{9,25},{17,1},{25,9},{2,18},{10... | collective-permute-start | bytes 2064392 | tf_op jit(solution)/shard_map/ppermute | solution.py:656
  591.5 38.3 %collective-permute-start.40 = (bf16[2,2,672,128]{3,2,1,0:T(8,128)(2,1)}, bf16[2,2,672,128]{3,2,1,0:T(8,128)(2,1)}, u32[]{:S(2)}, u32[]{:S(2)}) collective-permute-start(bf16[2,2,672,128]{3,2,1,0:T(8,128)(2,1)} %bitcast_dynamic-update-slice_fusion.50), channel_id=1, source_target_pairs={{0,16},{8,24},{16,0},{24,8},{1,17},{9,25},{17,1},{25,9},{2,18},{10... | collective-permute-start | bytes 2064392 | tf_op jit(solution)/shard_map/ppermute | solution.py:656
  592.4 10.9 %collective-permute-start.28 = (bf16[2,672,128]{2,1,0:T(8,128)(2,1)}, bf16[2,672,128]{2,1,0:T(8,128)(2,1)S(1)}, u32[]{:S(2)}, u32[]{:S(2)}) collective-permute-start(bf16[2,672,128]{2,1,0:T(8,128)(2,1)} %fusion.8), channel_id=1, source_target_pairs={{0,8},{8,0},{16,24},{24,16},{1,9},{9,1},{17,25},{25,17},{2,10},{10... | collective-permute-start | bytes 1032200 | tf_op jit(solution)/shard_map/ppermute | solution.py:656
  596.3 16.8 %collective-permute-start.43 = (bf16[2,672,128]{2,1,0:T(8,128)(2,1)}, bf16[2,672,128]{2,1,0:T(8,128)(2,1)}, u32[]{:S(2)}, u32[]{:S(2)}) collective-permute-start(bf16[2,672,128]{2,1,0:T(8,128)(2,1)} %fusion.6), channel_id=1, source_target_pairs={{0,8},{8,0},{16,24},{24,16},{1,9},{9,1},{17,25},{25,17},{2,10},{10... | collective-permute-start | bytes 1032200 | tf_op jit(solution)/shard_map/ppermute | solution.py:656
  603.3 31.6 %collective-permute-start.77 = (bf16[2,2,672,128]{3,2,1,0:T(8,128)(2,1)}, bf16[2,2,672,128]{3,2,1,0:T(8,128)(2,1)}, u32[]{:S(2)}, u32[]{:S(2)}) collective-permute-start(bf16[2,2,672,128]{3,2,1,0:T(8,128)(2,1)} %copy-done.24), channel_id=1, source_target_pairs={{0,8},{8,0},{16,24},{24,16},{1,9},{9,1},{17,25},{25,17},{2,10},{10... | collective-permute-start | bytes 2064392 | tf_op jit(solution)/shard_map/ppermute | solution.py:656
  613.1 35.5 %collective-permute-start.70 = (bf16[2,2,672,128]{3,2,1,0:T(8,128)(2,1)}, bf16[2,2,672,128]{3,2,1,0:T(8,128)(2,1)}, u32[]{:S(2)}, u32[]{:S(2)}) collective-permute-start(bf16[2,2,672,128]{3,2,1,0:T(8,128)(2,1)} %copy-done.25), channel_id=1, source_target_pairs={{0,8},{8,0},{16,24},{24,16},{1,9},{9,1},{17,25},{25,17},{2,10},{10... | collective-permute-start | bytes 2064392 | tf_op jit(solution)/shard_map/ppermute | solution.py:656
  616.3 100.2 %collective-permute-start.55 = (bf16[2,2,784,128]{3,2,1,0:T(8,128)(2,1)}, bf16[2,2,784,128]{3,2,1,0:T(8,128)(2,1)}, u32[]{:S(2)}, u32[]{:S(2)}) collective-permute-start(bf16[2,2,784,128]{3,2,1,0:T(8,128)(2,1)} %copy-done.22), channel_id=1, source_target_pairs={{0,16},{8,24},{16,0},{24,8},{1,17},{9,25},{17,1},{25,9},{2,18},{10... | collective-permute-start | bytes 2408456 | tf_op jit(solution)/shard_map/ppermute | solution.py:656
  619.3 86.6 %collective-permute-start.84 = (bf16[2,2,784,128]{3,2,1,0:T(8,128)(2,1)}, bf16[2,2,784,128]{3,2,1,0:T(8,128)(2,1)}, u32[]{:S(2)}, u32[]{:S(2)}) collective-permute-start(bf16[2,2,784,128]{3,2,1,0:T(8,128)(2,1)} %bitcast_dynamic-update-slice_fusion.38), channel_id=1, source_target_pairs={{0,8},{8,0},{16,24},{24,16},{1,9},{9,1},{17,25},{25,17},{2,10},{10... | collective-permute-start | bytes 2408456 | tf_op jit(solution)/shard_map/ppermute | solution.py:656
  629.8 50.8 %collective-permute-start.29 = (bf16[672,128]{1,0:T(8,128)(2,1)}, bf16[672,128]{1,0:T(8,128)(2,1)}, u32[]{:S(2)}, u32[]{:S(2)}) collective-permute-start(bf16[672,128]{1,0:T(8,128)(2,1)} %fusion.31), channel_id=1, source_target_pairs={{0,16},{8,24},{16,0},{24,8},{1,17},{9,25},{17,1},{25,9},{2,18},{10... | collective-permute-start | bytes 516104 | tf_op jit(solution)/shard_map/ppermute | solution.py:656
  634.9 49.9 %collective-permute-start.44 = (bf16[672,128]{1,0:T(8,128)(2,1)}, bf16[672,128]{1,0:T(8,128)(2,1)}, u32[]{:S(2)}, u32[]{:S(2)}) collective-permute-start(bf16[672,128]{1,0:T(8,128)(2,1)} %fusion.25), channel_id=1, source_target_pairs={{0,16},{8,24},{16,0},{24,8},{1,17},{9,25},{17,1},{25,9},{2,18},{10... | collective-permute-start | bytes 516104 | tf_op jit(solution)/shard_map/ppermute | solution.py:656
  648.6 48.6 %collective-permute-start.58 = (bf16[2,784,128]{2,1,0:T(8,128)(2,1)}, bf16[2,784,128]{2,1,0:T(8,128)(2,1)}, u32[]{:S(2)}, u32[]{:S(2)}) collective-permute-start(bf16[2,784,128]{2,1,0:T(8,128)(2,1)} %fusion.2), channel_id=1, source_target_pairs={{0,8},{8,0},{16,24},{24,16},{1,9},{9,1},{17,25},{25,17},{2,10},{10... | collective-permute-start | bytes 1204232 | tf_op jit(solution)/shard_map/ppermute | solution.py:656
  699.1 18.6 %collective-permute-start.59 = (bf16[784,128]{1,0:T(8,128)(2,1)}, bf16[784,128]{1,0:T(8,128)(2,1)}, u32[]{:S(2)}, u32[]{:S(2)}) collective-permute-start(bf16[784,128]{1,0:T(8,128)(2,1)} %fusion.13), channel_id=1, source_target_pairs={{0,16},{8,24},{16,0},{24,8},{1,17},{9,25},{17,1},{25,9},{2,18},{10... | collective-permute-start | bytes 602120 | tf_op jit(solution)/shard_map/ppermute | solution.py:656
  699.7 35.3 %collective-permute-start.32 = (bf16[2,672,128]{2,1,0:T(8,128)(2,1)S(1)}, bf16[2,672,128]{2,1,0:T(8,128)(2,1)}, u32[]{:S(2)}, u32[]{:S(2)}) collective-permute-start(bf16[2,672,128]{2,1,0:T(8,128)(2,1)S(1)} %bitcast_dynamic-update-slice_fusion.70), channel_id=1, source_target_pairs={{0,8},{8,0},{16,24},{24,16},{1,9},{9,1},{17,25},{25,17},{2,10},{10... | collective-permute-start | bytes 1032200 | tf_op jit(solution)/shard_map/ppermute | solution.py:656
  702.1 35.0 %collective-permute-start.47 = (bf16[2,672,128]{2,1,0:T(8,128)(2,1)}, bf16[2,672,128]{2,1,0:T(8,128)(2,1)}, u32[]{:S(2)}, u32[]{:S(2)}) collective-permute-start(bf16[2,672,128]{2,1,0:T(8,128)(2,1)} %bitcast_dynamic-update-slice_fusion.66), channel_id=1, source_target_pairs={{0,8},{8,0},{16,24},{24,16},{1,9},{9,1},{17,25},{25,17},{2,10},{10... | collective-permute-start | bytes 1032200 | tf_op jit(solution)/shard_map/ppermute | solution.py:656
  719.1 13.0 %collective-permute-start.60 = (bf16[784,128]{1,0:T(8,128)(2,1)S(1)}, bf16[784,128]{1,0:T(8,128)(2,1)S(1)}, u32[]{:S(2)}, u32[]{:S(2)}) collective-permute-start(bf16[784,128]{1,0:T(8,128)(2,1)S(1)} %fusion.15), channel_id=1, source_target_pairs={{0,4},{2,6},{4,0},{6,2},{1,5},{3,7},{5,1},{7,3},{8,12},{10,14},{12... | collective-permute-start | bytes 602120 | tf_op jit(solution)/shard_map/ppermute | solution.py:656
  736.0 18.4 %collective-permute-start.33 = (bf16[2,2,672,128]{3,2,1,0:T(8,128)(2,1)S(1)}, bf16[2,2,672,128]{3,2,1,0:T(8,128)(2,1)S(1)}, u32[]{:S(2)}, u32[]{:S(2)}) collective-permute-start(bf16[2,2,672,128]{3,2,1,0:T(8,128)(2,1)S(1)} %bitcast_dynamic-update-slice_fusion.52), channel_id=1, source_target_pairs={{0,2},{2,0},{4,6},{6,4},{1,3},{3,1},{5,7},{7,5},{8,10},{10,8},{12,... | collective-permute-start | bytes 2064392 | tf_op jit(solution)/shard_map/ppermute | solution.py:656
  738.2 31.1 %collective-permute-start.48 = (bf16[2,2,672,128]{3,2,1,0:T(8,128)(2,1)S(1)}, bf16[2,2,672,128]{3,2,1,0:T(8,128)(2,1)S(1)}, u32[]{:S(2)}, u32[]{:S(2)}) collective-permute-start(bf16[2,2,672,128]{3,2,1,0:T(8,128)(2,1)S(1)} %bitcast_dynamic-update-slice_fusion.48), channel_id=1, source_target_pairs={{0,2},{2,0},{4,6},{6,4},{1,3},{3,1},{5,7},{7,5},{8,10},{10,8},{12,... | collective-permute-start | bytes 2064392 | tf_op jit(solution)/shard_map/ppermute | solution.py:656
  748.2 61.1 %collective-permute-start.63 = (bf16[2,2,784,128]{3,2,1,0:T(8,128)(2,1)}, bf16[2,2,784,128]{3,2,1,0:T(8,128)(2,1)}, u32[]{:S(2)}, u32[]{:S(2)}) collective-permute-start(bf16[2,2,784,128]{3,2,1,0:T(8,128)(2,1)} %bitcast_dynamic-update-slice_fusion.40), channel_id=1, source_target_pairs={{0,2},{2,0},{4,6},{6,4},{1,3},{3,1},{5,7},{7,5},{8,10},{10,8},{12,... | collective-permute-start | bytes 2408456 | tf_op jit(solution)/shard_map/ppermute | solution.py:656
  (96 other events, 818.7 us)
Sparse Core Ops, SparseCore 0:
  601.2 138.0 all-reduce.3

commit v2 on v1

v2 whole, which is shorter than its diff:
```python
import functools

import jax
import jax.numpy as jnp
from jax import lax
from jax.experimental import pallas as pl
from jax.experimental.pallas import tpu as pltpu
from jax.sharding import PartitionSpec as P

HQ = 14
KVH = 2
HD = 64
WINDOW = 1024
PAIRS = HQ // 2
LANES = 128
HALF = 256

theta_base = 1000000.0
eps_norm = 1e-06
masked_score = -1e30
f32 = jnp.float32
bf16 = jnp.bfloat16
VMEM_BYTES = 58 * 1024 * 1024
WIDTHS = (1280, 1152)


def nn(a, b):
    return lax.dot_general(a, b, (((1,), (0,)), ((), ())), preferred_element_type=f32)


def nt(a, b):
    return lax.dot_general(a, b, (((1,), (1,)), ((), ())), preferred_element_type=f32)


def tn(a, b):
    return lax.dot_general(a, b, (((0,), (0,)), ((), ())), preferred_element_type=f32)


def flip_lanes_half(values):
    width = values.shape[-1]
    lane = lax.broadcasted_iota(jnp.int32, values.shape, len(values.shape) - 1)
    up = pltpu.roll(values, width - 32, len(values.shape) - 1)
    down = pltpu.roll(values, 32, len(values.shape) - 1)
    return jnp.where((lane & 63) < 32, -up, down)


def call(kernel, out_shape, flops, moved, **kwargs):
    return pl.pallas_call(
        kernel,
        out_shape=out_shape,
        compiler_params=pltpu.CompilerParams(vmem_limit_bytes=VMEM_BYTES),
        cost_estimate=pl.CostEstimate(flops=flops, bytes_accessed=moved, transcendentals=0),
        **kwargs,
    )


GAIN_ONE = slice(0, 896)
BIAS = slice(896, 2048)
GAIN_TWO = slice(2048, 2944)


def place_rows(target, own_ref, other_ref, me, columns=slice(None)):
    rows = own_ref.shape[0]
    target[pl.ds(pl.multiple_of(me * rows, rows), rows), columns] = own_ref[...]
    target[pl.ds(pl.multiple_of((1 - me) * rows, rows), rows), columns] = other_ref[...]


def project_kernel(
    place_ref, x_ref, params_ref, wq_ref, wk_ref, wv_ref, oq_ref, ok_ref, ov_ref, cos_ref, sin_ref,
    n1_ref, q_ref, kv_ref, w_ref,
):
    count = x_ref.shape[0]
    step = 256
    me = place_ref[0]
    width = HQ * HD
    place_rows(w_ref, wq_ref, oq_ref, me, slice(0, width))
    place_rows(w_ref, wk_ref, ok_ref, me, slice(width, width + LANES))
    place_rows(w_ref, wv_ref, ov_ref, me, slice(width + LANES, width + 2 * LANES))

    def body(i, carry):
        rows = pl.ds(pl.multiple_of(i * step, step), step)
        x = x_ref[rows, :].astype(f32)
        scale = lax.rsqrt(jnp.mean(x * x, -1, keepdims=True) + eps_norm)
        normed = (x * scale * params_ref[:, GAIN_ONE]).astype(bf16)
        n1_ref[rows, :] = normed
        cosine = cos_ref[rows, :]
        sine = sin_ref[rows, :]
        out = nn(normed, w_ref[...]) + params_ref[:, BIAS]
        for j in range(PAIRS + 1):
            part = out[:, j * LANES : (j + 1) * LANES]
            part = part * cosine + flip_lanes_half(part) * sine
            if j < PAIRS:
                q_ref[rows, j * LANES : (j + 1) * LANES] = (part * HD**-0.5).astype(bf16)
            else:
                kv_ref[rows, :LANES] = part.astype(bf16)
        kv_ref[rows, LANES:] = out[:, (PAIRS + 1) * LANES :].astype(bf16)
        return carry

    lax.fori_loop(0, count // step, body, 0)


def in_vmem(n):
    return [pl.BlockSpec(memory_space=pltpu.SMEM)] + [pl.BlockSpec(memory_space=pltpu.VMEM)] * n


def project(place, x, params, own, other, cosine, sine):
    count, width = x.shape
    columns = sum(w.shape[1] for w in own)
    return call(
        project_kernel,
        (
            jax.ShapeDtypeStruct((count, width), bf16),
            jax.ShapeDtypeStruct((count, HQ * HD), bf16),
            jax.ShapeDtypeStruct((count, 2 * KVH * HD), bf16),
            jax.ShapeDtypeStruct((width, columns), bf16),
        ),
        2 * count * width * columns,
        6 * 1024 * 1024,
        in_specs=in_vmem(10),
    )(place, x, params, *own, *other, cosine, sine)


def lane_low(shape):
    return lax.broadcasted_iota(jnp.int32, shape, len(shape) - 1) < HD


def spread_heads(source, target, row):
    values = source.astype(f32)
    other = pltpu.roll(values, HD, 1)
    low = lane_low(values.shape)
    rows = pl.ds(row, values.shape[0])
    target[0, 0, rows, :] = jnp.where(low, values, 0.0).astype(bf16)
    target[1, 0, rows, :] = jnp.where(low, 0.0, other).astype(bf16)
    target[0, 1, rows, :] = jnp.where(low, other, 0.0).astype(bf16)
    target[1, 1, rows, :] = jnp.where(low, 0.0, values).astype(bf16)


def turn_heads(source, target, column):
    values = source.astype(f32).T.astype(bf16)
    columns = pl.ds(column, values.shape[1])
    target[0, :, columns] = values[:HD]
    target[1, :, columns] = values[HD:]


def fill_bias(place_ref, seg_ref, near_ref, far_ref, count):
    ctx = place_ref[3]

    def segments(back):
        start = pl.multiple_of(jnp.maximum(ctx - back, 0) * count, count)
        row = seg_ref[:, pl.ds(start, count)].astype(f32)
        row = jnp.where(ctx >= back, row, -1.0)
        return row, jnp.broadcast_to(row, (LANES, count)).T

    own_row, own = segments(0)
    _, one = segments(1)
    _, two = segments(2)
    for t in range(count // LANES):
        columns = slice(t * LANES, (t + 1) * LANES)
        query = own_row[:, columns]
        near_ref[:, columns] = jnp.where(one == query, 0.0, masked_score)
        key = lax.broadcasted_iota(jnp.int32, (count, LANES), 0)
        token = lax.broadcasted_iota(jnp.int32, (count, LANES), 1) + t * LANES
        far = jnp.where(key <= token, own, two)
        far_ref[:, columns] = jnp.where(far == query, 0.0, masked_score)


def triangle():
    key = lax.broadcasted_iota(jnp.int32, (HALF, HALF), 0)
    token = lax.broadcasted_iota(jnp.int32, (HALF, HALF), 1)
    return key <= token


def tiles_of(t, count):
    if t == 0:
        plain = 2 * count + HALF
        plain_bias = HALF
    else:
        plain = 0
        plain_bias = 0
    diagonal = t * HALF
    return plain, plain_bias, diagonal, 2 * count + diagonal


def scores_of(keys, query, t, count, near_ref, far_ref, tri):
    plain, plain_bias, own, old = tiles_of(t, count)
    columns = slice(t * HALF, (t + 1) * HALF)
    near = nt(keys(count, count), query) + near_ref[:, columns]
    far = nt(keys(plain, HALF), query) + far_ref[plain_bias : plain_bias + HALF, columns]
    edge = jnp.where(tri, nt(keys(own, HALF), query), nt(keys(old, HALF), query))
    edge = edge + far_ref[own : own + HALF, columns]
    return near, far, edge


def attend_kernel(
    place_ref, q_ref, kv0_ref, kv1_ref, kv2_ref, seg_ref, o_ref, lse_ref, k_s, vt_s, near_s, far_s
):
    count = q_ref.shape[0]
    pair = pl.program_id(0)

    @pl.when(pair == 0)
    def _():
        for i, ref in enumerate((kv0_ref, kv1_ref, kv2_ref)):
            spread_heads(ref[:, :LANES], k_s, i * count)
            turn_heads(ref[:, LANES:], vt_s, i * count)
        fill_bias(place_ref, seg_ref, near_s, far_s, count)

    tri = triangle()
    for t in range(count // HALF):
        plain, _, own, old = tiles_of(t, count)
        rows = slice(t * HALF, (t + 1) * HALF)
        query = q_ref[rows, :]
        turned = []
        for half in range(2):
            group = (2 * pair + half) // (HQ // KVH)
            near, far, edge = scores_of(
                lambda start, size: k_s[half, group, start : start + size, :],
                query,
                t,
                count,
                near_s,
                far_s,
                tri,
            )
            top = jnp.maximum(
                jnp.max(near, 0, keepdims=True),
                jnp.maximum(jnp.max(far, 0, keepdims=True), jnp.max(edge, 0, keepdims=True)),
            )
            near = jnp.exp(near - top)
            far = jnp.exp(far - top)
            edge = jnp.exp(edge - top)
            total = (
                jnp.sum(near, 0, keepdims=True)
                + jnp.sum(far, 0, keepdims=True)
                + jnp.sum(edge, 0, keepdims=True)
            )
            lse_ref[0, half : half + 1, rows] = top + jnp.log(total)
            mixed = nn(vt_s[group, :, count : 2 * count], near.astype(bf16))
            mixed += nn(vt_s[group, :, plain : plain + HALF], far.astype(bf16))
            mixed += nn(vt_s[group, :, own : own + HALF], jnp.where(tri, edge, 0.0).astype(bf16))
            mixed += nn(vt_s[group, :, old : old + HALF], jnp.where(tri, 0.0, edge).astype(bf16))
            turned.append(mixed * (1.0 / total))
        o_ref[rows, :] = jnp.concatenate(turned, 0).T.astype(bf16)


def attend(place, q, kv0, kv1, kv2, seg):
    count = q.shape[0]
    whole = lambda p: (0, 0)
    return call(
        attend_kernel,
        (
            jax.ShapeDtypeStruct((count, HQ * HD), bf16),
            jax.ShapeDtypeStruct((PAIRS, 8, count), f32),
        ),
        4 * HQ * count * 1280 * 256,
        4 * 1024 * 1024,
        grid=(PAIRS,),
        in_specs=[
            pl.BlockSpec(memory_space=pltpu.SMEM),
            pl.BlockSpec((count, LANES), lambda p: (0, p)),
            pl.BlockSpec(kv0.shape, whole),
            pl.BlockSpec(kv1.shape, whole),
            pl.BlockSpec(kv2.shape, whole),
            pl.BlockSpec(seg.shape, whole),
        ],
        out_specs=(
            pl.BlockSpec((count, LANES), lambda p: (0, p)),
            pl.BlockSpec((1, 8, count), lambda p: (p, 0, 0)),
        ),
        scratch_shapes=[
            pltpu.VMEM((2, KVH, 3 * count, LANES), bf16),
            pltpu.VMEM((KVH, HD, 3 * count), bf16),
            pltpu.VMEM((count, count), f32),
            pltpu.VMEM((count, count), f32),
        ],
    )(place, q, kv0, kv1, kv2, seg)


def attend_back_kernel(*refs, first_pair, first, final):
    (place_ref, q_ref, do_ref, kv0_ref, kv1_ref, kv2_ref, seg_ref, lse_ref, cos_ref, sin_ref) = refs[:10]
    refs = refs[10:]
    if not first:
        dk_in, dv_in = refs[:2]
        refs = refs[2:]
    dq_ref = refs[0]
    refs = refs[1:]
    if final:
        own_ref, one_ref, two_ref = refs[:3]
        refs = refs[3:]
        k_s, v_s, kt_s, near_s, far_s, dk_s, dv_s = refs
    else:
        dk_s, dv_s = refs[:2]
        k_s, v_s, kt_s, near_s, far_s = refs[2:]
    count = q_ref.shape[0]
    step = pl.program_id(0)
    pair = step + first_pair

    @pl.when(step == 0)
    def _():
        for i, ref in enumerate((kv0_ref, kv1_ref, kv2_ref)):
            spread_heads(ref[:, :LANES], k_s, i * count)
            spread_heads(ref[:, LANES:], v_s, i * count)
            turn_heads(ref[:, :LANES], kt_s, i * count)
        fill_bias(place_ref, seg_ref, near_s, far_s, count)
        if first:
            dk_s[...] = jnp.zeros_like(dk_s)
            dv_s[...] = jnp.zeros_like(dv_s)
        else:
            dk_s[...] = dk_in[...]
            dv_s[...] = dv_in[...]

    tri = triangle()
    for t in range(count // HALF):
        plain, _, own, old = tiles_of(t, count)
        rows = slice(t * HALF, (t + 1) * HALF)
        query = q_ref[rows, :]
        grad = do_ref[rows, :]
        low = lane_low(query.shape)
        turned = []
        for half in range(2):
            group = (2 * pair + half) // (HQ // KVH)
            mine = low if half == 0 else jnp.logical_not(low)
            query_half = jnp.where(mine, query.astype(f32), 0.0).astype(bf16)
            grad_half = jnp.where(mine, grad.astype(f32), 0.0).astype(bf16)
            log_total = lse_ref[0, half : half + 1, rows]
            scores = scores_of(
                lambda start, size: k_s[half, group, start : start + size, :],
                query,
                t,
                count,
                near_s,
                far_s,
                tri,
            )
            near, far, edge = (jnp.exp(part - log_total) for part in scores)
            values = lambda start, size: v_s[half, group, start : start + size, :]
            near_p = nt(values(count, count), grad)
            far_p = nt(values(plain, HALF), grad)
            edge_p = jnp.where(tri, nt(values(own, HALF), grad), nt(values(old, HALF), grad))
            inner = (
                jnp.sum(near * near_p, 0, keepdims=True)
                + jnp.sum(far * far_p, 0, keepdims=True)
                + jnp.sum(edge * edge_p, 0, keepdims=True)
            )
            near_g = near * (near_p - inner)
            far_g = far * (far_p - inner)
            edge_g = edge * (edge_p - inner)
            blocks = (
                (count, count, near, near_g),
                (plain, HALF, far, far_g),
                (own, HALF, jnp.where(tri, edge, 0.0), jnp.where(tri, edge_g, 0.0)),
                (old, HALF, jnp.where(tri, 0.0, edge), jnp.where(tri, 0.0, edge_g)),
            )
            total = None
            for start, size, weight, change in blocks:
                change = change.astype(bf16)
                keys = slice(start, start + size)
                dv_s[group, keys, :] += nn(weight.astype(bf16), grad_half)
                dk_s[group, keys, :] += nn(change, query_half)
                part = nn(kt_s[group, :, keys], change)
                total = part if total is None else total + part
            turned.append(total)
        turned = jnp.concatenate(turned, 0).T * HD**-0.5
        back = turned * cos_ref[rows, :] - flip_lanes_half(turned * sin_ref[rows, :])
        dq_ref[rows, :] = back.astype(bf16)

    if final:

        @pl.when(pair == PAIRS - 1)
        def _():
            for i, (ref, cast) in enumerate(((own_ref, f32), (one_ref, bf16), (two_ref, bf16))):
                keys = slice(i * count, (i + 1) * count)
                for j, source in enumerate((dk_s, dv_s)):
                    one = source[0, keys, :]
                    two = source[1, keys, :]
                    one = one + pltpu.roll(one, HD, 1)
                    two = two + pltpu.roll(two, HD, 1)
                    both = jnp.where(lane_low(one.shape), one, two)
                    ref[:, j * LANES : (j + 1) * LANES] = both.astype(cast)


def attend_back(place, q, do, kv0, kv1, kv2, seg, lse, cosine, sine, sums, *, first_pair, pairs):
    count = q.shape[0]
    first = sums is None
    final = first_pair + pairs == PAIRS
    sums = () if first else tuple(sums)
    whole = lambda p: (0, 0)
    stacked = pl.BlockSpec((KVH, 3 * count, LANES), lambda p: (0, 0, 0))
    lane_block = pl.BlockSpec((count, LANES), lambda p: (0, p + first_pair))
    row_block = pl.BlockSpec((1, 8, count), lambda p: (p + first_pair, 0, 0))
    token_block = pl.BlockSpec((count, 2 * LANES), whole)
    stack = jax.ShapeDtypeStruct((KVH, 3 * count, LANES), f32)
    if final:
        outs = [jax.ShapeDtypeStruct((count, 2 * LANES), t) for t in (f32, bf16, bf16)]
        out_specs = [token_block] * 3
        scratch = [pltpu.VMEM(stack.shape, f32)] * 2
    else:
        outs = [stack, stack]
        out_specs = [stacked] * 2
        scratch = []
    return call(
        functools.partial(attend_back_kernel, first_pair=first_pair, first=first, final=final),
        (jax.ShapeDtypeStruct((count, pairs * LANES), bf16), *outs),
        10 * 2 * pairs * count * 1280 * 256,
        6 * 1024 * 1024,
        grid=(pairs,),
        in_specs=[
            pl.BlockSpec(memory_space=pltpu.SMEM),
            lane_block,
            lane_block,
            pl.BlockSpec(kv0.shape, whole),
            pl.BlockSpec(kv1.shape, whole),
            pl.BlockSpec(kv2.shape, whole),
            pl.BlockSpec(seg.shape, whole),
            row_block,
            pl.BlockSpec(cosine.shape, whole),
            pl.BlockSpec(sine.shape, whole),
        ]
        + [stacked] * len(sums),
        out_specs=(pl.BlockSpec((count, LANES), lambda p: (0, p)), *out_specs),
        scratch_shapes=[
            pltpu.VMEM((2, KVH, 3 * count, LANES), bf16),
            pltpu.VMEM((2, KVH, 3 * count, LANES), bf16),
            pltpu.VMEM((KVH, HD, 3 * count), bf16),
            pltpu.VMEM((count, count), f32),
            pltpu.VMEM((count, count), f32),
        ]
        + scratch,
    )(place, q, do, kv0, kv1, kv2, seg, lse, cosine, sine, *sums)


def merge_kernel(place_ref, x_ref, o_ref, own_ref, other_ref, params_ref, h1_ref, n2_ref, w_ref):
    step = 256
    place_rows(w_ref, own_ref, other_ref, place_ref[0])

    def body(i, carry):
        rows = pl.ds(pl.multiple_of(i * step, step), step)
        hidden = x_ref[rows, :].astype(f32) + nn(o_ref[rows, :], w_ref[...])
        h1_ref[rows, :] = hidden
        scale = lax.rsqrt(jnp.mean(hidden * hidden, -1, keepdims=True) + eps_norm)
        n2_ref[rows, :] = (hidden * scale * params_ref[:, GAIN_TWO]).astype(bf16)
        return carry

    lax.fori_loop(0, x_ref.shape[0] // step, body, 0)


def merge(place, x, o, own, other, params):
    return call(
        merge_kernel,
        (
            jax.ShapeDtypeStruct(x.shape, f32),
            jax.ShapeDtypeStruct(x.shape, bf16),
            jax.ShapeDtypeStruct((2 * own.shape[0], own.shape[1]), bf16),
        ),
        4 * x.shape[0] * own.shape[0] * own.shape[1],
        6 * 1024 * 1024,
        in_specs=in_vmem(5),
    )(place, x, o, own, other, params)


def change_kernel(ca_ref, cb_ref, down_ref, out_ref):
    count = ca_ref.shape[0]
    out_ref[:count, :] = nt(ca_ref[...], down_ref[...]).astype(bf16)
    out_ref[count:, :] = nt(cb_ref[...], down_ref[...]).astype(bf16)


def change(ca, cb, down):
    count, features = ca.shape
    hidden = down.shape[0]
    block = 2 * LANES
    steps = pl.cdiv(hidden, block)
    whole = pl.BlockSpec((count, features), lambda i: (0, 0))
    return call(
        change_kernel,
        jax.ShapeDtypeStruct((2 * count, hidden), bf16),
        4 * count * features * hidden,
        12 * 1024 * 1024,
        grid=(steps,),
        in_specs=[whole, whole, pl.BlockSpec((block, features), lambda i: (i, 0))],
        out_specs=pl.BlockSpec((2 * count, block), lambda i: (0, i)),
    )(ca, cb, down)


def feed_kernel(*refs, start, first, final, sides):
    n_grads = 1 if sides is None else 6
    place_ref, na_ref, nb_ref, ca_ref, cb_ref, gate_ref, gate_o_ref, up_ref, up_o_ref, down_ref, change_ref = refs[:11]
    refs = refs[11:]
    if not first:
        sums = refs[:4]
        refs = refs[4:]
    grad_refs = refs[:n_grads]
    outs = refs[n_grads : n_grads + 4]
    refs = refs[n_grads + 4 :]
    (na, nb, ca, cb, wg, wu, wd, change_s, inner_s, gate_s, up_s, *part_s) = refs[:14]
    refs = refs[14:]
    if not first:
        held = refs[:4]
        refs = refs[4:]
    totals = refs[:4]
    in_sem, sum_sem, out_sem = refs[4:]
    count, features = na.shape
    width = wg.shape[1]
    rows_held = gate_ref.shape[0]
    hidden = down_ref.shape[0]
    me = place_ref[0]
    lanes = pl.ds(pl.multiple_of(me * hidden + start, LANES), width)
    own_rows = pl.ds(pl.multiple_of(me * rows_held, rows_held), rows_held)
    other_rows = pl.ds(pl.multiple_of((1 - me) * rows_held, rows_held), rows_held)

    moves = [
        (na_ref, na),
        (gate_ref.at[:, lanes], wg.at[own_rows, :]),
        (gate_o_ref.at[:, lanes], wg.at[other_rows, :]),
        (up_ref.at[:, lanes], wu.at[own_rows, :]),
        (up_o_ref.at[:, lanes], wu.at[other_rows, :]),
        (change_ref.at[:, pl.ds(start, width)], change_s),
        (down_ref.at[pl.ds(start, width), :], wd),
        (nb_ref, nb),
        (ca_ref, ca),
        (cb_ref, cb),
    ]
    copies = [pltpu.make_async_copy(a, b, in_sem.at[i]) for i, (a, b) in enumerate(moves)]
    for copy in copies:
        copy.start()
    sum_copies = []
    if not first:
        sum_copies = [pltpu.make_async_copy(sums[i], held[i], sum_sem.at[i]) for i in range(4)]
        for copy in sum_copies:
            copy.start()
    for copy in copies[:7]:
        copy.wait()
    step = 256
    for half, normed_ref in enumerate((na, nb)):
        if half == 1:
            for copy in copies[7:]:
                copy.wait()
        for copy in sum_copies[2 * half : 2 * half + 2]:
            copy.wait()

        def body(i, carry, half=half, normed_ref=normed_ref):
            rows = pl.ds(pl.multiple_of(i * step, step), step)
            both = pl.ds(pl.multiple_of(half * count + i * step, step), step)
            normed = normed_ref[rows, :]
            gate = nn(normed, wg[...])
            up = nn(normed, wu[...])
            change = change_s[both, :].astype(f32)
            sigmoid = 1.0 / (1.0 + jnp.exp(-gate))
            activated = gate * sigmoid
            inner = (activated * up).astype(bf16)
            gate_g = (change * up * sigmoid * (1.0 + gate * (1.0 - sigmoid))).astype(bf16)
            up_g = (change * activated).astype(bf16)
            inner_s[both, :] = inner
            gate_s[both, :] = gate_g
            up_s[both, :] = up_g
            result = nn(inner, wd[...])
            back = nt(gate_g, wg[...]) + nt(up_g, wu[...])
            if not first:
                result = result + held[2 * half][rows, :].astype(f32)
                back = back + held[2 * half + 1][rows, :].astype(f32)
            totals[2 * half][rows, :] = result.astype(totals[2 * half].dtype)
            totals[2 * half + 1][rows, :] = back.astype(totals[2 * half + 1].dtype)
            return carry

        lax.fori_loop(0, count // step, body, 0)
    leaving = []

    def leave(source, target):
        copy = pltpu.make_async_copy(source, target, out_sem.at[len(leaving)])
        copy.start()
        leaving.append(copy)

    for i in range(4):
        leave(totals[i], outs[i])

    def part_leaves(i):
        rows = part_s[i].shape[0]
        if sides is None:
            leave(part_s[i], grad_refs[0].at[pl.ds(i * rows, rows), :])
            return
        keep, send = grad_refs[2 * i : 2 * i + 2]
        rows = rows // 2
        side = place_ref[sides[i]]
        leave(part_s[i].at[pl.ds(pl.multiple_of((1 - side) * rows, 16), rows), :], send)
        leave(part_s[i].at[pl.ds(pl.multiple_of(side * rows, 16), rows), :], keep)

    mine_s, theirs_s, down_s = part_s
    for kind, source in enumerate((gate_s, up_s)):
        for place in range(0, width, HALF):
            size = min(HALF, width - place)
            columns = slice(place, place + size)
            grads = tn(na[...], source[:count, columns]) + tn(nb[...], source[count:, columns])
            grads = grads.astype(bf16)
            for j in range(size // LANES):
                row = ((kind * width + place) // LANES + j) * rows_held
                tile = grads[:, j * LANES : (j + 1) * LANES]

                @pl.when(me == 0)
                def _():
                    mine_s[row : row + rows_held, :] = tile[:rows_held]
                    theirs_s[row : row + rows_held, :] = tile[rows_held:]

                @pl.when(me == 1)
                def _():
                    mine_s[row : row + rows_held, :] = tile[rows_held:]
                    theirs_s[row : row + rows_held, :] = tile[:rows_held]

    part_leaves(0)
    part_leaves(1)
    for place in range(0, width, HALF):
        size = min(HALF, width - place)
        columns = slice(place, place + size)
        grads = tn(inner_s[:count, columns], ca[...]) + tn(inner_s[count:, columns], cb[...])
        grads = grads.astype(bf16)
        for j in range(features // LANES):
            row = j * width + place
            down_s[row : row + size, :] = grads[:, j * LANES : (j + 1) * LANES]
    part_leaves(2)
    for copy in leaving:
        copy.wait()


def feed(place, na, nb, ca, cb, gate, gate_o, up, up_o, down, change, sums, *, start, width, final, sides):
    count, features = na.shape
    first = sums is None
    sums = () if first else tuple(sums)
    anywhere = pl.BlockSpec(memory_space=pl.ANY)
    rows = features * width // LANES
    tokens = (count, features)
    types = [f32 if final and i < 2 else bf16 for i in range(4)]
    totals = [jax.ShapeDtypeStruct(tokens, t) for t in types]
    if sides is None:
        outs = [jax.ShapeDtypeStruct((3 * rows, LANES), bf16)]
    else:
        outs = [jax.ShapeDtypeStruct((rows // 2, LANES), bf16)] * 6
    scratch = [pltpu.VMEM(tokens, bf16)] * 4
    scratch += [pltpu.VMEM((features, width), bf16)] * 2 + [pltpu.VMEM((width, features), bf16)]
    scratch += [pltpu.VMEM((2 * count, width), bf16)] * 4
    scratch += [pltpu.VMEM((rows, LANES), bf16)] * 3
    if not first:
        scratch += [pltpu.VMEM(tokens, bf16)] * 4
    scratch += [pltpu.VMEM(tokens, t) for t in types]
    scratch += [pltpu.SemaphoreType.DMA((n,)) for n in (10, 4, 10)]
    return call(
        functools.partial(feed_kernel, start=start, first=first, final=final, sides=sides),
        (*outs, *totals),
        18 * 2 * count * features * width,
        30 * 1024 * 1024,
        in_specs=[pl.BlockSpec(memory_space=pltpu.SMEM)] + [anywhere] * (10 + len(sums)),
        out_specs=(anywhere,) * (len(outs) + 4),
        scratch_shapes=scratch,
    )(place, na, nb, ca, cb, gate, gate_o, up, up_o, down, change, *sums)


def middle_kernel(
    place_ref, part_ref, got_ref, h1_ref, dy_ref, params_ref, w_ref, o_ref,
    dh1_ref, do_ref, gg_ref, mine_ref, theirs_ref, low_s,
):
    count, features = part_ref.shape
    step = 256
    gg_ref[...] = jnp.zeros_like(gg_ref)

    def body(i, carry):
        rows = pl.ds(pl.multiple_of(i * step, step), step)
        back = part_ref[rows, :] + got_ref[rows, :].astype(f32)
        hidden = h1_ref[rows, :]
        scale = lax.rsqrt(jnp.mean(hidden * hidden, -1, keepdims=True) + eps_norm)
        normal = hidden * scale
        gg_ref[...] += jnp.sum(back * normal, 0, keepdims=True)
        change = back * params_ref[:, GAIN_TWO]
        grad = dy_ref[rows, :].astype(f32) + scale * (
            change - normal * jnp.mean(change * normal, -1, keepdims=True)
        )
        dh1_ref[rows, :] = grad
        low = grad.astype(bf16)
        low_s[rows, :] = low
        do_ref[rows, :] = nt(low, w_ref[...]).astype(bf16)
        return carry

    lax.fori_loop(0, count // step, body, 0)
    store_split(place_ref, tn(o_ref[...], low_s[...]).astype(bf16), mine_ref, theirs_ref, 0)


def store_split(place_ref, grads, mine_ref, theirs_ref, first_tile):
    half_rows = grads.shape[0] // 2
    me = place_ref[0]
    for j in range(grads.shape[1] // LANES):
        row = (first_tile + j) * half_rows
        tile = grads[:, j * LANES : (j + 1) * LANES]

        @pl.when(me == 0)
        def _():
            mine_ref[row : row + half_rows, :] = tile[:half_rows]
            theirs_ref[row : row + half_rows, :] = tile[half_rows:]

        @pl.when(me == 1)
        def _():
            mine_ref[row : row + half_rows, :] = tile[half_rows:]
            theirs_ref[row : row + half_rows, :] = tile[:half_rows]


def middle(place, part, got, h1, dy, params, w, o):
    count, features = part.shape
    rows = (features // 2) * (features // LANES)
    return call(
        middle_kernel,
        (
            jax.ShapeDtypeStruct((count, features), f32),
            jax.ShapeDtypeStruct((count, HQ * HD), bf16),
            jax.ShapeDtypeStruct((1, features), f32),
            jax.ShapeDtypeStruct((rows, LANES), bf16),
            jax.ShapeDtypeStruct((rows, LANES), bf16),
        ),
        4 * count * features * features,
        12 * 1024 * 1024,
        in_specs=in_vmem(7),
        scratch_shapes=[pltpu.VMEM((count, features), bf16)],
    )(place, part, got, h1, dy, params, w, o)


def query_kernel(
    place_ref, dqa_ref, dqb_ref, n1_ref, w_ref, back_ref, gb_ref, mine_ref, theirs_ref, dp_s
):
    count = n1_ref.shape[0]
    width = HQ * HD
    split_at = dqa_ref.shape[1]
    step = 256
    gb_ref[...] = jnp.zeros_like(gb_ref)

    def body(i, carry):
        rows = pl.ds(pl.multiple_of(i * step, step), step)
        dp_s[rows, :split_at] = dqa_ref[rows, :]
        dp_s[rows, split_at:] = dqb_ref[rows, :]
        grads = dp_s[rows, :]
        gb_ref[...] += jnp.sum(grads.astype(f32), 0, keepdims=True)
        back_ref[rows, :] = nt(grads, w_ref[:, :width])
        return carry

    lax.fori_loop(0, count // step, body, 0)
    store_split(place_ref, tn(n1_ref[...], dp_s[...]).astype(bf16), mine_ref, theirs_ref, 0)


def query_back(place, dqa, dqb, n1, w):
    count, features = n1.shape
    width = HQ * HD
    rows = (features // 2) * (width // LANES)
    return call(
        query_kernel,
        (
            jax.ShapeDtypeStruct((count, features), f32),
            jax.ShapeDtypeStruct((1, width), f32),
            jax.ShapeDtypeStruct((rows, LANES), bf16),
            jax.ShapeDtypeStruct((rows, LANES), bf16),
        ),
        4 * count * features * width,
        10 * 1024 * 1024,
        in_specs=in_vmem(4),
        scratch_shapes=[pltpu.VMEM((count, width), bf16)],
    )(place, dqa, dqb, n1, w)


VECTOR_ROWS = 128


def last_kernel(
    place_ref, own_ref, one_ref, two_ref, n1_ref, x_ref, params_ref, w_ref, part_ref, dh1_ref, cos_ref, sin_ref,
    qm_ref, qt_ref, om_ref, ot_ref, gbq_ref, ggt_ref, dx_ref, mine_ref, theirs_ref, dp_s, gg_ref, gb_ref,
):
    count = n1_ref.shape[0]
    width = HQ * HD
    step = 256
    gg_ref[...] = jnp.zeros_like(gg_ref)
    gb_ref[...] = jnp.zeros_like(gb_ref)

    def body(i, carry):
        rows = pl.ds(pl.multiple_of(i * step, step), step)
        pairs = own_ref[rows, :] + one_ref[rows, :].astype(f32) + two_ref[rows, :].astype(f32)
        key = pairs[:, :LANES]
        key = key * cos_ref[rows, :] - flip_lanes_half(key * sin_ref[rows, :])
        dp_s[rows, :LANES] = key.astype(bf16)
        dp_s[rows, LANES:] = pairs[:, LANES:].astype(bf16)
        grads = dp_s[rows, :]
        gb_ref[...] += jnp.sum(grads.astype(f32), 0, keepdims=True)
        back = part_ref[rows, :] + nt(grads, w_ref[:, width:])
        x = x_ref[rows, :].astype(f32)
        scale = lax.rsqrt(jnp.mean(x * x, -1, keepdims=True) + eps_norm)
        normal = x * scale
        gg_ref[...] += jnp.sum(back * normal, 0, keepdims=True)
        change = back * params_ref[:, GAIN_ONE]
        grad = dh1_ref[rows, :] + scale * (
            change - normal * jnp.mean(change * normal, -1, keepdims=True)
        )
        dx_ref[rows, :] = grad.astype(bf16)
        return carry

    lax.fori_loop(0, count // step, body, 0)
    at = qm_ref.shape[0]
    tiles = (w_ref.shape[1] - width) // LANES
    rows_held = at * LANES // width
    store_split(
        place_ref, tn(n1_ref[...], dp_s[...]).astype(bf16), mine_ref, theirs_ref, at // rows_held
    )
    mine_ref[:at, :] = qm_ref[...]
    theirs_ref[:at, :] = qt_ref[...]
    at += tiles * rows_held
    after = at + om_ref.shape[0]
    mine_ref[at:after, :] = om_ref[...]
    theirs_ref[at:after, :] = ot_ref[...]
    vectors = []
    for ref in (gg_ref, gbq_ref, gb_ref, ggt_ref):
        vectors += [ref[:, j * LANES : (j + 1) * LANES] for j in range(ref.shape[1] // LANES)]
    vectors.append(jnp.zeros((VECTOR_ROWS - len(vectors), LANES), f32))
    vectors = jnp.concatenate(vectors, 0).astype(bf16)
    mine_ref[after:, :] = vectors
    theirs_ref[after:, :] = vectors


def last(place, own, one, two, n1, x, params, w, part, dh1, cosine, sine, qm, qt, om, ot, gbq, ggt):
    count, features = n1.shape
    columns = w.shape[1] - HQ * HD
    rows = (features // 2) * (columns // LANES) + qm.shape[0] + om.shape[0] + VECTOR_ROWS
    return call(
        last_kernel,
        (
            jax.ShapeDtypeStruct((count, features), bf16),
            jax.ShapeDtypeStruct((rows, LANES), bf16),
            jax.ShapeDtypeStruct((rows, LANES), bf16),
        ),
        4 * count * features * columns,
        14 * 1024 * 1024,
        in_specs=in_vmem(17),
        scratch_shapes=[
            pltpu.VMEM((count, columns), bf16),
            pltpu.VMEM((1, features), f32),
            pltpu.VMEM((1, columns), f32),
        ],
    )(place, own, one, two, n1, x, params, w, part, dh1, cosine, sine, qm, qt, om, ot, gbq, ggt)


def swap(values):
    return lax.ppermute(values, "fsdp", [(0, 1), (1, 0)])


def flip(values, dim):
    axis, bit = dim
    size = lax.axis_size(axis)
    return lax.ppermute(values, axis, [(i, i ^ (1 << bit)) for i in range(size)])


def side(dim):
    axis, bit = dim
    return (lax.axis_index(axis) >> bit) & 1


def add(*terms):
    total = terms[0].astype(f32)
    for term in terms[1:]:
        total = total + term.astype(f32)
    return total.astype(bf16)


def take(array, index):
    return lax.dynamic_index_in_dim(array, index, 0, False)


def join(low, other, index):
    out = jnp.zeros((2,) + low.shape, low.dtype)
    out = lax.dynamic_update_index_in_dim(out, low, index, 0)
    return lax.dynamic_update_index_in_dim(out, other, 1 - index, 0)


def rest_of_seq(values):
    for bit in range(2, lax.axis_size("seq").bit_length() - 1):
        values = add(values, flip(values, ("seq", bit)))
    return values


class Order:
    def __init__(self):
        self.token = None

    def __call__(self, step, *operands):
        if self.token is not None:
            operands, _ = lax.optimization_barrier((operands, self.token))
        out = step(*operands)
        self.token = jax.tree.leaves(out)[0]
        return out


def fold_kernel(place_ref, *refs, sides):
    n = 2 * len(sides)
    for i, number in enumerate(sides):
        kept, got = refs[2 * i : 2 * i + 2]
        keep, send = refs[n + 2 * i : n + 2 * i + 2]
        rows = keep.shape[0]
        side = place_ref[number]
        for target, at in ((keep, side), (send, 1 - side)):
            at = pl.ds(pl.multiple_of(at * rows, 16), rows)
            target[...] = (kept[at, :].astype(f32) + got[at, :].astype(f32)).astype(bf16)


def flatten(pairs):
    return [array for pair in pairs for array in pair]


def fold(place, pairs, sides):
    rows = [kept.shape[0] // 2 for kept, _ in pairs]
    outs = call(
        functools.partial(fold_kernel, sides=sides),
        tuple(jax.ShapeDtypeStruct((n, LANES), bf16) for n in rows for _ in range(2)),
        4 * sum(rows) * LANES,
        12 * sum(rows) * LANES,
        in_specs=in_vmem(2 * len(pairs)),
    )(place, *flatten(pairs))
    return list(zip(outs[::2], outs[1::2]))


def stack_kernel(*refs):
    total = refs[-1]
    at = 0
    for kept, got in zip(refs[:-1:2], refs[1:-1:2]):
        rows = kept.shape[0]
        total[at : at + rows, :] = (kept[...].astype(f32) + got[...].astype(f32)).astype(bf16)
        at += rows


def stack(pairs):
    rows = sum(kept.shape[0] for kept, _ in pairs)
    return call(
        stack_kernel, jax.ShapeDtypeStruct((rows, LANES), bf16), rows * LANES, 6 * rows * LANES
    )(*flatten(pairs))


def sum_kernel(*refs):
    n = 2 * len(refs) // 3
    for kept, got, total in zip(refs[:n:2], refs[1:n:2], refs[n:]):
        total[...] = (kept[...].astype(f32) + got[...].astype(f32)).astype(bf16)


def sum_parts(pairs):
    rows = [kept.shape[0] for kept, _ in pairs]
    return call(
        sum_kernel,
        tuple(jax.ShapeDtypeStruct((n, LANES), bf16) for n in rows),
        sum(rows) * LANES,
        6 * sum(rows) * LANES,
    )(*flatten(pairs))


def unstack_kernel(total, got, *parts):
    at = 0
    for part in parts:
        rows = part.shape[0]
        both = total[at : at + rows, :].astype(f32) + got[at : at + rows, :].astype(f32)
        part[...] = both.astype(bf16)
        at += rows


def unstack(total, got, sizes):
    return call(
        unstack_kernel,
        tuple(jax.ShapeDtypeStruct((n, LANES), bf16) for n in sizes),
        total.shape[0] * LANES,
        6 * total.shape[0] * LANES,
    )(total, got)


def join_kernel(place_ref, *refs, sides):
    for i, number in enumerate(sides):
        own, got = refs[2 * i : 2 * i + 2]
        both = refs[2 * len(sides) + i]
        rows = own.shape[0]
        side = place_ref[number]
        both[pl.ds(pl.multiple_of(side * rows, 16), rows), :] = own[...]
        both[pl.ds(pl.multiple_of((1 - side) * rows, 16), rows), :] = got[...]


def join_parts(place, pairs, sides):
    rows = [own.shape[0] for own, _ in pairs]
    return call(
        functools.partial(join_kernel, sides=sides),
        tuple(jax.ShapeDtypeStruct((2 * n, LANES), bf16) for n in rows),
        1,
        8 * sum(rows) * LANES,
        in_specs=in_vmem(2 * len(pairs)),
    )(place, *flatten(pairs))


def bring_halves(place_ref, refs, sides, targets, in_sem):
    copies = []
    for i, number in enumerate(sides):
        side = place_ref[number]
        rows = targets[i].shape[0] // 2
        for ref, at in ((refs[2 * i], side), (refs[2 * i + 1], 1 - side)):
            at = pl.ds(pl.multiple_of(at * rows, 16), rows)
            copy = pltpu.make_async_copy(ref, targets[i].at[at, :], in_sem.at[len(copies)])
            copy.start()
            copies.append(copy)
    for copy in copies:
        copy.wait()


def untile_kernel(*refs, start, width, first, sides, n_parts):
    place_ref = refs[0]
    parts = refs[1 : 1 + n_parts]
    refs = refs[1 + n_parts + (0 if first else 3) :]
    gate_ref, up_ref, down_ref, mine_s, theirs_s, downs_s, wide_s, down_s, in_sem, out_sem = refs
    me = place_ref[0]
    features = down_ref.shape[1]
    hidden = down_ref.shape[0]
    rows_held = gate_ref.shape[0]
    targets = (mine_s, theirs_s, downs_s)
    bring_halves(place_ref, parts, sides, targets, in_sem)
    leaving = []

    def leave(source, target):
        copy = pltpu.make_async_copy(source, target, out_sem.at[len(leaving)])
        copy.start()
        leaving.append(copy)

    tiles = width // LANES
    for i, (source, owner) in enumerate(((mine_s, me), (theirs_s, 1 - me))):
        lanes = pl.ds(pl.multiple_of(owner * hidden + start, LANES), width)
        for kind, target in enumerate((gate_ref, up_ref)):
            wide = wide_s.at[2 * i + kind]
            for j in range(tiles):
                row = (kind * tiles + j) * rows_held
                wide[:, j * LANES : (j + 1) * LANES] = source[row : row + rows_held, :].astype(f32)
            leave(wide, target.at[:, lanes])
    for j in range(features // LANES):
        row = j * width
        down_s[:, j * LANES : (j + 1) * LANES] = downs_s[row : row + width, :].astype(f32)
    leave(down_s, down_ref.at[pl.ds(start, width), :])
    for copy in leaving:
        copy.wait()


def untile(place, parts, outs, *, start, width, features, hidden, sides):
    first = outs is None
    rows_held = features // 2
    rows = features * width // LANES
    anywhere = pl.BlockSpec(memory_space=pl.ANY)
    outs = () if first else tuple(outs)
    n_parts = len(parts)
    return call(
        functools.partial(
            untile_kernel, start=start, width=width, first=first, sides=sides, n_parts=n_parts
        ),
        (
            jax.ShapeDtypeStruct((rows_held, 2 * hidden), f32),
            jax.ShapeDtypeStruct((rows_held, 2 * hidden), f32),
            jax.ShapeDtypeStruct((hidden, features), f32),
        ),
        3 * features * width,
        3 * features * width * 6,
        in_specs=[pl.BlockSpec(memory_space=pltpu.SMEM)] + [anywhere] * (n_parts + len(outs)),
        out_specs=(anywhere,) * 3,
        scratch_shapes=[pltpu.VMEM((rows, LANES), bf16)] * 3
        + [
            pltpu.VMEM((4, rows_held, width), f32),
            pltpu.VMEM((width, features), f32),
            pltpu.SemaphoreType.DMA((6,)),
            pltpu.SemaphoreType.DMA((5,)),
        ],
        input_output_aliases={} if first else {1 + n_parts + i: i for i in range(3)},
    )(place, *parts, *outs)


def split_kernel(place_ref, mine_ref, theirs_ref, *refs, sides):
    base = 0
    for i, number in enumerate(sides):
        side = place_ref[number]
        rows = refs[2 * i].shape[0]
        for target, at in zip(refs[2 * i : 2 * i + 2], (side, 1 - side)):
            at = pl.ds(pl.multiple_of(base + at * rows, 16), rows)
            target[...] = (mine_ref[at, :].astype(f32) + theirs_ref[at, :].astype(f32)).astype(bf16)
        base += 2 * rows


def split(place, mine, theirs, *, sides):
    rows = mine.shape[0] // (2 * len(sides))
    outs = call(
        functools.partial(split_kernel, sides=sides),
        (jax.ShapeDtypeStruct((rows, LANES), bf16),) * (2 * len(sides)),
        mine.shape[0] * LANES,
        6 * mine.shape[0] * LANES,
        in_specs=in_vmem(2),
    )(place, mine, theirs)
    return list(zip(outs[::2], outs[1::2]))


def untile_flat_kernel(*refs, sides):
    place_ref = refs[0]
    parts = refs[1 : 1 + 2 * len(sides)]
    *targets, vector_ref, flat_s, in_sem = refs[1 + 2 * len(sides) :]
    rows = flat_s.shape[0] // len(sides)
    halves = [flat_s.at[pl.ds(i * rows, rows), :] for i in range(len(sides))]
    bring_halves(place_ref, parts, sides, halves, in_sem)
    rows_held = targets[0].shape[0]
    row = 0
    for target in targets:
        for j in range(target.shape[1] // LANES):
            target[:, j * LANES : (j + 1) * LANES] = flat_s[row : row + rows_held, :].astype(f32)
            row += rows_held
    vector_ref[...] = flat_s[row:, :].astype(f32)


def untile_flat(place, parts, *, rows_held, widths, sides):
    rows = rows_held * sum(widths) // LANES + VECTOR_ROWS
    anywhere = pl.BlockSpec(memory_space=pl.ANY)
    return call(
        functools.partial(untile_flat_kernel, sides=sides),
        (
            *(jax.ShapeDtypeStruct((rows_held, width), f32) for width in widths),
            jax.ShapeDtypeStruct((VECTOR_ROWS, LANES), f32),
        ),
        rows * LANES,
        rows * LANES * 6,
        in_specs=[pl.BlockSpec(memory_space=pltpu.SMEM)] + [anywhere] * len(parts),
        out_specs=(pl.BlockSpec(memory_space=pltpu.VMEM),) * (len(widths) + 1),
        scratch_shapes=[
            pltpu.VMEM((rows, LANES), bf16), pltpu.SemaphoreType.DMA((2 * len(sides),))
        ],
    )(place, *parts)


class FlatSum:
    def __init__(self, place, order):
        self.place, self.order = place, order
        self.links, self.sides = ((X, Y), (Y, X)), ((1, 2), (2, 1))

    def over(self, arrays, level):
        return [flip(array, link) for array, link in zip(arrays, self.links[level])]

    def leave(self, mine, theirs):
        pairs = self.order(functools.partial(split, sides=self.sides[0]), self.place, mine, theirs)
        kept, sent = zip(*pairs)
        self.held = list(zip(kept, self.over(sent, 0)))

    def halve(self):
        pairs = self.order(lambda pairs: fold(self.place, pairs, self.sides[1]), self.held)
        kept, sent = zip(*pairs)
        self.held = list(zip(kept, self.over(sent, 1)))

    def sum(self):
        total = rest_of_seq(self.order(stack, self.held))
        self.total = total, flip(total, Z)

    def across(self):
        total = self.order(add, *self.total)
        for bit in range(2, lax.axis_size("ctx").bit_length() - 1):
            total = add(total, flip(total, ("ctx", bit)))
        self.total = total, flip(total, FAR)

    def turn(self):
        total, got = self.total
        sizes = (total.shape[0] // 2,) * 2
        own = self.order(lambda total, got: unstack(total, got, sizes), total, got)
        self.held = list(zip(own, self.over(own, 1)))

    def join(self):
        own = self.order(lambda pairs: join_parts(self.place, pairs, self.sides[1]), self.held)
        self.held = list(zip(own, self.over(own, 0)))


class LinkSum:
    def __init__(self, place, order):
        self.place, self.order = place, order
        links, numbers = (X, Y, Z), (1, 2, 4)
        self.links = [[links[(i + j) % 3] for i in range(3)] for j in range(3)]
        self.sides = [tuple(numbers[(i + j) % 3] for i in range(3)) for j in range(3)]

    def over(self, arrays, level):
        return [flip(array, link) for array, link in zip(arrays, self.links[level])]

    def leave(self, pairs):
        kept, sent = zip(*pairs)
        self.held = list(zip(kept, self.over(sent, 0)))

    def halve(self, level):
        pairs = self.order(lambda pairs: fold(self.place, pairs, self.sides[level]), self.held)
        kept, sent = zip(*pairs)
        self.held = list(zip(kept, self.over(sent, level)))

    def rest_of_axes(self, total):
        total = rest_of_seq(total)
        for bit in range(2, lax.axis_size("ctx").bit_length() - 1):
            total = add(total, flip(total, ("ctx", bit)))
        return total

    def across(self):
        self.sizes = [kept.shape[0] for kept, _ in self.held]
        total = self.rest_of_axes(self.order(stack, self.held))
        self.total = total, flip(total, FAR)

    def turn(self):
        own = list(self.order(lambda total, got: unstack(total, got, self.sizes), *self.total))
        own[1] = swap(own[1])
        self.held = list(zip(own, self.over(own, 2)))

    def across_each(self):
        totals = [self.rest_of_axes(total) for total in self.order(sum_parts, self.held)]
        self.held = [(total, flip(total, FAR)) for total in totals]

    def turn_each(self, i):
        own = self.order(add, *self.held[i])
        if i == 1:
            own = swap(own)
        self.held[i] = own, flip(own, self.links[2][i])

    def join(self, level):
        own = self.order(lambda pairs: join_parts(self.place, pairs, self.sides[level]), self.held)
        self.held = list(zip(own, self.over(own, level - 1)))

    @property
    def parts(self):
        return flatten(self.held)


X, Y, Z, FAR = ("seq", 0), ("seq", 1), ("ctx", 0), ("ctx", 1)


def on_device(
    block_input,
    segment_ids,
    out_cotangent,
    input_gain,
    query_weight,
    query_bias,
    key_weight,
    key_bias,
    value_weight,
    value_bias,
    output_weight,
    middle_gain,
    gate_weight,
    up_weight,
    down_weight,
):
    me = lax.axis_index("fsdp")
    ctx = lax.axis_index("ctx")
    chunks = lax.axis_size("ctx")
    place = jnp.stack([me, side(X), side(Y), ctx, side(Z)]).astype(jnp.int32)
    x = block_input[0]
    dy = out_cotangent[0]
    count, features = x.shape
    hidden = down_weight.shape[0]
    kv_width = KVH * HD

    own = (query_weight, key_weight, value_weight)
    other = tuple(swap(w) for w in own)
    vectors = (input_gain, query_bias, key_bias, value_bias, middle_gain)
    mine = jnp.concatenate(vectors)
    theirs = swap(mine)
    low = jnp.where(me == 0, mine, theirs).astype(f32)
    high = jnp.where(me == 0, theirs, mine).astype(f32)
    params = []
    at = 0
    for vector in vectors:
        size = vector.shape[0]
        params += [low[at : at + size], high[at : at + size]]
        at += size
    params = jnp.concatenate(params)[None]

    first = ctx * count
    positions = (first + jnp.arange(count, dtype=jnp.int32)).astype(f32)
    inverse = theta_base ** (-jnp.arange(0, HD, 2, dtype=f32) / HD)
    angle = positions[:, None] * jnp.tile(inverse, LANES // inverse.shape[0])[None, :]
    cosine, sine = jnp.cos(angle), jnp.sin(angle)

    n1, q, kv, w_in = project(place, x, params, own, other, cosine, sine)
    out_other = swap(output_weight)
    gate_other, up_other = swap(gate_weight), swap(up_weight)
    dy_other = swap(dy)

    reach = WINDOW // count
    before = [
        lax.ppermute(kv, "ctx", [(i, i + d) for i in range(chunks - d)])
        for d in range(1, reach + 1)
    ]
    order = Order()
    changes = order(change, dy, dy_other, down_weight)
    o, lse = order(attend, place, q, kv, *before, segment_ids)
    h1, n2, w_out = merge(place, x, o, output_weight, out_other, params)
    n2_other = swap(n2)

    widths = WIDTHS
    starts = tuple(sum(widths[:i]) for i in range(len(widths)))
    one, two = (LinkSum(place, order) for _ in range(2))
    first_sides = one.sides[0]

    def run_feed(i, token_sums):
        step = functools.partial(
            feed, start=starts[i], width=widths[i], final=i == len(widths) - 1, sides=first_sides
        )
        *grads, own_result, own_back, other_result, other_back = order(
            step, place, n2, n2_other, dy, dy_other, gate_weight, gate_other, up_weight, up_other,
            down_weight, changes, token_sums,
        )
        pairs = [(grads[2 * i], grads[2 * i + 1]) for i in range(3)]
        return pairs, (own_result, own_back, other_result, other_back)

    def run_untile(i, parts, outs):
        step = functools.partial(
            untile, start=starts[i], width=widths[i], features=features, hidden=hidden,
            sides=first_sides,
        )
        return order(step, place, parts, outs)

    pairs, token_sums = run_feed(0, None)
    one.leave(pairs)
    pairs, token_sums = run_feed(1, token_sums)
    own_result, own_back, other_result, other_back = token_sums
    got_back = swap(other_back)
    one.halve(1)

    dh1, do, gg_two, out_mine, out_theirs = order(
        middle, place, own_back, got_back, h1, dy, params, w_out, o
    )
    one.halve(2)
    one.across()
    pairs = order(lambda pairs: pairs, pairs)
    two.leave(pairs)
    back_operands = (place, q, do, kv, *before, segment_ids, lse, cosine, sine)
    dq_low, *pair_sums = order(
        functools.partial(attend_back, first_pair=0, pairs=4), *back_operands, None
    )
    two.halve(1)
    dq_high, own_pairs, *sent_pairs = order(
        functools.partial(attend_back, first_pair=4, pairs=3), *back_operands, pair_sums
    )
    got_pairs = [
        lax.ppermute(pairs, "ctx", [(i + d, i) for i in range(chunks - d)])
        for d, pairs in enumerate(sent_pairs, 1)
    ]
    one.turn()
    two.halve(2)
    back_part, gb_query, query_mine, query_theirs = order(
        query_back, place, dq_low, dq_high, n1, w_in
    )
    two.across_each()
    dx, mine, theirs = order(
        last, place, own_pairs, *got_pairs, n1, x, params, w_in, back_part, dh1, cosine, sine,
        query_mine, query_theirs, out_mine, out_theirs, gb_query, gg_two,
    )
    input_grad = dx[None]
    width = HQ * HD
    rest = FlatSum(place, order)
    got = swap(theirs)
    one.join(2)
    two.turn_each(0)
    rest.leave(mine, got)
    one.join(1)
    two.turn_each(1)
    rest.halve()
    two.turn_each(2)
    rest.sum()
    outs = run_untile(0, one.parts, None)
    two.join(2)
    rest.across()
    rest.turn()
    two.join(1)
    rest.join()
    block_output = order(
        lambda a, b, c: (a + b + c.astype(f32)).astype(bf16), h1, own_result, swap(other_result)
    )[None]
    gates, ups, gw_down = run_untile(1, two.parts, outs)
    gw_query, gw_key, gw_value, gw_out, vector = order(
        functools.partial(
            untile_flat, rows_held=features // 2, widths=(width, kv_width, kv_width, features),
            sides=rest.sides[0],
        ),
        place,
        flatten(rest.held),
    )
    vector = vector.reshape(-1)
    shares = []
    at = 0
    for size in (features, width, kv_width, kv_width, features):
        shares.append(lax.dynamic_slice_in_dim(vector, at + me * (size // 2), size // 2, 0))
        at += size
    gg_one, gb_query, gb_key, gb_value, gg_two = shares
    return (
        block_output,
        input_grad,
        gg_one,
        gw_query,
        gb_query,
        gw_key,
        gb_key,
        gw_value,
        gb_value,
        gw_out,
        gg_two,
        gates,
        ups,
        gw_down,
    )


def solution(mesh):
    return jax.shard_map(
        on_device,
        mesh=mesh,
        in_specs=(
            P(("seq", "fsdp"), "ctx", None),
            P(("seq", "fsdp"), None),
            P(("seq", "fsdp"), "ctx", None),
            P("fsdp"),
            P("fsdp", None),
            P("fsdp"),
            P("fsdp", None),
            P("fsdp"),
            P("fsdp", None),
            P("fsdp"),
            P("fsdp", None),
            P("fsdp"),
            P("fsdp", None),
            P("fsdp", None),
            P("fsdp", None),
        ),
        out_specs=(
            P(("seq", "fsdp"), "ctx", None),
            P(("seq", "fsdp"), "ctx", None),
            P("fsdp"),
            P("fsdp", None),
            P("fsdp"),
            P("fsdp", None),
            P("fsdp"),
            P("fsdp", None),
            P("fsdp"),
            P("fsdp", None),
            P("fsdp"),
            P("fsdp", None),
            P("fsdp", None),
            P("fsdp", None),
        ),
        check_vma=False,
    )
```

time: 829 us -> 505 us (0.61)
  local copies, waits for them, and re-layouts: 206 us -> 30.2 us
  Pallas kernels: 176 us -> 254 us
  other arithmetic: 78.2 us -> 5.09 us
  waiting for transfers between devices: 204 us -> 139 us
  starting transfers between devices: 103 us -> 64.6 us
  blocking collectives: 37.1 us -> 0 us
  between operations: 15.7 us -> 1.53 us
    pallas_call x4 -> x25, Pallas kernels: 123 us -> 203 us  [the longest x2 72.2 us: feed(): call(functools.partial(feed_kernel, start=start, first=first, final=final...]
    ppermute x63 -> x50, waiting for transfers between devices: 189 us -> 126 us  [flip(): return lax.ppermute(values, axis, [(i, i ^ 1 << bit) for i in range(size)])]
    dynamic_update_slice x69 -> x0, local copies, waits for them, and re-layouts: 63.1 us -> none  [the longest x35 29.9 us: join(): return lax.dynamic_update_index_in_dim(out, other, 1 - index, 0)]
    convert_element_type x21 -> x0, local copies, waits for them, and re-layouts: 48.3 us -> none  [the longest x8 18.6 us: on_device(): untile(total[:half], tiles).astype(f32)]
    convert_element_type x29 -> x4, other arithmetic: 39.9 us -> 0.33 us  [add(): return total.astype(bf16)]
    ppermute x63 -> x50, starting transfers between devices: 88.1 us -> 49.5 us  [flip(): return lax.ppermute(values, axis, [(i, i ^ 1 << bit) for i in range(size)])]
    psum x1 -> x0, blocking collectives: 37.1 us -> none  [on_device(): small_sums = lax.psum(jnp.concatenate(small), ('seq', 'ctx', 'fsdp'))]
    another operation x36 -> x1, local copies, waits for them, and re-layouts: 19.6 us -> 0.67 us  [on_device(): place = jnp.stack([me, side(X), side(Y), ctx, side(Z)]).astype(jnp.int32)]
  transfers between devices with their start and end apart: 86 -> 68, of which waited for: 34 -> 22; matrix products, arithmetic and copies ran while one was open for 32% -> 2% of each run, Pallas kernels for 18% -> 40%
where the time goes in v2:
time: 505 us; the launch traced here: 495 us
  Pallas kernels  254 us (50%)
  waiting for transfers between devices  139 us (28%)
  starting transfers between devices  64.6 us (13%)
  local copies, waits for them, and re-layouts  30.2 us (6%)
  other arithmetic  5.09 us (1%)
    ppermute x50, waiting for transfers between devices, flip(): return lax.ppermute(values, axis, [(i, i ^ 1 << bit) for i in range(size)])  126 us
    pallas_call x2, Pallas kernels, feed(): call(functools.partial(feed_kernel, start=start, first=first, final=final...  72.2 us
    ppermute x50, starting transfers between devices, flip(): return lax.ppermute(values, axis, [(i, i ^ 1 << bit) for i in range(size)])  49.5 us
    pallas_call x2, Pallas kernels, attend_back(): call(functools.partial(attend_back_kernel, first_pair=first_pair, first=f...  40.1 us
    unnamed x142, local copies, waits for them, and re-layouts  22.3 us
    pallas_call x1, Pallas kernels, attend(): call(attend_kernel, (jax.ShapeDtypeStruct((count, HQ * HD), bf16), jax.Sh...  22.2 us
    pallas_call x5, Pallas kernels, fold(): call(functools.partial(fold_kernel, sides=sides), tuple((jax.ShapeDtypeSt...  19.8 us
    pallas_call x2, Pallas kernels, untile(): call(functools.partial(untile_kernel, start=start, width=width, first=fir...  17.2 us
  transfers between devices with their start and end apart: 68, of which 22 were waited for; matrix products, arithmetic and copies ran while one was open for 2% of the time, Pallas kernels for 40%

profile of v2, /device:TPU:0, one launch (start us, length us, event | category | flops | bytes accessed | tf_op | source)
XLA Modules:
  0.0 494.7 jit_solution(16826185197900596406)
XLA Ops:
  1.2 3.5 concatenate.6
  5.8 1.8 multiply_sine_fusion
  8.7 5.0 %collective-permute-done.2.ok_ref = bf16[448,128]{1,0:T(8,128)(2,1)S(1)} collective-permute-done((bf16[448,128]{1,0:T(8,128)(2,1)}, bf16[448,128]{1,0:T(8,128)(2,1)S(1)}, u32[]{:S(2)}, u32[]{:S(2)}) %collective-permute-start.2) | collective-permute-done | bytes 114720 | tf_op jit(solution)/shard_map/ppermute | solution.py:839
  14.8 2.6 collective-permute-done.3.ov_ref
  18.7 6.0 %shard_map.254 = (bf16[512,896]{1,0:T(8,128)(2,1)}, bf16[512,896]{1,0:T(8,128)(2,1)}, bf16[512,256]{1,0:T(8,128)(2,1)}, bf16[896,1152]{1,0:T(8,128)(2,1)}) custom-call(s32[5]{0:T(128)} %stack.23.place_ref.refs_0_, bf16[512,896]{1,0:T(8,128)(2,1)} %bitcast.10, f32[1,2944]{1,0:T(1,128)} %broadcast_in_dim.10.params_ref, bf16[448,896]{1,0:T(8,128)(2,1)} %wq_ref.1, ...), custom_call_target="tpu_custom_call" | custom-call | flops 1056964608 | bytes 6291456 | tf_op jit(solution)/shard_map/pallas_call | solution.py:109
  24.7 4.6 collective-permute-start.4
  29.4 4.7 collective-permute-start.5
  34.1 11.8 %shard_map.255.refs_10_ = bf16[1024,2432]{1,0:T(8,128)(2,1)} custom-call(bf16[512,896]{1,0:T(8,128)(2,1)} %bitcast.14, bf16[512,896]{1,0:T(8,128)(2,1)} %copy-done.63, bf16[2432,896]{1,0:T(8,128)(2,1)} %refs_9_.1), custom_call_target="tpu_custom_call" | custom-call | flops 4462739456 | bytes 12582912 | tf_op jit(solution)/shard_map/pallas_call | solution.py:472
  46.7 22.2 %shard_map.256 = (bf16[512,896]{1,0:T(8,128)(2,1)}, f32[7,8,512]{2,1,0:T(8,128)}) custom-call(s32[5]{0:T(128)} %stack.23.place_ref.refs_0_, bf16[512,896]{1,0:T(8,128)(2,1)} %get-tuple-element.456.q_ref.refs_1_, bf16[512,256]{1,0:T(8,128)(2,1)} %get-tuple-element.458.kv0_ref.refs_3_, bf16[512,256]{1,0:T(8,128)(2,1)} %copy-done.67, ...), custom_call_target="tpu_custom_call" | custom-call | flops 9395240960 | bytes 4194304 | tf_op jit(solution)/shard_map/pallas_call | solution.py:248
  69.8 5.7 %shard_map.257 = (f32[512,896]{1,0:T(8,128)}, bf16[512,896]{1,0:T(8,128)(2,1)}, bf16[896,896]{1,0:T(8,128)(2,1)}) custom-call(s32[5]{0:T(128)} %stack.23.place_ref.refs_0_, bf16[512,896]{1,0:T(8,128)(2,1)} %bitcast.11, bf16[512,896]{1,0:T(8,128)(2,1)} %get-tuple-element.397.o_ref, bf16[448,896]{1,0:T(8,128)(2,1)} %own_ref.1, bf16[448,896]{1,0:T(8,128)(2,1)} %copy-done.18, ...), custom_call_target="tpu_custom_call" | custom-call | flops 822083584 | bytes 6291456 | tf_op jit(solution)/shard_map/pallas_call | solution.py:447
  75.5 2.7 collective-permute-done.8.refs_2_
  79.1 36.5 %shard_map.258 = (bf16[4480,128]{1,0:T(8,128)(2,1)}, bf16[4480,128]{1,0:T(8,128)(2,1)}, bf16[4480,128]{1,0:T(8,128)(2,1)}, bf16[4480,128]{1,0:T(8,128)(2,1)}, bf...) custom-call(s32[5]{0:T(128)} %stack.23.place_ref.refs_0_, ...), custom_call_target="tpu_custom_call" | custom-call | flops 21139292160 | bytes 31457280 | tf_op jit(solution)/shard_map/pallas_call | solution.py:642
  115.6 1.6 collective-permute-start.13
  118.7 2.6 collective-permute-start.15
  121.2 35.8 %shard_map.259 = (bf16[4032,128]{1,0:T(8,128)(2,1)}, bf16[4032,128]{1,0:T(8,128)(2,1)}, bf16[4032,128]{1,0:T(8,128)(2,1)}, bf16[4032,128]{1,0:T(8,128)(2,1)}, bf...) custom-call(s32[5]{0:T(128)} %stack.23.place_ref.refs_0_, ...), custom_call_target="tpu_custom_call" | custom-call | flops 19025362944 | bytes 31457280 | tf_op jit(solution)/shard_map/pallas_call | solution.py:642
  158.9 5.5 %shard_map.260 = (bf16[2240,128]{1,0:T(8,128)(2,1)}, bf16[2240,128]{1,0:T(8,128)(2,1)}, bf16[2240,128]{1,0:T(8,128)(2,1)}, bf16[2240,128]{1,0:T(8,128)(2,1)}, bf...) custom-call(s32[5]{0:T(128)} %stack.23.place_ref.refs_0_, bf16[4480,128]{1,0:T(8,128)(2,1)} %get-tuple-element.383.refs_0_, ...), custom_call_target="tpu_custom_call" | custom-call | flops 3440640 | bytes 10321920 | tf_op jit(solution)/shard_map/pallas_call | solution.py:906
  166.3 9.2 %shard_map.261 = (f32[512,896]{1,0:T(8,128)}, bf16[512,896]{1,0:T(8,128)(2,1)}, f32[1,896]{1,0:T(1,128)}, bf16[3136,128]{1,0:T(8,128)(2,1)}, bf16[3136,128]{1,0:T(8,128)(2,1)}) custom-call(s32[5]{0:T(128)} %stack.23.place_ref.refs_0_, f32[512,896]{1,0:T(8,128)} %get-tuple-element.391.part_ref, bf16[512,896]{1,0:T(8,128)(2,1)} %copy-done.16, ...), custom_call_target="tpu_custom_call" | custom-call | flops 1644167168 | bytes 12582912 | tf_op jit(solution)/shard_map/pallas_call | solution.py:703
  175.5 4.4 collective-permute-done.16.refs_1_
  181.1 3.5 shard_map.262
  184.6 1.6 collective-permute-start.19
  188.2 5.0 %collective-permute-done.19.refs_1_ = bf16[1120,128]{1,0:T(8,128)(2,1)S(1)} collective-permute-done((bf16[1120,128]{1,0:T(8,128)(2,1)}, bf16[1120,128]{1,0:T(8,128)(2,1)S(1)}, u32[]{:S(2)}, u32[]{:S(2)}) %collective-permute-start.19) | collective-permute-done | bytes 286752 | tf_op jit(solution)/shard_map/ppermute | solution.py:845
  194.9 2.5 shard_map.263.total
  197.4 3.3 collective-permute-start.30
  204.4 21.5 %shard_map.264 = (bf16[512,512]{1,0:T(8,128)(2,1)}, f32[2,1536,128]{2,1,0:T(8,128)}, f32[2,1536,128]{2,1,0:T(8,128)}) custom-call(s32[5]{0:T(128)} %stack.23.place_ref.refs_0_, bf16[512,896]{1,0:T(8,128)(2,1)} %get-tuple-element.456.q_ref.refs_1_, bf16[512,896]{1,0:T(8,128)(2,1)} %get-tuple-element.457.refs_2_, ...), custom_call_target="tpu_custom_call" | custom-call | flops 13421772800 | bytes 6291456 | tf_op jit(solution)/shard_map/pallas_call | solution.py:400
  226.0 16.6 %collective-permute-done.24.refs_5_ = bf16[4032,128]{1,0:T(8,128)(2,1)S(1)} collective-permute-done((bf16[4032,128]{1,0:T(8,128)(2,1)S(1)}, bf16[4032,128]{1,0:T(8,128)(2,1)S(1)}, u32[]{:S(2)}, u32[]{:S(2)}) %collective-permute-start.24) | collective-permute-done | bytes 1032224 | tf_op jit(solution)/shard_map/ppermute | solution.py:845
  243.7 5.1 %shard_map.265 = (bf16[2016,128]{1,0:T(8,128)(2,1)}, bf16[2016,128]{1,0:T(8,128)(2,1)}, bf16[2016,128]{1,0:T(8,128)(2,1)}, bf16[2016,128]{1,0:T(8,128)(2,1)}, bf...) custom-call(s32[5]{0:T(128)} %stack.23.place_ref.refs_0_, bf16[4032,128]{1,0:T(8,128)(2,1)} %get-tuple-element.448.refs_0_, ...), custom_call_target="tpu_custom_call" | custom-call | flops 3096576 | bytes 9289728 | tf_op jit(solution)/shard_map/pallas_call | solution.py:906
  250.8 18.6 %shard_map.266 = (bf16[512,384]{1,0:T(8,128)(2,1)}, f32[512,256]{1,0:T(8,128)}, bf16[512,256]{1,0:T(8,128)(2,1)}, bf16[512,256]{1,0:T(8,128)(2,1)}) custom-call(s32[5]{0:T(128)} %stack.23.place_ref.refs_0_, bf16[512,896]{1,0:T(8,128)(2,1)} %get-tuple-element.456.q_ref.refs_1_, bf16[512,896]{1,0:T(8,128)(2,1)} %get-tuple-element.457.refs_2_, ...), custom_call_target="tpu_custom_call" | custom-call | flops 10066329600 | bytes 6291456 | tf_op jit(solution)/shard_map/pallas_call | solution.py:400
  272.0 2.5 shard_map.267
  275.6 3.3 shard_map.268
  278.9 2.6 collective-permute-start.31
  283.7 6.7 %shard_map.269 = (f32[512,896]{1,0:T(8,128)}, f32[1,896]{1,0:T(1,128)}, bf16[3136,128]{1,0:T(8,128)(2,1)}, bf16[3136,128]{1,0:T(8,128)(2,1)}) custom-call(s32[5]{0:T(128)} %stack.23.place_ref.refs_0_, bf16[512,512]{1,0:T(8,128)(2,1)} %get-tuple-element.489.dqa_ref, bf16[512,384]{1,0:T(8,128)(2,1)} %get-tuple-element.490.dqb_ref, ...), custom_call_target="tpu_custom_call" | custom-call | flops 1644167168 | bytes 10485760 | tf_op jit(solution)/shard_map/pallas_call | solution.py:745
  291.3 2.4 shard_map.270
  294.6 8.8 %shard_map.271 = (bf16[512,896]{1,0:T(8,128)(2,1)}, bf16[7296,128]{1,0:T(8,128)(2,1)}, bf16[7296,128]{1,0:T(8,128)(2,1)}) custom-call(s32[5]{0:T(128)} %stack.23.place_ref.refs_0_, f32[512,256]{1,0:T(8,128)} %get-tuple-element.513.own_ref, bf16[512,256]{1,0:T(8,128)(2,1)} %copy-done.44, bf16[512,256]{1,0:T(8,128)(2,1)} %copy-done.45, ...), custom_call_target="tpu_custom_call" | custom-call | flops 469762048 | bytes 14680064 | tf_op jit(solution)/shard_map/pallas_call | solution.py:820
  304.7 2.5 collective-permute-done.37.refs_2_
  307.7 3.6 collective-permute-start.35
  311.2 4.5 collective-permute-done.36.refs_1_
  317.0 2.7 shard_map.272
  321.7 1.7 collective-permute-done.35
  324.7 3.8 shard_map.273
  328.5 1.6 collective-permute-start.40
  331.2 3.1 collective-permute-done.43.refs_1_
  335.1 5.6 %collective-permute-done.44.refs_3_ = bf16[2240,128]{1,0:T(8,128)(2,1)S(1)} collective-permute-done((bf16[2240,128]{1,0:T(8,128)(2,1)}, bf16[2240,128]{1,0:T(8,128)(2,1)S(1)}, u32[]{:S(2)}, u32[]{:S(2)}) %collective-permute-start.44) | collective-permute-done | bytes 573472 | tf_op jit(solution)/shard_map/ppermute | solution.py:845
  341.7 3.8 shard_map.274
  345.5 1.9 collective-permute-start.54
  349.4 2.5 shard_map.275
  353.4 7.2 %collective-permute-done.48 = bf16[1008,128]{1,0:T(8,128)(2,1)S(1)} collective-permute-done((bf16[1008,128]{1,0:T(8,128)(2,1)S(1)}, bf16[1008,128]{1,0:T(8,128)(2,1)S(1)}, u32[]{:S(2)}, u32[]{:S(2)}) %collective-permute-start.48) | collective-permute-done | bytes 258080 | tf_op jit(solution)/shard_map/ppermute | solution.py:845
  360.6 18.4 %collective-permute-done.46.refs_1_ = bf16[912,128]{1,0:T(8,128)(2,1)S(1)} collective-permute-done((bf16[912,128]{1,0:T(8,128)(2,1)}, bf16[912,128]{1,0:T(8,128)(2,1)S(1)}, u32[]{:S(2)}, u32[]{:S(2)}) %collective-permute-start.46) | collective-permute-done | bytes 233504 | tf_op jit(solution)/shard_map/ppermute | solution.py:845
  379.4 5.9 %collective-permute-done.47.refs_3_ = bf16[912,128]{1,0:T(8,128)(2,1)S(1)} collective-permute-done((bf16[912,128]{1,0:T(8,128)(2,1)}, bf16[912,128]{1,0:T(8,128)(2,1)S(1)}, u32[]{:S(2)}, u32[]{:S(2)}) %collective-permute-start.47) | collective-permute-done | bytes 233504 | tf_op jit(solution)/shard_map/ppermute | solution.py:845
  386.0 2.2 shard_map.276
  388.2 2.1 collective-permute-start.50
  393.0 8.9 %shard_map.277 = (f32[448,4864]{1,0:T(8,128)}, f32[448,4864]{1,0:T(8,128)}, f32[2432,896]{1,0:T(8,128)}) custom-call(s32[5]{0:T(128)} %stack.23.place_ref.refs_0_, bf16[4480,128]{1,0:T(8,128)(2,1)} %get-tuple-element.581.refs_1_, bf16[4480,128]{1,0:T(8,128)(2,1)} %copy-done.4, bf16[4480,128]{1,0:T(8,128)(2,1)} %get-tuple-element.583.refs_3_, ...), custom_call_target="tpu_custom_call" | custom-call | flops 3440640 | bytes 20643840 | tf_op jit(solution)/shard_map/pallas_call | solution.py:1043
  402.0 1.6 collective-permute-done.50.refs_1_
  404.4 2.7 shard_map.278
  409.3 19.5 %collective-permute-done.57.got = bf16[1824,128]{1,0:T(8,128)(2,1)S(1)} collective-permute-done((bf16[1824,128]{1,0:T(8,128)(2,1)S(1)}, bf16[1824,128]{1,0:T(8,128)(2,1)S(1)}, u32[]{:S(2)}, u32[]{:S(2)}) %collective-permute-start.57) | collective-permute-done | bytes 466976 | tf_op jit(solution)/shard_map/ppermute | solution.py:845
  429.6 2.0 shard_map.279
  432.7 3.7 shard_map.280
  436.5 1.7 collective-permute-start.65
  438.5 1.7 collective-permute-start.58
  440.2 24.8 %collective-permute-done.58.refs_1_ = bf16[912,128]{1,0:T(8,128)(2,1)S(1)} collective-permute-done((bf16[912,128]{1,0:T(8,128)(2,1)S(1)}, bf16[912,128]{1,0:T(8,128)(2,1)S(1)}, u32[]{:S(2)}, u32[]{:S(2)}) %collective-permute-start.58) | collective-permute-done | bytes 233504 | tf_op jit(solution)/shard_map/ppermute | solution.py:845
  465.3 5.8 %collective-permute-done.59.refs_3_ = bf16[912,128]{1,0:T(8,128)(2,1)S(1)} collective-permute-done((bf16[912,128]{1,0:T(8,128)(2,1)S(1)}, bf16[912,128]{1,0:T(8,128)(2,1)S(1)}, u32[]{:S(2)}, u32[]{:S(2)}) %collective-permute-start.59) | collective-permute-done | bytes 233504 | tf_op jit(solution)/shard_map/ppermute | solution.py:845
  471.8 2.3 shard_map.281
  474.6 2.9 add_convert_fusion
  478.6 8.3 %shard_map.282 = (f32[448,4864]{1,0:T(8,128)}, f32[448,4864]{1,0:T(8,128)}, f32[2432,896]{1,0:T(8,128)}) custom-call(s32[5]{0:T(128)} %stack.23.place_ref.refs_0_, bf16[4032,128]{1,0:T(8,128)(2,1)} %get-tuple-element.624.refs_1_, bf16[4032,128]{1,0:T(8,128)(2,1)} %copy-done.10, ...), custom_call_target="tpu_custom_call", output_to_operand_aliasing={{0}: (7, {}), {1}: (8, {}), {2}: (9, {})} | custom-call | flops 3096576 | bytes 18579456 | tf_op jit(solution)/shard_map/pallas_call | solution.py:1043
  487.7 4.0 shard_map.283
  (263 shorter events, 60.1 us)
Async XLA Ops:
  0.6 77.5 %collective-permute-start.10 = (bf16[448,4864]{1,0:T(8,128)(2,1)}, bf16[448,4864]{1,0:T(8,128)(2,1)}, u32[]{:S(2)}, u32[]{:S(2)}) collective-permute-start(bf16[448,4864]{1,0:T(8,128)(2,1)} %refs_7_.1), channel_id=1, source_target_pairs={{0,1},{1,0},{2,3},{3,2},{4,5},{5,4},{6,7},{7,6},{8,9},{9,8},{10,11... | collective-permute-start | bytes 13074440 | tf_op jit(solution)/shard_map/ppermute | solution.py:839
  1.2 77.0 %collective-permute-start.9 = (bf16[448,4864]{1,0:T(8,128)(2,1)}, bf16[448,4864]{1,0:T(8,128)(2,1)}, u32[]{:S(2)}, u32[]{:S(2)}) collective-permute-start(bf16[448,4864]{1,0:T(8,128)(2,1)} %refs_5_.1), channel_id=1, source_target_pairs={{0,1},{1,0},{2,3},{3,2},{4,5},{5,4},{6,7},{7,6},{8,9},{9,8},{10,11... | collective-permute-start | bytes 13074440 | tf_op jit(solution)/shard_map/ppermute | solution.py:839
  5.2 12.6 %collective-permute-start.1 = (bf16[448,896]{1,0:T(8,128)(2,1)}, bf16[448,896]{1,0:T(8,128)(2,1)S(1)}, u32[]{:S(2)}, u32[]{:S(2)}) collective-permute-start(bf16[448,896]{1,0:T(8,128)(2,1)} %wq_ref.1), channel_id=1, source_target_pairs={{0,1},{1,0},{2,3},{3,2},{4,5},{5,4},{6,7},{7,6},{8,9},{9,8},{10,11... | collective-permute-start | bytes 2408456 | tf_op jit(solution)/shard_map/ppermute | solution.py:839
  5.2 24.1 %collective-permute-start.6 = (bf16[512,896]{1,0:T(8,128)(2,1)}, bf16[512,896]{1,0:T(8,128)(2,1)S(1)}, u32[]{:S(2)}, u32[]{:S(2)}) collective-permute-start(bf16[512,896]{1,0:T(8,128)(2,1)} %bitcast.13), channel_id=1, source_target_pairs={{0,1},{1,0},{2,3},{3,2},{4,5},{5,4},{6,7},{7,6},{8,9},{9,8},{10,11... | collective-permute-start | bytes 2752520 | tf_op jit(solution)/shard_map/ppermute | solution.py:839
  8.3 5.4 %collective-permute-start.2 = (bf16[448,128]{1,0:T(8,128)(2,1)}, bf16[448,128]{1,0:T(8,128)(2,1)S(1)}, u32[]{:S(2)}, u32[]{:S(2)}) collective-permute-start(bf16[448,128]{1,0:T(8,128)(2,1)} %wk_ref.1), channel_id=1, source_target_pairs={{0,1},{1,0},{2,3},{3,2},{4,5},{5,4},{6,7},{7,6},{8,9},{9,8},{10,11... | collective-permute-start | bytes 344072 | tf_op jit(solution)/shard_map/ppermute | solution.py:839
  17.4 51.5 %collective-permute-start.7 = (bf16[448,896]{1,0:T(8,128)(2,1)}, bf16[448,896]{1,0:T(8,128)(2,1)S(1)}, u32[]{:S(2)}, u32[]{:S(2)}) collective-permute-start(bf16[448,896]{1,0:T(8,128)(2,1)} %own_ref.1), channel_id=1, source_target_pairs={{0,1},{1,0},{2,3},{3,2},{4,5},{5,4},{6,7},{7,6},{8,9},{9,8},{10,11... | collective-permute-start | bytes 2408456 | tf_op jit(solution)/shard_map/ppermute | solution.py:839
  24.7 21.1 %collective-permute-start.4 = (bf16[512,256]{1,0:T(8,128)(2,1)}, bf16[512,256]{1,0:T(8,128)(2,1)S(1)}, u32[]{:S(2)}, u32[]{:S(2)}) collective-permute-start(bf16[512,256]{1,0:T(8,128)(2,1)} %get-tuple-element.458.kv0_ref.refs_3_), channel_id=1, source_target_pairs={{0,2},{2,4},{4,6},{1,3},{3,5},{5,7},{8,10},{10,12},{12,14},{9,11},... | collective-permute-start | bytes 786440 | tf_op jit(solution)/shard_map/ppermute | solution.py:1276
  29.4 16.5 %collective-permute-start.5 = (bf16[512,256]{1,0:T(8,128)(2,1)}, bf16[512,256]{1,0:T(8,128)(2,1)S(1)}, u32[]{:S(2)}, u32[]{:S(2)}) collective-permute-start(bf16[512,256]{1,0:T(8,128)(2,1)} %get-tuple-element.458.kv0_ref.refs_3_), channel_id=1, source_target_pairs={{0,4},{2,6},{1,5},{3,7},{8,12},{10,14},{9,13},{11,15},{16,20},{18,... | collective-permute-start | bytes 786440 | tf_op jit(solution)/shard_map/ppermute | solution.py:1276
  115.6 41.5 %collective-permute-start.13 = (bf16[4480,128]{1,0:T(8,128)(2,1)}, bf16[4480,128]{1,0:T(8,128)(2,1)S(1)}, u32[]{:S(2)}, u32[]{:S(2)}) collective-permute-start(bf16[4480,128]{1,0:T(8,128)(2,1)} %get-tuple-element.377), channel_id=1, source_target_pairs={{0,8},{8,0},{16,24},{24,16},{1,9},{9,1},{17,25},{25,17},{2,10},{10... | collective-permute-start | bytes 3440648 | tf_op jit(solution)/shard_map/ppermute | solution.py:845
  117.1 40.0 %collective-permute-start.14 = (bf16[4480,128]{1,0:T(8,128)(2,1)}, bf16[4480,128]{1,0:T(8,128)(2,1)S(1)}, u32[]{:S(2)}, u32[]{:S(2)}) collective-permute-start(bf16[4480,128]{1,0:T(8,128)(2,1)} %get-tuple-element.379), channel_id=1, source_target_pairs={{0,16},{8,24},{16,0},{24,8},{1,17},{9,25},{17,1},{25,9},{2,18},{10... | collective-permute-start | bytes 3440648 | tf_op jit(solution)/shard_map/ppermute | solution.py:845
  118.7 38.5 %collective-permute-start.15 = (bf16[4480,128]{1,0:T(8,128)(2,1)}, bf16[4480,128]{1,0:T(8,128)(2,1)S(1)}, u32[]{:S(2)}, u32[]{:S(2)}) collective-permute-start(bf16[4480,128]{1,0:T(8,128)(2,1)} %get-tuple-element.381), channel_id=1, source_target_pairs={{0,2},{2,0},{4,6},{6,4},{1,3},{3,1},{5,7},{7,5},{8,10},{10,8},{12,... | collective-permute-start | bytes 3440648 | tf_op jit(solution)/shard_map/ppermute | solution.py:845
  157.0 8.4 %collective-permute-start.12 = (bf16[512,896]{1,0:T(8,128)(2,1)}, bf16[512,896]{1,0:T(8,128)(2,1)S(1)}, u32[]{:S(2)}, u32[]{:S(2)}) collective-permute-start(bf16[512,896]{1,0:T(8,128)(2,1)} %get-tuple-element.375), channel_id=1, source_target_pairs={{0,1},{1,0},{2,3},{3,2},{4,5},{5,4},{6,7},{7,6},{8,9},{9,8},{10,11... | collective-permute-start | bytes 2752520 | tf_op jit(solution)/shard_map/ppermute | solution.py:839
  164.3 15.6 %collective-permute-start.16 = (bf16[2240,128]{1,0:T(8,128)(2,1)}, bf16[2240,128]{1,0:T(8,128)(2,1)S(1)}, u32[]{:S(2)}, u32[]{:S(2)}) collective-permute-start(bf16[2240,128]{1,0:T(8,128)(2,1)} %get-tuple-element.405), channel_id=1, source_target_pairs={{0,16},{8,24},{16,0},{24,8},{1,17},{9,25},{17,1},{25,9},{2,18},{10... | collective-permute-start | bytes 1720328 | tf_op jit(solution)/shard_map/ppermute | solution.py:845
  164.8 15.3 %collective-permute-start.17 = (bf16[2240,128]{1,0:T(8,128)(2,1)}, bf16[2240,128]{1,0:T(8,128)(2,1)S(1)}, u32[]{:S(2)}, u32[]{:S(2)}) collective-permute-start(bf16[2240,128]{1,0:T(8,128)(2,1)} %get-tuple-element.407), channel_id=1, source_target_pairs={{0,2},{2,0},{4,6},{6,4},{1,3},{3,1},{5,7},{7,5},{8,10},{10,8},{12,... | collective-permute-start | bytes 1720328 | tf_op jit(solution)/shard_map/ppermute | solution.py:845
  164.8 15.3 %collective-permute-start.18 = (bf16[2240,128]{1,0:T(8,128)(2,1)}, bf16[2240,128]{1,0:T(8,128)(2,1)S(1)}, u32[]{:S(2)}, u32[]{:S(2)}) collective-permute-start(bf16[2240,128]{1,0:T(8,128)(2,1)} %get-tuple-element.409), channel_id=1, source_target_pairs={{0,8},{8,0},{16,24},{24,16},{1,9},{9,1},{17,25},{25,17},{2,10},{10... | collective-permute-start | bytes 1720328 | tf_op jit(solution)/shard_map/ppermute | solution.py:845
  184.6 8.6 %collective-permute-start.19 = (bf16[1120,128]{1,0:T(8,128)(2,1)}, bf16[1120,128]{1,0:T(8,128)(2,1)S(1)}, u32[]{:S(2)}, u32[]{:S(2)}) collective-permute-start(bf16[1120,128]{1,0:T(8,128)(2,1)} %get-tuple-element.418), channel_id=1, source_target_pairs={{0,2},{2,0},{4,6},{6,4},{1,3},{3,1},{5,7},{7,5},{8,10},{10,8},{12,... | collective-permute-start | bytes 860168 | tf_op jit(solution)/shard_map/ppermute | solution.py:845
  186.2 7.7 %collective-permute-start.20 = (bf16[1120,128]{1,0:T(8,128)(2,1)}, bf16[1120,128]{1,0:T(8,128)(2,1)S(1)}, u32[]{:S(2)}, u32[]{:S(2)}) collective-permute-start(bf16[1120,128]{1,0:T(8,128)(2,1)} %get-tuple-element.420), channel_id=1, source_target_pairs={{0,8},{8,0},{16,24},{24,16},{1,9},{9,1},{17,25},{25,17},{2,10},{10... | collective-permute-start | bytes 860168 | tf_op jit(solution)/shard_map/ppermute | solution.py:845
  186.7 7.5 %collective-permute-start.21 = (bf16[1120,128]{1,0:T(8,128)(2,1)}, bf16[1120,128]{1,0:T(8,128)(2,1)S(1)}, u32[]{:S(2)}, u32[]{:S(2)}) collective-permute-start(bf16[1120,128]{1,0:T(8,128)(2,1)} %get-tuple-element.422), channel_id=1, source_target_pairs={{0,16},{8,24},{16,0},{24,8},{1,17},{9,25},{17,1},{25,9},{2,18},{10... | collective-permute-start | bytes 860168 | tf_op jit(solution)/shard_map/ppermute | solution.py:845
  197.4 73.3 %collective-permute-start.30 = (bf16[3360,128]{1,0:T(8,128)(2,1)}, bf16[3360,128]{1,0:T(8,128)(2,1)S(1)}, u32[]{:S(2)}, u32[]{:S(2)}) collective-permute-start(bf16[3360,128]{1,0:T(8,128)(2,1)} %shard_map.263.total), channel_id=1, source_target_pairs={{0,4},{2,6},{4,0},{6,2},{1,5},{3,7},{5,1},{7,3},{8,12},{10,14},{12... | collective-permute-start | bytes 2580488 | tf_op jit(solution)/shard_map/ppermute | solution.py:845
  200.6 25.3 %collective-permute-start.22 = (bf16[4032,128]{1,0:T(8,128)(2,1)}, bf16[4032,128]{1,0:T(8,128)(2,1)S(1)}, u32[]{:S(2)}, u32[]{:S(2)}) collective-permute-start(bf16[4032,128]{1,0:T(8,128)(2,1)} %get-tuple-element.442), channel_id=1, source_target_pairs={{0,8},{8,0},{16,24},{24,16},{1,9},{9,1},{17,25},{25,17},{2,10},{10... | collective-permute-start | bytes 3096584 | tf_op jit(solution)/shard_map/ppermute | solution.py:845
  202.1 23.9 %collective-permute-start.23 = (bf16[4032,128]{1,0:T(8,128)(2,1)}, bf16[4032,128]{1,0:T(8,128)(2,1)S(1)}, u32[]{:S(2)}, u32[]{:S(2)}) collective-permute-start(bf16[4032,128]{1,0:T(8,128)(2,1)} %get-tuple-element.444), channel_id=1, source_target_pairs={{0,16},{8,24},{16,0},{24,8},{1,17},{9,25},{17,1},{25,9},{2,18},{10... | collective-permute-start | bytes 3096584 | tf_op jit(solution)/shard_map/ppermute | solution.py:845
  203.7 39.0 %collective-permute-start.24 = (bf16[4032,128]{1,0:T(8,128)(2,1)S(1)}, bf16[4032,128]{1,0:T(8,128)(2,1)S(1)}, u32[]{:S(2)}, u32[]{:S(2)}) collective-permute-start(bf16[4032,128]{1,0:T(8,128)(2,1)S(1)} %copy-done.62), channel_id=1, source_target_pairs={{0,2},{2,0},{4,6},{6,4},{1,3},{3,1},{5,7},{7,5},{8,10},{10,8},{12,... | collective-permute-start | bytes 3096584 | tf_op jit(solution)/shard_map/ppermute | solution.py:845
  248.8 25.7 %collective-permute-start.27 = (bf16[2016,128]{1,0:T(8,128)(2,1)}, bf16[2016,128]{1,0:T(8,128)(2,1)S(1)}, u32[]{:S(2)}, u32[]{:S(2)}) collective-permute-start(bf16[2016,128]{1,0:T(8,128)(2,1)} %get-tuple-element.473), channel_id=1, source_target_pairs={{0,16},{8,24},{16,0},{24,8},{1,17},{9,25},{17,1},{25,9},{2,18},{10... | collective-permute-start | bytes 1548296 | tf_op jit(solution)/shard_map/ppermute | solution.py:845
  249.5 24.9 %collective-permute-start.28 = (bf16[2016,128]{1,0:T(8,128)(2,1)}, bf16[2016,128]{1,0:T(8,128)(2,1)S(1)}, u32[]{:S(2)}, u32[]{:S(2)}) collective-permute-start(bf16[2016,128]{1,0:T(8,128)(2,1)} %get-tuple-element.475), channel_id=1, source_target_pairs={{0,2},{2,0},{4,6},{6,4},{1,3},{3,1},{5,7},{7,5},{8,10},{10,8},{12,... | collective-permute-start | bytes 1548296 | tf_op jit(solution)/shard_map/ppermute | solution.py:845
  249.5 24.9 %collective-permute-start.29 = (bf16[2016,128]{1,0:T(8,128)(2,1)}, bf16[2016,128]{1,0:T(8,128)(2,1)S(1)}, u32[]{:S(2)}, u32[]{:S(2)}) collective-permute-start(bf16[2016,128]{1,0:T(8,128)(2,1)} %get-tuple-element.477), channel_id=1, source_target_pairs={{0,8},{8,0},{16,24},{24,16},{1,9},{9,1},{17,25},{25,17},{2,10},{10... | collective-permute-start | bytes 1548296 | tf_op jit(solution)/shard_map/ppermute | solution.py:845
  269.4 24.4 %collective-permute-start.25 = (bf16[512,256]{1,0:T(8,128)(2,1)}, bf16[512,256]{1,0:T(8,128)(2,1)S(1)}, u32[]{:S(2)}, u32[]{:S(2)}) collective-permute-start(bf16[512,256]{1,0:T(8,128)(2,1)} %get-tuple-element.468), channel_id=1, source_target_pairs={{2,0},{4,2},{6,4},{3,1},{5,3},{7,5},{10,8},{12,10},{14,12},{11,9},... | collective-permute-start | bytes 786440 | tf_op jit(solution)/shard_map/ppermute | solution.py:1331
  270.7 23.1 %collective-permute-start.26 = (bf16[512,256]{1,0:T(8,128)(2,1)}, bf16[512,256]{1,0:T(8,128)(2,1)S(1)}, u32[]{:S(2)}, u32[]{:S(2)}) collective-permute-start(bf16[512,256]{1,0:T(8,128)(2,1)} %get-tuple-element.469), channel_id=1, source_target_pairs={{4,0},{6,2},{5,1},{7,3},{12,8},{14,10},{13,9},{15,11},{20,16},{22,... | collective-permute-start | bytes 786440 | tf_op jit(solution)/shard_map/ppermute | solution.py:1331
  278.9 11.5 %collective-permute-start.31 = (bf16[1008,128]{1,0:T(8,128)(2,1)}, bf16[1008,128]{1,0:T(8,128)(2,1)S(1)}, u32[]{:S(2)}, u32[]{:S(2)}) collective-permute-start(bf16[1008,128]{1,0:T(8,128)(2,1)} %get-tuple-element.500), channel_id=1, source_target_pairs={{0,2},{2,0},{4,6},{6,4},{1,3},{3,1},{5,7},{7,5},{8,10},{10,8},{12,... | collective-permute-start | bytes 774152 | tf_op jit(solution)/shard_map/ppermute | solution.py:845
  281.5 8.9 %collective-permute-start.32 = (bf16[1008,128]{1,0:T(8,128)(2,1)}, bf16[1008,128]{1,0:T(8,128)(2,1)S(1)}, u32[]{:S(2)}, u32[]{:S(2)}) collective-permute-start(bf16[1008,128]{1,0:T(8,128)(2,1)} %get-tuple-element.502), channel_id=1, source_target_pairs={{0,8},{8,0},{16,24},{24,16},{1,9},{9,1},{17,25},{25,17},{2,10},{10... | collective-permute-start | bytes 774152 | tf_op jit(solution)/shard_map/ppermute | solution.py:845
  282.4 8.1 %collective-permute-start.33 = (bf16[1008,128]{1,0:T(8,128)(2,1)}, bf16[1008,128]{1,0:T(8,128)(2,1)S(1)}, u32[]{:S(2)}, u32[]{:S(2)}) collective-permute-start(bf16[1008,128]{1,0:T(8,128)(2,1)} %get-tuple-element.504), channel_id=1, source_target_pairs={{0,16},{8,24},{16,0},{24,8},{1,17},{9,25},{17,1},{25,9},{2,18},{10... | collective-permute-start | bytes 774152 | tf_op jit(solution)/shard_map/ppermute | solution.py:845
  303.3 20.1 %collective-permute-start.34 = (bf16[7296,128]{1,0:T(8,128)(2,1)}, bf16[7296,128]{1,0:T(8,128)(2,1)S(1)}, u32[]{:S(2)}, u32[]{:S(2)}) collective-permute-start(bf16[7296,128]{1,0:T(8,128)(2,1)} %get-tuple-element.531), channel_id=1, source_target_pairs={{0,1},{1,0},{2,3},{3,2},{4,5},{5,4},{6,7},{7,6},{8,9},{9,8},{10,11... | collective-permute-start | bytes 5603336 | tf_op jit(solution)/shard_map/ppermute | solution.py:839
  303.9 11.9 %collective-permute-start.36 = (bf16[1120,128]{1,0:T(8,128)(2,1)S(1)}, bf16[1120,128]{1,0:T(8,128)(2,1)S(1)}, u32[]{:S(2)}, u32[]{:S(2)}) collective-permute-start(bf16[1120,128]{1,0:T(8,128)(2,1)S(1)} %copy-done.38), channel_id=1, source_target_pairs={{0,2},{2,0},{4,6},{6,4},{1,3},{3,1},{5,7},{7,5},{8,10},{10,8},{12,... | collective-permute-start | bytes 860168 | tf_op jit(solution)/shard_map/ppermute | solution.py:845
  303.9 11.8 %collective-permute-start.39 = (bf16[1120,128]{1,0:T(8,128)(2,1)S(1)}, bf16[1120,128]{1,0:T(8,128)(2,1)S(1)}, u32[]{:S(2)}, u32[]{:S(2)}) collective-permute-start(bf16[1120,128]{1,0:T(8,128)(2,1)S(1)} %copy-done.39), channel_id=1, source_target_pairs={{0,16},{8,24},{16,0},{24,8},{1,17},{9,25},{17,1},{25,9},{2,18},{10... | collective-permute-start | bytes 860168 | tf_op jit(solution)/shard_map/ppermute | solution.py:845
  307.2 9.1 %collective-permute-start.38 = (bf16[1120,128]{1,0:T(8,128)(2,1)S(1)}, bf16[1120,128]{1,0:T(8,128)(2,1)S(1)}, u32[]{:S(2)}, u32[]{:S(2)}) collective-permute-start(bf16[1120,128]{1,0:T(8,128)(2,1)S(1)} %collective-permute-done.37.refs_2_), channel_id=1, source_target_pairs={{0,8},{8,0},{16,24},{24,16},{1,9},{9,1},{17,25},{25,17},{2,10},{10... | collective-permute-start | bytes 860168 | tf_op jit(solution)/shard_map/ppermute | solution.py:845
  307.7 15.7 %collective-permute-start.35 = (bf16[1008,128]{1,0:T(8,128)(2,1)S(1)}, bf16[1008,128]{1,0:T(8,128)(2,1)S(1)}, u32[]{:S(2)}, u32[]{:S(2)}) collective-permute-start(bf16[1008,128]{1,0:T(8,128)(2,1)S(1)} %copy-done.48), channel_id=1, source_target_pairs={{0,4},{2,6},{4,0},{6,2},{1,5},{3,7},{5,1},{7,3},{8,12},{10,14},{12... | collective-permute-start | bytes 774152 | tf_op jit(solution)/shard_map/ppermute | solution.py:845
  319.7 14.6 %collective-permute-start.43 = (bf16[2240,128]{1,0:T(8,128)(2,1)}, bf16[2240,128]{1,0:T(8,128)(2,1)S(1)}, u32[]{:S(2)}, u32[]{:S(2)}) collective-permute-start(bf16[2240,128]{1,0:T(8,128)(2,1)} %get-tuple-element.554.refs_0_), channel_id=1, source_target_pairs={{0,16},{8,24},{16,0},{24,8},{1,17},{9,25},{17,1},{25,9},{2,18},{10... | collective-permute-start | bytes 1720328 | tf_op jit(solution)/shard_map/ppermute | solution.py:845
  320.5 20.2 %collective-permute-start.44 = (bf16[2240,128]{1,0:T(8,128)(2,1)}, bf16[2240,128]{1,0:T(8,128)(2,1)S(1)}, u32[]{:S(2)}, u32[]{:S(2)}) collective-permute-start(bf16[2240,128]{1,0:T(8,128)(2,1)} %get-tuple-element.556.refs_2_), channel_id=1, source_target_pairs={{0,2},{2,0},{4,6},{6,4},{1,3},{3,1},{5,7},{7,5},{8,10},{10,8},{12,... | collective-permute-start | bytes 1720328 | tf_op jit(solution)/shard_map/ppermute | solution.py:845
  320.5 20.2 %collective-permute-start.45 = (bf16[2240,128]{1,0:T(8,128)(2,1)}, bf16[2240,128]{1,0:T(8,128)(2,1)S(1)}, u32[]{:S(2)}, u32[]{:S(2)}) collective-permute-start(bf16[2240,128]{1,0:T(8,128)(2,1)} %get-tuple-element.558.refs_4_), channel_id=1, source_target_pairs={{0,8},{8,0},{16,24},{24,16},{1,9},{9,1},{17,25},{25,17},{2,10},{10... | collective-permute-start | bytes 1720328 | tf_op jit(solution)/shard_map/ppermute | solution.py:845
  328.5 19.1 %collective-permute-start.40 = (bf16[1824,128]{1,0:T(8,128)(2,1)}, bf16[1824,128]{1,0:T(8,128)(2,1)S(1)}, u32[]{:S(2)}, u32[]{:S(2)}) collective-permute-start(bf16[1824,128]{1,0:T(8,128)(2,1)} %get-tuple-element.548), channel_id=1, source_target_pairs={{0,8},{8,0},{16,24},{24,16},{1,9},{9,1},{17,25},{25,17},{2,10},{10... | collective-permute-start | bytes 1400840 | tf_op jit(solution)/shard_map/ppermute | solution.py:845
  330.1 17.6 %collective-permute-start.42 = (bf16[1008,128]{1,0:T(8,128)(2,1)S(1)}, bf16[1008,128]{1,0:T(8,128)(2,1)S(1)}, u32[]{:S(2)}, u32[]{:S(2)}) collective-permute-start(bf16[1008,128]{1,0:T(8,128)(2,1)S(1)} %copy-done.47), channel_id=1, source_target_pairs={{0,4},{2,6},{4,0},{6,2},{1,5},{3,7},{5,1},{7,3},{8,12},{10,14},{12... | collective-permute-start | bytes 774152 | tf_op jit(solution)/shard_map/ppermute | solution.py:845
  334.4 14.2 %collective-permute-start.41 = (bf16[1824,128]{1,0:T(8,128)(2,1)}, bf16[1824,128]{1,0:T(8,128)(2,1)S(1)}, u32[]{:S(2)}, u32[]{:S(2)}) collective-permute-start(bf16[1824,128]{1,0:T(8,128)(2,1)} %get-tuple-element.550), channel_id=1, source_target_pairs={{0,16},{8,24},{16,0},{24,8},{1,17},{9,25},{17,1},{25,9},{2,18},{10... | collective-permute-start | bytes 1400840 | tf_op jit(solution)/shard_map/ppermute | solution.py:845
  345.5 44.7 %collective-permute-start.54 = (bf16[4480,128]{1,0:T(8,128)(2,1)}, bf16[4480,128]{1,0:T(8,128)(2,1)S(1)}, u32[]{:S(2)}, u32[]{:S(2)}) collective-permute-start(bf16[4480,128]{1,0:T(8,128)(2,1)} %get-tuple-element.581.refs_1_), channel_id=1, source_target_pairs={{0,8},{8,0},{16,24},{24,16},{1,9},{9,1},{17,25},{25,17},{2,10},{10... | collective-permute-start | bytes 3440648 | tf_op jit(solution)/shard_map/ppermute | solution.py:845
  347.4 43.1 %collective-permute-start.55 = (bf16[4480,128]{1,0:T(8,128)(2,1)}, bf16[4480,128]{1,0:T(8,128)(2,1)S(1)}, u32[]{:S(2)}, u32[]{:S(2)}) collective-permute-start(bf16[4480,128]{1,0:T(8,128)(2,1)} %get-tuple-element.583.refs_3_), channel_id=1, source_target_pairs={{0,16},{8,24},{16,0},{24,8},{1,17},{9,25},{17,1},{25,9},{2,18},{10... | collective-permute-start | bytes 3440648 | tf_op jit(solution)/shard_map/ppermute | solution.py:845
  347.6 13.0 %collective-permute-start.48 = (bf16[1008,128]{1,0:T(8,128)(2,1)S(1)}, bf16[1008,128]{1,0:T(8,128)(2,1)S(1)}, u32[]{:S(2)}, u32[]{:S(2)}) collective-permute-start(bf16[1008,128]{1,0:T(8,128)(2,1)S(1)} %copy-done.46), channel_id=1, source_target_pairs={{0,4},{2,6},{4,0},{6,2},{1,5},{3,7},{5,1},{7,3},{8,12},{10,14},{12... | collective-permute-start | bytes 774152 | tf_op jit(solution)/shard_map/ppermute | solution.py:845
  347.7 44.3 %collective-permute-start.56 = (bf16[4480,128]{1,0:T(8,128)(2,1)}, bf16[4480,128]{1,0:T(8,128)(2,1)S(1)}, u32[]{:S(2)}, u32[]{:S(2)}) collective-permute-start(bf16[4480,128]{1,0:T(8,128)(2,1)} %get-tuple-element.585.refs_5_), channel_id=1, source_target_pairs={{0,2},{2,0},{4,6},{6,4},{1,3},{3,1},{5,7},{7,5},{8,10},{10,8},{12,... | collective-permute-start | bytes 3440648 | tf_op jit(solution)/shard_map/ppermute | solution.py:845
  351.9 27.1 %collective-permute-start.46 = (bf16[912,128]{1,0:T(8,128)(2,1)}, bf16[912,128]{1,0:T(8,128)(2,1)S(1)}, u32[]{:S(2)}, u32[]{:S(2)}) collective-permute-start(bf16[912,128]{1,0:T(8,128)(2,1)} %get-tuple-element.568), channel_id=1, source_target_pairs={{0,16},{8,24},{16,0},{24,8},{1,17},{9,25},{17,1},{25,9},{2,18},{10... | collective-permute-start | bytes 700424 | tf_op jit(solution)/shard_map/ppermute | solution.py:845
  360.6 27.5 %collective-permute-start.51 = (bf16[1008,128]{1,0:T(8,128)(2,1)S(1)}, bf16[1008,128]{1,0:T(8,128)(2,1)S(1)}, u32[]{:S(2)}, u32[]{:S(2)}) collective-permute-start(bf16[1008,128]{1,0:T(8,128)(2,1)S(1)} %add_convert_fusion.3), channel_id=1, source_target_pairs={{0,1},{1,0},{2,3},{3,2},{4,5},{5,4},{6,7},{7,6},{8,9},{9,8},{10,11... | collective-permute-start | bytes 774152 | tf_op jit(solution)/shard_map/ppermute | solution.py:839
  379.0 6.3 %collective-permute-start.47 = (bf16[912,128]{1,0:T(8,128)(2,1)}, bf16[912,128]{1,0:T(8,128)(2,1)S(1)}, u32[]{:S(2)}, u32[]{:S(2)}) collective-permute-start(bf16[912,128]{1,0:T(8,128)(2,1)} %get-tuple-element.570), channel_id=1, source_target_pairs={{0,8},{8,0},{16,24},{24,16},{1,9},{9,1},{17,25},{25,17},{2,10},{10... | collective-permute-start | bytes 700424 | tf_op jit(solution)/shard_map/ppermute | solution.py:845
  388.1 20.8 %collective-permute-start.49 = (bf16[1824,128]{1,0:T(8,128)(2,1)}, bf16[1824,128]{1,0:T(8,128)(2,1)S(1)}, u32[]{:S(2)}, u32[]{:S(2)}) collective-permute-start(bf16[1824,128]{1,0:T(8,128)(2,1)} %shard_map.276), channel_id=1, source_target_pairs={{0,2},{2,0},{4,6},{6,4},{1,3},{3,1},{5,7},{7,5},{8,10},{10,8},{12,... | collective-permute-start | bytes 1400840 | tf_op jit(solution)/shard_map/ppermute | solution.py:845
  388.2 15.4 %collective-permute-start.50 = (bf16[1008,128]{1,0:T(8,128)(2,1)S(1)}, bf16[1008,128]{1,0:T(8,128)(2,1)S(1)}, u32[]{:S(2)}, u32[]{:S(2)}) collective-permute-start(bf16[1008,128]{1,0:T(8,128)(2,1)S(1)} %add_convert_fusion.4.refs_0_), channel_id=1, source_target_pairs={{0,2},{2,0},{4,6},{6,4},{1,3},{3,1},{5,7},{7,5},{8,10},{10,8},{12,... | collective-permute-start | bytes 774152 | tf_op jit(solution)/shard_map/ppermute | solution.py:845
  390.2 13.3 %collective-permute-start.52 = (bf16[1008,128]{1,0:T(8,128)(2,1)S(1)}, bf16[1008,128]{1,0:T(8,128)(2,1)S(1)}, u32[]{:S(2)}, u32[]{:S(2)}) collective-permute-start(bf16[1008,128]{1,0:T(8,128)(2,1)S(1)} %collective-permute-done.51.refs_2_), channel_id=1, source_target_pairs={{0,8},{8,0},{16,24},{24,16},{1,9},{9,1},{17,25},{25,17},{2,10},{10... | collective-permute-start | bytes 774152 | tf_op jit(solution)/shard_map/ppermute | solution.py:845
  390.5 13.1 %collective-permute-start.53 = (bf16[1008,128]{1,0:T(8,128)(2,1)S(1)}, bf16[1008,128]{1,0:T(8,128)(2,1)S(1)}, u32[]{:S(2)}, u32[]{:S(2)}) collective-permute-start(bf16[1008,128]{1,0:T(8,128)(2,1)S(1)} %add_convert_fusion.2.refs_4_), channel_id=1, source_target_pairs={{0,16},{8,24},{16,0},{24,8},{1,17},{9,25},{17,1},{25,9},{2,18},{10... | collective-permute-start | bytes 774152 | tf_op jit(solution)/shard_map/ppermute | solution.py:845
  407.1 24.4 %collective-permute-start.60 = (bf16[2016,128]{1,0:T(8,128)(2,1)}, bf16[2016,128]{1,0:T(8,128)(2,1)S(1)}, u32[]{:S(2)}, u32[]{:S(2)}) collective-permute-start(bf16[2016,128]{1,0:T(8,128)(2,1)} %get-tuple-element.603.refs_0_), channel_id=1, source_target_pairs={{0,16},{8,24},{16,0},{24,8},{1,17},{9,25},{17,1},{25,9},{2,18},{10... | collective-permute-start | bytes 1548296 | tf_op jit(solution)/shard_map/ppermute | solution.py:845
  408.3 23.3 %collective-permute-start.61 = (bf16[2016,128]{1,0:T(8,128)(2,1)}, bf16[2016,128]{1,0:T(8,128)(2,1)S(1)}, u32[]{:S(2)}, u32[]{:S(2)}) collective-permute-start(bf16[2016,128]{1,0:T(8,128)(2,1)} %get-tuple-element.605.refs_2_), channel_id=1, source_target_pairs={{0,2},{2,0},{4,6},{6,4},{1,3},{3,1},{5,7},{7,5},{8,10},{10,8},{12,... | collective-permute-start | bytes 1548296 | tf_op jit(solution)/shard_map/ppermute | solution.py:845
  408.6 23.0 %collective-permute-start.62 = (bf16[2016,128]{1,0:T(8,128)(2,1)}, bf16[2016,128]{1,0:T(8,128)(2,1)S(1)}, u32[]{:S(2)}, u32[]{:S(2)}) collective-permute-start(bf16[2016,128]{1,0:T(8,128)(2,1)} %get-tuple-element.607.refs_4_), channel_id=1, source_target_pairs={{0,8},{8,0},{16,24},{24,16},{1,9},{9,1},{17,25},{25,17},{2,10},{10... | collective-permute-start | bytes 1548296 | tf_op jit(solution)/shard_map/ppermute | solution.py:845
  409.1 19.7 %collective-permute-start.57 = (bf16[1824,128]{1,0:T(8,128)(2,1)S(1)}, bf16[1824,128]{1,0:T(8,128)(2,1)S(1)}, u32[]{:S(2)}, u32[]{:S(2)}) collective-permute-start(bf16[1824,128]{1,0:T(8,128)(2,1)S(1)} %add_convert_fusion.1.total), channel_id=1, source_target_pairs={{0,4},{2,6},{4,0},{6,2},{1,5},{3,7},{5,1},{7,3},{8,12},{10,14},{12... | collective-permute-start | bytes 1400840 | tf_op jit(solution)/shard_map/ppermute | solution.py:845
  409.2 65.2 %collective-permute-start.11 = (bf16[512,896]{1,0:T(8,128)(2,1)}, bf16[512,896]{1,0:T(8,128)(2,1)}, u32[]{:S(2)}, u32[]{:S(2)}) collective-permute-start(bf16[512,896]{1,0:T(8,128)(2,1)} %get-tuple-element.373), channel_id=1, source_target_pairs={{0,1},{1,0},{2,3},{3,2},{4,5},{5,4},{6,7},{7,6},{8,9},{9,8},{10,11... | collective-permute-start | bytes 2752520 | tf_op jit(solution)/shard_map/ppermute | solution.py:839
  436.5 41.1 %collective-permute-start.65 = (bf16[4032,128]{1,0:T(8,128)(2,1)}, bf16[4032,128]{1,0:T(8,128)(2,1)S(1)}, u32[]{:S(2)}, u32[]{:S(2)}) collective-permute-start(bf16[4032,128]{1,0:T(8,128)(2,1)} %get-tuple-element.624.refs_1_), channel_id=1, source_target_pairs={{0,8},{8,0},{16,24},{24,16},{1,9},{9,1},{17,25},{25,17},{2,10},{10... | collective-permute-start | bytes 3096584 | tf_op jit(solution)/shard_map/ppermute | solution.py:845
  438.2 39.4 %collective-permute-start.66 = (bf16[4032,128]{1,0:T(8,128)(2,1)}, bf16[4032,128]{1,0:T(8,128)(2,1)}, u32[]{:S(2)}, u32[]{:S(2)}) collective-permute-start(bf16[4032,128]{1,0:T(8,128)(2,1)} %get-tuple-element.626.refs_3_), channel_id=1, source_target_pairs={{0,16},{8,24},{16,0},{24,8},{1,17},{9,25},{17,1},{25,9},{2,18},{10... | collective-permute-start | bytes 3096584 | tf_op jit(solution)/shard_map/ppermute | solution.py:845
  438.5 39.1 %collective-permute-start.67 = (bf16[4032,128]{1,0:T(8,128)(2,1)}, bf16[4032,128]{1,0:T(8,128)(2,1)}, u32[]{:S(2)}, u32[]{:S(2)}) collective-permute-start(bf16[4032,128]{1,0:T(8,128)(2,1)} %get-tuple-element.628.refs_5_), channel_id=1, source_target_pairs={{0,2},{2,0},{4,6},{6,4},{1,3},{3,1},{5,7},{7,5},{8,10},{10,8},{12,... | collective-permute-start | bytes 3096584 | tf_op jit(solution)/shard_map/ppermute | solution.py:845
  438.5 26.5 %collective-permute-start.58 = (bf16[912,128]{1,0:T(8,128)(2,1)S(1)}, bf16[912,128]{1,0:T(8,128)(2,1)S(1)}, u32[]{:S(2)}, u32[]{:S(2)}) collective-permute-start(bf16[912,128]{1,0:T(8,128)(2,1)S(1)} %copy-done.56), channel_id=1, source_target_pairs={{0,16},{8,24},{16,0},{24,8},{1,17},{9,25},{17,1},{25,9},{2,18},{10... | collective-permute-start | bytes 700424 | tf_op jit(solution)/shard_map/ppermute | solution.py:845
  465.0 6.1 %collective-permute-start.59 = (bf16[912,128]{1,0:T(8,128)(2,1)S(1)}, bf16[912,128]{1,0:T(8,128)(2,1)S(1)}, u32[]{:S(2)}, u32[]{:S(2)}) collective-permute-start(bf16[912,128]{1,0:T(8,128)(2,1)S(1)} %copy-done.57), channel_id=1, source_target_pairs={{0,8},{8,0},{16,24},{24,16},{1,9},{9,1},{17,25},{25,17},{2,10},{10... | collective-permute-start | bytes 700424 | tf_op jit(solution)/shard_map/ppermute | solution.py:845
  474.1 12.8 %collective-permute-start.63 = (bf16[1824,128]{1,0:T(8,128)(2,1)}, bf16[1824,128]{1,0:T(8,128)(2,1)S(1)}, u32[]{:S(2)}, u32[]{:S(2)}) collective-permute-start(bf16[1824,128]{1,0:T(8,128)(2,1)} %get-tuple-element.635.refs_1_), channel_id=1, source_target_pairs={{0,8},{8,0},{16,24},{24,16},{1,9},{9,1},{17,25},{25,17},{2,10},{10... | collective-permute-start | bytes 1400840 | tf_op jit(solution)/shard_map/ppermute | solution.py:845
  474.4 12.6 %collective-permute-start.64 = (bf16[1824,128]{1,0:T(8,128)(2,1)}, bf16[1824,128]{1,0:T(8,128)(2,1)}, u32[]{:S(2)}, u32[]{:S(2)}) collective-permute-start(bf16[1824,128]{1,0:T(8,128)(2,1)} %get-tuple-element.637.refs_3_), channel_id=1, source_target_pairs={{0,16},{8,24},{16,0},{24,8},{1,17},{9,25},{17,1},{25,9},{2,18},{10... | collective-permute-start | bytes 1400840 | tf_op jit(solution)/shard_map/ppermute | solution.py:845
  (75 other events, 424.1 us)

commit v3 on v2

--- a/solution.py
+++ b/solution.py
@@ -480,24 +480,24 @@
     )(ca, cb, down)
 
 
-def feed_kernel(*refs, start, first, final, sides):
-    n_grads = 1 if sides is None else 6
+def feed_kernel(*refs, start, first, sides):
     place_ref, na_ref, nb_ref, ca_ref, cb_ref, gate_ref, gate_o_ref, up_ref, up_o_ref, down_ref, change_ref = refs[:11]
     refs = refs[11:]
     if not first:
         sums = refs[:4]
         refs = refs[4:]
-    grad_refs = refs[:n_grads]
-    outs = refs[n_grads : n_grads + 4]
-    refs = refs[n_grads + 4 :]
-    (na, nb, ca, cb, wg, wu, wd, change_s, inner_s, gate_s, up_s, *part_s) = refs[:14]
-    refs = refs[14:]
+    grad_refs = refs[:6]
+    outs = refs[6:10]
+    refs = refs[10:]
+    (n_s, c_s, wg, wu, wd, change_s, inner_s, gate_s, up_s, *part_s) = refs[:12]
+    refs = refs[12:]
     if not first:
-        held = refs[:4]
-        refs = refs[4:]
-    totals = refs[:4]
-    in_sem, sum_sem, out_sem = refs[4:]
-    count, features = na.shape
+        held = refs[:2]
+        refs = refs[2:]
+    totals = refs[:2]
+    in_sem, sum_sem, out_sem = refs[2:]
+    tokens, features = n_s.shape
+    count = tokens // 2
     width = wg.shape[1]
     rows_held = gate_ref.shape[0]
     hidden = down_ref.shape[0]
@@ -505,62 +505,62 @@
     lanes = pl.ds(pl.multiple_of(me * hidden + start, LANES), width)
     own_rows = pl.ds(pl.multiple_of(me * rows_held, rows_held), rows_held)
     other_rows = pl.ds(pl.multiple_of((1 - me) * rows_held, rows_held), rows_held)
+    low, high = pl.ds(0, count), pl.ds(count, count)
 
     moves = [
-        (na_ref, na),
+        (na_ref, n_s.at[low, :]),
+        (nb_ref, n_s.at[high, :]),
         (gate_ref.at[:, lanes], wg.at[own_rows, :]),
         (gate_o_ref.at[:, lanes], wg.at[other_rows, :]),
         (up_ref.at[:, lanes], wu.at[own_rows, :]),
         (up_o_ref.at[:, lanes], wu.at[other_rows, :]),
         (change_ref.at[:, pl.ds(start, width)], change_s),
         (down_ref.at[pl.ds(start, width), :], wd),
-        (nb_ref, nb),
-        (ca_ref, ca),
-        (cb_ref, cb),
+        (ca_ref, c_s.at[low, :]),
+        (cb_ref, c_s.at[high, :]),
     ]
     copies = [pltpu.make_async_copy(a, b, in_sem.at[i]) for i, (a, b) in enumerate(moves)]
     for copy in copies:
         copy.start()
     sum_copies = []
     if not first:
-        sum_copies = [pltpu.make_async_copy(sums[i], held[i], sum_sem.at[i]) for i in range(4)]
+        places = ((held[0], low), (held[1], low), (held[0], high), (held[1], high))
+        sum_copies = [
+            pltpu.make_async_copy(sums[i], target.at[rows, :], sum_sem.at[i])
+            for i, (target, rows) in enumerate(places)
+        ]
         for copy in sum_copies:
             copy.start()
-    for copy in copies[:7]:
+    for copy in copies[:8] + sum_copies:
         copy.wait()
     step = 256
-    for half, normed_ref in enumerate((na, nb)):
-        if half == 1:
-            for copy in copies[7:]:
-                copy.wait()
-        for copy in sum_copies[2 * half : 2 * half + 2]:
-            copy.wait()
-
-        def body(i, carry, half=half, normed_ref=normed_ref):
-            rows = pl.ds(pl.multiple_of(i * step, step), step)
-            both = pl.ds(pl.multiple_of(half * count + i * step, step), step)
-            normed = normed_ref[rows, :]
-            gate = nn(normed, wg[...])
-            up = nn(normed, wu[...])
-            change = change_s[both, :].astype(f32)
-            sigmoid = 1.0 / (1.0 + jnp.exp(-gate))
-            activated = gate * sigmoid
-            inner = (activated * up).astype(bf16)
-            gate_g = (change * up * sigmoid * (1.0 + gate * (1.0 - sigmoid))).astype(bf16)
-            up_g = (change * activated).astype(bf16)
-            inner_s[both, :] = inner
-            gate_s[both, :] = gate_g
-            up_s[both, :] = up_g
-            result = nn(inner, wd[...])
-            back = nt(gate_g, wg[...]) + nt(up_g, wu[...])
-            if not first:
-                result = result + held[2 * half][rows, :].astype(f32)
-                back = back + held[2 * half + 1][rows, :].astype(f32)
-            totals[2 * half][rows, :] = result.astype(totals[2 * half].dtype)
-            totals[2 * half + 1][rows, :] = back.astype(totals[2 * half + 1].dtype)
-            return carry
-
-        lax.fori_loop(0, count // step, body, 0)
+
+    def body(i, carry):
+        rows = pl.ds(pl.multiple_of(i * step, step), step)
+        normed = n_s[rows, :]
+        gate = nn(normed, wg[...])
+        up = nn(normed, wu[...])
+        change = change_s[rows, :].astype(f32)
+        sigmoid = 1.0 / (1.0 + jnp.exp(-gate))
+        activated = gate * sigmoid
+        inner = (activated * up).astype(bf16)
+        gate_g = (change * up * sigmoid * (1.0 + gate * (1.0 - sigmoid))).astype(bf16)
+        up_g = (change * activated).astype(bf16)
+        inner_s[rows, :] = inner
+        gate_s[rows, :] = gate_g
+        up_s[rows, :] = up_g
+        result = nn(inner, wd[...])
+        back = nt(gate_g, wg[...]) + nt(up_g, wu[...])
+        if not first:
+            result = result + held[0][rows, :].astype(f32)
+            back = back + held[1][rows, :].astype(f32)
+        totals[0][rows, :] = result.astype(bf16)
+        totals[1][rows, :] = back.astype(bf16)
+        return carry
+
+    lax.fori_loop(0, tokens // step, body, 0)
+    for copy in copies[8:]:
+        copy.wait()
     leaving = []
 
     def leave(source, target):
@@ -568,84 +568,88 @@
         copy.start()
         leaving.append(copy)
 
-    for i in range(4):
-        leave(totals[i], outs[i])
+    for i, (total, rows) in enumerate(
+        ((totals[0], low), (totals[1], low), (totals[0], high), (totals[1], high))
+    ):
+        leave(total.at[rows, :], outs[i])
 
     def part_leaves(i):
-        rows = part_s[i].shape[0]
-        if sides is None:
-            leave(part_s[i], grad_refs[0].at[pl.ds(i * rows, rows), :])
-            return
         keep, send = grad_refs[2 * i : 2 * i + 2]
-        rows = rows // 2
+        rows = part_s[i].shape[0] // 2
         side = place_ref[sides[i]]
         leave(part_s[i].at[pl.ds(pl.multiple_of((1 - side) * rows, 16), rows), :], send)
         leave(part_s[i].at[pl.ds(pl.multiple_of(side * rows, 16), rows), :], keep)
 
     mine_s, theirs_s, down_s = part_s
-    for kind, source in enumerate((gate_s, up_s)):
-        for place in range(0, width, HALF):
-            size = min(HALF, width - place)
-            columns = slice(place, place + size)
-            grads = tn(na[...], source[:count, columns]) + tn(nb[...], source[count:, columns])
-            grads = grads.astype(bf16)
+
+    def tiles_loop(body):
+        def step(i, carry):
+            body(i * HALF, HALF)
+            return carry
+
+        lax.fori_loop(0, width // HALF, step, 0)
+        if width % HALF:
+            body(width // HALF * HALF, width % HALF)
+
+    def columns_of(at, size):
+        return pl.ds(at if isinstance(at, int) else pl.multiple_of(at, HALF), size)
+
+    def wide_grads(at, size):
+        for kind, source in enumerate((gate_s, up_s)):
+            grads = tn(n_s[...], source[:, columns_of(at, size)]).astype(bf16)
             for j in range(size // LANES):
-                row = ((kind * width + place) // LANES + j) * rows_held
+                row = (kind * width // LANES + at // LANES + j) * rows_held
+                rows = pl.ds(row if isinstance(row, int) else pl.multiple_of(row, 16), rows_held)
                 tile = grads[:, j * LANES : (j + 1) * LANES]
 
                 @pl.when(me == 0)
                 def _():
-                    mine_s[row : row + rows_held, :] = tile[:rows_held]
-                    theirs_s[row : row + rows_held, :] = tile[rows_held:]
+                    mine_s[rows, :] = tile[:rows_held]
+                    theirs_s[rows, :] = tile[rows_held:]
 
                 @pl.when(me == 1)
                 def _():
-                    mine_s[row : row + rows_held, :] = tile[rows_held:]
-                    theirs_s[row : row + rows_held, :] = tile[:rows_held]
-
+                    mine_s[rows, :] = tile[rows_held:]
+                    theirs_s[rows, :] = tile[:rows_held]
+
+    def down_grads(at, size):
+        grads = tn(inner_s[:, columns_of(at, size)], c_s[...]).astype(bf16)
+        for j in range(features // LANES):
+            row = j * width + at
+            rows = pl.ds(row if isinstance(row, int) else pl.multiple_of(row, 16), size)
+            down_s[rows, :] = grads[:, j * LANES : (j + 1) * LANES]
+
+    tiles_loop(wide_grads)
     part_leaves(0)
     part_leaves(1)
-    for place in range(0, width, HALF):
-        size = min(HALF, width - place)
-        columns = slice(place, place + size)
-        grads = tn(inner_s[:count, columns], ca[...]) + tn(inner_s[count:, columns], cb[...])
-        grads = grads.astype(bf16)
-        for j in range(features // LANES):
-            row = j * width + place
-            down_s[row : row + size, :] = grads[:, j * LANES : (j + 1) * LANES]
+    tiles_loop(down_grads)
     part_leaves(2)
     for copy in leaving:
         copy.wait()
 
 
-def feed(place, na, nb, ca, cb, gate, gate_o, up, up_o, down, change, sums, *, start, width, final, sides):
+def feed(place, na, nb, ca, cb, gate, gate_o, up, up_o, down, change, sums, *, start, width, sides):
     count, features = na.shape
     first = sums is None
     sums = () if first else tuple(sums)
     anywhere = pl.BlockSpec(memory_space=pl.ANY)
     rows = features * width // LANES
-    tokens = (count, features)
-    types = [f32 if final and i < 2 else bf16 for i in range(4)]
-    totals = [jax.ShapeDtypeStruct(tokens, t) for t in types]
-    if sides is None:
-        outs = [jax.ShapeDtypeStruct((3 * rows, LANES), bf16)]
-    else:
-        outs = [jax.ShapeDtypeStruct((rows // 2, LANES), bf16)] * 6
-    scratch = [pltpu.VMEM(tokens, bf16)] * 4
+    tokens = (2 * count, features)
+    outs = [jax.ShapeDtypeStruct((rows // 2, LANES), bf16)] * 6
+    outs += [jax.ShapeDtypeStruct((count, features), bf16)] * 4
+    scratch = [pltpu.VMEM(tokens, bf16)] * 2
     scratch += [pltpu.VMEM((features, width), bf16)] * 2 + [pltpu.VMEM((width, features), bf16)]
     scratch += [pltpu.VMEM((2 * count, width), bf16)] * 4
     scratch += [pltpu.VMEM((rows, LANES), bf16)] * 3
-    if not first:
-        scratch += [pltpu.VMEM(tokens, bf16)] * 4
-    scratch += [pltpu.VMEM(tokens, t) for t in types]
+    scratch += [pltpu.VMEM(tokens, bf16)] * (2 if first else 4)
     scratch += [pltpu.SemaphoreType.DMA((n,)) for n in (10, 4, 10)]
     return call(
-        functools.partial(feed_kernel, start=start, first=first, final=final, sides=sides),
-        (*outs, *totals),
+        functools.partial(feed_kernel, start=start, first=first, sides=sides),
+        tuple(outs),
         18 * 2 * count * features * width,
         30 * 1024 * 1024,
         in_specs=[pl.BlockSpec(memory_space=pltpu.SMEM)] + [anywhere] * (10 + len(sums)),
-        out_specs=(anywhere,) * (len(outs) + 4),
+        out_specs=(anywhere,) * 10,
         scratch_shapes=scratch,
     )(place, na, nb, ca, cb, gate, gate_o, up, up_o, down, change, *sums)
 
@@ -660,7 +664,7 @@
 
     def body(i, carry):
         rows = pl.ds(pl.multiple_of(i * step, step), step)
-        back = part_ref[rows, :] + got_ref[rows, :].astype(f32)
+        back = part_ref[rows, :].astype(f32) + got_ref[rows, :].astype(f32)
         hidden = h1_ref[rows, :]
         scale = lax.rsqrt(jnp.mean(hidden * hidden, -1, keepdims=True) + eps_norm)
         normal = hidden * scale
@@ -1289,7 +1293,7 @@
 
     def run_feed(i, token_sums):
         step = functools.partial(
-            feed, start=starts[i], width=widths[i], final=i == len(widths) - 1, sides=first_sides
+            feed, start=starts[i], width=widths[i], sides=first_sides
         )
         *grads, own_result, own_back, other_result, other_back = order(
             step, place, n2, n2_other, dy, dy_other, gate_weight, gate_other, up_weight, up_other,
@@ -1350,6 +1354,9 @@
     rest.leave(mine, got)
     one.join(1)
     two.turn_each(1)
+    block_output = order(
+        lambda a, b, c: (a + b.astype(f32) + c.astype(f32)).astype(bf16), h1, own_result, swap(other_result)
+    )[None]
     rest.halve()
     two.turn_each(2)
     rest.sum()
@@ -1359,9 +1366,6 @@
     rest.turn()
     two.join(1)
     rest.join()
-    block_output = order(
-        lambda a, b, c: (a + b + c.astype(f32)).astype(bf16), h1, own_result, swap(other_result)
-    )[None]
     gates, ups, gw_down = run_untile(1, two.parts, outs)
     gw_query, gw_key, gw_value, gw_out, vector = order(
         functools.partial(

time: 505 us -> 505 us (level)
  waiting for transfers between devices: 139 us -> 130 us
  starting transfers between devices: 64.6 us -> 71.8 us
    ppermute x50, waiting for transfers between devices: 126 us -> 117 us  [flip(): return lax.ppermute(values, axis, [(i, i ^ 1 << bit) for i in range(size)])]
    ppermute x50, starting transfers between devices: 49.5 us -> 56.6 us  [flip(): return lax.ppermute(values, axis, [(i, i ^ 1 << bit) for i in range(size)])]
    unnamed x142 -> x148, local copies, waits for them, and re-layouts: 22.3 us -> 23 us
  transfers between devices with their start and end apart: 68 -> 68, of which waited for: 22 -> 22; matrix products, arithmetic and copies ran while one was open for 2% -> 3% of each run, Pallas kernels for 40% -> 40%
where the time goes in v3:
time: 505 us; the launch traced here: 499 us
  Pallas kernels  258 us (51%)
  waiting for transfers between devices  130 us (26%)
  starting transfers between devices  71.8 us (14%)
  local copies, waits for them, and re-layouts  30.8 us (6%)
  other arithmetic  7.61 us (2%)
    ppermute x50, waiting for transfers between devices, flip(): return lax.ppermute(values, axis, [(i, i ^ 1 << bit) for i in range(size)])  117 us
    pallas_call x2, Pallas kernels, feed(): call(functools.partial(feed_kernel, start=start, first=first, sides=sides...  76.2 us
    ppermute x50, starting transfers between devices, flip(): return lax.ppermute(values, axis, [(i, i ^ 1 << bit) for i in range(size)])  56.6 us
    pallas_call x2, Pallas kernels, attend_back(): call(functools.partial(attend_back_kernel, first_pair=first_pair, first=f...  39.9 us
    unnamed x148, local copies, waits for them, and re-layouts  23 us
    pallas_call x1, Pallas kernels, attend(): call(attend_kernel, (jax.ShapeDtypeStruct((count, HQ * HD), bf16), jax.Sh...  22.3 us
    pallas_call x5, Pallas kernels, fold(): call(functools.partial(fold_kernel, sides=sides), tuple((jax.ShapeDtypeSt...  19.7 us
    pallas_call x2, Pallas kernels, untile(): call(functools.partial(untile_kernel, start=start, width=width, first=fir...  17.2 us
  transfers between devices with their start and end apart: 68, of which 22 were waited for; matrix products, arithmetic and copies ran while one was open for 3% of the time, Pallas kernels for 40%

profile of v3, /device:TPU:0, one launch (start us, length us, event | category | flops | bytes accessed | tf_op | source)
XLA Modules:
  0.0 499.2 jit_solution(17779452143627226588)
XLA Ops:
  1.2 3.5 concatenate.6
  5.8 1.8 multiply_sine_fusion
  8.7 5.0 collective-permute-done.2.ok_ref
  14.8 2.6 collective-permute-done.3.ov_ref
  18.7 6.0 %shard_map.254 = (bf16[512,896]{1,0:T(8,128)(2,1)}, bf16[512,896]{1,0:T(8,128)(2,1)}, bf16[512,256]{1,0:T(8,128)(2,1)}, bf16[896,1152]{1,0:T(8,128)(2,1)}) custom-call(s32[5]{0:T(128)} %stack.23.place_ref.refs_0_, bf16[512,896]{1,0:T(8,128)(2,1)} %bitcast.10, f32[1,2944]{1,0:T(1,128)} %broadcast_in_dim.10.params_ref, bf16[448,896]{1,0:T(8,128)(2,1)} %wq_ref.1, ...), custom_call_target="tpu_custom_call" | custom-call | flops 1056964608 | bytes 6291456 | tf_op jit(solution)/shard_map/pallas_call | solution.py:109
  24.7 4.6 collective-permute-start.4
  29.4 4.8 collective-permute-start.5
  34.2 11.8 %shard_map.255.refs_10_ = bf16[1024,2432]{1,0:T(8,128)(2,1)} custom-call(bf16[512,896]{1,0:T(8,128)(2,1)} %bitcast.14, bf16[512,896]{1,0:T(8,128)(2,1)} %copy-done.66, bf16[2432,896]{1,0:T(8,128)(2,1)} %refs_9_.1), custom_call_target="tpu_custom_call" | custom-call | flops 4462739456 | bytes 12582912 | tf_op jit(solution)/shard_map/pallas_call | solution.py:472
  46.8 22.3 %shard_map.256 = (bf16[512,896]{1,0:T(8,128)(2,1)}, f32[7,8,512]{2,1,0:T(8,128)}) custom-call(s32[5]{0:T(128)} %stack.23.place_ref.refs_0_, bf16[512,896]{1,0:T(8,128)(2,1)} %get-tuple-element.461.q_ref.refs_1_, bf16[512,256]{1,0:T(8,128)(2,1)} %get-tuple-element.463.kv0_ref.refs_3_, bf16[512,256]{1,0:T(8,128)(2,1)} %copy-done.70, ...), custom_call_target="tpu_custom_call" | custom-call | flops 9395240960 | bytes 4194304 | tf_op jit(solution)/shard_map/pallas_call | solution.py:248
  69.9 5.7 %shard_map.257 = (f32[512,896]{1,0:T(8,128)}, bf16[512,896]{1,0:T(8,128)(2,1)}, bf16[896,896]{1,0:T(8,128)(2,1)}) custom-call(s32[5]{0:T(128)} %stack.23.place_ref.refs_0_, bf16[512,896]{1,0:T(8,128)(2,1)} %bitcast.11, bf16[512,896]{1,0:T(8,128)(2,1)} %get-tuple-element.407.o_ref, bf16[448,896]{1,0:T(8,128)(2,1)} %own_ref.1, bf16[448,896]{1,0:T(8,128)(2,1)} %copy-done.21, ...), custom_call_target="tpu_custom_call" | custom-call | flops 822083584 | bytes 6291456 | tf_op jit(solution)/shard_map/pallas_call | solution.py:447
  75.6 2.7 collective-permute-done.8.refs_2_
  79.2 37.7 %shard_map.258 = (bf16[4480,128]{1,0:T(8,128)(2,1)}, bf16[4480,128]{1,0:T(8,128)(2,1)}, bf16[4480,128]{1,0:T(8,128)(2,1)}, bf16[4480,128]{1,0:T(8,128)(2,1)}, bf...) custom-call(s32[5]{0:T(128)} %stack.23.place_ref.refs_0_, ...), custom_call_target="tpu_custom_call" | custom-call | flops 21139292160 | bytes 31457280 | tf_op jit(solution)/shard_map/pallas_call | solution.py:646
  116.9 1.5 collective-permute-start.12
  119.9 2.5 collective-permute-start.14
  122.4 38.5 %shard_map.259 = (bf16[4032,128]{1,0:T(8,128)(2,1)}, bf16[4032,128]{1,0:T(8,128)(2,1)}, bf16[4032,128]{1,0:T(8,128)(2,1)}, bf16[4032,128]{1,0:T(8,128)(2,1)}, bf...) custom-call(s32[5]{0:T(128)} %stack.23.place_ref.refs_0_, ...), custom_call_target="tpu_custom_call" | custom-call | flops 19025362944 | bytes 31457280 | tf_op jit(solution)/shard_map/pallas_call | solution.py:646
  162.8 5.4 %shard_map.260 = (bf16[2240,128]{1,0:T(8,128)(2,1)}, bf16[2240,128]{1,0:T(8,128)(2,1)}, bf16[2240,128]{1,0:T(8,128)(2,1)}, bf16[2240,128]{1,0:T(8,128)(2,1)}, bf...) custom-call(s32[5]{0:T(128)} %stack.23.place_ref.refs_0_, bf16[4480,128]{1,0:T(8,128)(2,1)} %get-tuple-element.385.refs_0_, ...), custom_call_target="tpu_custom_call" | custom-call | flops 3440640 | bytes 10321920 | tf_op jit(solution)/shard_map/pallas_call | solution.py:910
  170.2 8.9 %shard_map.261 = (f32[512,896]{1,0:T(8,128)}, bf16[512,896]{1,0:T(8,128)(2,1)}, f32[1,896]{1,0:T(1,128)}, bf16[3136,128]{1,0:T(8,128)(2,1)}, bf16[3136,128]{1,0:T(8,128)(2,1)}) custom-call(s32[5]{0:T(128)} %stack.23.place_ref.refs_0_, bf16[512,896]{1,0:T(8,128)(2,1)} %get-tuple-element.401.part_ref, bf16[512,896]{1,0:T(8,128)(2,1)} %copy-done.19, ...), custom_call_target="tpu_custom_call" | custom-call | flops 1644167168 | bytes 12582912 | tf_op jit(solution)/shard_map/pallas_call | solution.py:707
  179.1 4.7 collective-permute-done.15.refs_1_
  185.0 3.4 shard_map.262
  188.5 1.6 collective-permute-start.19
  192.1 5.0 %collective-permute-done.19.refs_1_ = bf16[1120,128]{1,0:T(8,128)(2,1)S(1)} collective-permute-done((bf16[1120,128]{1,0:T(8,128)(2,1)}, bf16[1120,128]{1,0:T(8,128)(2,1)S(1)}, u32[]{:S(2)}, u32[]{:S(2)}) %collective-permute-start.19) | collective-permute-done | bytes 286752 | tf_op jit(solution)/shard_map/ppermute | solution.py:849
  198.8 2.5 shard_map.263.total
  201.3 3.3 collective-permute-start.28
  208.3 21.5 %shard_map.264 = (bf16[512,512]{1,0:T(8,128)(2,1)}, f32[2,1536,128]{2,1,0:T(8,128)}, f32[2,1536,128]{2,1,0:T(8,128)}) custom-call(s32[5]{0:T(128)} %stack.23.place_ref.refs_0_, bf16[512,896]{1,0:T(8,128)(2,1)} %get-tuple-element.461.q_ref.refs_1_, bf16[512,896]{1,0:T(8,128)(2,1)} %get-tuple-element.462.refs_2_, ...), custom_call_target="tpu_custom_call" | custom-call | flops 13421772800 | bytes 6291456 | tf_op jit(solution)/shard_map/pallas_call | solution.py:400
  229.9 16.6 %collective-permute-done.24.refs_5_ = bf16[4032,128]{1,0:T(8,128)(2,1)S(1)} collective-permute-done((bf16[4032,128]{1,0:T(8,128)(2,1)S(1)}, bf16[4032,128]{1,0:T(8,128)(2,1)S(1)}, u32[]{:S(2)}, u32[]{:S(2)}) %collective-permute-start.24) | collective-permute-done | bytes 1032224 | tf_op jit(solution)/shard_map/ppermute | solution.py:849
  247.5 5.1 %shard_map.265 = (bf16[2016,128]{1,0:T(8,128)(2,1)}, bf16[2016,128]{1,0:T(8,128)(2,1)}, bf16[2016,128]{1,0:T(8,128)(2,1)}, bf16[2016,128]{1,0:T(8,128)(2,1)}, bf...) custom-call(s32[5]{0:T(128)} %stack.23.place_ref.refs_0_, bf16[4032,128]{1,0:T(8,128)(2,1)} %get-tuple-element.446.refs_0_, ...), custom_call_target="tpu_custom_call" | custom-call | flops 3096576 | bytes 9289728 | tf_op jit(solution)/shard_map/pallas_call | solution.py:910
  254.6 18.4 %shard_map.266 = (bf16[512,384]{1,0:T(8,128)(2,1)}, f32[512,256]{1,0:T(8,128)}, bf16[512,256]{1,0:T(8,128)(2,1)}, bf16[512,256]{1,0:T(8,128)(2,1)}) custom-call(s32[5]{0:T(128)} %stack.23.place_ref.refs_0_, bf16[512,896]{1,0:T(8,128)(2,1)} %get-tuple-element.461.q_ref.refs_1_, bf16[512,896]{1,0:T(8,128)(2,1)} %get-tuple-element.462.refs_2_, ...), custom_call_target="tpu_custom_call" | custom-call | flops 10066329600 | bytes 6291456 | tf_op jit(solution)/shard_map/pallas_call | solution.py:400
  275.6 2.4 shard_map.267
  279.2 3.2 shard_map.268
  282.4 2.6 collective-permute-start.29
  287.2 6.7 %shard_map.269 = (f32[512,896]{1,0:T(8,128)}, f32[1,896]{1,0:T(1,128)}, bf16[3136,128]{1,0:T(8,128)(2,1)}, bf16[3136,128]{1,0:T(8,128)(2,1)}) custom-call(s32[5]{0:T(128)} %stack.23.place_ref.refs_0_, bf16[512,512]{1,0:T(8,128)(2,1)} %get-tuple-element.491.dqa_ref, bf16[512,384]{1,0:T(8,128)(2,1)} %get-tuple-element.492.dqb_ref, ...), custom_call_target="tpu_custom_call" | custom-call | flops 1644167168 | bytes 10485760 | tf_op jit(solution)/shard_map/pallas_call | solution.py:749
  294.8 2.4 shard_map.270
  298.1 8.8 %shard_map.271 = (bf16[512,896]{1,0:T(8,128)(2,1)}, bf16[7296,128]{1,0:T(8,128)(2,1)}, bf16[7296,128]{1,0:T(8,128)(2,1)}) custom-call(s32[5]{0:T(128)} %stack.23.place_ref.refs_0_, f32[512,256]{1,0:T(8,128)} %get-tuple-element.516.own_ref, bf16[512,256]{1,0:T(8,128)(2,1)} %copy-done.45, bf16[512,256]{1,0:T(8,128)(2,1)} %copy-done.46, ...), custom_call_target="tpu_custom_call" | custom-call | flops 469762048 | bytes 14680064 | tf_op jit(solution)/shard_map/pallas_call | solution.py:824
  308.2 2.6 collective-permute-done.34.refs_2_
  311.2 3.6 collective-permute-start.43
  314.8 4.6 collective-permute-done.33.refs_1_
  320.6 2.7 shard_map.272
  324.0 2.8 collective-permute-done.43
  326.8 1.6 collective-permute-start.41
  329.6 3.7 shard_map.273
  333.3 4.6 collective-permute-done.39.refs_1_
  338.3 6.8 %collective-permute-done.40.refs_3_ = bf16[2240,128]{1,0:T(8,128)(2,1)S(1)} collective-permute-done((bf16[2240,128]{1,0:T(8,128)(2,1)}, bf16[2240,128]{1,0:T(8,128)(2,1)S(1)}, u32[]{:S(2)}, u32[]{:S(2)}) %collective-permute-start.40) | collective-permute-done | bytes 573472 | tf_op jit(solution)/shard_map/ppermute | solution.py:849
  346.7 3.9 shard_map.274
  353.9 1.8 add_convert_fusion.3
  357.2 2.4 collective-permute-start.56
  359.6 2.7 add_convert_fusion
  362.3 3.4 collective-permute-done.45.refs_3_
  366.5 2.5 shard_map.275
  369.7 24.1 %collective-permute-done.46.refs_1_ = bf16[912,128]{1,0:T(8,128)(2,1)S(1)} collective-permute-done((bf16[912,128]{1,0:T(8,128)(2,1)}, bf16[912,128]{1,0:T(8,128)(2,1)S(1)}, u32[]{:S(2)}, u32[]{:S(2)}) %collective-permute-start.46) | collective-permute-done | bytes 233504 | tf_op jit(solution)/shard_map/ppermute | solution.py:849
  395.7 4.6 collective-permute-done.47.refs_3_
  401.0 2.2 shard_map.276
  403.2 2.1 collective-permute-start.50
  408.4 8.9 %shard_map.277 = (f32[448,4864]{1,0:T(8,128)}, f32[448,4864]{1,0:T(8,128)}, f32[2432,896]{1,0:T(8,128)}) custom-call(s32[5]{0:T(128)} %stack.23.place_ref.refs_0_, bf16[4480,128]{1,0:T(8,128)(2,1)} %get-tuple-element.584.refs_1_, bf16[4480,128]{1,0:T(8,128)(2,1)} %copy-done.4, bf16[4480,128]{1,0:T(8,128)(2,1)} %get-tuple-element.586.refs_3_, ...), custom_call_target="tpu_custom_call" | custom-call | flops 3440640 | bytes 20643840 | tf_op jit(solution)/shard_map/pallas_call | solution.py:1047
  417.4 1.8 collective-permute-done.50.refs_1_
  420.1 2.7 shard_map.278
  425.3 4.1 collective-permute-start.57
  429.4 17.0 %collective-permute-done.57.got = bf16[1824,128]{1,0:T(8,128)(2,1)S(1)} collective-permute-done((bf16[1824,128]{1,0:T(8,128)(2,1)S(1)}, bf16[1824,128]{1,0:T(8,128)(2,1)S(1)}, u32[]{:S(2)}, u32[]{:S(2)}) %collective-permute-start.57) | collective-permute-done | bytes 466976 | tf_op jit(solution)/shard_map/ppermute | solution.py:849
  447.3 2.0 shard_map.279
  450.5 3.6 shard_map.280
  454.1 2.5 collective-permute-start.67
  458.5 18.9 %collective-permute-done.58.refs_1_ = bf16[912,128]{1,0:T(8,128)(2,1)S(1)} collective-permute-done((bf16[912,128]{1,0:T(8,128)(2,1)S(1)}, bf16[912,128]{1,0:T(8,128)(2,1)S(1)}, u32[]{:S(2)}, u32[]{:S(2)}) %collective-permute-start.58) | collective-permute-done | bytes 233504 | tf_op jit(solution)/shard_map/ppermute | solution.py:849
  478.8 2.3 shard_map.281
  483.8 8.3 %shard_map.282 = (f32[448,4864]{1,0:T(8,128)}, f32[448,4864]{1,0:T(8,128)}, f32[2432,896]{1,0:T(8,128)}) custom-call(s32[5]{0:T(128)} %stack.23.place_ref.refs_0_, bf16[4032,128]{1,0:T(8,128)(2,1)} %get-tuple-element.624.refs_1_, bf16[4032,128]{1,0:T(8,128)(2,1)} %copy-done.10, ...), custom_call_target="tpu_custom_call", output_to_operand_aliasing={{0}: (7, {}), {1}: (8, {}), {2}: (9, {})} | custom-call | flops 3096576 | bytes 18579456 | tf_op jit(solution)/shard_map/pallas_call | solution.py:1047
  492.1 4.0 shard_map.283
  (269 shorter events, 65.1 us)
Async XLA Ops:
  0.6 77.7 %collective-permute-start.10 = (bf16[448,4864]{1,0:T(8,128)(2,1)}, bf16[448,4864]{1,0:T(8,128)(2,1)}, u32[]{:S(2)}, u32[]{:S(2)}) collective-permute-start(bf16[448,4864]{1,0:T(8,128)(2,1)} %refs_7_.1), channel_id=1, source_target_pairs={{0,1},{1,0},{2,3},{3,2},{4,5},{5,4},{6,7},{7,6},{8,9},{9,8},{10,11... | collective-permute-start | bytes 13074440 | tf_op jit(solution)/shard_map/ppermute | solution.py:843
  1.2 77.1 %collective-permute-start.9 = (bf16[448,4864]{1,0:T(8,128)(2,1)}, bf16[448,4864]{1,0:T(8,128)(2,1)}, u32[]{:S(2)}, u32[]{:S(2)}) collective-permute-start(bf16[448,4864]{1,0:T(8,128)(2,1)} %refs_5_.1), channel_id=1, source_target_pairs={{0,1},{1,0},{2,3},{3,2},{4,5},{5,4},{6,7},{7,6},{8,9},{9,8},{10,11... | collective-permute-start | bytes 13074440 | tf_op jit(solution)/shard_map/ppermute | solution.py:843
  5.2 12.6 %collective-permute-start.1 = (bf16[448,896]{1,0:T(8,128)(2,1)}, bf16[448,896]{1,0:T(8,128)(2,1)S(1)}, u32[]{:S(2)}, u32[]{:S(2)}) collective-permute-start(bf16[448,896]{1,0:T(8,128)(2,1)} %wq_ref.1), channel_id=1, source_target_pairs={{0,1},{1,0},{2,3},{3,2},{4,5},{5,4},{6,7},{7,6},{8,9},{9,8},{10,11... | collective-permute-start | bytes 2408456 | tf_op jit(solution)/shard_map/ppermute | solution.py:843
  5.2 24.1 %collective-permute-start.6 = (bf16[512,896]{1,0:T(8,128)(2,1)}, bf16[512,896]{1,0:T(8,128)(2,1)S(1)}, u32[]{:S(2)}, u32[]{:S(2)}) collective-permute-start(bf16[512,896]{1,0:T(8,128)(2,1)} %bitcast.13), channel_id=1, source_target_pairs={{0,1},{1,0},{2,3},{3,2},{4,5},{5,4},{6,7},{7,6},{8,9},{9,8},{10,11... | collective-permute-start | bytes 2752520 | tf_op jit(solution)/shard_map/ppermute | solution.py:843
  8.3 5.4 %collective-permute-start.2 = (bf16[448,128]{1,0:T(8,128)(2,1)}, bf16[448,128]{1,0:T(8,128)(2,1)S(1)}, u32[]{:S(2)}, u32[]{:S(2)}) collective-permute-start(bf16[448,128]{1,0:T(8,128)(2,1)} %wk_ref.1), channel_id=1, source_target_pairs={{0,1},{1,0},{2,3},{3,2},{4,5},{5,4},{6,7},{7,6},{8,9},{9,8},{10,11... | collective-permute-start | bytes 344072 | tf_op jit(solution)/shard_map/ppermute | solution.py:843
  17.4 51.6 %collective-permute-start.7 = (bf16[448,896]{1,0:T(8,128)(2,1)}, bf16[448,896]{1,0:T(8,128)(2,1)S(1)}, u32[]{:S(2)}, u32[]{:S(2)}) collective-permute-start(bf16[448,896]{1,0:T(8,128)(2,1)} %own_ref.1), channel_id=1, source_target_pairs={{0,1},{1,0},{2,3},{3,2},{4,5},{5,4},{6,7},{7,6},{8,9},{9,8},{10,11... | collective-permute-start | bytes 2408456 | tf_op jit(solution)/shard_map/ppermute | solution.py:843
  24.7 21.3 %collective-permute-start.4 = (bf16[512,256]{1,0:T(8,128)(2,1)}, bf16[512,256]{1,0:T(8,128)(2,1)S(1)}, u32[]{:S(2)}, u32[]{:S(2)}) collective-permute-start(bf16[512,256]{1,0:T(8,128)(2,1)} %get-tuple-element.463.kv0_ref.refs_3_), channel_id=1, source_target_pairs={{0,2},{2,4},{4,6},{1,3},{3,5},{5,7},{8,10},{10,12},{12,14},{9,11},... | collective-permute-start | bytes 786440 | tf_op jit(solution)/shard_map/ppermute | solution.py:1280
  29.4 16.6 %collective-permute-start.5 = (bf16[512,256]{1,0:T(8,128)(2,1)}, bf16[512,256]{1,0:T(8,128)(2,1)S(1)}, u32[]{:S(2)}, u32[]{:S(2)}) collective-permute-start(bf16[512,256]{1,0:T(8,128)(2,1)} %get-tuple-element.463.kv0_ref.refs_3_), channel_id=1, source_target_pairs={{0,4},{2,6},{1,5},{3,7},{8,12},{10,14},{9,13},{11,15},{16,20},{18,... | collective-permute-start | bytes 786440 | tf_op jit(solution)/shard_map/ppermute | solution.py:1280
  116.9 44.1 %collective-permute-start.12 = (bf16[4480,128]{1,0:T(8,128)(2,1)}, bf16[4480,128]{1,0:T(8,128)(2,1)S(1)}, u32[]{:S(2)}, u32[]{:S(2)}) collective-permute-start(bf16[4480,128]{1,0:T(8,128)(2,1)} %get-tuple-element.380), channel_id=1, source_target_pairs={{0,8},{8,0},{16,24},{24,16},{1,9},{9,1},{17,25},{25,17},{2,10},{10... | collective-permute-start | bytes 3440648 | tf_op jit(solution)/shard_map/ppermute | solution.py:849
  118.4 42.6 %collective-permute-start.13 = (bf16[4480,128]{1,0:T(8,128)(2,1)}, bf16[4480,128]{1,0:T(8,128)(2,1)S(1)}, u32[]{:S(2)}, u32[]{:S(2)}) collective-permute-start(bf16[4480,128]{1,0:T(8,128)(2,1)} %get-tuple-element.382), channel_id=1, source_target_pairs={{0,16},{8,24},{16,0},{24,8},{1,17},{9,25},{17,1},{25,9},{2,18},{10... | collective-permute-start | bytes 3440648 | tf_op jit(solution)/shard_map/ppermute | solution.py:849
  119.9 41.1 %collective-permute-start.14 = (bf16[4480,128]{1,0:T(8,128)(2,1)}, bf16[4480,128]{1,0:T(8,128)(2,1)S(1)}, u32[]{:S(2)}, u32[]{:S(2)}) collective-permute-start(bf16[4480,128]{1,0:T(8,128)(2,1)} %get-tuple-element.384), channel_id=1, source_target_pairs={{0,2},{2,0},{4,6},{6,4},{1,3},{3,1},{5,7},{7,5},{8,10},{10,8},{12,... | collective-permute-start | bytes 3440648 | tf_op jit(solution)/shard_map/ppermute | solution.py:849
  160.9 8.4 %collective-permute-start.18 = (bf16[512,896]{1,0:T(8,128)(2,1)}, bf16[512,896]{1,0:T(8,128)(2,1)S(1)}, u32[]{:S(2)}, u32[]{:S(2)}) collective-permute-start(bf16[512,896]{1,0:T(8,128)(2,1)} %get-tuple-element.398), channel_id=1, source_target_pairs={{0,1},{1,0},{2,3},{3,2},{4,5},{5,4},{6,7},{7,6},{8,9},{9,8},{10,11... | collective-permute-start | bytes 2752520 | tf_op jit(solution)/shard_map/ppermute | solution.py:843
  168.2 15.6 %collective-permute-start.15 = (bf16[2240,128]{1,0:T(8,128)(2,1)}, bf16[2240,128]{1,0:T(8,128)(2,1)S(1)}, u32[]{:S(2)}, u32[]{:S(2)}) collective-permute-start(bf16[2240,128]{1,0:T(8,128)(2,1)} %get-tuple-element.392), channel_id=1, source_target_pairs={{0,16},{8,24},{16,0},{24,8},{1,17},{9,25},{17,1},{25,9},{2,18},{10... | collective-permute-start | bytes 1720328 | tf_op jit(solution)/shard_map/ppermute | solution.py:849
  168.7 15.3 %collective-permute-start.16 = (bf16[2240,128]{1,0:T(8,128)(2,1)}, bf16[2240,128]{1,0:T(8,128)(2,1)S(1)}, u32[]{:S(2)}, u32[]{:S(2)}) collective-permute-start(bf16[2240,128]{1,0:T(8,128)(2,1)} %get-tuple-element.394), channel_id=1, source_target_pairs={{0,2},{2,0},{4,6},{6,4},{1,3},{3,1},{5,7},{7,5},{8,10},{10,8},{12,... | collective-permute-start | bytes 1720328 | tf_op jit(solution)/shard_map/ppermute | solution.py:849
  168.7 15.3 %collective-permute-start.17 = (bf16[2240,128]{1,0:T(8,128)(2,1)}, bf16[2240,128]{1,0:T(8,128)(2,1)S(1)}, u32[]{:S(2)}, u32[]{:S(2)}) collective-permute-start(bf16[2240,128]{1,0:T(8,128)(2,1)} %get-tuple-element.396), channel_id=1, source_target_pairs={{0,8},{8,0},{16,24},{24,16},{1,9},{9,1},{17,25},{25,17},{2,10},{10... | collective-permute-start | bytes 1720328 | tf_op jit(solution)/shard_map/ppermute | solution.py:849
  188.5 8.7 %collective-permute-start.19 = (bf16[1120,128]{1,0:T(8,128)(2,1)}, bf16[1120,128]{1,0:T(8,128)(2,1)S(1)}, u32[]{:S(2)}, u32[]{:S(2)}) collective-permute-start(bf16[1120,128]{1,0:T(8,128)(2,1)} %get-tuple-element.416), channel_id=1, source_target_pairs={{0,2},{2,0},{4,6},{6,4},{1,3},{3,1},{5,7},{7,5},{8,10},{10,8},{12,... | collective-permute-start | bytes 860168 | tf_op jit(solution)/shard_map/ppermute | solution.py:849
  190.1 7.7 %collective-permute-start.20 = (bf16[1120,128]{1,0:T(8,128)(2,1)}, bf16[1120,128]{1,0:T(8,128)(2,1)S(1)}, u32[]{:S(2)}, u32[]{:S(2)}) collective-permute-start(bf16[1120,128]{1,0:T(8,128)(2,1)} %get-tuple-element.418), channel_id=1, source_target_pairs={{0,8},{8,0},{16,24},{24,16},{1,9},{9,1},{17,25},{25,17},{2,10},{10... | collective-permute-start | bytes 860168 | tf_op jit(solution)/shard_map/ppermute | solution.py:849
  190.6 7.5 %collective-permute-start.21 = (bf16[1120,128]{1,0:T(8,128)(2,1)}, bf16[1120,128]{1,0:T(8,128)(2,1)S(1)}, u32[]{:S(2)}, u32[]{:S(2)}) collective-permute-start(bf16[1120,128]{1,0:T(8,128)(2,1)} %get-tuple-element.420), channel_id=1, source_target_pairs={{0,16},{8,24},{16,0},{24,8},{1,17},{9,25},{17,1},{25,9},{2,18},{10... | collective-permute-start | bytes 860168 | tf_op jit(solution)/shard_map/ppermute | solution.py:849
  201.3 73.0 %collective-permute-start.28 = (bf16[3360,128]{1,0:T(8,128)(2,1)}, bf16[3360,128]{1,0:T(8,128)(2,1)S(1)}, u32[]{:S(2)}, u32[]{:S(2)}) collective-permute-start(bf16[3360,128]{1,0:T(8,128)(2,1)} %shard_map.263.total), channel_id=1, source_target_pairs={{0,4},{2,6},{4,0},{6,2},{1,5},{3,7},{5,1},{7,3},{8,12},{10,14},{12... | collective-permute-start | bytes 2580488 | tf_op jit(solution)/shard_map/ppermute | solution.py:849
  204.6 25.3 %collective-permute-start.22 = (bf16[4032,128]{1,0:T(8,128)(2,1)}, bf16[4032,128]{1,0:T(8,128)(2,1)S(1)}, u32[]{:S(2)}, u32[]{:S(2)}) collective-permute-start(bf16[4032,128]{1,0:T(8,128)(2,1)} %get-tuple-element.428), channel_id=1, source_target_pairs={{0,8},{8,0},{16,24},{24,16},{1,9},{9,1},{17,25},{25,17},{2,10},{10... | collective-permute-start | bytes 3096584 | tf_op jit(solution)/shard_map/ppermute | solution.py:849
  206.0 23.9 %collective-permute-start.23 = (bf16[4032,128]{1,0:T(8,128)(2,1)S(1)}, bf16[4032,128]{1,0:T(8,128)(2,1)S(1)}, u32[]{:S(2)}, u32[]{:S(2)}) collective-permute-start(bf16[4032,128]{1,0:T(8,128)(2,1)S(1)} %copy-done.65), channel_id=1, source_target_pairs={{0,16},{8,24},{16,0},{24,8},{1,17},{9,25},{17,1},{25,9},{2,18},{10... | collective-permute-start | bytes 3096584 | tf_op jit(solution)/shard_map/ppermute | solution.py:849
  207.6 39.0 %collective-permute-start.24 = (bf16[4032,128]{1,0:T(8,128)(2,1)S(1)}, bf16[4032,128]{1,0:T(8,128)(2,1)S(1)}, u32[]{:S(2)}, u32[]{:S(2)}) collective-permute-start(bf16[4032,128]{1,0:T(8,128)(2,1)S(1)} %copy-done.64), channel_id=1, source_target_pairs={{0,2},{2,0},{4,6},{6,4},{1,3},{3,1},{5,7},{7,5},{8,10},{10,8},{12,... | collective-permute-start | bytes 3096584 | tf_op jit(solution)/shard_map/ppermute | solution.py:849
  252.6 25.4 %collective-permute-start.25 = (bf16[2016,128]{1,0:T(8,128)(2,1)}, bf16[2016,128]{1,0:T(8,128)(2,1)S(1)}, u32[]{:S(2)}, u32[]{:S(2)}) collective-permute-start(bf16[2016,128]{1,0:T(8,128)(2,1)} %get-tuple-element.453), channel_id=1, source_target_pairs={{0,16},{8,24},{16,0},{24,8},{1,17},{9,25},{17,1},{25,9},{2,18},{10... | collective-permute-start | bytes 1548296 | tf_op jit(solution)/shard_map/ppermute | solution.py:849
  253.4 24.7 %collective-permute-start.26 = (bf16[2016,128]{1,0:T(8,128)(2,1)}, bf16[2016,128]{1,0:T(8,128)(2,1)S(1)}, u32[]{:S(2)}, u32[]{:S(2)}) collective-permute-start(bf16[2016,128]{1,0:T(8,128)(2,1)} %get-tuple-element.455), channel_id=1, source_target_pairs={{0,2},{2,0},{4,6},{6,4},{1,3},{3,1},{5,7},{7,5},{8,10},{10,8},{12,... | collective-permute-start | bytes 1548296 | tf_op jit(solution)/shard_map/ppermute | solution.py:849
  253.4 24.7 %collective-permute-start.27 = (bf16[2016,128]{1,0:T(8,128)(2,1)}, bf16[2016,128]{1,0:T(8,128)(2,1)S(1)}, u32[]{:S(2)}, u32[]{:S(2)}) collective-permute-start(bf16[2016,128]{1,0:T(8,128)(2,1)} %get-tuple-element.457), channel_id=1, source_target_pairs={{0,8},{8,0},{16,24},{24,16},{1,9},{9,1},{17,25},{25,17},{2,10},{10... | collective-permute-start | bytes 1548296 | tf_op jit(solution)/shard_map/ppermute | solution.py:849
  273.0 24.3 %collective-permute-start.37 = (bf16[512,256]{1,0:T(8,128)(2,1)}, bf16[512,256]{1,0:T(8,128)(2,1)S(1)}, u32[]{:S(2)}, u32[]{:S(2)}) collective-permute-start(bf16[512,256]{1,0:T(8,128)(2,1)} %get-tuple-element.506), channel_id=1, source_target_pairs={{2,0},{4,2},{6,4},{3,1},{5,3},{7,5},{10,8},{12,10},{14,12},{11,9},... | collective-permute-start | bytes 786440 | tf_op jit(solution)/shard_map/ppermute | solution.py:1335
  274.3 22.9 %collective-permute-start.38 = (bf16[512,256]{1,0:T(8,128)(2,1)}, bf16[512,256]{1,0:T(8,128)(2,1)S(1)}, u32[]{:S(2)}, u32[]{:S(2)}) collective-permute-start(bf16[512,256]{1,0:T(8,128)(2,1)} %get-tuple-element.507), channel_id=1, source_target_pairs={{4,0},{6,2},{5,1},{7,3},{12,8},{14,10},{13,9},{15,11},{20,16},{22,... | collective-permute-start | bytes 786440 | tf_op jit(solution)/shard_map/ppermute | solution.py:1335
  282.4 11.5 %collective-permute-start.29 = (bf16[1008,128]{1,0:T(8,128)(2,1)}, bf16[1008,128]{1,0:T(8,128)(2,1)S(1)}, u32[]{:S(2)}, u32[]{:S(2)}) collective-permute-start(bf16[1008,128]{1,0:T(8,128)(2,1)} %get-tuple-element.483), channel_id=1, source_target_pairs={{0,2},{2,0},{4,6},{6,4},{1,3},{3,1},{5,7},{7,5},{8,10},{10,8},{12,... | collective-permute-start | bytes 774152 | tf_op jit(solution)/shard_map/ppermute | solution.py:849
  285.1 8.9 %collective-permute-start.30 = (bf16[1008,128]{1,0:T(8,128)(2,1)}, bf16[1008,128]{1,0:T(8,128)(2,1)S(1)}, u32[]{:S(2)}, u32[]{:S(2)}) collective-permute-start(bf16[1008,128]{1,0:T(8,128)(2,1)} %get-tuple-element.485), channel_id=1, source_target_pairs={{0,8},{8,0},{16,24},{24,16},{1,9},{9,1},{17,25},{25,17},{2,10},{10... | collective-permute-start | bytes 774152 | tf_op jit(solution)/shard_map/ppermute | solution.py:849
  285.9 8.1 %collective-permute-start.31 = (bf16[1008,128]{1,0:T(8,128)(2,1)}, bf16[1008,128]{1,0:T(8,128)(2,1)S(1)}, u32[]{:S(2)}, u32[]{:S(2)}) collective-permute-start(bf16[1008,128]{1,0:T(8,128)(2,1)} %get-tuple-element.487), channel_id=1, source_target_pairs={{0,16},{8,24},{16,0},{24,8},{1,17},{9,25},{17,1},{25,9},{2,18},{10... | collective-permute-start | bytes 774152 | tf_op jit(solution)/shard_map/ppermute | solution.py:849
  306.9 21.5 %collective-permute-start.42 = (bf16[7296,128]{1,0:T(8,128)(2,1)}, bf16[7296,128]{1,0:T(8,128)(2,1)S(1)}, u32[]{:S(2)}, u32[]{:S(2)}) collective-permute-start(bf16[7296,128]{1,0:T(8,128)(2,1)} %get-tuple-element.544), channel_id=1, source_target_pairs={{0,1},{1,0},{2,3},{3,2},{4,5},{5,4},{6,7},{7,6},{8,9},{9,8},{10,11... | collective-permute-start | bytes 5603336 | tf_op jit(solution)/shard_map/ppermute | solution.py:843
  307.4 11.9 %collective-permute-start.33 = (bf16[1120,128]{1,0:T(8,128)(2,1)S(1)}, bf16[1120,128]{1,0:T(8,128)(2,1)S(1)}, u32[]{:S(2)}, u32[]{:S(2)}) collective-permute-start(bf16[1120,128]{1,0:T(8,128)(2,1)S(1)} %copy-done.39), channel_id=1, source_target_pairs={{0,2},{2,0},{4,6},{6,4},{1,3},{3,1},{5,7},{7,5},{8,10},{10,8},{12,... | collective-permute-start | bytes 860168 | tf_op jit(solution)/shard_map/ppermute | solution.py:849
  307.5 11.9 %collective-permute-start.36 = (bf16[1120,128]{1,0:T(8,128)(2,1)S(1)}, bf16[1120,128]{1,0:T(8,128)(2,1)S(1)}, u32[]{:S(2)}, u32[]{:S(2)}) collective-permute-start(bf16[1120,128]{1,0:T(8,128)(2,1)S(1)} %copy-done.40), channel_id=1, source_target_pairs={{0,16},{8,24},{16,0},{24,8},{1,17},{9,25},{17,1},{25,9},{2,18},{10... | collective-permute-start | bytes 860168 | tf_op jit(solution)/shard_map/ppermute | solution.py:849
  310.8 9.1 %collective-permute-start.35 = (bf16[1120,128]{1,0:T(8,128)(2,1)S(1)}, bf16[1120,128]{1,0:T(8,128)(2,1)S(1)}, u32[]{:S(2)}, u32[]{:S(2)}) collective-permute-start(bf16[1120,128]{1,0:T(8,128)(2,1)S(1)} %collective-permute-done.34.refs_2_), channel_id=1, source_target_pairs={{0,8},{8,0},{16,24},{24,16},{1,9},{9,1},{17,25},{25,17},{2,10},{10... | collective-permute-start | bytes 860168 | tf_op jit(solution)/shard_map/ppermute | solution.py:849
  311.2 15.6 %collective-permute-start.43 = (bf16[1008,128]{1,0:T(8,128)(2,1)S(1)}, bf16[1008,128]{1,0:T(8,128)(2,1)S(1)}, u32[]{:S(2)}, u32[]{:S(2)}) collective-permute-start(bf16[1008,128]{1,0:T(8,128)(2,1)S(1)} %copy-done.48), channel_id=1, source_target_pairs={{0,4},{2,6},{4,0},{6,2},{1,5},{3,7},{5,1},{7,3},{8,12},{10,14},{12... | collective-permute-start | bytes 774152 | tf_op jit(solution)/shard_map/ppermute | solution.py:849
  323.3 14.6 %collective-permute-start.39 = (bf16[2240,128]{1,0:T(8,128)(2,1)}, bf16[2240,128]{1,0:T(8,128)(2,1)S(1)}, u32[]{:S(2)}, u32[]{:S(2)}) collective-permute-start(bf16[2240,128]{1,0:T(8,128)(2,1)} %get-tuple-element.551.refs_0_), channel_id=1, source_target_pairs={{0,16},{8,24},{16,0},{24,8},{1,17},{9,25},{17,1},{25,9},{2,18},{10... | collective-permute-start | bytes 1720328 | tf_op jit(solution)/shard_map/ppermute | solution.py:849
  324.0 31.8 %collective-permute-start.11 = (bf16[512,896]{1,0:T(8,128)(2,1)}, bf16[512,896]{1,0:T(8,128)(2,1)S(1)}, u32[]{:S(2)}, u32[]{:S(2)}) collective-permute-start(bf16[512,896]{1,0:T(8,128)(2,1)} %get-tuple-element.373), channel_id=1, source_target_pairs={{0,1},{1,0},{2,3},{3,2},{4,5},{5,4},{6,7},{7,6},{8,9},{9,8},{10,11... | collective-permute-start | bytes 2752520 | tf_op jit(solution)/shard_map/ppermute | solution.py:843
  324.0 21.1 %collective-permute-start.40 = (bf16[2240,128]{1,0:T(8,128)(2,1)}, bf16[2240,128]{1,0:T(8,128)(2,1)S(1)}, u32[]{:S(2)}, u32[]{:S(2)}) collective-permute-start(bf16[2240,128]{1,0:T(8,128)(2,1)} %get-tuple-element.553.refs_2_), channel_id=1, source_target_pairs={{0,2},{2,0},{4,6},{6,4},{1,3},{3,1},{5,7},{7,5},{8,10},{10,8},{12,... | collective-permute-start | bytes 1720328 | tf_op jit(solution)/shard_map/ppermute | solution.py:849
  326.8 18.3 %collective-permute-start.41 = (bf16[2240,128]{1,0:T(8,128)(2,1)}, bf16[2240,128]{1,0:T(8,128)(2,1)S(1)}, u32[]{:S(2)}, u32[]{:S(2)}) collective-permute-start(bf16[2240,128]{1,0:T(8,128)(2,1)} %get-tuple-element.555.refs_4_), channel_id=1, source_target_pairs={{0,8},{8,0},{16,24},{24,16},{1,9},{9,1},{17,25},{25,17},{2,10},{10... | collective-permute-start | bytes 1720328 | tf_op jit(solution)/shard_map/ppermute | solution.py:849
  328.4 23.5 %collective-permute-start.32 = (bf16[1008,128]{1,0:T(8,128)(2,1)}, bf16[1008,128]{1,0:T(8,128)(2,1)S(1)}, u32[]{:S(2)}, u32[]{:S(2)}) collective-permute-start(bf16[1008,128]{1,0:T(8,128)(2,1)} %get-tuple-element.558), channel_id=1, source_target_pairs={{0,4},{2,6},{4,0},{6,2},{1,5},{3,7},{5,1},{7,3},{8,12},{10,14},{12... | collective-permute-start | bytes 774152 | tf_op jit(solution)/shard_map/ppermute | solution.py:849
  337.9 19.3 %collective-permute-start.44 = (bf16[1824,128]{1,0:T(8,128)(2,1)}, bf16[1824,128]{1,0:T(8,128)(2,1)}, u32[]{:S(2)}, u32[]{:S(2)}) collective-permute-start(bf16[1824,128]{1,0:T(8,128)(2,1)} %get-tuple-element.563), channel_id=1, source_target_pairs={{0,8},{8,0},{16,24},{24,16},{1,9},{9,1},{17,25},{25,17},{2,10},{10... | collective-permute-start | bytes 1400840 | tf_op jit(solution)/shard_map/ppermute | solution.py:849
  350.7 54.6 %collective-permute-start.54 = (bf16[4480,128]{1,0:T(8,128)(2,1)}, bf16[4480,128]{1,0:T(8,128)(2,1)S(1)}, u32[]{:S(2)}, u32[]{:S(2)}) collective-permute-start(bf16[4480,128]{1,0:T(8,128)(2,1)} %get-tuple-element.584.refs_1_), channel_id=1, source_target_pairs={{0,8},{8,0},{16,24},{24,16},{1,9},{9,1},{17,25},{25,17},{2,10},{10... | collective-permute-start | bytes 3440648 | tf_op jit(solution)/shard_map/ppermute | solution.py:849
  351.9 13.8 %collective-permute-start.45 = (bf16[1824,128]{1,0:T(8,128)(2,1)}, bf16[1824,128]{1,0:T(8,128)(2,1)S(1)}, u32[]{:S(2)}, u32[]{:S(2)}) collective-permute-start(bf16[1824,128]{1,0:T(8,128)(2,1)} %get-tuple-element.565), channel_id=1, source_target_pairs={{0,16},{8,24},{16,0},{24,8},{1,17},{9,25},{17,1},{25,9},{2,18},{10... | collective-permute-start | bytes 1400840 | tf_op jit(solution)/shard_map/ppermute | solution.py:849
  352.6 53.5 %collective-permute-start.55 = (bf16[4480,128]{1,0:T(8,128)(2,1)}, bf16[4480,128]{1,0:T(8,128)(2,1)S(1)}, u32[]{:S(2)}, u32[]{:S(2)}) collective-permute-start(bf16[4480,128]{1,0:T(8,128)(2,1)} %get-tuple-element.586.refs_3_), channel_id=1, source_target_pairs={{0,16},{8,24},{16,0},{24,8},{1,17},{9,25},{17,1},{25,9},{2,18},{10... | collective-permute-start | bytes 3440648 | tf_op jit(solution)/shard_map/ppermute | solution.py:849
  355.8 14.0 %collective-permute-start.48 = (bf16[1008,128]{1,0:T(8,128)(2,1)}, bf16[1008,128]{1,0:T(8,128)(2,1)}, u32[]{:S(2)}, u32[]{:S(2)}) collective-permute-start(bf16[1008,128]{1,0:T(8,128)(2,1)} %get-tuple-element.575), channel_id=1, source_target_pairs={{0,4},{2,6},{4,0},{6,2},{1,5},{3,7},{5,1},{7,3},{8,12},{10,14},{12... | collective-permute-start | bytes 774152 | tf_op jit(solution)/shard_map/ppermute | solution.py:849
  357.2 50.1 %collective-permute-start.56 = (bf16[4480,128]{1,0:T(8,128)(2,1)}, bf16[4480,128]{1,0:T(8,128)(2,1)S(1)}, u32[]{:S(2)}, u32[]{:S(2)}) collective-permute-start(bf16[4480,128]{1,0:T(8,128)(2,1)} %get-tuple-element.588.refs_5_), channel_id=1, source_target_pairs={{0,2},{2,0},{4,6},{6,4},{1,3},{3,1},{5,7},{7,5},{8,10},{10,8},{12,... | collective-permute-start | bytes 3440648 | tf_op jit(solution)/shard_map/ppermute | solution.py:849
  369.0 24.8 %collective-permute-start.46 = (bf16[912,128]{1,0:T(8,128)(2,1)}, bf16[912,128]{1,0:T(8,128)(2,1)S(1)}, u32[]{:S(2)}, u32[]{:S(2)}) collective-permute-start(bf16[912,128]{1,0:T(8,128)(2,1)} %get-tuple-element.571), channel_id=1, source_target_pairs={{0,16},{8,24},{16,0},{24,8},{1,17},{9,25},{17,1},{25,9},{2,18},{10... | collective-permute-start | bytes 700424 | tf_op jit(solution)/shard_map/ppermute | solution.py:849
  369.7 33.4 %collective-permute-start.51 = (bf16[1008,128]{1,0:T(8,128)(2,1)S(1)}, bf16[1008,128]{1,0:T(8,128)(2,1)S(1)}, u32[]{:S(2)}, u32[]{:S(2)}) collective-permute-start(bf16[1008,128]{1,0:T(8,128)(2,1)S(1)} %copy-done.49), channel_id=1, source_target_pairs={{0,1},{1,0},{2,3},{3,2},{4,5},{5,4},{6,7},{7,6},{8,9},{9,8},{10,11... | collective-permute-start | bytes 774152 | tf_op jit(solution)/shard_map/ppermute | solution.py:843
  393.8 6.4 %collective-permute-start.47 = (bf16[912,128]{1,0:T(8,128)(2,1)}, bf16[912,128]{1,0:T(8,128)(2,1)S(1)}, u32[]{:S(2)}, u32[]{:S(2)}) collective-permute-start(bf16[912,128]{1,0:T(8,128)(2,1)} %get-tuple-element.573), channel_id=1, source_target_pairs={{0,8},{8,0},{16,24},{24,16},{1,9},{9,1},{17,25},{25,17},{2,10},{10... | collective-permute-start | bytes 700424 | tf_op jit(solution)/shard_map/ppermute | solution.py:849
  403.1 22.0 %collective-permute-start.49 = (bf16[1824,128]{1,0:T(8,128)(2,1)}, bf16[1824,128]{1,0:T(8,128)(2,1)S(1)}, u32[]{:S(2)}, u32[]{:S(2)}) collective-permute-start(bf16[1824,128]{1,0:T(8,128)(2,1)} %shard_map.276), channel_id=1, source_target_pairs={{0,2},{2,0},{4,6},{6,4},{1,3},{3,1},{5,7},{7,5},{8,10},{10,8},{12,... | collective-permute-start | bytes 1400840 | tf_op jit(solution)/shard_map/ppermute | solution.py:849
  403.2 16.0 %collective-permute-start.50 = (bf16[1008,128]{1,0:T(8,128)(2,1)S(1)}, bf16[1008,128]{1,0:T(8,128)(2,1)S(1)}, u32[]{:S(2)}, u32[]{:S(2)}) collective-permute-start(bf16[1008,128]{1,0:T(8,128)(2,1)S(1)} %add_convert_fusion.4.refs_0_), channel_id=1, source_target_pairs={{0,2},{2,0},{4,6},{6,4},{1,3},{3,1},{5,7},{7,5},{8,10},{10,8},{12,... | collective-permute-start | bytes 774152 | tf_op jit(solution)/shard_map/ppermute | solution.py:849
  405.2 14.0 %collective-permute-start.52 = (bf16[1008,128]{1,0:T(8,128)(2,1)S(1)}, bf16[1008,128]{1,0:T(8,128)(2,1)S(1)}, u32[]{:S(2)}, u32[]{:S(2)}) collective-permute-start(bf16[1008,128]{1,0:T(8,128)(2,1)S(1)} %collective-permute-done.51.refs_2_), channel_id=1, source_target_pairs={{0,8},{8,0},{16,24},{24,16},{1,9},{9,1},{17,25},{25,17},{2,10},{10... | collective-permute-start | bytes 774152 | tf_op jit(solution)/shard_map/ppermute | solution.py:849
  406.1 13.1 %collective-permute-start.53 = (bf16[1008,128]{1,0:T(8,128)(2,1)S(1)}, bf16[1008,128]{1,0:T(8,128)(2,1)S(1)}, u32[]{:S(2)}, u32[]{:S(2)}) collective-permute-start(bf16[1008,128]{1,0:T(8,128)(2,1)S(1)} %add_convert_fusion.2.refs_4_), channel_id=1, source_target_pairs={{0,16},{8,24},{16,0},{24,8},{1,17},{9,25},{17,1},{25,9},{2,18},{10... | collective-permute-start | bytes 774152 | tf_op jit(solution)/shard_map/ppermute | solution.py:849
  422.8 26.5 %collective-permute-start.60 = (bf16[2016,128]{1,0:T(8,128)(2,1)}, bf16[2016,128]{1,0:T(8,128)(2,1)S(1)}, u32[]{:S(2)}, u32[]{:S(2)}) collective-permute-start(bf16[2016,128]{1,0:T(8,128)(2,1)} %get-tuple-element.606.refs_0_), channel_id=1, source_target_pairs={{0,16},{8,24},{16,0},{24,8},{1,17},{9,25},{17,1},{25,9},{2,18},{10... | collective-permute-start | bytes 1548296 | tf_op jit(solution)/shard_map/ppermute | solution.py:849
  423.5 25.8 %collective-permute-start.61 = (bf16[2016,128]{1,0:T(8,128)(2,1)}, bf16[2016,128]{1,0:T(8,128)(2,1)S(1)}, u32[]{:S(2)}, u32[]{:S(2)}) collective-permute-start(bf16[2016,128]{1,0:T(8,128)(2,1)} %get-tuple-element.608.refs_2_), channel_id=1, source_target_pairs={{0,2},{2,0},{4,6},{6,4},{1,3},{3,1},{5,7},{7,5},{8,10},{10,8},{12,... | collective-permute-start | bytes 1548296 | tf_op jit(solution)/shard_map/ppermute | solution.py:849
  423.8 25.5 %collective-permute-start.62 = (bf16[2016,128]{1,0:T(8,128)(2,1)}, bf16[2016,128]{1,0:T(8,128)(2,1)S(1)}, u32[]{:S(2)}, u32[]{:S(2)}) collective-permute-start(bf16[2016,128]{1,0:T(8,128)(2,1)} %get-tuple-element.610.refs_4_), channel_id=1, source_target_pairs={{0,8},{8,0},{16,24},{24,16},{1,9},{9,1},{17,25},{25,17},{2,10},{10... | collective-permute-start | bytes 1548296 | tf_op jit(solution)/shard_map/ppermute | solution.py:849
  425.3 21.2 %collective-permute-start.57 = (bf16[1824,128]{1,0:T(8,128)(2,1)S(1)}, bf16[1824,128]{1,0:T(8,128)(2,1)S(1)}, u32[]{:S(2)}, u32[]{:S(2)}) collective-permute-start(bf16[1824,128]{1,0:T(8,128)(2,1)S(1)} %add_convert_fusion.1.total), channel_id=1, source_target_pairs={{0,4},{2,6},{4,0},{6,2},{1,5},{3,7},{5,1},{7,3},{8,12},{10,14},{12... | collective-permute-start | bytes 1400840 | tf_op jit(solution)/shard_map/ppermute | solution.py:849
  454.1 28.0 %collective-permute-start.65 = (bf16[4032,128]{1,0:T(8,128)(2,1)}, bf16[4032,128]{1,0:T(8,128)(2,1)S(1)}, u32[]{:S(2)}, u32[]{:S(2)}) collective-permute-start(bf16[4032,128]{1,0:T(8,128)(2,1)} %get-tuple-element.624.refs_1_), channel_id=1, source_target_pairs={{0,8},{8,0},{16,24},{24,16},{1,9},{9,1},{17,25},{25,17},{2,10},{10... | collective-permute-start | bytes 3096584 | tf_op jit(solution)/shard_map/ppermute | solution.py:849
  454.1 28.0 %collective-permute-start.66 = (bf16[4032,128]{1,0:T(8,128)(2,1)}, bf16[4032,128]{1,0:T(8,128)(2,1)S(1)}, u32[]{:S(2)}, u32[]{:S(2)}) collective-permute-start(bf16[4032,128]{1,0:T(8,128)(2,1)} %get-tuple-element.626.refs_3_), channel_id=1, source_target_pairs={{0,16},{8,24},{16,0},{24,8},{1,17},{9,25},{17,1},{25,9},{2,18},{10... | collective-permute-start | bytes 3096584 | tf_op jit(solution)/shard_map/ppermute | solution.py:849
  454.1 28.0 %collective-permute-start.67 = (bf16[4032,128]{1,0:T(8,128)(2,1)}, bf16[4032,128]{1,0:T(8,128)(2,1)S(1)}, u32[]{:S(2)}, u32[]{:S(2)}) collective-permute-start(bf16[4032,128]{1,0:T(8,128)(2,1)} %get-tuple-element.628.refs_5_), channel_id=1, source_target_pairs={{0,2},{2,0},{4,6},{6,4},{1,3},{3,1},{5,7},{7,5},{8,10},{10,8},{12,... | collective-permute-start | bytes 3096584 | tf_op jit(solution)/shard_map/ppermute | solution.py:849
  456.6 20.7 %collective-permute-start.58 = (bf16[912,128]{1,0:T(8,128)(2,1)S(1)}, bf16[912,128]{1,0:T(8,128)(2,1)S(1)}, u32[]{:S(2)}, u32[]{:S(2)}) collective-permute-start(bf16[912,128]{1,0:T(8,128)(2,1)S(1)} %copy-done.58), channel_id=1, source_target_pairs={{0,16},{8,24},{16,0},{24,8},{1,17},{9,25},{17,1},{25,9},{2,18},{10... | collective-permute-start | bytes 700424 | tf_op jit(solution)/shard_map/ppermute | solution.py:849
  458.0 19.4 %collective-permute-start.59 = (bf16[912,128]{1,0:T(8,128)(2,1)S(1)}, bf16[912,128]{1,0:T(8,128)(2,1)S(1)}, u32[]{:S(2)}, u32[]{:S(2)}) collective-permute-start(bf16[912,128]{1,0:T(8,128)(2,1)S(1)} %copy-done.59), channel_id=1, source_target_pairs={{0,8},{8,0},{16,24},{24,16},{1,9},{9,1},{17,25},{25,17},{2,10},{10... | collective-permute-start | bytes 700424 | tf_op jit(solution)/shard_map/ppermute | solution.py:849
  481.0 11.1 %collective-permute-start.63 = (bf16[1824,128]{1,0:T(8,128)(2,1)}, bf16[1824,128]{1,0:T(8,128)(2,1)}, u32[]{:S(2)}, u32[]{:S(2)}) collective-permute-start(bf16[1824,128]{1,0:T(8,128)(2,1)} %get-tuple-element.635.refs_1_), channel_id=1, source_target_pairs={{0,8},{8,0},{16,24},{24,16},{1,9},{9,1},{17,25},{25,17},{2,10},{10... | collective-permute-start | bytes 1400840 | tf_op jit(solution)/shard_map/ppermute | solution.py:849
  481.6 10.5 %collective-permute-start.64 = (bf16[1824,128]{1,0:T(8,128)(2,1)}, bf16[1824,128]{1,0:T(8,128)(2,1)}, u32[]{:S(2)}, u32[]{:S(2)}) collective-permute-start(bf16[1824,128]{1,0:T(8,128)(2,1)} %get-tuple-element.637.refs_3_), channel_id=1, source_target_pairs={{0,16},{8,24},{16,0},{24,8},{1,17},{9,25},{17,1},{25,9},{2,18},{10... | collective-permute-start | bytes 1400840 | tf_op jit(solution)/shard_map/ppermute | solution.py:849
  (78 other events, 416.0 us)

commit v4 on v3

--- a/solution.py
+++ b/solution.py
@@ -1348,24 +1348,23 @@
     input_grad = dx[None]
     width = HQ * HD
     rest = FlatSum(place, order)
-    got = swap(theirs)
+    two.turn_each(0)
+    rest.leave(mine, swap(theirs))
+    two.turn_each(1)
+    rest.halve()
     one.join(2)
-    two.turn_each(0)
-    rest.leave(mine, got)
-    one.join(1)
-    two.turn_each(1)
-    block_output = order(
-        lambda a, b, c: (a + b.astype(f32) + c.astype(f32)).astype(bf16), h1, own_result, swap(other_result)
-    )[None]
-    rest.halve()
     two.turn_each(2)
     rest.sum()
-    outs = run_untile(0, one.parts, None)
+    one.join(1)
     two.join(2)
     rest.across()
     rest.turn()
     two.join(1)
     rest.join()
+    outs = run_untile(0, one.parts, None)
+    block_output = order(
+        lambda a, b, c: (a + b.astype(f32) + c.astype(f32)).astype(bf16), h1, own_result, swap(other_result)
+    )[None]
     gates, ups, gw_down = run_untile(1, two.parts, outs)
     gw_query, gw_key, gw_value, gw_out, vector = order(
         functools.partial(

time: 505 us -> 482 us (0.954)
  waiting for transfers between devices: 130 us -> 115 us
    ppermute x50, waiting for transfers between devices: 117 us -> 105 us  [flip(): return lax.ppermute(values, axis, [(i, i ^ 1 << bit) for i in range(size)])]
    unnamed x148 -> x136, local copies, waits for them, and re-layouts: 23 us -> 18.2 us
  transfers between devices with their start and end apart: 68 -> 68, of which waited for: 22 -> 24; matrix products, arithmetic and copies ran while one was open for 3% -> 2% of each run, Pallas kernels for 40% -> 41%
where the time goes in v4:
time: 482 us; the launch traced here: 478 us
  Pallas kernels  258 us (54%)
  waiting for transfers between devices  115 us (24%)
  starting transfers between devices  73.1 us (15%)
  local copies, waits for them, and re-layouts  25.9 us (5%)
    ppermute x50, waiting for transfers between devices, flip(): return lax.ppermute(values, axis, [(i, i ^ 1 << bit) for i in range(size)])  105 us
    pallas_call x2, Pallas kernels, feed(): call(functools.partial(feed_kernel, start=start, first=first, sides=sides...  75.9 us
    ppermute x50, starting transfers between devices, flip(): return lax.ppermute(values, axis, [(i, i ^ 1 << bit) for i in range(size)])  58.4 us
    pallas_call x2, Pallas kernels, attend_back(): call(functools.partial(attend_back_kernel, first_pair=first_pair, first=f...  39.9 us
    pallas_call x1, Pallas kernels, attend(): call(attend_kernel, (jax.ShapeDtypeStruct((count, HQ * HD), bf16), jax.Sh...  22.3 us
    pallas_call x5, Pallas kernels, fold(): call(functools.partial(fold_kernel, sides=sides), tuple((jax.ShapeDtypeSt...  19.8 us
    unnamed x136, local copies, waits for them, and re-layouts  18.2 us
    pallas_call x2, Pallas kernels, untile(): call(functools.partial(untile_kernel, start=start, width=width, first=fir...  17.7 us
  transfers between devices with their start and end apart: 68, of which 24 were waited for; matrix products, arithmetic and copies ran while one was open for 2% of the time, Pallas kernels for 41%

profile of v4, /device:TPU:0, one launch (start us, length us, event | category | flops | bytes accessed | tf_op | source)
XLA Modules:
  0.0 478.1 jit_solution(16858073522640370333)
XLA Ops:
  1.2 3.5 concatenate.6
  5.8 1.8 multiply_sine_fusion
  8.7 5.0 %collective-permute-done.2.ok_ref = bf16[448,128]{1,0:T(8,128)(2,1)S(1)} collective-permute-done((bf16[448,128]{1,0:T(8,128)(2,1)}, bf16[448,128]{1,0:T(8,128)(2,1)S(1)}, u32[]{:S(2)}, u32[]{:S(2)}) %collective-permute-start.2) | collective-permute-done | bytes 114720 | tf_op jit(solution)/shard_map/ppermute | solution.py:843
  14.8 2.6 collective-permute-done.3.ov_ref
  18.7 6.0 %shard_map.254 = (bf16[512,896]{1,0:T(8,128)(2,1)}, bf16[512,896]{1,0:T(8,128)(2,1)}, bf16[512,256]{1,0:T(8,128)(2,1)}, bf16[896,1152]{1,0:T(8,128)(2,1)}) custom-call(s32[5]{0:T(128)} %stack.23.place_ref.refs_0_, bf16[512,896]{1,0:T(8,128)(2,1)} %bitcast.10, f32[1,2944]{1,0:T(1,128)} %broadcast_in_dim.10.params_ref, bf16[448,896]{1,0:T(8,128)(2,1)} %wq_ref.1, ...), custom_call_target="tpu_custom_call" | custom-call | flops 1056964608 | bytes 6291456 | tf_op jit(solution)/shard_map/pallas_call | solution.py:109
  24.7 4.6 collective-permute-start.4
  29.4 4.8 %collective-permute-start.5 = (bf16[512,256]{1,0:T(8,128)(2,1)}, bf16[512,256]{1,0:T(8,128)(2,1)S(1)}, u32[]{:S(2)}, u32[]{:S(2)}) collective-permute-start(bf16[512,256]{1,0:T(8,128)(2,1)} %get-tuple-element.458.kv0_ref.refs_3_), channel_id=1, source_target_pairs={{0,4},{2,6},{1,5},{3,7},{8,12},{10,14},{9,13},{11,15},{16,20},{18,... | collective-permute-start | bytes 786440 | tf_op jit(solution)/shard_map/ppermute | solution.py:1280
  34.2 11.8 %shard_map.255.refs_10_ = bf16[1024,2432]{1,0:T(8,128)(2,1)} custom-call(bf16[512,896]{1,0:T(8,128)(2,1)} %bitcast.14, bf16[512,896]{1,0:T(8,128)(2,1)} %copy-done.60, bf16[2432,896]{1,0:T(8,128)(2,1)} %refs_9_.1), custom_call_target="tpu_custom_call" | custom-call | flops 4462739456 | bytes 12582912 | tf_op jit(solution)/shard_map/pallas_call | solution.py:472
  46.8 22.3 %shard_map.256 = (bf16[512,896]{1,0:T(8,128)(2,1)}, f32[7,8,512]{2,1,0:T(8,128)}) custom-call(s32[5]{0:T(128)} %stack.23.place_ref.refs_0_, bf16[512,896]{1,0:T(8,128)(2,1)} %get-tuple-element.456.q_ref.refs_1_, bf16[512,256]{1,0:T(8,128)(2,1)} %get-tuple-element.458.kv0_ref.refs_3_, bf16[512,256]{1,0:T(8,128)(2,1)} %copy-done.64, ...), custom_call_target="tpu_custom_call" | custom-call | flops 9395240960 | bytes 4194304 | tf_op jit(solution)/shard_map/pallas_call | solution.py:248
  70.0 5.7 %shard_map.257 = (f32[512,896]{1,0:T(8,128)}, bf16[512,896]{1,0:T(8,128)(2,1)}, bf16[896,896]{1,0:T(8,128)(2,1)}) custom-call(s32[5]{0:T(128)} %stack.23.place_ref.refs_0_, bf16[512,896]{1,0:T(8,128)(2,1)} %bitcast.11, bf16[512,896]{1,0:T(8,128)(2,1)} %get-tuple-element.402.o_ref, bf16[448,896]{1,0:T(8,128)(2,1)} %own_ref.1, bf16[448,896]{1,0:T(8,128)(2,1)} %copy-done.21, ...), custom_call_target="tpu_custom_call" | custom-call | flops 822083584 | bytes 6291456 | tf_op jit(solution)/shard_map/pallas_call | solution.py:447
  75.6 2.7 collective-permute-done.8.refs_2_
  79.2 37.4 %shard_map.258 = (bf16[4480,128]{1,0:T(8,128)(2,1)}, bf16[4480,128]{1,0:T(8,128)(2,1)}, bf16[4480,128]{1,0:T(8,128)(2,1)}, bf16[4480,128]{1,0:T(8,128)(2,1)}, bf...) custom-call(s32[5]{0:T(128)} %stack.23.place_ref.refs_0_, ...), custom_call_target="tpu_custom_call" | custom-call | flops 21139292160 | bytes 31457280 | tf_op jit(solution)/shard_map/pallas_call | solution.py:646
  119.7 2.5 collective-permute-start.14
  122.2 38.5 %shard_map.259 = (bf16[4032,128]{1,0:T(8,128)(2,1)}, bf16[4032,128]{1,0:T(8,128)(2,1)}, bf16[4032,128]{1,0:T(8,128)(2,1)}, bf16[4032,128]{1,0:T(8,128)(2,1)}, bf...) custom-call(s32[5]{0:T(128)} %stack.23.place_ref.refs_0_, ...), custom_call_target="tpu_custom_call" | custom-call | flops 19025362944 | bytes 31457280 | tf_op jit(solution)/shard_map/pallas_call | solution.py:646
  162.6 5.4 %shard_map.260 = (bf16[2240,128]{1,0:T(8,128)(2,1)}, bf16[2240,128]{1,0:T(8,128)(2,1)}, bf16[2240,128]{1,0:T(8,128)(2,1)}, bf16[2240,128]{1,0:T(8,128)(2,1)}, bf...) custom-call(s32[5]{0:T(128)} %stack.23.place_ref.refs_0_, bf16[4480,128]{1,0:T(8,128)(2,1)} %get-tuple-element.380.refs_0_, ...), custom_call_target="tpu_custom_call" | custom-call | flops 3440640 | bytes 10321920 | tf_op jit(solution)/shard_map/pallas_call | solution.py:910
  169.9 8.8 %shard_map.261 = (f32[512,896]{1,0:T(8,128)}, bf16[512,896]{1,0:T(8,128)(2,1)}, f32[1,896]{1,0:T(1,128)}, bf16[3136,128]{1,0:T(8,128)(2,1)}, bf16[3136,128]{1,0:T(8,128)(2,1)}) custom-call(s32[5]{0:T(128)} %stack.23.place_ref.refs_0_, bf16[512,896]{1,0:T(8,128)(2,1)} %get-tuple-element.396.part_ref, bf16[512,896]{1,0:T(8,128)(2,1)} %copy-done.19, ...), custom_call_target="tpu_custom_call" | custom-call | flops 1644167168 | bytes 12582912 | tf_op jit(solution)/shard_map/pallas_call | solution.py:707
  178.8 4.8 collective-permute-done.15.refs_1_
  184.8 3.4 shard_map.262
  188.2 1.6 collective-permute-start.19
  191.9 5.0 %collective-permute-done.19.refs_1_ = bf16[1120,128]{1,0:T(8,128)(2,1)S(1)} collective-permute-done((bf16[1120,128]{1,0:T(8,128)(2,1)}, bf16[1120,128]{1,0:T(8,128)(2,1)S(1)}, u32[]{:S(2)}, u32[]{:S(2)}) %collective-permute-start.19) | collective-permute-done | bytes 286752 | tf_op jit(solution)/shard_map/ppermute | solution.py:849
  198.6 2.5 shard_map.263.total
  201.1 3.3 collective-permute-start.22
  208.2 21.6 %shard_map.264 = (bf16[512,512]{1,0:T(8,128)(2,1)}, f32[2,1536,128]{2,1,0:T(8,128)}, f32[2,1536,128]{2,1,0:T(8,128)}) custom-call(s32[5]{0:T(128)} %stack.23.place_ref.refs_0_, bf16[512,896]{1,0:T(8,128)(2,1)} %get-tuple-element.456.q_ref.refs_1_, bf16[512,896]{1,0:T(8,128)(2,1)} %get-tuple-element.457.refs_2_, ...), custom_call_target="tpu_custom_call" | custom-call | flops 13421772800 | bytes 6291456 | tf_op jit(solution)/shard_map/pallas_call | solution.py:400
  229.8 16.6 %collective-permute-done.25.refs_5_ = bf16[4032,128]{1,0:T(8,128)(2,1)S(1)} collective-permute-done((bf16[4032,128]{1,0:T(8,128)(2,1)S(1)}, bf16[4032,128]{1,0:T(8,128)(2,1)S(1)}, u32[]{:S(2)}, u32[]{:S(2)}) %collective-permute-start.25) | collective-permute-done | bytes 1032224 | tf_op jit(solution)/shard_map/ppermute | solution.py:849
  247.3 5.1 %shard_map.265 = (bf16[2016,128]{1,0:T(8,128)(2,1)}, bf16[2016,128]{1,0:T(8,128)(2,1)}, bf16[2016,128]{1,0:T(8,128)(2,1)}, bf16[2016,128]{1,0:T(8,128)(2,1)}, bf...) custom-call(s32[5]{0:T(128)} %stack.23.place_ref.refs_0_, bf16[4032,128]{1,0:T(8,128)(2,1)} %get-tuple-element.448.refs_0_, ...), custom_call_target="tpu_custom_call" | custom-call | flops 3096576 | bytes 9289728 | tf_op jit(solution)/shard_map/pallas_call | solution.py:910
  254.4 18.4 %shard_map.266 = (bf16[512,384]{1,0:T(8,128)(2,1)}, f32[512,256]{1,0:T(8,128)}, bf16[512,256]{1,0:T(8,128)(2,1)}, bf16[512,256]{1,0:T(8,128)(2,1)}) custom-call(s32[5]{0:T(128)} %stack.23.place_ref.refs_0_, bf16[512,896]{1,0:T(8,128)(2,1)} %get-tuple-element.456.q_ref.refs_1_, bf16[512,896]{1,0:T(8,128)(2,1)} %get-tuple-element.457.refs_2_, ...), custom_call_target="tpu_custom_call" | custom-call | flops 10066329600 | bytes 6291456 | tf_op jit(solution)/shard_map/pallas_call | solution.py:400
  275.4 2.4 shard_map.267
  279.0 3.2 shard_map.268
  282.2 2.6 collective-permute-start.35
  286.9 6.7 %shard_map.269 = (f32[512,896]{1,0:T(8,128)}, f32[1,896]{1,0:T(1,128)}, bf16[3136,128]{1,0:T(8,128)(2,1)}, bf16[3136,128]{1,0:T(8,128)(2,1)}) custom-call(s32[5]{0:T(128)} %stack.23.place_ref.refs_0_, bf16[512,512]{1,0:T(8,128)(2,1)} %get-tuple-element.491.dqa_ref, bf16[512,384]{1,0:T(8,128)(2,1)} %get-tuple-element.492.dqb_ref, ...), custom_call_target="tpu_custom_call" | custom-call | flops 1644167168 | bytes 10485760 | tf_op jit(solution)/shard_map/pallas_call | solution.py:749
  294.6 2.4 shard_map.270
  297.8 8.8 %shard_map.271 = (bf16[512,896]{1,0:T(8,128)(2,1)}, bf16[7296,128]{1,0:T(8,128)(2,1)}, bf16[7296,128]{1,0:T(8,128)(2,1)}) custom-call(s32[5]{0:T(128)} %stack.23.place_ref.refs_0_, f32[512,256]{1,0:T(8,128)} %get-tuple-element.515.own_ref, bf16[512,256]{1,0:T(8,128)(2,1)} %copy-done.45, bf16[512,256]{1,0:T(8,128)(2,1)} %copy-done.46, ...), custom_call_target="tpu_custom_call" | custom-call | flops 469762048 | bytes 14680064 | tf_op jit(solution)/shard_map/pallas_call | solution.py:824
  306.6 3.6 collective-permute-start.39
  310.2 11.8 %collective-permute-done.39 = bf16[1008,128]{1,0:T(8,128)(2,1)S(1)} collective-permute-done((bf16[1008,128]{1,0:T(8,128)(2,1)S(1)}, bf16[1008,128]{1,0:T(8,128)(2,1)S(1)}, u32[]{:S(2)}, u32[]{:S(2)}) %collective-permute-start.39) | collective-permute-done | bytes 258080 | tf_op jit(solution)/shard_map/ppermute | solution.py:849
  323.4 3.8 shard_map.272
  327.8 1.6 collective-permute-start.41
  329.4 3.1 collective-permute-start.26
  333.1 9.8 %collective-permute-done.42 = bf16[1008,128]{1,0:T(8,128)(2,1)S(1)} collective-permute-done((bf16[1008,128]{1,0:T(8,128)(2,1)S(1)}, bf16[1008,128]{1,0:T(8,128)(2,1)S(1)}, u32[]{:S(2)}, u32[]{:S(2)}) %collective-permute-start.42) | collective-permute-done | bytes 258080 | tf_op jit(solution)/shard_map/ppermute | solution.py:849
  345.4 2.6 shard_map.273
  348.8 2.8 collective-permute-done.28.refs_3_
  352.3 2.6 shard_map.274
  357.8 1.6 collective-permute-start.45
  359.4 6.6 %collective-permute-done.47.refs_3_ = bf16[912,128]{1,0:T(8,128)(2,1)S(1)} collective-permute-done((bf16[912,128]{1,0:T(8,128)(2,1)}, bf16[912,128]{1,0:T(8,128)(2,1)S(1)}, u32[]{:S(2)}, u32[]{:S(2)}) %collective-permute-start.47) | collective-permute-done | bytes 233504 | tf_op jit(solution)/shard_map/ppermute | solution.py:849
  366.8 2.2 shard_map.275
  373.0 5.4 %collective-permute-done.45.refs_5_ = bf16[2240,128]{1,0:T(8,128)(2,1)S(1)} collective-permute-done((bf16[2240,128]{1,0:T(8,128)(2,1)}, bf16[2240,128]{1,0:T(8,128)(2,1)S(1)}, u32[]{:S(2)}, u32[]{:S(2)}) %collective-permute-start.45) | collective-permute-done | bytes 573472 | tf_op jit(solution)/shard_map/ppermute | solution.py:849
  379.2 3.8 shard_map.276
  383.1 2.9 collective-permute-done.53.refs_1_
  387.5 2.7 shard_map.277
  392.6 1.6 collective-permute-start.57
  396.0 6.1 %collective-permute-done.60.refs_1_ = bf16[2016,128]{1,0:T(8,128)(2,1)S(1)} collective-permute-done((bf16[2016,128]{1,0:T(8,128)(2,1)}, bf16[2016,128]{1,0:T(8,128)(2,1)S(1)}, u32[]{:S(2)}, u32[]{:S(2)}) %collective-permute-start.60) | collective-permute-done | bytes 516128 | tf_op jit(solution)/shard_map/ppermute | solution.py:849
  403.4 10.1 %collective-permute-done.57.got = bf16[1824,128]{1,0:T(8,128)(2,1)S(1)} collective-permute-done((bf16[1824,128]{1,0:T(8,128)(2,1)S(1)}, bf16[1824,128]{1,0:T(8,128)(2,1)S(1)}, u32[]{:S(2)}, u32[]{:S(2)}) %collective-permute-start.57) | collective-permute-done | bytes 466976 | tf_op jit(solution)/shard_map/ppermute | solution.py:849
  414.4 2.0 shard_map.278
  417.4 5.7 %collective-permute-done.62.refs_5_ = bf16[2016,128]{1,0:T(8,128)(2,1)} collective-permute-done((bf16[2016,128]{1,0:T(8,128)(2,1)}, bf16[2016,128]{1,0:T(8,128)(2,1)}, u32[]{:S(2)}, u32[]{:S(2)}) %collective-permute-start.62) | collective-permute-done | bytes 516128 | tf_op jit(solution)/shard_map/ppermute | solution.py:849
  424.1 3.6 shard_map.279
  427.7 4.4 collective-permute-done.58.refs_1_
  433.6 1.7 collective-permute-start.67
  435.3 2.3 shard_map.280
  437.6 2.0 collective-permute-start.63
  439.6 3.1 collective-permute-done.51.refs_6_
  443.7 9.3 %shard_map.281 = (f32[448,4864]{1,0:T(8,128)}, f32[448,4864]{1,0:T(8,128)}, f32[2432,896]{1,0:T(8,128)}) custom-call(s32[5]{0:T(128)} %stack.23.place_ref.refs_0_, bf16[4480,128]{1,0:T(8,128)(2,1)} %get-tuple-element.608.refs_1_, bf16[4480,128]{1,0:T(8,128)(2,1)} %copy-done.6, bf16[4480,128]{1,0:T(8,128)(2,1)} %get-tuple-element.610.refs_3_, ...), custom_call_target="tpu_custom_call" | custom-call | flops 3440640 | bytes 20643840 | tf_op jit(solution)/shard_map/pallas_call | solution.py:1047
  454.3 3.4 collective-permute-done.65.refs_2_
  458.3 3.6 collective-permute-done.67.refs_6_
  461.9 8.3 %shard_map.282 = (f32[448,4864]{1,0:T(8,128)}, f32[448,4864]{1,0:T(8,128)}, f32[2432,896]{1,0:T(8,128)}) custom-call(s32[5]{0:T(128)} %stack.23.place_ref.refs_0_, bf16[4032,128]{1,0:T(8,128)(2,1)} %get-tuple-element.624.refs_1_, bf16[4032,128]{1,0:T(8,128)(2,1)} %collective-permute-done.65.refs_2_, ...), custom_call_target="tpu_custom_call", output_to_operand_aliasing={{0}: (7, {}), {1}: (8, {}), {2}: (9, {})} | custom-call | flops 3096576 | bytes 18579456 | tf_op jit(solution)/shard_map/pallas_call | solution.py:1047
  471.1 4.0 shard_map.283
  (257 shorter events, 66.3 us)
Async XLA Ops:
  0.6 77.7 %collective-permute-start.10 = (bf16[448,4864]{1,0:T(8,128)(2,1)}, bf16[448,4864]{1,0:T(8,128)(2,1)}, u32[]{:S(2)}, u32[]{:S(2)}) collective-permute-start(bf16[448,4864]{1,0:T(8,128)(2,1)} %refs_7_.1), channel_id=1, source_target_pairs={{0,1},{1,0},{2,3},{3,2},{4,5},{5,4},{6,7},{7,6},{8,9},{9,8},{10,11... | collective-permute-start | bytes 13074440 | tf_op jit(solution)/shard_map/ppermute | solution.py:843
  1.2 77.2 %collective-permute-start.9 = (bf16[448,4864]{1,0:T(8,128)(2,1)}, bf16[448,4864]{1,0:T(8,128)(2,1)}, u32[]{:S(2)}, u32[]{:S(2)}) collective-permute-start(bf16[448,4864]{1,0:T(8,128)(2,1)} %refs_5_.1), channel_id=1, source_target_pairs={{0,1},{1,0},{2,3},{3,2},{4,5},{5,4},{6,7},{7,6},{8,9},{9,8},{10,11... | collective-permute-start | bytes 13074440 | tf_op jit(solution)/shard_map/ppermute | solution.py:843
  5.2 12.6 %collective-permute-start.1 = (bf16[448,896]{1,0:T(8,128)(2,1)}, bf16[448,896]{1,0:T(8,128)(2,1)S(1)}, u32[]{:S(2)}, u32[]{:S(2)}) collective-permute-start(bf16[448,896]{1,0:T(8,128)(2,1)} %wq_ref.1), channel_id=1, source_target_pairs={{0,1},{1,0},{2,3},{3,2},{4,5},{5,4},{6,7},{7,6},{8,9},{9,8},{10,11... | collective-permute-start | bytes 2408456 | tf_op jit(solution)/shard_map/ppermute | solution.py:843
  5.2 24.1 %collective-permute-start.6 = (bf16[512,896]{1,0:T(8,128)(2,1)}, bf16[512,896]{1,0:T(8,128)(2,1)S(1)}, u32[]{:S(2)}, u32[]{:S(2)}) collective-permute-start(bf16[512,896]{1,0:T(8,128)(2,1)} %bitcast.13), channel_id=1, source_target_pairs={{0,1},{1,0},{2,3},{3,2},{4,5},{5,4},{6,7},{7,6},{8,9},{9,8},{10,11... | collective-permute-start | bytes 2752520 | tf_op jit(solution)/shard_map/ppermute | solution.py:843
  8.2 5.4 %collective-permute-start.2 = (bf16[448,128]{1,0:T(8,128)(2,1)}, bf16[448,128]{1,0:T(8,128)(2,1)S(1)}, u32[]{:S(2)}, u32[]{:S(2)}) collective-permute-start(bf16[448,128]{1,0:T(8,128)(2,1)} %wk_ref.1), channel_id=1, source_target_pairs={{0,1},{1,0},{2,3},{3,2},{4,5},{5,4},{6,7},{7,6},{8,9},{9,8},{10,11... | collective-permute-start | bytes 344072 | tf_op jit(solution)/shard_map/ppermute | solution.py:843
  17.4 51.6 %collective-permute-start.7 = (bf16[448,896]{1,0:T(8,128)(2,1)}, bf16[448,896]{1,0:T(8,128)(2,1)S(1)}, u32[]{:S(2)}, u32[]{:S(2)}) collective-permute-start(bf16[448,896]{1,0:T(8,128)(2,1)} %own_ref.1), channel_id=1, source_target_pairs={{0,1},{1,0},{2,3},{3,2},{4,5},{5,4},{6,7},{7,6},{8,9},{9,8},{10,11... | collective-permute-start | bytes 2408456 | tf_op jit(solution)/shard_map/ppermute | solution.py:843
  24.7 21.3 %collective-permute-start.4 = (bf16[512,256]{1,0:T(8,128)(2,1)}, bf16[512,256]{1,0:T(8,128)(2,1)S(1)}, u32[]{:S(2)}, u32[]{:S(2)}) collective-permute-start(bf16[512,256]{1,0:T(8,128)(2,1)} %get-tuple-element.458.kv0_ref.refs_3_), channel_id=1, source_target_pairs={{0,2},{2,4},{4,6},{1,3},{3,5},{5,7},{8,10},{10,12},{12,14},{9,11},... | collective-permute-start | bytes 786440 | tf_op jit(solution)/shard_map/ppermute | solution.py:1280
  29.4 16.6 %collective-permute-start.5 = (bf16[512,256]{1,0:T(8,128)(2,1)}, bf16[512,256]{1,0:T(8,128)(2,1)S(1)}, u32[]{:S(2)}, u32[]{:S(2)}) collective-permute-start(bf16[512,256]{1,0:T(8,128)(2,1)} %get-tuple-element.458.kv0_ref.refs_3_), channel_id=1, source_target_pairs={{0,4},{2,6},{1,5},{3,7},{8,12},{10,14},{9,13},{11,15},{16,20},{18,... | collective-permute-start | bytes 786440 | tf_op jit(solution)/shard_map/ppermute | solution.py:1280
  116.6 44.1 %collective-permute-start.12 = (bf16[4480,128]{1,0:T(8,128)(2,1)}, bf16[4480,128]{1,0:T(8,128)(2,1)S(1)}, u32[]{:S(2)}, u32[]{:S(2)}) collective-permute-start(bf16[4480,128]{1,0:T(8,128)(2,1)} %get-tuple-element.374), channel_id=1, source_target_pairs={{0,8},{8,0},{16,24},{24,16},{1,9},{9,1},{17,25},{25,17},{2,10},{10... | collective-permute-start | bytes 3440648 | tf_op jit(solution)/shard_map/ppermute | solution.py:849
  118.2 42.6 %collective-permute-start.13 = (bf16[4480,128]{1,0:T(8,128)(2,1)}, bf16[4480,128]{1,0:T(8,128)(2,1)S(1)}, u32[]{:S(2)}, u32[]{:S(2)}) collective-permute-start(bf16[4480,128]{1,0:T(8,128)(2,1)} %get-tuple-element.376), channel_id=1, source_target_pairs={{0,16},{8,24},{16,0},{24,8},{1,17},{9,25},{17,1},{25,9},{2,18},{10... | collective-permute-start | bytes 3440648 | tf_op jit(solution)/shard_map/ppermute | solution.py:849
  119.7 41.1 %collective-permute-start.14 = (bf16[4480,128]{1,0:T(8,128)(2,1)}, bf16[4480,128]{1,0:T(8,128)(2,1)S(1)}, u32[]{:S(2)}, u32[]{:S(2)}) collective-permute-start(bf16[4480,128]{1,0:T(8,128)(2,1)} %get-tuple-element.378), channel_id=1, source_target_pairs={{0,2},{2,0},{4,6},{6,4},{1,3},{3,1},{5,7},{7,5},{8,10},{10,8},{12,... | collective-permute-start | bytes 3440648 | tf_op jit(solution)/shard_map/ppermute | solution.py:849
  160.7 8.3 %collective-permute-start.18 = (bf16[512,896]{1,0:T(8,128)(2,1)}, bf16[512,896]{1,0:T(8,128)(2,1)S(1)}, u32[]{:S(2)}, u32[]{:S(2)}) collective-permute-start(bf16[512,896]{1,0:T(8,128)(2,1)} %get-tuple-element.393), channel_id=1, source_target_pairs={{0,1},{1,0},{2,3},{3,2},{4,5},{5,4},{6,7},{7,6},{8,9},{9,8},{10,11... | collective-permute-start | bytes 2752520 | tf_op jit(solution)/shard_map/ppermute | solution.py:843
  168.0 15.6 %collective-permute-start.15 = (bf16[2240,128]{1,0:T(8,128)(2,1)}, bf16[2240,128]{1,0:T(8,128)(2,1)S(1)}, u32[]{:S(2)}, u32[]{:S(2)}) collective-permute-start(bf16[2240,128]{1,0:T(8,128)(2,1)} %get-tuple-element.387), channel_id=1, source_target_pairs={{0,16},{8,24},{16,0},{24,8},{1,17},{9,25},{17,1},{25,9},{2,18},{10... | collective-permute-start | bytes 1720328 | tf_op jit(solution)/shard_map/ppermute | solution.py:849
  168.5 15.3 %collective-permute-start.16 = (bf16[2240,128]{1,0:T(8,128)(2,1)}, bf16[2240,128]{1,0:T(8,128)(2,1)S(1)}, u32[]{:S(2)}, u32[]{:S(2)}) collective-permute-start(bf16[2240,128]{1,0:T(8,128)(2,1)} %get-tuple-element.389), channel_id=1, source_target_pairs={{0,2},{2,0},{4,6},{6,4},{1,3},{3,1},{5,7},{7,5},{8,10},{10,8},{12,... | collective-permute-start | bytes 1720328 | tf_op jit(solution)/shard_map/ppermute | solution.py:849
  168.5 15.3 %collective-permute-start.17 = (bf16[2240,128]{1,0:T(8,128)(2,1)}, bf16[2240,128]{1,0:T(8,128)(2,1)S(1)}, u32[]{:S(2)}, u32[]{:S(2)}) collective-permute-start(bf16[2240,128]{1,0:T(8,128)(2,1)} %get-tuple-element.391), channel_id=1, source_target_pairs={{0,8},{8,0},{16,24},{24,16},{1,9},{9,1},{17,25},{25,17},{2,10},{10... | collective-permute-start | bytes 1720328 | tf_op jit(solution)/shard_map/ppermute | solution.py:849
  188.2 8.7 %collective-permute-start.19 = (bf16[1120,128]{1,0:T(8,128)(2,1)}, bf16[1120,128]{1,0:T(8,128)(2,1)S(1)}, u32[]{:S(2)}, u32[]{:S(2)}) collective-permute-start(bf16[1120,128]{1,0:T(8,128)(2,1)} %get-tuple-element.411), channel_id=1, source_target_pairs={{0,2},{2,0},{4,6},{6,4},{1,3},{3,1},{5,7},{7,5},{8,10},{10,8},{12,... | collective-permute-start | bytes 860168 | tf_op jit(solution)/shard_map/ppermute | solution.py:849
  189.9 7.7 %collective-permute-start.20 = (bf16[1120,128]{1,0:T(8,128)(2,1)}, bf16[1120,128]{1,0:T(8,128)(2,1)S(1)}, u32[]{:S(2)}, u32[]{:S(2)}) collective-permute-start(bf16[1120,128]{1,0:T(8,128)(2,1)} %get-tuple-element.413), channel_id=1, source_target_pairs={{0,8},{8,0},{16,24},{24,16},{1,9},{9,1},{17,25},{25,17},{2,10},{10... | collective-permute-start | bytes 860168 | tf_op jit(solution)/shard_map/ppermute | solution.py:849
  190.4 7.5 %collective-permute-start.21 = (bf16[1120,128]{1,0:T(8,128)(2,1)}, bf16[1120,128]{1,0:T(8,128)(2,1)S(1)}, u32[]{:S(2)}, u32[]{:S(2)}) collective-permute-start(bf16[1120,128]{1,0:T(8,128)(2,1)} %get-tuple-element.415), channel_id=1, source_target_pairs={{0,16},{8,24},{16,0},{24,8},{1,17},{9,25},{17,1},{25,9},{2,18},{10... | collective-permute-start | bytes 860168 | tf_op jit(solution)/shard_map/ppermute | solution.py:849
  201.1 73.0 %collective-permute-start.22 = (bf16[3360,128]{1,0:T(8,128)(2,1)}, bf16[3360,128]{1,0:T(8,128)(2,1)S(1)}, u32[]{:S(2)}, u32[]{:S(2)}) collective-permute-start(bf16[3360,128]{1,0:T(8,128)(2,1)} %shard_map.263.total), channel_id=1, source_target_pairs={{0,4},{2,6},{4,0},{6,2},{1,5},{3,7},{5,1},{7,3},{8,12},{10,14},{12... | collective-permute-start | bytes 2580488 | tf_op jit(solution)/shard_map/ppermute | solution.py:849
  204.3 25.4 %collective-permute-start.23 = (bf16[4032,128]{1,0:T(8,128)(2,1)}, bf16[4032,128]{1,0:T(8,128)(2,1)S(1)}, u32[]{:S(2)}, u32[]{:S(2)}) collective-permute-start(bf16[4032,128]{1,0:T(8,128)(2,1)} %get-tuple-element.442), channel_id=1, source_target_pairs={{0,8},{8,0},{16,24},{24,16},{1,9},{9,1},{17,25},{25,17},{2,10},{10... | collective-permute-start | bytes 3096584 | tf_op jit(solution)/shard_map/ppermute | solution.py:849
  205.8 23.9 %collective-permute-start.24 = (bf16[4032,128]{1,0:T(8,128)(2,1)S(1)}, bf16[4032,128]{1,0:T(8,128)(2,1)S(1)}, u32[]{:S(2)}, u32[]{:S(2)}) collective-permute-start(bf16[4032,128]{1,0:T(8,128)(2,1)S(1)} %copy-done.59), channel_id=1, source_target_pairs={{0,16},{8,24},{16,0},{24,8},{1,17},{9,25},{17,1},{25,9},{2,18},{10... | collective-permute-start | bytes 3096584 | tf_op jit(solution)/shard_map/ppermute | solution.py:849
  207.4 39.0 %collective-permute-start.25 = (bf16[4032,128]{1,0:T(8,128)(2,1)S(1)}, bf16[4032,128]{1,0:T(8,128)(2,1)S(1)}, u32[]{:S(2)}, u32[]{:S(2)}) collective-permute-start(bf16[4032,128]{1,0:T(8,128)(2,1)S(1)} %copy-done.58), channel_id=1, source_target_pairs={{0,2},{2,0},{4,6},{6,4},{1,3},{3,1},{5,7},{7,5},{8,10},{10,8},{12,... | collective-permute-start | bytes 3096584 | tf_op jit(solution)/shard_map/ppermute | solution.py:849
  252.4 25.4 %collective-permute-start.32 = (bf16[2016,128]{1,0:T(8,128)(2,1)}, bf16[2016,128]{1,0:T(8,128)(2,1)S(1)}, u32[]{:S(2)}, u32[]{:S(2)}) collective-permute-start(bf16[2016,128]{1,0:T(8,128)(2,1)} %get-tuple-element.478), channel_id=1, source_target_pairs={{0,16},{8,24},{16,0},{24,8},{1,17},{9,25},{17,1},{25,9},{2,18},{10... | collective-permute-start | bytes 1548296 | tf_op jit(solution)/shard_map/ppermute | solution.py:849
  253.2 24.7 %collective-permute-start.33 = (bf16[2016,128]{1,0:T(8,128)(2,1)}, bf16[2016,128]{1,0:T(8,128)(2,1)S(1)}, u32[]{:S(2)}, u32[]{:S(2)}) collective-permute-start(bf16[2016,128]{1,0:T(8,128)(2,1)} %get-tuple-element.480), channel_id=1, source_target_pairs={{0,2},{2,0},{4,6},{6,4},{1,3},{3,1},{5,7},{7,5},{8,10},{10,8},{12,... | collective-permute-start | bytes 1548296 | tf_op jit(solution)/shard_map/ppermute | solution.py:849
  253.2 24.7 %collective-permute-start.34 = (bf16[2016,128]{1,0:T(8,128)(2,1)}, bf16[2016,128]{1,0:T(8,128)(2,1)S(1)}, u32[]{:S(2)}, u32[]{:S(2)}) collective-permute-start(bf16[2016,128]{1,0:T(8,128)(2,1)} %get-tuple-element.482), channel_id=1, source_target_pairs={{0,8},{8,0},{16,24},{24,16},{1,9},{9,1},{17,25},{25,17},{2,10},{10... | collective-permute-start | bytes 1548296 | tf_op jit(solution)/shard_map/ppermute | solution.py:849
  272.8 24.2 %collective-permute-start.30 = (bf16[512,256]{1,0:T(8,128)(2,1)}, bf16[512,256]{1,0:T(8,128)(2,1)S(1)}, u32[]{:S(2)}, u32[]{:S(2)}) collective-permute-start(bf16[512,256]{1,0:T(8,128)(2,1)} %get-tuple-element.474), channel_id=1, source_target_pairs={{2,0},{4,2},{6,4},{3,1},{5,3},{7,5},{10,8},{12,10},{14,12},{11,9},... | collective-permute-start | bytes 786440 | tf_op jit(solution)/shard_map/ppermute | solution.py:1335
  274.1 22.9 %collective-permute-start.31 = (bf16[512,256]{1,0:T(8,128)(2,1)}, bf16[512,256]{1,0:T(8,128)(2,1)S(1)}, u32[]{:S(2)}, u32[]{:S(2)}) collective-permute-start(bf16[512,256]{1,0:T(8,128)(2,1)} %get-tuple-element.475), channel_id=1, source_target_pairs={{4,0},{6,2},{5,1},{7,3},{12,8},{14,10},{13,9},{15,11},{20,16},{22,... | collective-permute-start | bytes 786440 | tf_op jit(solution)/shard_map/ppermute | solution.py:1335
  282.2 11.5 %collective-permute-start.35 = (bf16[1008,128]{1,0:T(8,128)(2,1)}, bf16[1008,128]{1,0:T(8,128)(2,1)S(1)}, u32[]{:S(2)}, u32[]{:S(2)}) collective-permute-start(bf16[1008,128]{1,0:T(8,128)(2,1)} %get-tuple-element.502), channel_id=1, source_target_pairs={{0,2},{2,0},{4,6},{6,4},{1,3},{3,1},{5,7},{7,5},{8,10},{10,8},{12,... | collective-permute-start | bytes 774152 | tf_op jit(solution)/shard_map/ppermute | solution.py:849
  284.9 8.8 %collective-permute-start.36 = (bf16[1008,128]{1,0:T(8,128)(2,1)}, bf16[1008,128]{1,0:T(8,128)(2,1)S(1)}, u32[]{:S(2)}, u32[]{:S(2)}) collective-permute-start(bf16[1008,128]{1,0:T(8,128)(2,1)} %get-tuple-element.504), channel_id=1, source_target_pairs={{0,8},{8,0},{16,24},{24,16},{1,9},{9,1},{17,25},{25,17},{2,10},{10... | collective-permute-start | bytes 774152 | tf_op jit(solution)/shard_map/ppermute | solution.py:849
  285.7 8.0 %collective-permute-start.37 = (bf16[1008,128]{1,0:T(8,128)(2,1)}, bf16[1008,128]{1,0:T(8,128)(2,1)S(1)}, u32[]{:S(2)}, u32[]{:S(2)}) collective-permute-start(bf16[1008,128]{1,0:T(8,128)(2,1)} %get-tuple-element.506), channel_id=1, source_target_pairs={{0,16},{8,24},{16,0},{24,8},{1,17},{9,25},{17,1},{25,9},{2,18},{10... | collective-permute-start | bytes 774152 | tf_op jit(solution)/shard_map/ppermute | solution.py:849
  306.6 15.5 %collective-permute-start.38 = (bf16[7296,128]{1,0:T(8,128)(2,1)}, bf16[7296,128]{1,0:T(8,128)(2,1)S(1)}, u32[]{:S(2)}, u32[]{:S(2)}) collective-permute-start(bf16[7296,128]{1,0:T(8,128)(2,1)} %get-tuple-element.533), channel_id=1, source_target_pairs={{0,1},{1,0},{2,3},{3,2},{4,5},{5,4},{6,7},{7,6},{8,9},{9,8},{10,11... | collective-permute-start | bytes 5603336 | tf_op jit(solution)/shard_map/ppermute | solution.py:843
  306.6 15.4 %collective-permute-start.39 = (bf16[1008,128]{1,0:T(8,128)(2,1)S(1)}, bf16[1008,128]{1,0:T(8,128)(2,1)S(1)}, u32[]{:S(2)}, u32[]{:S(2)}) collective-permute-start(bf16[1008,128]{1,0:T(8,128)(2,1)S(1)} %copy-done.49), channel_id=1, source_target_pairs={{0,4},{2,6},{4,0},{6,2},{1,5},{3,7},{5,1},{7,3},{8,12},{10,14},{12... | collective-permute-start | bytes 774152 | tf_op jit(solution)/shard_map/ppermute | solution.py:849
  327.2 17.2 %collective-permute-start.40 = (bf16[1824,128]{1,0:T(8,128)(2,1)}, bf16[1824,128]{1,0:T(8,128)(2,1)S(1)}, u32[]{:S(2)}, u32[]{:S(2)}) collective-permute-start(bf16[1824,128]{1,0:T(8,128)(2,1)} %get-tuple-element.541), channel_id=1, source_target_pairs={{0,8},{8,0},{16,24},{24,16},{1,9},{9,1},{17,25},{25,17},{2,10},{10... | collective-permute-start | bytes 1400840 | tf_op jit(solution)/shard_map/ppermute | solution.py:849
  327.7 15.2 %collective-permute-start.42 = (bf16[1008,128]{1,0:T(8,128)(2,1)S(1)}, bf16[1008,128]{1,0:T(8,128)(2,1)S(1)}, u32[]{:S(2)}, u32[]{:S(2)}) collective-permute-start(bf16[1008,128]{1,0:T(8,128)(2,1)S(1)} %copy-done.48), channel_id=1, source_target_pairs={{0,4},{2,6},{4,0},{6,2},{1,5},{3,7},{5,1},{7,3},{8,12},{10,14},{12... | collective-permute-start | bytes 774152 | tf_op jit(solution)/shard_map/ppermute | solution.py:849
  327.8 16.8 %collective-permute-start.41 = (bf16[1824,128]{1,0:T(8,128)(2,1)}, bf16[1824,128]{1,0:T(8,128)(2,1)S(1)}, u32[]{:S(2)}, u32[]{:S(2)}) collective-permute-start(bf16[1824,128]{1,0:T(8,128)(2,1)} %get-tuple-element.543), channel_id=1, source_target_pairs={{0,16},{8,24},{16,0},{24,8},{1,17},{9,25},{17,1},{25,9},{2,18},{10... | collective-permute-start | bytes 1400840 | tf_op jit(solution)/shard_map/ppermute | solution.py:849
  329.4 19.4 %collective-permute-start.26 = (bf16[1120,128]{1,0:T(8,128)(2,1)S(1)}, bf16[1120,128]{1,0:T(8,128)(2,1)S(1)}, u32[]{:S(2)}, u32[]{:S(2)}) collective-permute-start(bf16[1120,128]{1,0:T(8,128)(2,1)S(1)} %copy-done.39), channel_id=1, source_target_pairs={{0,2},{2,0},{4,6},{6,4},{1,3},{3,1},{5,7},{7,5},{8,10},{10,8},{12,... | collective-permute-start | bytes 860168 | tf_op jit(solution)/shard_map/ppermute | solution.py:849
  332.5 16.3 %collective-permute-start.29 = (bf16[1120,128]{1,0:T(8,128)(2,1)S(1)}, bf16[1120,128]{1,0:T(8,128)(2,1)S(1)}, u32[]{:S(2)}, u32[]{:S(2)}) collective-permute-start(bf16[1120,128]{1,0:T(8,128)(2,1)S(1)} %copy-done.40), channel_id=1, source_target_pairs={{0,16},{8,24},{16,0},{24,8},{1,17},{9,25},{17,1},{25,9},{2,18},{10... | collective-permute-start | bytes 860168 | tf_op jit(solution)/shard_map/ppermute | solution.py:849
  342.9 8.7 %collective-permute-start.28 = (bf16[1120,128]{1,0:T(8,128)(2,1)S(1)}, bf16[1120,128]{1,0:T(8,128)(2,1)S(1)}, u32[]{:S(2)}, u32[]{:S(2)}) collective-permute-start(bf16[1120,128]{1,0:T(8,128)(2,1)S(1)} %collective-permute-done.27.refs_2_), channel_id=1, source_target_pairs={{0,8},{8,0},{16,24},{24,16},{1,9},{9,1},{17,25},{25,17},{2,10},{10... | collective-permute-start | bytes 860168 | tf_op jit(solution)/shard_map/ppermute | solution.py:849
  344.4 12.9 %collective-permute-start.48 = (bf16[1008,128]{1,0:T(8,128)(2,1)S(1)}, bf16[1008,128]{1,0:T(8,128)(2,1)S(1)}, u32[]{:S(2)}, u32[]{:S(2)}) collective-permute-start(bf16[1008,128]{1,0:T(8,128)(2,1)S(1)} %copy-done.47), channel_id=1, source_target_pairs={{0,4},{2,6},{4,0},{6,2},{1,5},{3,7},{5,1},{7,3},{8,12},{10,14},{12... | collective-permute-start | bytes 774152 | tf_op jit(solution)/shard_map/ppermute | solution.py:849
  348.0 9.8 %collective-permute-start.46 = (bf16[912,128]{1,0:T(8,128)(2,1)}, bf16[912,128]{1,0:T(8,128)(2,1)S(1)}, u32[]{:S(2)}, u32[]{:S(2)}) collective-permute-start(bf16[912,128]{1,0:T(8,128)(2,1)} %get-tuple-element.561), channel_id=1, source_target_pairs={{0,16},{8,24},{16,0},{24,8},{1,17},{9,25},{17,1},{25,9},{2,18},{10... | collective-permute-start | bytes 700424 | tf_op jit(solution)/shard_map/ppermute | solution.py:849
  354.9 16.1 %collective-permute-start.43 = (bf16[2240,128]{1,0:T(8,128)(2,1)}, bf16[2240,128]{1,0:T(8,128)(2,1)S(1)}, u32[]{:S(2)}, u32[]{:S(2)}) collective-permute-start(bf16[2240,128]{1,0:T(8,128)(2,1)} %get-tuple-element.571.refs_0_), channel_id=1, source_target_pairs={{0,16},{8,24},{16,0},{24,8},{1,17},{9,25},{17,1},{25,9},{2,18},{10... | collective-permute-start | bytes 1720328 | tf_op jit(solution)/shard_map/ppermute | solution.py:849
  356.4 15.1 %collective-permute-start.44 = (bf16[2240,128]{1,0:T(8,128)(2,1)}, bf16[2240,128]{1,0:T(8,128)(2,1)S(1)}, u32[]{:S(2)}, u32[]{:S(2)}) collective-permute-start(bf16[2240,128]{1,0:T(8,128)(2,1)} %get-tuple-element.573.refs_2_), channel_id=1, source_target_pairs={{0,2},{2,0},{4,6},{6,4},{1,3},{3,1},{5,7},{7,5},{8,10},{10,8},{12,... | collective-permute-start | bytes 1720328 | tf_op jit(solution)/shard_map/ppermute | solution.py:849
  356.4 13.6 %collective-permute-start.54 = (bf16[1008,128]{1,0:T(8,128)(2,1)S(1)}, bf16[1008,128]{1,0:T(8,128)(2,1)}, u32[]{:S(2)}, u32[]{:S(2)}) collective-permute-start(bf16[1008,128]{1,0:T(8,128)(2,1)S(1)} %add_convert_fusion.3), channel_id=1, source_target_pairs={{0,1},{1,0},{2,3},{3,2},{4,5},{5,4},{6,7},{7,6},{8,9},{9,8},{10,11... | collective-permute-start | bytes 774152 | tf_op jit(solution)/shard_map/ppermute | solution.py:843
  357.3 8.8 %collective-permute-start.47 = (bf16[912,128]{1,0:T(8,128)(2,1)}, bf16[912,128]{1,0:T(8,128)(2,1)S(1)}, u32[]{:S(2)}, u32[]{:S(2)}) collective-permute-start(bf16[912,128]{1,0:T(8,128)(2,1)} %get-tuple-element.563), channel_id=1, source_target_pairs={{0,8},{8,0},{16,24},{24,16},{1,9},{9,1},{17,25},{25,17},{2,10},{10... | collective-permute-start | bytes 700424 | tf_op jit(solution)/shard_map/ppermute | solution.py:849
  357.8 20.6 %collective-permute-start.45 = (bf16[2240,128]{1,0:T(8,128)(2,1)}, bf16[2240,128]{1,0:T(8,128)(2,1)S(1)}, u32[]{:S(2)}, u32[]{:S(2)}) collective-permute-start(bf16[2240,128]{1,0:T(8,128)(2,1)} %get-tuple-element.575.refs_4_), channel_id=1, source_target_pairs={{0,8},{8,0},{16,24},{24,16},{1,9},{9,1},{17,25},{25,17},{2,10},{10... | collective-permute-start | bytes 1720328 | tf_op jit(solution)/shard_map/ppermute | solution.py:849
  369.0 22.5 %collective-permute-start.52 = (bf16[1824,128]{1,0:T(8,128)(2,1)}, bf16[1824,128]{1,0:T(8,128)(2,1)}, u32[]{:S(2)}, u32[]{:S(2)}) collective-permute-start(bf16[1824,128]{1,0:T(8,128)(2,1)} %shard_map.275), channel_id=1, source_target_pairs={{0,2},{2,0},{4,6},{6,4},{1,3},{3,1},{5,7},{7,5},{8,10},{10,8},{12,... | collective-permute-start | bytes 1400840 | tf_op jit(solution)/shard_map/ppermute | solution.py:849
  370.0 15.9 %collective-permute-start.53 = (bf16[1008,128]{1,0:T(8,128)(2,1)S(1)}, bf16[1008,128]{1,0:T(8,128)(2,1)S(1)}, u32[]{:S(2)}, u32[]{:S(2)}) collective-permute-start(bf16[1008,128]{1,0:T(8,128)(2,1)S(1)} %add_convert_fusion.4.refs_0_), channel_id=1, source_target_pairs={{0,2},{2,0},{4,6},{6,4},{1,3},{3,1},{5,7},{7,5},{8,10},{10,8},{12,... | collective-permute-start | bytes 774152 | tf_op jit(solution)/shard_map/ppermute | solution.py:849
  371.0 16.5 %collective-permute-start.55 = (bf16[1008,128]{1,0:T(8,128)(2,1)}, bf16[1008,128]{1,0:T(8,128)(2,1)}, u32[]{:S(2)}, u32[]{:S(2)}) collective-permute-start(bf16[1008,128]{1,0:T(8,128)(2,1)} %collective-permute-done.54.refs_2_), channel_id=1, source_target_pairs={{0,8},{8,0},{16,24},{24,16},{1,9},{9,1},{17,25},{25,17},{2,10},{10... | collective-permute-start | bytes 774152 | tf_op jit(solution)/shard_map/ppermute | solution.py:849
  371.5 16.0 %collective-permute-start.56 = (bf16[1008,128]{1,0:T(8,128)(2,1)S(1)}, bf16[1008,128]{1,0:T(8,128)(2,1)}, u32[]{:S(2)}, u32[]{:S(2)}) collective-permute-start(bf16[1008,128]{1,0:T(8,128)(2,1)S(1)} %add_convert_fusion.2.refs_4_), channel_id=1, source_target_pairs={{0,16},{8,24},{16,0},{24,8},{1,17},{9,25},{17,1},{25,9},{2,18},{10... | collective-permute-start | bytes 774152 | tf_op jit(solution)/shard_map/ppermute | solution.py:849
  378.4 16.8 %collective-permute-start.11 = (bf16[512,896]{1,0:T(8,128)(2,1)}, bf16[512,896]{1,0:T(8,128)(2,1)S(1)}, u32[]{:S(2)}, u32[]{:S(2)}) collective-permute-start(bf16[512,896]{1,0:T(8,128)(2,1)} %get-tuple-element.373), channel_id=1, source_target_pairs={{0,1},{1,0},{2,3},{3,2},{4,5},{5,4},{6,7},{7,6},{8,9},{9,8},{10,11... | collective-permute-start | bytes 2752520 | tf_op jit(solution)/shard_map/ppermute | solution.py:843
  386.6 46.9 %collective-permute-start.49 = (bf16[4480,128]{1,0:T(8,128)(2,1)}, bf16[4480,128]{1,0:T(8,128)(2,1)S(1)}, u32[]{:S(2)}, u32[]{:S(2)}) collective-permute-start(bf16[4480,128]{1,0:T(8,128)(2,1)} %get-tuple-element.608.refs_1_), channel_id=1, source_target_pairs={{0,8},{8,0},{16,24},{24,16},{1,9},{9,1},{17,25},{25,17},{2,10},{10... | collective-permute-start | bytes 3440648 | tf_op jit(solution)/shard_map/ppermute | solution.py:849
  390.2 11.9 %collective-permute-start.60 = (bf16[2016,128]{1,0:T(8,128)(2,1)}, bf16[2016,128]{1,0:T(8,128)(2,1)S(1)}, u32[]{:S(2)}, u32[]{:S(2)}) collective-permute-start(bf16[2016,128]{1,0:T(8,128)(2,1)} %get-tuple-element.595.refs_0_), channel_id=1, source_target_pairs={{0,16},{8,24},{16,0},{24,8},{1,17},{9,25},{17,1},{25,9},{2,18},{10... | collective-permute-start | bytes 1548296 | tf_op jit(solution)/shard_map/ppermute | solution.py:849
  392.6 21.0 %collective-permute-start.57 = (bf16[1824,128]{1,0:T(8,128)(2,1)S(1)}, bf16[1824,128]{1,0:T(8,128)(2,1)S(1)}, u32[]{:S(2)}, u32[]{:S(2)}) collective-permute-start(bf16[1824,128]{1,0:T(8,128)(2,1)S(1)} %add_convert_fusion.1.total), channel_id=1, source_target_pairs={{0,4},{2,6},{4,0},{6,2},{1,5},{3,7},{5,1},{7,3},{8,12},{10,14},{12... | collective-permute-start | bytes 1400840 | tf_op jit(solution)/shard_map/ppermute | solution.py:849
  394.2 22.2 %collective-permute-start.61 = (bf16[2016,128]{1,0:T(8,128)(2,1)}, bf16[2016,128]{1,0:T(8,128)(2,1)}, u32[]{:S(2)}, u32[]{:S(2)}) collective-permute-start(bf16[2016,128]{1,0:T(8,128)(2,1)} %get-tuple-element.597.refs_2_), channel_id=1, source_target_pairs={{0,2},{2,0},{4,6},{6,4},{1,3},{3,1},{5,7},{7,5},{8,10},{10,8},{12,... | collective-permute-start | bytes 1548296 | tf_op jit(solution)/shard_map/ppermute | solution.py:849
  395.2 27.9 %collective-permute-start.62 = (bf16[2016,128]{1,0:T(8,128)(2,1)}, bf16[2016,128]{1,0:T(8,128)(2,1)}, u32[]{:S(2)}, u32[]{:S(2)}) collective-permute-start(bf16[2016,128]{1,0:T(8,128)(2,1)} %get-tuple-element.599.refs_4_), channel_id=1, source_target_pairs={{0,8},{8,0},{16,24},{24,16},{1,9},{9,1},{17,25},{25,17},{2,10},{10... | collective-permute-start | bytes 1548296 | tf_op jit(solution)/shard_map/ppermute | solution.py:849
  402.1 35.5 %collective-permute-start.50 = (bf16[4480,128]{1,0:T(8,128)(2,1)S(1)}, bf16[4480,128]{1,0:T(8,128)(2,1)S(1)}, u32[]{:S(2)}, u32[]{:S(2)}) collective-permute-start(bf16[4480,128]{1,0:T(8,128)(2,1)S(1)} %copy-done.4), channel_id=1, source_target_pairs={{0,16},{8,24},{16,0},{24,8},{1,17},{9,25},{17,1},{25,9},{2,18},{10... | collective-permute-start | bytes 3440648 | tf_op jit(solution)/shard_map/ppermute | solution.py:849
  414.4 28.3 %collective-permute-start.51 = (bf16[4480,128]{1,0:T(8,128)(2,1)S(1)}, bf16[4480,128]{1,0:T(8,128)(2,1)}, u32[]{:S(2)}, u32[]{:S(2)}) collective-permute-start(bf16[4480,128]{1,0:T(8,128)(2,1)S(1)} %copy-done.5), channel_id=1, source_target_pairs={{0,2},{2,0},{4,6},{6,4},{1,3},{3,1},{5,7},{7,5},{8,10},{10,8},{12,... | collective-permute-start | bytes 3440648 | tf_op jit(solution)/shard_map/ppermute | solution.py:849
  416.4 15.7 %collective-permute-start.58 = (bf16[912,128]{1,0:T(8,128)(2,1)}, bf16[912,128]{1,0:T(8,128)(2,1)S(1)}, u32[]{:S(2)}, u32[]{:S(2)}) collective-permute-start(bf16[912,128]{1,0:T(8,128)(2,1)} %get-tuple-element.602.refs_0_), channel_id=1, source_target_pairs={{0,16},{8,24},{16,0},{24,8},{1,17},{9,25},{17,1},{25,9},{2,18},{10... | collective-permute-start | bytes 700424 | tf_op jit(solution)/shard_map/ppermute | solution.py:849
  423.1 9.1 %collective-permute-start.59 = (bf16[912,128]{1,0:T(8,128)(2,1)}, bf16[912,128]{1,0:T(8,128)(2,1)S(1)}, u32[]{:S(2)}, u32[]{:S(2)}) collective-permute-start(bf16[912,128]{1,0:T(8,128)(2,1)} %get-tuple-element.604.refs_2_), channel_id=1, source_target_pairs={{0,8},{8,0},{16,24},{24,16},{1,9},{9,1},{17,25},{25,17},{2,10},{10... | collective-permute-start | bytes 700424 | tf_op jit(solution)/shard_map/ppermute | solution.py:849
  432.1 25.6 %collective-permute-start.65 = (bf16[4032,128]{1,0:T(8,128)(2,1)}, bf16[4032,128]{1,0:T(8,128)(2,1)}, u32[]{:S(2)}, u32[]{:S(2)}) collective-permute-start(bf16[4032,128]{1,0:T(8,128)(2,1)} %get-tuple-element.624.refs_1_), channel_id=1, source_target_pairs={{0,8},{8,0},{16,24},{24,16},{1,9},{9,1},{17,25},{25,17},{2,10},{10... | collective-permute-start | bytes 3096584 | tf_op jit(solution)/shard_map/ppermute | solution.py:849
  432.3 26.1 %collective-permute-start.66 = (bf16[4032,128]{1,0:T(8,128)(2,1)}, bf16[4032,128]{1,0:T(8,128)(2,1)}, u32[]{:S(2)}, u32[]{:S(2)}) collective-permute-start(bf16[4032,128]{1,0:T(8,128)(2,1)} %get-tuple-element.626.refs_3_), channel_id=1, source_target_pairs={{0,16},{8,24},{16,0},{24,8},{1,17},{9,25},{17,1},{25,9},{2,18},{10... | collective-permute-start | bytes 3096584 | tf_op jit(solution)/shard_map/ppermute | solution.py:849
  433.6 28.4 %collective-permute-start.67 = (bf16[4032,128]{1,0:T(8,128)(2,1)}, bf16[4032,128]{1,0:T(8,128)(2,1)}, u32[]{:S(2)}, u32[]{:S(2)}) collective-permute-start(bf16[4032,128]{1,0:T(8,128)(2,1)} %get-tuple-element.628.refs_5_), channel_id=1, source_target_pairs={{0,2},{2,0},{4,6},{6,4},{1,3},{3,1},{5,7},{7,5},{8,10},{10,8},{12,... | collective-permute-start | bytes 3096584 | tf_op jit(solution)/shard_map/ppermute | solution.py:849
  437.6 32.6 %collective-permute-start.63 = (bf16[1824,128]{1,0:T(8,128)(2,1)}, bf16[1824,128]{1,0:T(8,128)(2,1)}, u32[]{:S(2)}, u32[]{:S(2)}) collective-permute-start(bf16[1824,128]{1,0:T(8,128)(2,1)} %get-tuple-element.635.refs_1_), channel_id=1, source_target_pairs={{0,8},{8,0},{16,24},{24,16},{1,9},{9,1},{17,25},{25,17},{2,10},{10... | collective-permute-start | bytes 1400840 | tf_op jit(solution)/shard_map/ppermute | solution.py:849
  442.7 27.6 %collective-permute-start.64 = (bf16[1824,128]{1,0:T(8,128)(2,1)}, bf16[1824,128]{1,0:T(8,128)(2,1)S(1)}, u32[]{:S(2)}, u32[]{:S(2)}) collective-permute-start(bf16[1824,128]{1,0:T(8,128)(2,1)} %get-tuple-element.637.refs_3_), channel_id=1, source_target_pairs={{0,16},{8,24},{16,0},{24,8},{1,17},{9,25},{17,1},{25,9},{2,18},{10... | collective-permute-start | bytes 1400840 | tf_op jit(solution)/shard_map/ppermute | solution.py:849
  (72 other events, 473.7 us)

commit v5 on v4

--- a/solution.py
+++ b/solution.py
@@ -21,7 +21,7 @@
 f32 = jnp.float32
 bf16 = jnp.bfloat16
 VMEM_BYTES = 58 * 1024 * 1024
-WIDTHS = (1280, 1152)
+WIDTHS = (1408, 1024)
 
 
 def nn(a, b):

time: 482 us -> 497 us (1.031)
  waiting for transfers between devices: 115 us -> 135 us
    ppermute x50, waiting for transfers between devices: 105 us -> 123 us  [flip(): return lax.ppermute(values, axis, [(i, i ^ 1 << bit) for i in range(size)])]
    unnamed x136 -> x138, local copies, waits for them, and re-layouts: 18.2 us -> 16.8 us
  transfers between devices with their start and end apart: 68 -> 68, of which waited for: 24 -> 24; matrix products, arithmetic and copies ran while one was open for 2% -> 2% of each run, Pallas kernels for 41% -> 39%
where the time goes in v5:
time: 497 us; the launch traced here: 494 us
  Pallas kernels  258 us (52%)
  waiting for transfers between devices  135 us (27%)
  starting transfers between devices  70.8 us (14%)
  local copies, waits for them, and re-layouts  24.7 us (5%)
    ppermute x50, waiting for transfers between devices, flip(): return lax.ppermute(values, axis, [(i, i ^ 1 << bit) for i in range(size)])  123 us
    pallas_call x2, Pallas kernels, feed(): call(functools.partial(feed_kernel, start=start, first=first, sides=sides...  75.4 us
    ppermute x50, starting transfers between devices, flip(): return lax.ppermute(values, axis, [(i, i ^ 1 << bit) for i in range(size)])  55.9 us
    pallas_call x2, Pallas kernels, attend_back(): call(functools.partial(attend_back_kernel, first_pair=first_pair, first=f...  40.3 us
    pallas_call x1, Pallas kernels, attend(): call(attend_kernel, (jax.ShapeDtypeStruct((count, HQ * HD), bf16), jax.Sh...  22.3 us
    pallas_call x5, Pallas kernels, fold(): call(functools.partial(fold_kernel, sides=sides), tuple((jax.ShapeDtypeSt...  19.7 us
    pallas_call x2, Pallas kernels, untile(): call(functools.partial(untile_kernel, start=start, width=width, first=fir...  17.5 us
    unnamed x138, local copies, waits for them, and re-layouts  16.8 us
  transfers between devices with their start and end apart: 68, of which 24 were waited for; matrix products, arithmetic and copies ran while one was open for 2% of the time, Pallas kernels for 39%

profile of v5, /device:TPU:0, one launch (start us, length us, event | category | flops | bytes accessed | tf_op | source)
XLA Modules:
  0.0 493.8 jit_solution(4113863002527786745)
XLA Ops:
  1.2 3.5 concatenate.6
  5.8 1.8 multiply_sine_fusion
  8.7 5.0 %collective-permute-done.2.ok_ref = bf16[448,128]{1,0:T(8,128)(2,1)S(1)} collective-permute-done((bf16[448,128]{1,0:T(8,128)(2,1)}, bf16[448,128]{1,0:T(8,128)(2,1)S(1)}, u32[]{:S(2)}, u32[]{:S(2)}) %collective-permute-start.2) | collective-permute-done | bytes 114720 | tf_op jit(solution)/shard_map/ppermute | solution.py:843
  14.8 2.6 collective-permute-done.3.ov_ref
  18.7 6.0 %shard_map.254 = (bf16[512,896]{1,0:T(8,128)(2,1)}, bf16[512,896]{1,0:T(8,128)(2,1)}, bf16[512,256]{1,0:T(8,128)(2,1)}, bf16[896,1152]{1,0:T(8,128)(2,1)}) custom-call(s32[5]{0:T(128)} %stack.23.place_ref.refs_0_, bf16[512,896]{1,0:T(8,128)(2,1)} %bitcast.10, f32[1,2944]{1,0:T(1,128)} %broadcast_in_dim.10.params_ref, bf16[448,896]{1,0:T(8,128)(2,1)} %wq_ref.1, ...), custom_call_target="tpu_custom_call" | custom-call | flops 1056964608 | bytes 6291456 | tf_op jit(solution)/shard_map/pallas_call | solution.py:109
  24.7 4.6 collective-permute-start.4
  29.4 5.0 %collective-permute-start.5 = (bf16[512,256]{1,0:T(8,128)(2,1)}, bf16[512,256]{1,0:T(8,128)(2,1)S(1)}, u32[]{:S(2)}, u32[]{:S(2)}) collective-permute-start(bf16[512,256]{1,0:T(8,128)(2,1)} %get-tuple-element.458.kv0_ref.refs_3_), channel_id=1, source_target_pairs={{0,4},{2,6},{1,5},{3,7},{8,12},{10,14},{9,13},{11,15},{16,20},{18,... | collective-permute-start | bytes 786440 | tf_op jit(solution)/shard_map/ppermute | solution.py:1280
  34.3 11.8 %shard_map.255.refs_10_ = bf16[1024,2432]{1,0:T(8,128)(2,1)} custom-call(bf16[512,896]{1,0:T(8,128)(2,1)} %bitcast.14, bf16[512,896]{1,0:T(8,128)(2,1)} %copy-done.57, bf16[2432,896]{1,0:T(8,128)(2,1)} %refs_9_.1), custom_call_target="tpu_custom_call" | custom-call | flops 4462739456 | bytes 12582912 | tf_op jit(solution)/shard_map/pallas_call | solution.py:472
  46.9 22.3 %shard_map.256 = (bf16[512,896]{1,0:T(8,128)(2,1)}, f32[7,8,512]{2,1,0:T(8,128)}) custom-call(s32[5]{0:T(128)} %stack.23.place_ref.refs_0_, bf16[512,896]{1,0:T(8,128)(2,1)} %get-tuple-element.456.q_ref.refs_1_, bf16[512,256]{1,0:T(8,128)(2,1)} %get-tuple-element.458.kv0_ref.refs_3_, bf16[512,256]{1,0:T(8,128)(2,1)} %copy-done.63, ...), custom_call_target="tpu_custom_call" | custom-call | flops 9395240960 | bytes 4194304 | tf_op jit(solution)/shard_map/pallas_call | solution.py:248
  70.1 5.7 %shard_map.257 = (f32[512,896]{1,0:T(8,128)}, bf16[512,896]{1,0:T(8,128)(2,1)}, bf16[896,896]{1,0:T(8,128)(2,1)}) custom-call(s32[5]{0:T(128)} %stack.23.place_ref.refs_0_, bf16[512,896]{1,0:T(8,128)(2,1)} %bitcast.11, bf16[512,896]{1,0:T(8,128)(2,1)} %get-tuple-element.402.o_ref, bf16[448,896]{1,0:T(8,128)(2,1)} %own_ref.1, bf16[448,896]{1,0:T(8,128)(2,1)} %copy-done.18, ...), custom_call_target="tpu_custom_call" | custom-call | flops 822083584 | bytes 6291456 | tf_op jit(solution)/shard_map/pallas_call | solution.py:447
  75.8 2.7 collective-permute-done.8.refs_2_
  79.4 43.0 %shard_map.258 = (bf16[4928,128]{1,0:T(8,128)(2,1)}, bf16[4928,128]{1,0:T(8,128)(2,1)}, bf16[4928,128]{1,0:T(8,128)(2,1)}, bf16[4928,128]{1,0:T(8,128)(2,1)}, bf...) custom-call(s32[5]{0:T(128)} %stack.23.place_ref.refs_0_, ...), custom_call_target="tpu_custom_call" | custom-call | flops 23253221376 | bytes 31457280 | tf_op jit(solution)/shard_map/pallas_call | solution.py:646
  122.4 1.6 collective-permute-start.12
  124.0 1.5 collective-permute-start.13
  125.5 2.3 collective-permute-start.14
  127.8 32.4 %shard_map.259 = (bf16[3584,128]{1,0:T(8,128)(2,1)}, bf16[3584,128]{1,0:T(8,128)(2,1)}, bf16[3584,128]{1,0:T(8,128)(2,1)}, bf16[3584,128]{1,0:T(8,128)(2,1)}, bf...) custom-call(s32[5]{0:T(128)} %stack.23.place_ref.refs_0_, ...), custom_call_target="tpu_custom_call" | custom-call | flops 16911433728 | bytes 31457280 | tf_op jit(solution)/shard_map/pallas_call | solution.py:646
  162.2 5.8 %shard_map.260 = (bf16[2464,128]{1,0:T(8,128)(2,1)}, bf16[2464,128]{1,0:T(8,128)(2,1)}, bf16[2464,128]{1,0:T(8,128)(2,1)}, bf16[2464,128]{1,0:T(8,128)(2,1)}, bf...) custom-call(s32[5]{0:T(128)} %stack.23.place_ref.refs_0_, bf16[4928,128]{1,0:T(8,128)(2,1)} %get-tuple-element.380.refs_0_, ...), custom_call_target="tpu_custom_call" | custom-call | flops 3784704 | bytes 11354112 | tf_op jit(solution)/shard_map/pallas_call | solution.py:910
  169.9 8.7 %shard_map.261 = (f32[512,896]{1,0:T(8,128)}, bf16[512,896]{1,0:T(8,128)(2,1)}, f32[1,896]{1,0:T(1,128)}, bf16[3136,128]{1,0:T(8,128)(2,1)}, bf16[3136,128]{1,0:T(8,128)(2,1)}) custom-call(s32[5]{0:T(128)} %stack.23.place_ref.refs_0_, bf16[512,896]{1,0:T(8,128)(2,1)} %get-tuple-element.396.part_ref, bf16[512,896]{1,0:T(8,128)(2,1)} %copy-done.14, ...), custom_call_target="tpu_custom_call" | custom-call | flops 1644167168 | bytes 12582912 | tf_op jit(solution)/shard_map/pallas_call | solution.py:707
  178.6 6.1 %collective-permute-done.15.refs_1_ = bf16[2464,128]{1,0:T(8,128)(2,1)S(1)} collective-permute-done((bf16[2464,128]{1,0:T(8,128)(2,1)}, bf16[2464,128]{1,0:T(8,128)(2,1)S(1)}, u32[]{:S(2)}, u32[]{:S(2)}) %collective-permute-start.15) | collective-permute-done | bytes 630816 | tf_op jit(solution)/shard_map/ppermute | solution.py:849
  186.0 3.7 shard_map.262
  189.7 1.6 collective-permute-start.19
  191.9 1.5 collective-permute-start.21
  193.4 5.7 %collective-permute-done.19.refs_1_ = bf16[1232,128]{1,0:T(8,128)(2,1)S(1)} collective-permute-done((bf16[1232,128]{1,0:T(8,128)(2,1)}, bf16[1232,128]{1,0:T(8,128)(2,1)S(1)}, u32[]{:S(2)}, u32[]{:S(2)}) %collective-permute-start.19) | collective-permute-done | bytes 315424 | tf_op jit(solution)/shard_map/ppermute | solution.py:849
  200.6 2.6 shard_map.263.total
  203.2 3.3 collective-permute-start.22
  208.0 1.5 collective-permute-start.24
  210.3 21.8 %shard_map.264 = (bf16[512,512]{1,0:T(8,128)(2,1)}, f32[2,1536,128]{2,1,0:T(8,128)}, f32[2,1536,128]{2,1,0:T(8,128)}) custom-call(s32[5]{0:T(128)} %stack.23.place_ref.refs_0_, bf16[512,896]{1,0:T(8,128)(2,1)} %get-tuple-element.456.q_ref.refs_1_, bf16[512,896]{1,0:T(8,128)(2,1)} %get-tuple-element.457.refs_2_, ...), custom_call_target="tpu_custom_call" | custom-call | flops 13421772800 | bytes 6291456 | tf_op jit(solution)/shard_map/pallas_call | solution.py:400
  232.1 15.8 %collective-permute-done.25.refs_5_ = bf16[3584,128]{1,0:T(8,128)(2,1)S(1)} collective-permute-done((bf16[3584,128]{1,0:T(8,128)(2,1)S(1)}, bf16[3584,128]{1,0:T(8,128)(2,1)S(1)}, u32[]{:S(2)}, u32[]{:S(2)}) %collective-permute-start.25) | collective-permute-done | bytes 917536 | tf_op jit(solution)/shard_map/ppermute | solution.py:849
  248.9 4.7 shard_map.265
  255.5 18.5 %shard_map.266 = (bf16[512,384]{1,0:T(8,128)(2,1)}, f32[512,256]{1,0:T(8,128)}, bf16[512,256]{1,0:T(8,128)(2,1)}, bf16[512,256]{1,0:T(8,128)(2,1)}) custom-call(s32[5]{0:T(128)} %stack.23.place_ref.refs_0_, bf16[512,896]{1,0:T(8,128)(2,1)} %get-tuple-element.456.q_ref.refs_1_, bf16[512,896]{1,0:T(8,128)(2,1)} %get-tuple-element.457.refs_2_, ...), custom_call_target="tpu_custom_call" | custom-call | flops 10066329600 | bytes 6291456 | tf_op jit(solution)/shard_map/pallas_call | solution.py:400
  276.7 2.5 shard_map.267
  280.2 3.0 shard_map.268
  283.3 2.6 collective-permute-start.35
  288.0 6.7 %shard_map.269 = (f32[512,896]{1,0:T(8,128)}, f32[1,896]{1,0:T(1,128)}, bf16[3136,128]{1,0:T(8,128)(2,1)}, bf16[3136,128]{1,0:T(8,128)(2,1)}) custom-call(s32[5]{0:T(128)} %stack.23.place_ref.refs_0_, bf16[512,512]{1,0:T(8,128)(2,1)} %get-tuple-element.491.dqa_ref, bf16[512,384]{1,0:T(8,128)(2,1)} %get-tuple-element.492.dqb_ref, ...), custom_call_target="tpu_custom_call" | custom-call | flops 1644167168 | bytes 10485760 | tf_op jit(solution)/shard_map/pallas_call | solution.py:749
  295.6 2.3 shard_map.270
  298.7 8.5 %shard_map.271 = (bf16[512,896]{1,0:T(8,128)(2,1)}, bf16[7296,128]{1,0:T(8,128)(2,1)}, bf16[7296,128]{1,0:T(8,128)(2,1)}) custom-call(s32[5]{0:T(128)} %stack.23.place_ref.refs_0_, f32[512,256]{1,0:T(8,128)} %get-tuple-element.515.own_ref, bf16[512,256]{1,0:T(8,128)(2,1)} %copy-done.43, bf16[512,256]{1,0:T(8,128)(2,1)} %copy-done.44, ...), custom_call_target="tpu_custom_call" | custom-call | flops 469762048 | bytes 14680064 | tf_op jit(solution)/shard_map/pallas_call | solution.py:824
  307.3 3.6 collective-permute-start.39
  310.9 10.6 %collective-permute-done.39 = bf16[896,128]{1,0:T(8,128)(2,1)S(1)} collective-permute-done((bf16[896,128]{1,0:T(8,128)(2,1)S(1)}, bf16[896,128]{1,0:T(8,128)(2,1)S(1)}, u32[]{:S(2)}, u32[]{:S(2)}) %collective-permute-start.39) | collective-permute-done | bytes 229408 | tf_op jit(solution)/shard_map/ppermute | solution.py:849
  322.9 3.8 shard_map.272
  327.1 1.6 collective-permute-start.41
  328.8 3.1 collective-permute-start.26
  332.4 8.6 %collective-permute-done.42 = bf16[896,128]{1,0:T(8,128)(2,1)S(1)} collective-permute-done((bf16[896,128]{1,0:T(8,128)(2,1)S(1)}, bf16[896,128]{1,0:T(8,128)(2,1)S(1)}, u32[]{:S(2)}, u32[]{:S(2)}) %collective-permute-start.42) | collective-permute-done | bytes 229408 | tf_op jit(solution)/shard_map/ppermute | solution.py:849
  341.0 1.6 collective-permute-start.28
  343.6 2.5 shard_map.273
  347.1 3.1 collective-permute-done.28.refs_3_
  351.0 2.8 shard_map.274
  353.8 1.6 collective-permute-start.43
  357.9 16.3 %collective-permute-done.46.refs_1_ = bf16[912,128]{1,0:T(8,128)(2,1)S(1)} collective-permute-done((bf16[912,128]{1,0:T(8,128)(2,1)S(1)}, bf16[912,128]{1,0:T(8,128)(2,1)S(1)}, u32[]{:S(2)}, u32[]{:S(2)}) %collective-permute-start.46) | collective-permute-done | bytes 233504 | tf_op jit(solution)/shard_map/ppermute | solution.py:849
  376.2 2.2 shard_map.275
  378.4 1.7 collective-permute-start.52
  384.8 4.1 shard_map.276
  388.9 5.0 %collective-permute-done.53.refs_1_ = bf16[896,128]{1,0:T(8,128)(2,1)S(1)} collective-permute-done((bf16[896,128]{1,0:T(8,128)(2,1)S(1)}, bf16[896,128]{1,0:T(8,128)(2,1)S(1)}, u32[]{:S(2)}, u32[]{:S(2)}) %collective-permute-start.53) | collective-permute-done | bytes 229408 | tf_op jit(solution)/shard_map/ppermute | solution.py:849
  394.8 2.6 shard_map.277
  402.6 11.1 %collective-permute-done.60.refs_1_ = bf16[1792,128]{1,0:T(8,128)(2,1)S(1)} collective-permute-done((bf16[1792,128]{1,0:T(8,128)(2,1)}, bf16[1792,128]{1,0:T(8,128)(2,1)S(1)}, u32[]{:S(2)}, u32[]{:S(2)}) %collective-permute-start.60) | collective-permute-done | bytes 458784 | tf_op jit(solution)/shard_map/ppermute | solution.py:849
  414.2 4.9 collective-permute-done.57.got
  420.2 2.0 shard_map.278
  422.2 24.5 %collective-permute-done.61.refs_3_ = bf16[1792,128]{1,0:T(8,128)(2,1)} collective-permute-done((bf16[1792,128]{1,0:T(8,128)(2,1)}, bf16[1792,128]{1,0:T(8,128)(2,1)}, u32[]{:S(2)}, u32[]{:S(2)}) %collective-permute-start.61) | collective-permute-done | bytes 458784 | tf_op jit(solution)/shard_map/ppermute | solution.py:849
  448.9 3.4 shard_map.279
  452.3 3.1 collective-permute-done.58.refs_1_
  457.7 2.7 shard_map.280
  462.5 9.7 %shard_map.281 = (f32[448,4864]{1,0:T(8,128)}, f32[448,4864]{1,0:T(8,128)}, f32[2432,896]{1,0:T(8,128)}) custom-call(s32[5]{0:T(128)} %stack.23.place_ref.refs_0_, bf16[4928,128]{1,0:T(8,128)(2,1)} %get-tuple-element.608.refs_1_, bf16[4928,128]{1,0:T(8,128)(2,1)} %copy-done.6, bf16[4928,128]{1,0:T(8,128)(2,1)} %get-tuple-element.610.refs_3_, ...), custom_call_target="tpu_custom_call" | custom-call | flops 3784704 | bytes 22708224 | tf_op jit(solution)/shard_map/pallas_call | solution.py:1047
  473.5 3.5 collective-permute-done.65.refs_2_
  477.8 7.8 %shard_map.282 = (f32[448,4864]{1,0:T(8,128)}, f32[448,4864]{1,0:T(8,128)}, f32[2432,896]{1,0:T(8,128)}) custom-call(s32[5]{0:T(128)} %stack.23.place_ref.refs_0_, bf16[3584,128]{1,0:T(8,128)(2,1)} %get-tuple-element.624.refs_1_, bf16[3584,128]{1,0:T(8,128)(2,1)} %collective-permute-done.65.refs_2_, ...), custom_call_target="tpu_custom_call", output_to_operand_aliasing={{0}: (7, {}), {1}: (8, {}), {2}: (9, {})} | custom-call | flops 2752512 | bytes 16515072 | tf_op jit(solution)/shard_map/pallas_call | solution.py:1047
  486.5 4.0 shard_map.283
  (259 shorter events, 61.7 us)
Async XLA Ops:
  0.6 77.8 %collective-permute-start.10 = (bf16[448,4864]{1,0:T(8,128)(2,1)}, bf16[448,4864]{1,0:T(8,128)(2,1)}, u32[]{:S(2)}, u32[]{:S(2)}) collective-permute-start(bf16[448,4864]{1,0:T(8,128)(2,1)} %refs_7_.1), channel_id=1, source_target_pairs={{0,1},{1,0},{2,3},{3,2},{4,5},{5,4},{6,7},{7,6},{8,9},{9,8},{10,11... | collective-permute-start | bytes 13074440 | tf_op jit(solution)/shard_map/ppermute | solution.py:843
  1.2 77.3 %collective-permute-start.9 = (bf16[448,4864]{1,0:T(8,128)(2,1)}, bf16[448,4864]{1,0:T(8,128)(2,1)}, u32[]{:S(2)}, u32[]{:S(2)}) collective-permute-start(bf16[448,4864]{1,0:T(8,128)(2,1)} %refs_5_.1), channel_id=1, source_target_pairs={{0,1},{1,0},{2,3},{3,2},{4,5},{5,4},{6,7},{7,6},{8,9},{9,8},{10,11... | collective-permute-start | bytes 13074440 | tf_op jit(solution)/shard_map/ppermute | solution.py:843
  5.2 12.6 %collective-permute-start.1 = (bf16[448,896]{1,0:T(8,128)(2,1)}, bf16[448,896]{1,0:T(8,128)(2,1)S(1)}, u32[]{:S(2)}, u32[]{:S(2)}) collective-permute-start(bf16[448,896]{1,0:T(8,128)(2,1)} %wq_ref.1), channel_id=1, source_target_pairs={{0,1},{1,0},{2,3},{3,2},{4,5},{5,4},{6,7},{7,6},{8,9},{9,8},{10,11... | collective-permute-start | bytes 2408456 | tf_op jit(solution)/shard_map/ppermute | solution.py:843
  5.2 24.1 %collective-permute-start.6 = (bf16[512,896]{1,0:T(8,128)(2,1)}, bf16[512,896]{1,0:T(8,128)(2,1)S(1)}, u32[]{:S(2)}, u32[]{:S(2)}) collective-permute-start(bf16[512,896]{1,0:T(8,128)(2,1)} %bitcast.13), channel_id=1, source_target_pairs={{0,1},{1,0},{2,3},{3,2},{4,5},{5,4},{6,7},{7,6},{8,9},{9,8},{10,11... | collective-permute-start | bytes 2752520 | tf_op jit(solution)/shard_map/ppermute | solution.py:843
  8.2 5.4 %collective-permute-start.2 = (bf16[448,128]{1,0:T(8,128)(2,1)}, bf16[448,128]{1,0:T(8,128)(2,1)S(1)}, u32[]{:S(2)}, u32[]{:S(2)}) collective-permute-start(bf16[448,128]{1,0:T(8,128)(2,1)} %wk_ref.1), channel_id=1, source_target_pairs={{0,1},{1,0},{2,3},{3,2},{4,5},{5,4},{6,7},{7,6},{8,9},{9,8},{10,11... | collective-permute-start | bytes 344072 | tf_op jit(solution)/shard_map/ppermute | solution.py:843
  17.4 51.8 %collective-permute-start.7 = (bf16[448,896]{1,0:T(8,128)(2,1)}, bf16[448,896]{1,0:T(8,128)(2,1)S(1)}, u32[]{:S(2)}, u32[]{:S(2)}) collective-permute-start(bf16[448,896]{1,0:T(8,128)(2,1)} %own_ref.1), channel_id=1, source_target_pairs={{0,1},{1,0},{2,3},{3,2},{4,5},{5,4},{6,7},{7,6},{8,9},{9,8},{10,11... | collective-permute-start | bytes 2408456 | tf_op jit(solution)/shard_map/ppermute | solution.py:843
  24.7 21.4 %collective-permute-start.4 = (bf16[512,256]{1,0:T(8,128)(2,1)}, bf16[512,256]{1,0:T(8,128)(2,1)S(1)}, u32[]{:S(2)}, u32[]{:S(2)}) collective-permute-start(bf16[512,256]{1,0:T(8,128)(2,1)} %get-tuple-element.458.kv0_ref.refs_3_), channel_id=1, source_target_pairs={{0,2},{2,4},{4,6},{1,3},{3,5},{5,7},{8,10},{10,12},{12,14},{9,11},... | collective-permute-start | bytes 786440 | tf_op jit(solution)/shard_map/ppermute | solution.py:1280
  29.4 16.8 %collective-permute-start.5 = (bf16[512,256]{1,0:T(8,128)(2,1)}, bf16[512,256]{1,0:T(8,128)(2,1)S(1)}, u32[]{:S(2)}, u32[]{:S(2)}) collective-permute-start(bf16[512,256]{1,0:T(8,128)(2,1)} %get-tuple-element.458.kv0_ref.refs_3_), channel_id=1, source_target_pairs={{0,4},{2,6},{1,5},{3,7},{8,12},{10,14},{9,13},{11,15},{16,20},{18,... | collective-permute-start | bytes 786440 | tf_op jit(solution)/shard_map/ppermute | solution.py:1280
  122.4 37.9 %collective-permute-start.12 = (bf16[4928,128]{1,0:T(8,128)(2,1)}, bf16[4928,128]{1,0:T(8,128)(2,1)S(1)}, u32[]{:S(2)}, u32[]{:S(2)}) collective-permute-start(bf16[4928,128]{1,0:T(8,128)(2,1)} %get-tuple-element.374), channel_id=1, source_target_pairs={{0,8},{8,0},{16,24},{24,16},{1,9},{9,1},{17,25},{25,17},{2,10},{10... | collective-permute-start | bytes 3784712 | tf_op jit(solution)/shard_map/ppermute | solution.py:849
  124.0 36.3 %collective-permute-start.13 = (bf16[4928,128]{1,0:T(8,128)(2,1)}, bf16[4928,128]{1,0:T(8,128)(2,1)S(1)}, u32[]{:S(2)}, u32[]{:S(2)}) collective-permute-start(bf16[4928,128]{1,0:T(8,128)(2,1)} %get-tuple-element.376), channel_id=1, source_target_pairs={{0,16},{8,24},{16,0},{24,8},{1,17},{9,25},{17,1},{25,9},{2,18},{10... | collective-permute-start | bytes 3784712 | tf_op jit(solution)/shard_map/ppermute | solution.py:849
  125.5 34.8 %collective-permute-start.14 = (bf16[4928,128]{1,0:T(8,128)(2,1)}, bf16[4928,128]{1,0:T(8,128)(2,1)S(1)}, u32[]{:S(2)}, u32[]{:S(2)}) collective-permute-start(bf16[4928,128]{1,0:T(8,128)(2,1)} %get-tuple-element.378), channel_id=1, source_target_pairs={{0,2},{2,0},{4,6},{6,4},{1,3},{3,1},{5,7},{7,5},{8,10},{10,8},{12,... | collective-permute-start | bytes 3784712 | tf_op jit(solution)/shard_map/ppermute | solution.py:849
  160.2 8.8 %collective-permute-start.18 = (bf16[512,896]{1,0:T(8,128)(2,1)}, bf16[512,896]{1,0:T(8,128)(2,1)S(1)}, u32[]{:S(2)}, u32[]{:S(2)}) collective-permute-start(bf16[512,896]{1,0:T(8,128)(2,1)} %get-tuple-element.393), channel_id=1, source_target_pairs={{0,1},{1,0},{2,3},{3,2},{4,5},{5,4},{6,7},{7,6},{8,9},{9,8},{10,11... | collective-permute-start | bytes 2752520 | tf_op jit(solution)/shard_map/ppermute | solution.py:843
  168.0 16.8 %collective-permute-start.15 = (bf16[2464,128]{1,0:T(8,128)(2,1)}, bf16[2464,128]{1,0:T(8,128)(2,1)S(1)}, u32[]{:S(2)}, u32[]{:S(2)}) collective-permute-start(bf16[2464,128]{1,0:T(8,128)(2,1)} %get-tuple-element.387), channel_id=1, source_target_pairs={{0,16},{8,24},{16,0},{24,8},{1,17},{9,25},{17,1},{25,9},{2,18},{10... | collective-permute-start | bytes 1892360 | tf_op jit(solution)/shard_map/ppermute | solution.py:849
  168.5 16.5 %collective-permute-start.16 = (bf16[2464,128]{1,0:T(8,128)(2,1)}, bf16[2464,128]{1,0:T(8,128)(2,1)S(1)}, u32[]{:S(2)}, u32[]{:S(2)}) collective-permute-start(bf16[2464,128]{1,0:T(8,128)(2,1)} %get-tuple-element.389), channel_id=1, source_target_pairs={{0,2},{2,0},{4,6},{6,4},{1,3},{3,1},{5,7},{7,5},{8,10},{10,8},{12,... | collective-permute-start | bytes 1892360 | tf_op jit(solution)/shard_map/ppermute | solution.py:849
  168.5 16.5 %collective-permute-start.17 = (bf16[2464,128]{1,0:T(8,128)(2,1)}, bf16[2464,128]{1,0:T(8,128)(2,1)S(1)}, u32[]{:S(2)}, u32[]{:S(2)}) collective-permute-start(bf16[2464,128]{1,0:T(8,128)(2,1)} %get-tuple-element.391), channel_id=1, source_target_pairs={{0,8},{8,0},{16,24},{24,16},{1,9},{9,1},{17,25},{25,17},{2,10},{10... | collective-permute-start | bytes 1892360 | tf_op jit(solution)/shard_map/ppermute | solution.py:849
  189.7 9.3 %collective-permute-start.19 = (bf16[1232,128]{1,0:T(8,128)(2,1)}, bf16[1232,128]{1,0:T(8,128)(2,1)S(1)}, u32[]{:S(2)}, u32[]{:S(2)}) collective-permute-start(bf16[1232,128]{1,0:T(8,128)(2,1)} %get-tuple-element.411), channel_id=1, source_target_pairs={{0,2},{2,0},{4,6},{6,4},{1,3},{3,1},{5,7},{7,5},{8,10},{10,8},{12,... | collective-permute-start | bytes 946184 | tf_op jit(solution)/shard_map/ppermute | solution.py:849
  191.3 8.3 %collective-permute-start.20 = (bf16[1232,128]{1,0:T(8,128)(2,1)}, bf16[1232,128]{1,0:T(8,128)(2,1)S(1)}, u32[]{:S(2)}, u32[]{:S(2)}) collective-permute-start(bf16[1232,128]{1,0:T(8,128)(2,1)} %get-tuple-element.413), channel_id=1, source_target_pairs={{0,8},{8,0},{16,24},{24,16},{1,9},{9,1},{17,25},{25,17},{2,10},{10... | collective-permute-start | bytes 946184 | tf_op jit(solution)/shard_map/ppermute | solution.py:849
  191.9 8.1 %collective-permute-start.21 = (bf16[1232,128]{1,0:T(8,128)(2,1)}, bf16[1232,128]{1,0:T(8,128)(2,1)S(1)}, u32[]{:S(2)}, u32[]{:S(2)}) collective-permute-start(bf16[1232,128]{1,0:T(8,128)(2,1)} %get-tuple-element.415), channel_id=1, source_target_pairs={{0,16},{8,24},{16,0},{24,8},{1,17},{9,25},{17,1},{25,9},{2,18},{10... | collective-permute-start | bytes 946184 | tf_op jit(solution)/shard_map/ppermute | solution.py:849
  203.2 72.1 %collective-permute-start.22 = (bf16[3696,128]{1,0:T(8,128)(2,1)}, bf16[3696,128]{1,0:T(8,128)(2,1)S(1)}, u32[]{:S(2)}, u32[]{:S(2)}) collective-permute-start(bf16[3696,128]{1,0:T(8,128)(2,1)} %shard_map.263.total), channel_id=1, source_target_pairs={{0,4},{2,6},{4,0},{6,2},{1,5},{3,7},{5,1},{7,3},{8,12},{10,14},{12... | collective-permute-start | bytes 2838536 | tf_op jit(solution)/shard_map/ppermute | solution.py:849
  206.5 25.6 %collective-permute-start.23 = (bf16[3584,128]{1,0:T(8,128)(2,1)}, bf16[3584,128]{1,0:T(8,128)(2,1)S(1)}, u32[]{:S(2)}, u32[]{:S(2)}) collective-permute-start(bf16[3584,128]{1,0:T(8,128)(2,1)} %get-tuple-element.442), channel_id=1, source_target_pairs={{0,8},{8,0},{16,24},{24,16},{1,9},{9,1},{17,25},{25,17},{2,10},{10... | collective-permute-start | bytes 2752520 | tf_op jit(solution)/shard_map/ppermute | solution.py:849
  208.0 24.1 %collective-permute-start.24 = (bf16[3584,128]{1,0:T(8,128)(2,1)S(1)}, bf16[3584,128]{1,0:T(8,128)(2,1)S(1)}, u32[]{:S(2)}, u32[]{:S(2)}) collective-permute-start(bf16[3584,128]{1,0:T(8,128)(2,1)S(1)} %copy-done.59), channel_id=1, source_target_pairs={{0,16},{8,24},{16,0},{24,8},{1,17},{9,25},{17,1},{25,9},{2,18},{10... | collective-permute-start | bytes 2752520 | tf_op jit(solution)/shard_map/ppermute | solution.py:849
  209.5 38.4 %collective-permute-start.25 = (bf16[3584,128]{1,0:T(8,128)(2,1)S(1)}, bf16[3584,128]{1,0:T(8,128)(2,1)S(1)}, u32[]{:S(2)}, u32[]{:S(2)}) collective-permute-start(bf16[3584,128]{1,0:T(8,128)(2,1)S(1)} %copy-done.58), channel_id=1, source_target_pairs={{0,2},{2,0},{4,6},{6,4},{1,3},{3,1},{5,7},{7,5},{8,10},{10,8},{12,... | collective-permute-start | bytes 2752520 | tf_op jit(solution)/shard_map/ppermute | solution.py:849
  253.5 25.6 %collective-permute-start.32 = (bf16[1792,128]{1,0:T(8,128)(2,1)}, bf16[1792,128]{1,0:T(8,128)(2,1)S(1)}, u32[]{:S(2)}, u32[]{:S(2)}) collective-permute-start(bf16[1792,128]{1,0:T(8,128)(2,1)} %get-tuple-element.478), channel_id=1, source_target_pairs={{0,16},{8,24},{16,0},{24,8},{1,17},{9,25},{17,1},{25,9},{2,18},{10... | collective-permute-start | bytes 1376264 | tf_op jit(solution)/shard_map/ppermute | solution.py:849
  254.3 24.9 %collective-permute-start.33 = (bf16[1792,128]{1,0:T(8,128)(2,1)}, bf16[1792,128]{1,0:T(8,128)(2,1)S(1)}, u32[]{:S(2)}, u32[]{:S(2)}) collective-permute-start(bf16[1792,128]{1,0:T(8,128)(2,1)} %get-tuple-element.480), channel_id=1, source_target_pairs={{0,2},{2,0},{4,6},{6,4},{1,3},{3,1},{5,7},{7,5},{8,10},{10,8},{12,... | collective-permute-start | bytes 1376264 | tf_op jit(solution)/shard_map/ppermute | solution.py:849
  254.3 24.9 %collective-permute-start.34 = (bf16[1792,128]{1,0:T(8,128)(2,1)}, bf16[1792,128]{1,0:T(8,128)(2,1)S(1)}, u32[]{:S(2)}, u32[]{:S(2)}) collective-permute-start(bf16[1792,128]{1,0:T(8,128)(2,1)} %get-tuple-element.482), channel_id=1, source_target_pairs={{0,8},{8,0},{16,24},{24,16},{1,9},{9,1},{17,25},{25,17},{2,10},{10... | collective-permute-start | bytes 1376264 | tf_op jit(solution)/shard_map/ppermute | solution.py:849
  274.0 23.9 %collective-permute-start.30 = (bf16[512,256]{1,0:T(8,128)(2,1)}, bf16[512,256]{1,0:T(8,128)(2,1)S(1)}, u32[]{:S(2)}, u32[]{:S(2)}) collective-permute-start(bf16[512,256]{1,0:T(8,128)(2,1)} %get-tuple-element.474), channel_id=1, source_target_pairs={{2,0},{4,2},{6,4},{3,1},{5,3},{7,5},{10,8},{12,10},{14,12},{11,9},... | collective-permute-start | bytes 786440 | tf_op jit(solution)/shard_map/ppermute | solution.py:1335
  275.4 22.6 %collective-permute-start.31 = (bf16[512,256]{1,0:T(8,128)(2,1)}, bf16[512,256]{1,0:T(8,128)(2,1)S(1)}, u32[]{:S(2)}, u32[]{:S(2)}) collective-permute-start(bf16[512,256]{1,0:T(8,128)(2,1)} %get-tuple-element.475), channel_id=1, source_target_pairs={{4,0},{6,2},{5,1},{7,3},{12,8},{14,10},{13,9},{15,11},{20,16},{22,... | collective-permute-start | bytes 786440 | tf_op jit(solution)/shard_map/ppermute | solution.py:1335
  283.3 11.5 %collective-permute-start.35 = (bf16[896,128]{1,0:T(8,128)(2,1)}, bf16[896,128]{1,0:T(8,128)(2,1)S(1)}, u32[]{:S(2)}, u32[]{:S(2)}) collective-permute-start(bf16[896,128]{1,0:T(8,128)(2,1)} %get-tuple-element.502), channel_id=1, source_target_pairs={{0,2},{2,0},{4,6},{6,4},{1,3},{3,1},{5,7},{7,5},{8,10},{10,8},{12,... | collective-permute-start | bytes 688136 | tf_op jit(solution)/shard_map/ppermute | solution.py:849
  285.9 8.9 %collective-permute-start.36 = (bf16[896,128]{1,0:T(8,128)(2,1)}, bf16[896,128]{1,0:T(8,128)(2,1)S(1)}, u32[]{:S(2)}, u32[]{:S(2)}) collective-permute-start(bf16[896,128]{1,0:T(8,128)(2,1)} %get-tuple-element.504), channel_id=1, source_target_pairs={{0,8},{8,0},{16,24},{24,16},{1,9},{9,1},{17,25},{25,17},{2,10},{10... | collective-permute-start | bytes 688136 | tf_op jit(solution)/shard_map/ppermute | solution.py:849
  286.7 8.1 %collective-permute-start.37 = (bf16[896,128]{1,0:T(8,128)(2,1)}, bf16[896,128]{1,0:T(8,128)(2,1)S(1)}, u32[]{:S(2)}, u32[]{:S(2)}) collective-permute-start(bf16[896,128]{1,0:T(8,128)(2,1)} %get-tuple-element.506), channel_id=1, source_target_pairs={{0,16},{8,24},{16,0},{24,8},{1,17},{9,25},{17,1},{25,9},{2,18},{10... | collective-permute-start | bytes 688136 | tf_op jit(solution)/shard_map/ppermute | solution.py:849
  307.3 14.3 %collective-permute-start.38 = (bf16[7296,128]{1,0:T(8,128)(2,1)}, bf16[7296,128]{1,0:T(8,128)(2,1)S(1)}, u32[]{:S(2)}, u32[]{:S(2)}) collective-permute-start(bf16[7296,128]{1,0:T(8,128)(2,1)} %get-tuple-element.533), channel_id=1, source_target_pairs={{0,1},{1,0},{2,3},{3,2},{4,5},{5,4},{6,7},{7,6},{8,9},{9,8},{10,11... | collective-permute-start | bytes 5603336 | tf_op jit(solution)/shard_map/ppermute | solution.py:843
  307.3 14.2 %collective-permute-start.39 = (bf16[896,128]{1,0:T(8,128)(2,1)S(1)}, bf16[896,128]{1,0:T(8,128)(2,1)S(1)}, u32[]{:S(2)}, u32[]{:S(2)}) collective-permute-start(bf16[896,128]{1,0:T(8,128)(2,1)S(1)} %copy-done.53), channel_id=1, source_target_pairs={{0,4},{2,6},{4,0},{6,2},{1,5},{3,7},{5,1},{7,3},{8,12},{10,14},{12... | collective-permute-start | bytes 688136 | tf_op jit(solution)/shard_map/ppermute | solution.py:849
  326.7 16.0 %collective-permute-start.40 = (bf16[1824,128]{1,0:T(8,128)(2,1)}, bf16[1824,128]{1,0:T(8,128)(2,1)S(1)}, u32[]{:S(2)}, u32[]{:S(2)}) collective-permute-start(bf16[1824,128]{1,0:T(8,128)(2,1)} %get-tuple-element.541), channel_id=1, source_target_pairs={{0,8},{8,0},{16,24},{24,16},{1,9},{9,1},{17,25},{25,17},{2,10},{10... | collective-permute-start | bytes 1400840 | tf_op jit(solution)/shard_map/ppermute | solution.py:849
  327.0 4.9 collective-permute-start.27
  327.1 13.9 %collective-permute-start.42 = (bf16[896,128]{1,0:T(8,128)(2,1)S(1)}, bf16[896,128]{1,0:T(8,128)(2,1)S(1)}, u32[]{:S(2)}, u32[]{:S(2)}) collective-permute-start(bf16[896,128]{1,0:T(8,128)(2,1)S(1)} %copy-done.52), channel_id=1, source_target_pairs={{0,4},{2,6},{4,0},{6,2},{1,5},{3,7},{5,1},{7,3},{8,12},{10,14},{12... | collective-permute-start | bytes 688136 | tf_op jit(solution)/shard_map/ppermute | solution.py:849
  327.1 15.7 %collective-permute-start.41 = (bf16[1824,128]{1,0:T(8,128)(2,1)}, bf16[1824,128]{1,0:T(8,128)(2,1)S(1)}, u32[]{:S(2)}, u32[]{:S(2)}) collective-permute-start(bf16[1824,128]{1,0:T(8,128)(2,1)} %get-tuple-element.543), channel_id=1, source_target_pairs={{0,16},{8,24},{16,0},{24,8},{1,17},{9,25},{17,1},{25,9},{2,18},{10... | collective-permute-start | bytes 1400840 | tf_op jit(solution)/shard_map/ppermute | solution.py:849
  328.8 17.3 %collective-permute-start.26 = (bf16[1232,128]{1,0:T(8,128)(2,1)S(1)}, bf16[1232,128]{1,0:T(8,128)(2,1)S(1)}, u32[]{:S(2)}, u32[]{:S(2)}) collective-permute-start(bf16[1232,128]{1,0:T(8,128)(2,1)S(1)} %copy-done.34), channel_id=1, source_target_pairs={{0,2},{2,0},{4,6},{6,4},{1,3},{3,1},{5,7},{7,5},{8,10},{10,8},{12,... | collective-permute-start | bytes 946184 | tf_op jit(solution)/shard_map/ppermute | solution.py:849
  331.9 15.2 %collective-permute-start.29 = (bf16[1232,128]{1,0:T(8,128)(2,1)S(1)}, bf16[1232,128]{1,0:T(8,128)(2,1)S(1)}, u32[]{:S(2)}, u32[]{:S(2)}) collective-permute-start(bf16[1232,128]{1,0:T(8,128)(2,1)S(1)} %copy-done.35), channel_id=1, source_target_pairs={{0,16},{8,24},{16,0},{24,8},{1,17},{9,25},{17,1},{25,9},{2,18},{10... | collective-permute-start | bytes 946184 | tf_op jit(solution)/shard_map/ppermute | solution.py:849
  341.0 9.3 %collective-permute-start.28 = (bf16[1232,128]{1,0:T(8,128)(2,1)S(1)}, bf16[1232,128]{1,0:T(8,128)(2,1)S(1)}, u32[]{:S(2)}, u32[]{:S(2)}) collective-permute-start(bf16[1232,128]{1,0:T(8,128)(2,1)S(1)} %collective-permute-done.27.refs_2_), channel_id=1, source_target_pairs={{0,8},{8,0},{16,24},{24,16},{1,9},{9,1},{17,25},{25,17},{2,10},{10... | collective-permute-start | bytes 946184 | tf_op jit(solution)/shard_map/ppermute | solution.py:849
  342.6 13.5 %collective-permute-start.48 = (bf16[896,128]{1,0:T(8,128)(2,1)S(1)}, bf16[896,128]{1,0:T(8,128)(2,1)S(1)}, u32[]{:S(2)}, u32[]{:S(2)}) collective-permute-start(bf16[896,128]{1,0:T(8,128)(2,1)S(1)} %copy-done.51), channel_id=1, source_target_pairs={{0,4},{2,6},{4,0},{6,2},{1,5},{3,7},{5,1},{7,3},{8,12},{10,14},{12... | collective-permute-start | bytes 688136 | tf_op jit(solution)/shard_map/ppermute | solution.py:849
  353.8 28.1 %collective-permute-start.43 = (bf16[2464,128]{1,0:T(8,128)(2,1)}, bf16[2464,128]{1,0:T(8,128)(2,1)S(1)}, u32[]{:S(2)}, u32[]{:S(2)}) collective-permute-start(bf16[2464,128]{1,0:T(8,128)(2,1)} %get-tuple-element.571.refs_0_), channel_id=1, source_target_pairs={{0,16},{8,24},{16,0},{24,8},{1,17},{9,25},{17,1},{25,9},{2,18},{10... | collective-permute-start | bytes 1892360 | tf_op jit(solution)/shard_map/ppermute | solution.py:849
  355.3 27.3 %collective-permute-start.44 = (bf16[2464,128]{1,0:T(8,128)(2,1)}, bf16[2464,128]{1,0:T(8,128)(2,1)S(1)}, u32[]{:S(2)}, u32[]{:S(2)}) collective-permute-start(bf16[2464,128]{1,0:T(8,128)(2,1)} %get-tuple-element.573.refs_2_), channel_id=1, source_target_pairs={{0,2},{2,0},{4,6},{6,4},{1,3},{3,1},{5,7},{7,5},{8,10},{10,8},{12,... | collective-permute-start | bytes 1892360 | tf_op jit(solution)/shard_map/ppermute | solution.py:849
  355.3 28.7 %collective-permute-start.45 = (bf16[2464,128]{1,0:T(8,128)(2,1)}, bf16[2464,128]{1,0:T(8,128)(2,1)S(1)}, u32[]{:S(2)}, u32[]{:S(2)}) collective-permute-start(bf16[2464,128]{1,0:T(8,128)(2,1)} %get-tuple-element.575.refs_4_), channel_id=1, source_target_pairs={{0,8},{8,0},{16,24},{24,16},{1,9},{9,1},{17,25},{25,17},{2,10},{10... | collective-permute-start | bytes 1892360 | tf_op jit(solution)/shard_map/ppermute | solution.py:849
  356.1 18.0 %collective-permute-start.46 = (bf16[912,128]{1,0:T(8,128)(2,1)S(1)}, bf16[912,128]{1,0:T(8,128)(2,1)S(1)}, u32[]{:S(2)}, u32[]{:S(2)}) collective-permute-start(bf16[912,128]{1,0:T(8,128)(2,1)S(1)} %copy-done.66), channel_id=1, source_target_pairs={{0,16},{8,24},{16,0},{24,8},{1,17},{9,25},{17,1},{25,9},{2,18},{10... | collective-permute-start | bytes 700424 | tf_op jit(solution)/shard_map/ppermute | solution.py:849
  357.4 18.0 %collective-permute-start.47 = (bf16[912,128]{1,0:T(8,128)(2,1)S(1)}, bf16[912,128]{1,0:T(8,128)(2,1)S(1)}, u32[]{:S(2)}, u32[]{:S(2)}) collective-permute-start(bf16[912,128]{1,0:T(8,128)(2,1)S(1)} %copy-done.65), channel_id=1, source_target_pairs={{0,8},{8,0},{16,24},{24,16},{1,9},{9,1},{17,25},{25,17},{2,10},{10... | collective-permute-start | bytes 700424 | tf_op jit(solution)/shard_map/ppermute | solution.py:849
  378.4 19.0 %collective-permute-start.52 = (bf16[1824,128]{1,0:T(8,128)(2,1)}, bf16[1824,128]{1,0:T(8,128)(2,1)}, u32[]{:S(2)}, u32[]{:S(2)}) collective-permute-start(bf16[1824,128]{1,0:T(8,128)(2,1)} %shard_map.275), channel_id=1, source_target_pairs={{0,2},{2,0},{4,6},{6,4},{1,3},{3,1},{5,7},{7,5},{8,10},{10,8},{12,... | collective-permute-start | bytes 1400840 | tf_op jit(solution)/shard_map/ppermute | solution.py:849
  381.6 12.4 %collective-permute-start.53 = (bf16[896,128]{1,0:T(8,128)(2,1)S(1)}, bf16[896,128]{1,0:T(8,128)(2,1)S(1)}, u32[]{:S(2)}, u32[]{:S(2)}) collective-permute-start(bf16[896,128]{1,0:T(8,128)(2,1)S(1)} %add_convert_fusion.4.refs_0_), channel_id=1, source_target_pairs={{0,2},{2,0},{4,6},{6,4},{1,3},{3,1},{5,7},{7,5},{8,10},{10,8},{12,... | collective-permute-start | bytes 688136 | tf_op jit(solution)/shard_map/ppermute | solution.py:849
  381.9 12.9 %collective-permute-start.55 = (bf16[896,128]{1,0:T(8,128)(2,1)S(1)}, bf16[896,128]{1,0:T(8,128)(2,1)}, u32[]{:S(2)}, u32[]{:S(2)}) collective-permute-start(bf16[896,128]{1,0:T(8,128)(2,1)S(1)} %collective-permute-done.54.refs_2_), channel_id=1, source_target_pairs={{0,8},{8,0},{16,24},{24,16},{1,9},{9,1},{17,25},{25,17},{2,10},{10... | collective-permute-start | bytes 688136 | tf_op jit(solution)/shard_map/ppermute | solution.py:849
  382.7 12.1 %collective-permute-start.56 = (bf16[896,128]{1,0:T(8,128)(2,1)S(1)}, bf16[896,128]{1,0:T(8,128)(2,1)}, u32[]{:S(2)}, u32[]{:S(2)}) collective-permute-start(bf16[896,128]{1,0:T(8,128)(2,1)S(1)} %add_convert_fusion.2.refs_4_), channel_id=1, source_target_pairs={{0,16},{8,24},{16,0},{24,8},{1,17},{9,25},{17,1},{25,9},{2,18},{10... | collective-permute-start | bytes 688136 | tf_op jit(solution)/shard_map/ppermute | solution.py:849
  384.0 18.0 %collective-permute-start.11 = (bf16[512,896]{1,0:T(8,128)(2,1)}, bf16[512,896]{1,0:T(8,128)(2,1)S(1)}, u32[]{:S(2)}, u32[]{:S(2)}) collective-permute-start(bf16[512,896]{1,0:T(8,128)(2,1)} %get-tuple-element.373), channel_id=1, source_target_pairs={{0,1},{1,0},{2,3},{3,2},{4,5},{5,4},{6,7},{7,6},{8,9},{9,8},{10,11... | collective-permute-start | bytes 2752520 | tf_op jit(solution)/shard_map/ppermute | solution.py:843
  393.9 63.7 %collective-permute-start.49 = (bf16[4928,128]{1,0:T(8,128)(2,1)}, bf16[4928,128]{1,0:T(8,128)(2,1)S(1)}, u32[]{:S(2)}, u32[]{:S(2)}) collective-permute-start(bf16[4928,128]{1,0:T(8,128)(2,1)} %get-tuple-element.608.refs_1_), channel_id=1, source_target_pairs={{0,8},{8,0},{16,24},{24,16},{1,9},{9,1},{17,25},{25,17},{2,10},{10... | collective-permute-start | bytes 3784712 | tf_op jit(solution)/shard_map/ppermute | solution.py:849
  398.5 20.6 %collective-permute-start.57 = (bf16[1824,128]{1,0:T(8,128)(2,1)S(1)}, bf16[1824,128]{1,0:T(8,128)(2,1)S(1)}, u32[]{:S(2)}, u32[]{:S(2)}) collective-permute-start(bf16[1824,128]{1,0:T(8,128)(2,1)S(1)} %add_convert_fusion.1.total), channel_id=1, source_target_pairs={{0,4},{2,6},{4,0},{6,2},{1,5},{3,7},{5,1},{7,3},{8,12},{10,14},{12... | collective-permute-start | bytes 1400840 | tf_op jit(solution)/shard_map/ppermute | solution.py:849
  400.0 13.7 %collective-permute-start.60 = (bf16[1792,128]{1,0:T(8,128)(2,1)}, bf16[1792,128]{1,0:T(8,128)(2,1)S(1)}, u32[]{:S(2)}, u32[]{:S(2)}) collective-permute-start(bf16[1792,128]{1,0:T(8,128)(2,1)} %get-tuple-element.595.refs_0_), channel_id=1, source_target_pairs={{0,16},{8,24},{16,0},{24,8},{1,17},{9,25},{17,1},{25,9},{2,18},{10... | collective-permute-start | bytes 1376264 | tf_op jit(solution)/shard_map/ppermute | solution.py:849
  401.3 59.1 %collective-permute-start.50 = (bf16[4928,128]{1,0:T(8,128)(2,1)S(1)}, bf16[4928,128]{1,0:T(8,128)(2,1)}, u32[]{:S(2)}, u32[]{:S(2)}) collective-permute-start(bf16[4928,128]{1,0:T(8,128)(2,1)S(1)} %copy-done.4), channel_id=1, source_target_pairs={{0,16},{8,24},{16,0},{24,8},{1,17},{9,25},{17,1},{25,9},{2,18},{10... | collective-permute-start | bytes 3784712 | tf_op jit(solution)/shard_map/ppermute | solution.py:849
  402.0 59.5 %collective-permute-start.51 = (bf16[4928,128]{1,0:T(8,128)(2,1)S(1)}, bf16[4928,128]{1,0:T(8,128)(2,1)}, u32[]{:S(2)}, u32[]{:S(2)}) collective-permute-start(bf16[4928,128]{1,0:T(8,128)(2,1)S(1)} %copy-done.5), channel_id=1, source_target_pairs={{0,2},{2,0},{4,6},{6,4},{1,3},{3,1},{5,7},{7,5},{8,10},{10,8},{12,... | collective-permute-start | bytes 3784712 | tf_op jit(solution)/shard_map/ppermute | solution.py:849
  413.7 33.1 %collective-permute-start.61 = (bf16[1792,128]{1,0:T(8,128)(2,1)}, bf16[1792,128]{1,0:T(8,128)(2,1)}, u32[]{:S(2)}, u32[]{:S(2)}) collective-permute-start(bf16[1792,128]{1,0:T(8,128)(2,1)} %get-tuple-element.597.refs_2_), channel_id=1, source_target_pairs={{0,2},{2,0},{4,6},{6,4},{1,3},{3,1},{5,7},{7,5},{8,10},{10,8},{12,... | collective-permute-start | bytes 1376264 | tf_op jit(solution)/shard_map/ppermute | solution.py:849
  419.1 28.8 %collective-permute-start.62 = (bf16[1792,128]{1,0:T(8,128)(2,1)}, bf16[1792,128]{1,0:T(8,128)(2,1)}, u32[]{:S(2)}, u32[]{:S(2)}) collective-permute-start(bf16[1792,128]{1,0:T(8,128)(2,1)} %get-tuple-element.599.refs_4_), channel_id=1, source_target_pairs={{0,8},{8,0},{16,24},{24,16},{1,9},{9,1},{17,25},{25,17},{2,10},{10... | collective-permute-start | bytes 1376264 | tf_op jit(solution)/shard_map/ppermute | solution.py:849
  446.7 8.7 %collective-permute-start.58 = (bf16[912,128]{1,0:T(8,128)(2,1)}, bf16[912,128]{1,0:T(8,128)(2,1)S(1)}, u32[]{:S(2)}, u32[]{:S(2)}) collective-permute-start(bf16[912,128]{1,0:T(8,128)(2,1)} %get-tuple-element.602.refs_0_), channel_id=1, source_target_pairs={{0,16},{8,24},{16,0},{24,8},{1,17},{9,25},{17,1},{25,9},{2,18},{10... | collective-permute-start | bytes 700424 | tf_op jit(solution)/shard_map/ppermute | solution.py:849
  447.9 8.8 %collective-permute-start.59 = (bf16[912,128]{1,0:T(8,128)(2,1)}, bf16[912,128]{1,0:T(8,128)(2,1)S(1)}, u32[]{:S(2)}, u32[]{:S(2)}) collective-permute-start(bf16[912,128]{1,0:T(8,128)(2,1)} %get-tuple-element.604.refs_2_), channel_id=1, source_target_pairs={{0,8},{8,0},{16,24},{24,16},{1,9},{9,1},{17,25},{25,17},{2,10},{10... | collective-permute-start | bytes 700424 | tf_op jit(solution)/shard_map/ppermute | solution.py:849
  455.4 21.6 %collective-permute-start.65 = (bf16[3584,128]{1,0:T(8,128)(2,1)}, bf16[3584,128]{1,0:T(8,128)(2,1)}, u32[]{:S(2)}, u32[]{:S(2)}) collective-permute-start(bf16[3584,128]{1,0:T(8,128)(2,1)} %get-tuple-element.624.refs_1_), channel_id=1, source_target_pairs={{0,8},{8,0},{16,24},{24,16},{1,9},{9,1},{17,25},{25,17},{2,10},{10... | collective-permute-start | bytes 2752520 | tf_op jit(solution)/shard_map/ppermute | solution.py:849
  456.8 21.0 %collective-permute-start.66 = (bf16[3584,128]{1,0:T(8,128)(2,1)}, bf16[3584,128]{1,0:T(8,128)(2,1)}, u32[]{:S(2)}, u32[]{:S(2)}) collective-permute-start(bf16[3584,128]{1,0:T(8,128)(2,1)} %get-tuple-element.626.refs_3_), channel_id=1, source_target_pairs={{0,16},{8,24},{16,0},{24,8},{1,17},{9,25},{17,1},{25,9},{2,18},{10... | collective-permute-start | bytes 2752520 | tf_op jit(solution)/shard_map/ppermute | solution.py:849
  457.7 20.1 %collective-permute-start.67 = (bf16[3584,128]{1,0:T(8,128)(2,1)}, bf16[3584,128]{1,0:T(8,128)(2,1)}, u32[]{:S(2)}, u32[]{:S(2)}) collective-permute-start(bf16[3584,128]{1,0:T(8,128)(2,1)} %get-tuple-element.628.refs_5_), channel_id=1, source_target_pairs={{0,2},{2,0},{4,6},{6,4},{1,3},{3,1},{5,7},{7,5},{8,10},{10,8},{12,... | collective-permute-start | bytes 2752520 | tf_op jit(solution)/shard_map/ppermute | solution.py:849
  460.4 25.1 %collective-permute-start.63 = (bf16[1824,128]{1,0:T(8,128)(2,1)}, bf16[1824,128]{1,0:T(8,128)(2,1)S(1)}, u32[]{:S(2)}, u32[]{:S(2)}) collective-permute-start(bf16[1824,128]{1,0:T(8,128)(2,1)} %get-tuple-element.635.refs_1_), channel_id=1, source_target_pairs={{0,8},{8,0},{16,24},{24,16},{1,9},{9,1},{17,25},{25,17},{2,10},{10... | collective-permute-start | bytes 1400840 | tf_op jit(solution)/shard_map/ppermute | solution.py:849
  461.5 24.1 %collective-permute-start.64 = (bf16[1824,128]{1,0:T(8,128)(2,1)}, bf16[1824,128]{1,0:T(8,128)(2,1)S(1)}, u32[]{:S(2)}, u32[]{:S(2)}) collective-permute-start(bf16[1824,128]{1,0:T(8,128)(2,1)} %get-tuple-element.637.refs_3_), channel_id=1, source_target_pairs={{0,16},{8,24},{16,0},{24,8},{1,17},{9,25},{17,1},{25,9},{2,18},{10... | collective-permute-start | bytes 1400840 | tf_op jit(solution)/shard_map/ppermute | solution.py:849
  (73 other events, 460.2 us)
